TPU v7x, 32 devices: a whole 2x2x4 slice. The times are simulated.
32 devices in a mesh: mem: 4 (over y, core), strip: 8 (over z, x).
Axes of the slice: x: 2, y: 2, z: 4, core: 2. Of those that a mesh axis runs over, the one named last changes fastest.
Arguments:
- gradient: float32 [8, 256, 1024], P('mem', 'strip'), may hold values from -6 to 6
- perturbations: bfloat16 [64, 8, 256, 1024], P('mem', None, 'strip'), may hold values from -6 to 6
- counts: int32 [256, 1024], P('strip'), may hold values from 1 to 4, as said below
Outputs:
- increment: float32 [8, 256, 1024], P('mem', 'strip')
Inputs may be any that keep to these rules, and one draw needn't show every extreme that they name: `counts`: counts are drawn band by band of 32 rows along the first dimension, each band under a cap of its own; some cell reaches 4.
All inputs are finite; a program needn't handle non-finite values.
Results may differ from a plain program's by a relative error of at most 0.0003.
Values sent between devices are 32-bit elements; how exact they have to be, the bound alone decides.
No kernel may reach another device: no remote copies, remote signals or barrier semaphores. Data moves between devices by JAX's collectives and lax.ppermute only.
A program may use at most 64 MiB of HBM per device.

v0:
```python
import math

import jax
import jax.numpy as jnp
from jax import lax
from jax.sharding import PartitionSpec as P

SLOTS = 2
VARS = 4
FIELDS = 8
SWEEPS = 4


COEFF_X = 0.35
COEFF_Y = 0.12


def with_halo(x, sides, width):
    for axis, dim in sides:
        size, length = (lax.axis_size(axis), x.shape[dim])
        up = [(i, (i + 1) % size) for i in range(size - 1)]
        down = [(j, i) for i, j in up]
        last = lax.slice_in_dim(x, length - width, length, axis=dim)
        initial = lax.slice_in_dim(x, 0, width, axis=dim)
        before = lax.ppermute(last, axis, up)
        after = lax.ppermute(initial, axis, down)
        x = jnp.concatenate([before, x, after], axis=dim)
    return x


def advance(padded_x, active):
    padded = jnp.pad(padded_x, ((0, 0), (0, 0), (0, 0), (1, 1)))
    centre = padded[:, :, 1:-1, 1:-1]
    along_x = padded[:, :, 2:, 1:-1] + padded[:, :, :-2, 1:-1] - 2.0 * centre
    along_y = padded[:, :, 1:-1, 2:] + padded[:, :, 1:-1, :-2] - 2.0 * centre
    return centre + active * (COEFF_X * along_x + COEFF_Y * along_y)


def sweep_once(state_field, active):
    padded_x = jnp.pad(state_field, ((0, 0), (0, 0), (1, 1), (0, 0)))
    return advance(padded_x, active)


def diffuse(state_field, counts):
    cells_x = counts.shape[0]
    extended = with_halo(state_field, (("strip", 2),), SWEEPS)
    limits = with_halo(counts, (("strip", 0),), SWEEPS)
    for sweep_index in range(SWEEPS):
        extended = sweep_once(extended, (limits > sweep_index).astype(jnp.float32))
    return extended[:, :, SWEEPS : SWEEPS + cells_x]


def settle(projected, pert_block, counts, own_rows, norm_scale):
    smooth = diffuse(projected, counts)
    first_row = jnp.int32(0)
    results = []
    for row_offset in range(own_rows * lax.axis_size("mem")):
        row_index = first_row + row_offset
        slot_index = row_index // VARS
        pert_row = lax.dynamic_index_in_dim(pert_block, row_index, 1, keepdims=False).astype(
            jnp.float32
        )
        chosen = lax.dynamic_index_in_dim(smooth, slot_index, 1, keepdims=False)
        results.append(jnp.sum(pert_row * chosen, axis=0) * norm_scale)
    return lax.psum_scatter(jnp.stack(results, axis=0), "mem", scatter_dimension=0, tiled=True)


def per_device(gradient, perturbations, counts):
    members = perturbations.shape[0]
    cells_x, cells_y = counts.shape
    own_rows = gradient.shape[0]
    norm_scale = 1.0 / math.sqrt(members * lax.axis_size("mem") * FIELDS)
    zero_sum = jnp.zeros((members, SLOTS, cells_x, cells_y), jnp.float32)
    running = zero_sum
    piece_rows = lax.all_gather(gradient, "mem", axis=0, tiled=True)
    first_row = jnp.int32(0)
    for row_offset in range(piece_rows.shape[0]):
        row_index = first_row + row_offset
        slot_index = row_index // VARS
        pert_row = lax.dynamic_index_in_dim(perturbations, row_index, 1, keepdims=False).astype(
            jnp.float32
        )
        product_row = pert_row * piece_rows[row_offset][None]
        current = lax.dynamic_index_in_dim(running, slot_index, 1, keepdims=False)
        running = lax.dynamic_update_index_in_dim(running, current + product_row, slot_index, 1)
    increment = settle(running, perturbations, counts, own_rows, norm_scale)
    return increment


def solution(mesh):
    return jax.shard_map(
        per_device,
        mesh=mesh,
        in_specs=(P("mem", "strip", None), P("mem", None, "strip", None), P("strip", None)),
        out_specs=P("mem", "strip", None),
        check_vma=False,
    )
```

profile of v0, /device:TPU:3, one launch (start us, length us, event | category | flops | bytes accessed | tf_op | source)
XLA Modules:
  0.0 142.5 jit_solution(13776959407293700840)
XLA Ops:
  6.5 0.7 all-gather.2.cloned.1.call-update
  7.3 0.0 reduce-scatter.2.cloned.1.call-start
  7.3 5.8 %fusion.46 = (bf16[16,1,32,1024]{3,2,1,0:T(8,128)(2,1)S(1)}, bf16[16,1,32,1024]{3,2,1,0:T(8,128)(2,1)}, bf16[16,1,32,1024]{3,2,1,0:T(8,128)(2,1)}, bf16[16,1,32,...) fusion(bf16[16,8,32,1024]{3,2,1,0:T(8,128)(2,1)} %param.4), kind=kLoop, calls=%fused_computation.92 | loop fusion | bytes 16777216 | tf_op jit(solution)/shard_map/jit(dynamic_index_in_dim)/dynamic_slice | solution.py:80
  13.1 14.2 %all-gather.2.cloned.1.call-done = f32[8,32,1024]{2,1,0:T(8,128)} async-done(((f32[2,32,1024]{2,1,0:T(8,128)}), f32[8,32,1024]{2,1,0:T(8,128)}) %all-gather.2.cloned.1.call-update) | async-done | bytes 1048592 | tf_op jit(solution)/shard_map/all_gather | solution.py:75
  27.3 1.4 slice_bitcast_fusion
  28.7 0.7 convert_multiply_fusion.15
  29.4 0.6 dynamic_update_slice.25
  30.0 0.0 copy-start.9
  30.0 1.4 fusion.44
  31.4 2.1 %fusion.42 = f32[16,2,32,1024]{3,0,2,1:T(8,128)S(1)} fusion(f32[16,2,32,1024]{3,0,2,1:T(8,128)S(1)} %fusion.44, f32[32,1024]{1,0:T(8,128)S(1)} %get-tuple-element.30, bf16[16,1,32,1024]{3,2,1,0:T(8,128)(2,1)S(1)} %copy-done.4, f32[32,1024]{1,0:T(8,128)S(1)} %get-tuple-element.31, bf16[16,1,32,1024]{3,2,1,0:T(8,128)(2,1)S(1)} %get-tuple-element.21, ...), kind=kLoop, calls=%fused_computation.67 | loop fusion | flops 4194304 | bytes 5636096 | tf_op jit(solution)/shard_map/jit(dynamic_update_index_in_dim)/dynamic_update_slice | solution.py:85
  33.5 2.8 %fusion.30 = f32[16,2,32,1024]{3,0,2,1:T(8,128)S(1)} fusion(f32[16,2,32,1024]{3,0,2,1:T(8,128)S(1)} %fusion.42, f32[32,1024]{1,0:T(8,128)S(1)} %get-tuple-element.29, f32[32,1024]{1,0:T(8,128)S(1)} %get-tuple-element.30, bf16[16,1,32,1024]{3,2,1,0:T(8,128)(2,1)S(1)} %copy-done.9, bf16[16,1,32,1024]{3,2,1,0:T(8,128)(2,1)S(1)} %copy-done.4, ...), kind=kLoop, calls=%fused_computation.55 | loop fusion | flops 5767168 | bytes 6815744 | tf_op jit(solution)/shard_map/jit(dynamic_update_index_in_dim)/dynamic_update_slice | solution.py:85
  36.3 0.0 copy-start.2
  36.3 0.6 copy.58
  36.9 0.0 copy-start.8
  36.9 0.6 copy-done.2
  37.5 1.1 fusion.43
  38.6 1.5 %constant_dynamic-update-slice_fusion = (f32[16,2,32,1024]{3,0,2,1:T(8,128)S(1)}, f32[16,1,32,1024]{3,0,2,1:T(8,128)S(1)}) fusion(f32[16,2,32,1024]{3,0,2,1:T(8,128)S(1)} %fusion.43, f32[32,1024]{1,0:T(8,128)S(1)} %get-tuple-element.27, bf16[16,1,32,1024]{3,2,1,0:T(8,128)(2,1)S(1)} %copy-done.8, f32[32,1024]{1,0:T(8,128)S(1)} %get-tuple-element.28, ...), kind=kLoop, calls=%fused_computation.91 | loop fusion | flops 3145728 | bytes 8650752 | tf_op jit(solution)/shard_map/jit(dynamic_update_index_in_dim)/dynamic_update_slice | solution.py:85
  40.2 0.8 fusion.41
  41.0 0.0 copy-start.14
  41.0 1.7 %fusion.39 = f32[16,2,32,1024]{3,0,2,1:T(8,128)S(1)} fusion(f32[16,2,32,1024]{3,0,2,1:T(8,128)S(1)} %fusion.41, f32[16,1,32,1024]{3,0,2,1:T(8,128)S(1)} %get-tuple-element.14, f32[32,1024]{1,0:T(8,128)S(1)} %get-tuple-element.25, f32[32,1024]{1,0:T(8,128)S(1)} %get-tuple-element.26, bf16[16,1,32,1024]{3,2,1,0:T(8,128)(2,1)S(1)} %get-tuple-element.15, ...), kind=kLoop, calls=%fused_computation.64 | loop fusion | flops 3145728 | bytes 6553600 | tf_op jit(solution)/shard_map/jit(dynamic_update_index_in_dim)/dynamic_update_slice | solution.py:85
  42.7 0.1 fusion.47
  42.8 3.1 %collective-permute-start = (f32[16,2,4,1024]{3,0,2,1:T(8,128)S(1)}, f32[16,2,4,1024]{3,0,2,1:T(8,128)S(1)}, u32[]{:S(2)}, u32[]{:S(2)}) collective-permute-start(f32[16,2,4,1024]{3,0,2,1:T(8,128)S(1)} %get-tuple-element.23), channel_id=1, source_target_pairs={{0,1},{1,2},{2,3},{3,4},{4,5},{5,6},{6,7},{8,9},{9,10},{10,11},{11... | collective-permute-start | bytes 1572872 | tf_op jit(solution)/shard_map/ppermute | solution.py:25
  45.9 2.2 %collective-permute-start.1 = (f32[16,2,4,1024]{3,0,2,1:T(8,128)S(1)}, f32[16,2,4,1024]{3,0,2,1:T(8,128)S(1)}, u32[]{:S(2)}, u32[]{:S(2)}) collective-permute-start(f32[16,2,4,1024]{3,0,2,1:T(8,128)S(1)} %get-tuple-element.24), channel_id=1, source_target_pairs={{1,0},{2,1},{3,2},{4,3},{5,4},{6,5},{7,6},{9,8},{10,9},{11,10},{12... | collective-permute-start | bytes 1572872 | tf_op jit(solution)/shard_map/ppermute | solution.py:26
  48.2 4.0 %collective-permute-start.2 = (s32[4,1024]{1,0:T(4,128)S(1)}, s32[4,1024]{1,0:T(4,128)S(1)}, u32[]{:S(2)}, u32[]{:S(2)}) collective-permute-start(s32[4,1024]{1,0:T(4,128)S(1)} %get-tuple-element.37), channel_id=1, source_target_pairs={{0,1},{1,2},{2,3},{3,4},{4,5},{5,6},{6,7},{8,9},{9,10},{10,11},{11... | collective-permute-start | bytes 49160 | tf_op jit(solution)/shard_map/ppermute | solution.py:25
  52.2 1.9 %collective-permute-start.3 = (s32[4,1024]{1,0:T(4,128)S(1)}, s32[4,1024]{1,0:T(4,128)S(1)}, u32[]{:S(2)}, u32[]{:S(2)}) collective-permute-start(s32[4,1024]{1,0:T(4,128)S(1)} %get-tuple-element.38), channel_id=1, source_target_pairs={{1,0},{2,1},{3,2},{4,3},{5,4},{6,5},{7,6},{9,8},{10,9},{11,10},{12... | collective-permute-start | bytes 49160 | tf_op jit(solution)/shard_map/ppermute | solution.py:26
  54.1 15.8 %collective-permute-done.2 = s32[4,1024]{1,0:T(4,128)S(1)} collective-permute-done((s32[4,1024]{1,0:T(4,128)S(1)}, s32[4,1024]{1,0:T(4,128)S(1)}, u32[]{:S(2)}, u32[]{:S(2)}) %collective-permute-start.2) | collective-permute-done | bytes 16416 | tf_op jit(solution)/shard_map/ppermute | solution.py:25
  69.9 0.0 collective-permute-done.3
  69.9 0.8 compare_convert_fusion
  70.7 0.0 collective-permute-done
  70.7 0.0 collective-permute-done.1
  70.7 0.8 copy-done.10
  71.5 0.8 pad_maximum_fusion
  72.4 0.9 pad.27
  73.2 5.5 %fusion.5 = f32[16,2,40,1024]{3,0,2,1:T(8,128)S(1)} fusion(f32[16,2,42,1024]{3,0,2,1:T(8,128)S(1)} %pad.27, f32[40,1024]{1,0:T(8,128)} %get-tuple-element.36, f32[16,2,4,1024]{3,0,2,1:T(8,128)} %copy-done.10, f32[16,2,32,1024]{3,0,2,1:T(8,128)S(1)} %fusion.39, f32[16,2,4,1024]{3,0,2,1:T(8,128)S(1)} %collective-permute-done), kind=kLoop, calls=%fused_computation.13 | loop fusion | flops 15728640 | bytes 26640384 | tf_op jit(solution)/shard_map/add | solution.py:36
  78.7 0.0 copy-start.13
  78.7 0.5 pad.29
  79.2 0.4 copy-done.13
  79.6 3.9 %fusion.11 = f32[16,2,40,1024]{3,0,2,1:T(8,128)S(1)} fusion(f32[16,2,40,1024]{3,0,2,1:T(8,128)S(1)} %fusion.5, f32[16,2,42,1024]{3,0,2,1:T(8,128)S(1)} %pad.29, f32[40,1024]{1,0:T(8,128)S(1)} %copy-done.13), kind=kLoop, calls=%fused_computation.19 | loop fusion | flops 13107200 | bytes 26640384 | tf_op jit(solution)/shard_map/add | solution.py:36
  83.5 0.5 pad.31
  84.0 0.4 copy-done.12
  84.4 3.9 %fusion.17 = f32[16,2,40,1024]{3,0,2,1:T(8,128)S(1)} fusion(f32[16,2,40,1024]{3,0,2,1:T(8,128)S(1)} %fusion.11, f32[16,2,42,1024]{3,0,2,1:T(8,128)S(1)} %pad.31, f32[40,1024]{1,0:T(8,128)S(1)} %copy-done.12), kind=kLoop, calls=%fused_computation.25 | loop fusion | flops 13107200 | bytes 26640384 | tf_op jit(solution)/shard_map/add | solution.py:36
  88.2 0.9 pad.33
  89.1 4.0 %fusion.23 = f32[16,2,40,1024]{3,0,2,1:T(8,128)S(1)} fusion(f32[16,2,40,1024]{3,0,2,1:T(8,128)S(1)} %fusion.17, f32[16,2,42,1024]{3,0,2,1:T(8,128)S(1)} %pad.33, f32[40,1024]{1,0:T(8,128)S(1)} %get-tuple-element.33), kind=kLoop, calls=%fused_computation.31 | loop fusion | flops 13107200 | bytes 26640384 | tf_op jit(solution)/shard_map/add | solution.py:36
  93.1 0.0 copy-done.1
  93.2 15.8 %fusion.40 = (f32[32,1024]{1,0:T(8,128)S(1)}, f32[32,1024]{1,0:T(8,128)S(1)}, f32[32,1024]{1,0:T(8,128)S(1)}, f32[32,1024]{1,0:T(8,128)S(1)}, f32[32,1024]{1,0:T...) fusion(f32[16,2,40,1024]{3,0,2,1:T(8,128)S(1)} %fusion.23, ...), kind=kLoop, calls=%fused_computation.65 | loop fusion | flops 12320768 | bytes 13631488 | tf_op jit(solution)/shard_map/reduce_sum | solution.py:64
  109.2 1.0 copy-done.11
  110.2 0.0 reduce-scatter.2.cloned.1.call-update
  110.2 25.5 %reduce-scatter.2.cloned.1.call-done = f32[2,32,1024]{2,1,0:T(8,128)} async-done(((f32[8,32,1024]{2,1,0:T(8,128)}), f32[2,32,1024]{2,1,0:T(8,128)}) %reduce-scatter.2.cloned.1.call-update) | async-done | bytes 262160 | tf_op jit(solution)/shard_map/reduce_scatter | solution.py:65
  (29 shorter events, 0.2 us)
Async XLA Ops:
  6.5 20.8 %all-gather.2.cloned.1.call-start = ((), (), s32[]{:S(2)}) async-start(), calls=%async_computation.1 | async-start | bytes 1310720 | tf_op jit(solution)/shard_map/all_gather | solution.py:75
  7.3 128.4 %reduce-scatter.2.cloned.1.call-start = ((), (), s32[]{:S(2)}) async-start(), calls=%async_computation.2 | async-start | bytes 1310720 | tf_op jit(solution)/shard_map/reduce_scatter | solution.py:65
  13.1 27.8 %copy-start.6 = (bf16[16,1,32,1024]{3,2,1,0:T(8,128)(2,1)}, bf16[16,1,32,1024]{3,2,1,0:T(8,128)(2,1)S(1)}, u32[]{:S(2)}) copy-start(bf16[16,1,32,1024]{3,2,1,0:T(8,128)(2,1)S(1)} %get-tuple-element.15) | copy-start | bytes 3145732
  29.3 2.0 %copy-start.4 = (bf16[16,1,32,1024]{3,2,1,0:T(8,128)(2,1)S(1)}, bf16[16,1,32,1024]{3,2,1,0:T(8,128)(2,1)}, u32[]{:S(2)}) copy-start(bf16[16,1,32,1024]{3,2,1,0:T(8,128)(2,1)} %get-tuple-element.20) | copy-start | bytes 3145732
  30.0 3.5 %copy-start.9 = (bf16[16,1,32,1024]{3,2,1,0:T(8,128)(2,1)S(1)}, bf16[16,1,32,1024]{3,2,1,0:T(8,128)(2,1)}, u32[]{:S(2)}) copy-start(bf16[16,1,32,1024]{3,2,1,0:T(8,128)(2,1)} %get-tuple-element.19) | copy-start | bytes 3145732
  36.3 1.2 copy-start.2
  36.9 1.7 %copy-start.8 = (bf16[16,1,32,1024]{3,2,1,0:T(8,128)(2,1)S(1)}, bf16[16,1,32,1024]{3,2,1,0:T(8,128)(2,1)}, u32[]{:S(2)}) copy-start(bf16[16,1,32,1024]{3,2,1,0:T(8,128)(2,1)} %get-tuple-element.17) | copy-start | bytes 3145732
  38.6 1.6 %copy-start = (bf16[16,1,32,1024]{3,2,1,0:T(8,128)(2,1)S(1)}, bf16[16,1,32,1024]{3,2,1,0:T(8,128)(2,1)}, u32[]{:S(2)}) copy-start(bf16[16,1,32,1024]{3,2,1,0:T(8,128)(2,1)} %get-tuple-element.16) | copy-start | bytes 3145732
  41.0 7.2 %copy-start.14 = (s32[32,1024]{1,0:T(8,128)S(1)}, s32[32,1024]{1,0:T(8,128)}, u32[]{:S(2)}) copy-start(s32[32,1024]{1,0:T(8,128)} %param.5) | copy-start | bytes 393220
  42.8 27.9 %collective-permute-start = (f32[16,2,4,1024]{3,0,2,1:T(8,128)S(1)}, f32[16,2,4,1024]{3,0,2,1:T(8,128)S(1)}, u32[]{:S(2)}, u32[]{:S(2)}) collective-permute-start(f32[16,2,4,1024]{3,0,2,1:T(8,128)S(1)} %get-tuple-element.23), channel_id=1, source_target_pairs={{0,1},{1,2},{2,3},{3,4},{4,5},{5,6},{6,7},{8,9},{9,10},{10,11},{11... | collective-permute-start | bytes 1572872 | tf_op jit(solution)/shard_map/ppermute | solution.py:25
  45.9 24.8 %collective-permute-start.1 = (f32[16,2,4,1024]{3,0,2,1:T(8,128)S(1)}, f32[16,2,4,1024]{3,0,2,1:T(8,128)S(1)}, u32[]{:S(2)}, u32[]{:S(2)}) collective-permute-start(f32[16,2,4,1024]{3,0,2,1:T(8,128)S(1)} %get-tuple-element.24), channel_id=1, source_target_pairs={{1,0},{2,1},{3,2},{4,3},{5,4},{6,5},{7,6},{9,8},{10,9},{11,10},{12... | collective-permute-start | bytes 1572872 | tf_op jit(solution)/shard_map/ppermute | solution.py:26
  48.2 21.7 %collective-permute-start.2 = (s32[4,1024]{1,0:T(4,128)S(1)}, s32[4,1024]{1,0:T(4,128)S(1)}, u32[]{:S(2)}, u32[]{:S(2)}) collective-permute-start(s32[4,1024]{1,0:T(4,128)S(1)} %get-tuple-element.37), channel_id=1, source_target_pairs={{0,1},{1,2},{2,3},{3,4},{4,5},{5,6},{6,7},{8,9},{9,10},{10,11},{11... | collective-permute-start | bytes 49160 | tf_op jit(solution)/shard_map/ppermute | solution.py:25
  52.2 17.7 %collective-permute-start.3 = (s32[4,1024]{1,0:T(4,128)S(1)}, s32[4,1024]{1,0:T(4,128)S(1)}, u32[]{:S(2)}, u32[]{:S(2)}) collective-permute-start(s32[4,1024]{1,0:T(4,128)S(1)} %get-tuple-element.38), channel_id=1, source_target_pairs={{1,0},{2,1},{3,2},{4,3},{5,4},{6,5},{7,6},{9,8},{10,9},{11,10},{12... | collective-permute-start | bytes 49160 | tf_op jit(solution)/shard_map/ppermute | solution.py:26
  70.7 0.8 copy-start.10
  78.7 0.9 copy-start.13
  83.5 0.9 copy-start.12
  89.1 4.0 %copy-start.1 = (bf16[16,1,32,1024]{3,2,1,0:T(8,128)(2,1)S(1)}, bf16[16,1,32,1024]{3,2,1,0:T(8,128)(2,1)}, u32[]{:S(2)}) copy-start(bf16[16,1,32,1024]{3,2,1,0:T(8,128)(2,1)} %get-tuple-element.16) | copy-start | bytes 3145732
  89.1 4.0 %copy-start.3 = (bf16[16,1,32,1024]{3,2,1,0:T(8,128)(2,1)S(1)}, bf16[16,1,32,1024]{3,2,1,0:T(8,128)(2,1)}, u32[]{:S(2)}) copy-start(bf16[16,1,32,1024]{3,2,1,0:T(8,128)(2,1)} %get-tuple-element.18) | copy-start | bytes 3145732
  89.1 4.0 %copy-start.5 = (bf16[16,1,32,1024]{3,2,1,0:T(8,128)(2,1)S(1)}, bf16[16,1,32,1024]{3,2,1,0:T(8,128)(2,1)}, u32[]{:S(2)}) copy-start(bf16[16,1,32,1024]{3,2,1,0:T(8,128)(2,1)} %get-tuple-element.20) | copy-start | bytes 3145732
  89.1 4.0 %copy-start.7 = (bf16[16,1,32,1024]{3,2,1,0:T(8,128)(2,1)S(1)}, bf16[16,1,32,1024]{3,2,1,0:T(8,128)(2,1)}, u32[]{:S(2)}) copy-start(bf16[16,1,32,1024]{3,2,1,0:T(8,128)(2,1)} %copy-done.6) | copy-start | bytes 3145732
  109.2 1.0 copy-start.11
Sparse Core Ops, SparseCore 0:
  8.9 18.3 all-gather.1
  110.3 25.2 reduce-scatter.1
where the time goes:
time: 144 us; the launch traced here: 143 us
  waiting for transfers between devices  56.2 us (39%)
  other arithmetic  46.8 us (32%)
  local copies, waits for them, and re-layouts  14.4 us (10%)
  between operations  13.8 us (10%)
  starting transfers between devices  11.3 us (8%)
    reduce_scatter x1, waiting for transfers between devices, settle(): lax.psum_scatter(jnp.stack(results, axis=0), 'mem', scatter_dimension=0,...  25.5 us
    add x4, other arithmetic, advance(): return centre + active * (COEFF_X * along_x + COEFF_Y * along_y)  17.1 us
    reduce_sum x1, other arithmetic, settle(): results.append(jnp.sum(pert_row * chosen, axis=0) * norm_scale)  15.8 us
    ppermute x2, waiting for transfers between devices, with_halo(): before = lax.ppermute(last, axis, up)  15.8 us
    all_gather x1, waiting for transfers between devices, per_device(): piece_rows = lax.all_gather(gradient, 'mem', axis=0, tiled=True)  14.2 us
    dynamic_update_slice x7, other arithmetic, per_device(): lax.dynamic_update_index_in_dim(running, current + product_row, slot_inde...  11.4 us
    ppermute x2, starting transfers between devices, with_halo(): before = lax.ppermute(last, axis, up)  7.09 us
    dynamic_slice x1, local copies, waits for them, and re-layouts, per_device(): lax.dynamic_index_in_dim(perturbations, row_index, 1, keepdims=False)  5.8 us
  transfers between devices with their start and end apart: 6, of which 3 were waited for; matrix products, arithmetic and copies ran while one was open for 5% of the time, Pallas kernels for 0%

commit v1 on v0

v1 whole, which is shorter than its diff:
```python
import math

import jax
import jax.numpy as jnp
from jax import lax
from jax.experimental import pallas as pl
from jax.experimental.pallas import tpu as pltpu
from jax.sharding import PartitionSpec as P

SLOTS = 2
VARS = 4
FIELDS = 8
SWEEPS = 4

COEFF_X = 0.35
COEFF_Y = 0.12
CENTRE = 1.0 - 2.0 * COEFF_X - 2.0 * COEFF_Y
RATIO = COEFF_Y / COEFF_X

LANES = 128
TILE = 8
HALF = 16
VMEM_BYTES = 40 * 2**20


def kernel_call(body, out_shape, scratch, flops, name):
    def call(*args):
        moved = sum(a.size * a.dtype.itemsize for a in args)
        return pl.pallas_call(
            body,
            out_shape=out_shape,
            in_specs=[pl.BlockSpec(memory_space=pltpu.VMEM)] * len(args),
            out_specs=jax.tree.map(lambda _: pl.BlockSpec(memory_space=pltpu.VMEM), out_shape),
            scratch_shapes=scratch,
            compiler_params=pltpu.CompilerParams(vmem_limit_bytes=VMEM_BYTES),
            cost_estimate=pl.CostEstimate(flops=flops, bytes_accessed=moved, transcendentals=0),
            name=name,
        )(*args)

    return call


def lane_masks():
    lane = lax.broadcasted_iota(jnp.int32, (TILE, LANES), 1)
    return lane == 0, lane == LANES - 1


def top_half():
    return lax.broadcasted_iota(jnp.int32, (TILE, LANES), 0) < TILE // 2


def cols(j):
    return pl.ds(j * LANES, LANES)


def sides(values, first, last):
    before = [pltpu.roll(v, 1, 1) for v in values]
    after = [pltpu.roll(v, LANES - 1, 1) for v in values]
    zero = jnp.zeros_like(values[0])
    count = len(values)
    sums = []
    for j in range(count):
        left = jnp.where(first, before[j - 1] if j else zero, before[j])
        right = jnp.where(last, after[j + 1] if j + 1 < count else zero, after[j])
        sums.append(left + right)
    return sums


def fields_of(local, own):
    shares = VARS // own
    mem = lax.axis_index("mem")
    slot = mem // shares
    slot = slot if local else SLOTS - 1 - slot
    share = mem % shares
    return [slot * VARS + at * own + k for at in (share, shares - 1 - share) for k in range(own)]


def project_edges(local, p_ref, ga_ref, gb_ref, *rest):
    if local:
        counts_ref, e_ref, o_ref, u_ref = rest
    else:
        e_ref, o_ref, u_ref = rest
    members, _, rows, ny = p_ref.shape
    own = ga_ref.shape[0]
    grows = ga_ref.shape[1]
    even = lax.axis_index("strip") % 2 == 0
    half = top_half()
    fields = fields_of(local, own)
    grads = [(ga_ref, k) for k in range(own)] + [(gb_ref, k) for k in range(own)]

    def put(row, j, top, bottom):
        e_ref[row, :, cols(j)] = jnp.where(even, bottom, top)
        o_ref[row, :, cols(j)] = jnp.where(even, top, bottom)

    if local:
        for j in range(ny // LANES):
            top = counts_ref[0:TILE, cols(j)].astype(jnp.float32)
            bottom = counts_ref[rows - TILE : rows, cols(j)].astype(jnp.float32)
            put(members // 2, j, top, pltpu.roll(bottom, TILE // 2, 0))

    def pair(q, carry):
        for j in range(ny // LANES):
            tops, bottoms = [], []
            for m in (2 * q, 2 * q + 1):
                top = bottom = None
                for f, (g_ref, k) in zip(fields, grads):
                    low = p_ref[m, f, 0:HALF, cols(j)].astype(jnp.float32)[0:TILE]
                    high = p_ref[m, f, rows - HALF : rows, cols(j)].astype(jnp.float32)[HALF - TILE :]
                    low = low * g_ref[k, 0:TILE, cols(j)]
                    high = high * g_ref[k, grows - TILE : grows, cols(j)]
                    top = low if top is None else top + low
                    bottom = high if bottom is None else bottom + high
                u_ref[m, 0:TILE, cols(j)] = top
                u_ref[m, TILE : 2 * TILE, cols(j)] = bottom
                tops.append(top)
                bottoms.append(bottom)
            top = jnp.where(half, tops[0], pltpu.roll(tops[1], TILE // 2, 0))
            bottom = jnp.where(half, pltpu.roll(bottoms[0], TILE // 2, 0), bottoms[1])
            put(q, j, top, bottom)
        return carry

    lax.fori_loop(0, members // 2, pair, 0)


def interior(local, p_ref, ga_ref, gb_ref, counts_ref, own_ref, other_ref, coef, buf_a, buf_b):
    members, _, rows, ny = p_ref.shape
    own = ga_ref.shape[0]
    blocks = ny // LANES
    group = buf_a.shape[0]
    first, last = lane_masks()
    fields = fields_of(local, own)
    grads = [(ga_ref, k) for k in range(own)] + [(gb_ref, k) for k in range(own)]
    sums = [(own_ref, k) for k in range(own)] + [(other_ref, k) for k in range(own)]
    for t in range(1, SWEEPS):
        for j in range(blocks):
            active = (counts_ref[:, cols(j)] > t).astype(jnp.float32)
            coef[t - 1, 0, j] = active * COEFF_X
            coef[t - 1, 1, j] = 1.0 - active * (1.0 - CENTRE)
    zero = jnp.zeros((TILE, LANES), jnp.float32)
    for buf in (buf_a, buf_b):
        for i in range(group):
            for j in range(blocks):
                buf[i, j, 0:TILE] = zero
                buf[i, j, TILE + rows :] = zero
    own_ref[...] = jnp.zeros_like(own_ref)
    other_ref[...] = jnp.zeros_like(other_ref)

    def step(s, carry):
        base = s * group
        for r in range(0, rows, HALF):
            for j in range(blocks):
                weights = [g_ref[k, r : r + HALF, cols(j)] for g_ref, k in grads]
                for i in range(group):
                    total = None
                    for f, w in zip(fields, weights):
                        term = p_ref[base + i, f, r : r + HALF, cols(j)].astype(jnp.float32) * w
                        total = term if total is None else total + term
                    buf_a[i, j, TILE + r : TILE + r + HALF] = total
        src, dst = buf_a, buf_b
        for t in range(SWEEPS):
            for r in range(0, rows, TILE):
                at = TILE + r
                for i in range(group):
                    centre = [src[i, j, at : at + TILE] for j in range(blocks)]
                    lateral = sides(centre, first, last)
                    for j in range(blocks):
                        stacked = src[i, j, at - 1 : at - 1 + TILE] + src[i, j, at + 1 : at + 1 + TILE]
                        moved = stacked + RATIO * lateral[j]
                        if t == 0:
                            new = COEFF_X * moved + CENTRE * centre[j]
                        else:
                            new = coef[t - 1, 0, j, r : r + TILE] * moved + coef[t - 1, 1, j, r : r + TILE] * centre[j]
                        dst[i, j, at : at + TILE] = new
            src, dst = dst, src
        for r in range(0, rows, HALF):
            for j in range(blocks):
                smooth = [src[i, j, TILE + r : TILE + r + HALF] for i in range(group)]
                for f, (ref, k) in zip(fields, sums):
                    total = ref[k, r : r + HALF, cols(j)]
                    for i in range(group):
                        total = total + p_ref[base + i, f, r : r + HALF, cols(j)].astype(jnp.float32) * smooth[i]
                    ref[k, r : r + HALF, cols(j)] = total
        return carry

    lax.fori_loop(0, members // group, step, 0)


def edges(local, p_ref, u_ref, e_ref, o_ref, ce_ref, co_ref, counts_ref, own_ref, other_ref, coef, buf_a, buf_b, halo):
    members, _, rows, ny = p_ref.shape
    own = own_ref.shape[0]
    blocks = ny // LANES
    first, last = lane_masks()
    half = top_half()
    even = lax.axis_index("strip") % 2 == 0
    fields = fields_of(local, own)
    sums = [(own_ref, k) for k in range(own)] + [(other_ref, k) for k in range(own)]
    crow = ce_ref.shape[0] - 1
    for j in range(blocks):
        e, o = ce_ref[crow, :, cols(j)], co_ref[crow, :, cols(j)]
        above, below = jnp.where(even, o, e), jnp.where(even, e, o)
        halo[0, j, 4:12] = above
        halo[0, j, 24:32] = below
        halo[0, j, 8:16] = counts_ref[0:TILE, cols(j)].astype(jnp.float32)
        halo[0, j, 16:24] = counts_ref[rows - TILE : rows, cols(j)].astype(jnp.float32)
        for t in range(SWEEPS):
            active = (halo[0, j, 0:32] > t).astype(jnp.float32)
            coef[t, 0, j, 0:32] = active * COEFF_X
            coef[t, 1, j, 0:32] = 1.0 - active * (1.0 - CENTRE)
        for buf in (buf_a, buf_b):
            for i in range(2):
                buf[i, j] = jnp.zeros_like(buf[i, j])
        coef[0, 0, j, 32:40] = jnp.zeros((TILE, LANES), jnp.float32)
        coef[0, 1, j, 32:40] = jnp.zeros((TILE, LANES), jnp.float32)
    own_ref[...] = jnp.zeros_like(own_ref)
    other_ref[...] = jnp.zeros_like(other_ref)
    starts = [(5, 13, 21), (6, 18), (6, 18)]

    def step(q, carry):
        for j in range(blocks):
            e, o = e_ref[q, :, cols(j)], o_ref[q, :, cols(j)]
            above, below = jnp.where(even, o, e), jnp.where(even, e, o)
            buf_a[0, j, 4:12] = above
            buf_a[0, j, 24:32] = below
            buf_a[1, j, 0:8] = above
            buf_a[1, j, 20:28] = below
            for i in range(2):
                buf_a[i, j, 8:16] = u_ref[2 * q + i, 0:TILE, cols(j)]
                buf_a[i, j, 16:24] = u_ref[2 * q + i, TILE : 2 * TILE, cols(j)]
        src, dst = buf_a, buf_b
        for t in range(SWEEPS - 1):
            for at in starts[t]:
                weights = [[coef[t, c, j, at : at + TILE] for j in range(blocks)] for c in range(2)]
                for i in range(2):
                    centre = [src[i, j, at : at + TILE] for j in range(blocks)]
                    lateral = sides(centre, first, last)
                    for j in range(blocks):
                        stacked = src[i, j, at - 1 : at - 1 + TILE] + src[i, j, at + 1 : at + 1 + TILE]
                        moved = stacked + RATIO * lateral[j]
                        dst[i, j, at : at + TILE] = weights[0][j] * moved + weights[1][j] * centre[j]
            src, dst = dst, src
        both = lambda ref, *at: jnp.where(half, ref[(*at[:-1], pl.ds(8 + at[-1], TILE))], ref[(*at[:-1], pl.ds(16 + at[-1], TILE))])
        t = SWEEPS - 1
        weights = [[both(coef, t, c, j, 0) for j in range(blocks)] for c in range(2)]
        smooth = []
        for i in range(2):
            centre = [both(src, i, j, 0) for j in range(blocks)]
            lateral = sides(centre, first, last)
            result = []
            for j in range(blocks):
                moved = both(src, i, j, -1) + both(src, i, j, 1) + RATIO * lateral[j]
                result.append(weights[0][j] * moved + weights[1][j] * centre[j])
            smooth.append(result)
        for j in range(blocks):
            for f, (ref, k) in zip(fields, sums):
                total = ref[k, :, cols(j)]
                for i in range(2):
                    low = p_ref[2 * q + i, f, 0:HALF, cols(j)].astype(jnp.float32)[0:TILE]
                    high = p_ref[2 * q + i, f, rows - HALF : rows, cols(j)].astype(jnp.float32)[HALF - TILE :]
                    total = total + jnp.where(half, low, high) * smooth[i][j]
                ref[k, :, cols(j)] = total
        return carry

    lax.fori_loop(0, members // 2, step, 0)


def finish(scale, a_ref, b_ref, c_ref, ea_ref, eb_ref, ec_ref, out_ref):
    own, rows, ny = out_ref.shape
    half = top_half()
    for k in range(own):
        for j in range(ny // LANES):
            edge = ea_ref[k, :, cols(j)] + eb_ref[k, :, cols(j)] + ec_ref[k, :, cols(j)]
            inner = a_ref[k, :, cols(j)] + b_ref[k, :, cols(j)] + c_ref[k, :, cols(j)]
            out_ref[k, 0:TILE, cols(j)] = jnp.where(half, edge, inner[0:TILE]) * scale
            out_ref[k, TILE : rows - TILE, cols(j)] = inner[TILE : rows - TILE] * scale
            out_ref[k, rows - TILE :, cols(j)] = jnp.where(half, inner[rows - TILE :], edge) * scale


def per_device(gradient, perturbations, counts):
    members, _, rows, ny = perturbations.shape
    own = gradient.shape[0]
    mem, strips = lax.axis_size("mem"), lax.axis_size("strip")
    shares = VARS // own
    blocks = ny // LANES
    assert shares == 2 and mem == shares * SLOTS and members % 2 == 0
    scale = 1.0 / math.sqrt(members * mem * FIELDS)
    f32 = jnp.float32

    near = [(i, i ^ 1) for i in range(mem)]
    across = [(i, (i + shares) % mem) for i in range(mem)]
    even = [(i, i ^ 1) for i in range(strips) if i ^ 1 < strips]
    odd = [(i, i + 1) for i in range(1, strips - 1, 2)]
    odd = odd + [(j, i) for i, j in odd]

    def shape(*dims):
        return jax.ShapeDtypeStruct(dims, f32)

    def window(*lead):
        return pltpu.VMEM((*lead, blocks, 40, LANES), f32)

    def send_shapes(extra):
        pairs = members // 2
        return (shape(pairs + extra, TILE, ny), shape(pairs + extra, TILE, ny), shape(members, 2 * TILE, ny))

    tile_flops = members * ny * 2 * VARS

    def call_edges(local):
        outs = (shape(own, TILE, ny), shape(own, TILE, ny))
        return kernel_call(
            lambda *refs: edges(local, *refs), outs,
            [window(SWEEPS, 2), window(2), window(2), window(1)],
            tile_flops * 200, "edges",
        )

    def call_interior(local):
        outs = (shape(own, rows, ny), shape(own, rows, ny))
        buf = pltpu.VMEM((2, blocks, rows + 2 * TILE, LANES), f32)
        return kernel_call(
            lambda *refs: interior(local, *refs), outs,
            [pltpu.VMEM((SWEEPS - 1, 2, blocks, rows, LANES), f32), buf, buf],
            tile_flops * 400, "interior",
        )

    def call_project(local):
        return kernel_call(
            lambda *refs: project_edges(local, *refs), send_shapes(1 if local else 0), [], tile_flops * 20, "project"
        )

    partner = lax.ppermute(gradient, "mem", near)
    rim = jnp.concatenate([gradient[:, :TILE], gradient[:, rows - TILE :]], axis=1)
    rim_far = lax.ppermute(rim, "mem", across)
    rim_far_partner = lax.ppermute(rim_far, "mem", near)

    e0, o0, u0 = call_project(True)(perturbations, gradient, partner, counts)
    e0 = lax.ppermute(e0, "strip", even)
    o0 = lax.ppermute(o0, "strip", odd)
    e1, o1, u1 = call_project(False)(perturbations, rim_far, rim_far_partner)
    e1 = lax.ppermute(e1, "strip", even)
    o1 = lax.ppermute(o1, "strip", odd)

    far = lax.ppermute(gradient, "mem", across)
    far_partner = lax.ppermute(far, "mem", near)
    own0, other0 = call_interior(True)(perturbations, gradient, partner, counts)
    own1, other1 = call_interior(False)(perturbations, far, far_partner, counts)
    near0 = lax.ppermute(other0, "mem", near)
    far_sum = own1 + lax.ppermute(other1, "mem", near)
    far1 = lax.ppermute(far_sum, "mem", across)

    eown0, eother0 = call_edges(True)(perturbations, u0, e0, o0, e0, o0, counts)
    eown1, eother1 = call_edges(False)(perturbations, u1, e1, o1, e0, o0, counts)
    enear0 = lax.ppermute(eother0, "mem", near)
    efar_sum = eown1 + lax.ppermute(eother1, "mem", near)
    efar1 = lax.ppermute(efar_sum, "mem", across)

    return kernel_call(
        lambda *refs: finish(scale, *refs), shape(own, rows, ny), [], own * rows * ny * 4, "finish"
    )(own0, near0, far1, eown0, enear0, efar1)


def solution(mesh):
    return jax.shard_map(
        per_device,
        mesh=mesh,
        in_specs=(P("mem", "strip", None), P("mem", None, "strip", None), P("strip", None)),
        out_specs=P("mem", "strip", None),
        check_vma=False,
    )
```

time: 144 us -> 66.6 us (0.46)
  the two profiles are of different devices: /device:TPU:3 before, /device:TPU:0 now
where the time goes in v1:
time: 66.6 us; the launch traced here: 66.4 us
  waiting for transfers between devices  26.7 us (40%)
  Pallas kernels  21.5 us (32%)
  starting transfers between devices  12.9 us (19%)
  local copies, waits for them, and re-layouts  5.18 us (8%)
    pallas_call x7, Pallas kernels, call(): pl.pallas_call(body, out_shape=out_shape, in_specs=[pl.BlockSpec(memory_s...  21.5 us
    ppermute x1, waiting for transfers between devices, per_device(): e1 = lax.ppermute(e1, 'strip', even)  10.5 us
    ppermute x1, waiting for transfers between devices, per_device(): far = lax.ppermute(gradient, 'mem', across)  5.63 us
    unnamed x8, local copies, waits for them, and re-layouts  4.29 us
    ppermute x1, waiting for transfers between devices, per_device(): rim_far = lax.ppermute(rim, 'mem', across)  3.94 us
    ppermute x1, waiting for transfers between devices, per_device(): e0 = lax.ppermute(e0, 'strip', even)  3.88 us
    ppermute x1, starting transfers between devices, per_device(): far = lax.ppermute(gradient, 'mem', across)  2.97 us
    ppermute x1, waiting for transfers between devices, per_device(): efar1 = lax.ppermute(efar_sum, 'mem', across)  2.74 us
  transfers between devices with their start and end apart: 15, of which 5 were waited for; matrix products, arithmetic and copies ran while one was open for 1% of the time, Pallas kernels for 31%

profile of v1, /device:TPU:0, one launch (start us, length us, event | category | flops | bytes accessed | tf_op | source)
XLA Modules:
  0.0 66.4 jit_solution(12350064246209948786)
XLA Ops:
  0.0 3.0 %collective-permute-start.2 = (f32[2,32,1024]{2,1,0:T(8,128)}, f32[2,32,1024]{2,1,0:T(8,128)S(1)}, u32[]{:S(2)}, u32[]{:S(2)}) collective-permute-start(f32[2,32,1024]{2,1,0:T(8,128)} %refs_1_.3), channel_id=1, source_target_pairs={{0,16},{8,24},{16,0},{24,8},{1,17},{9,25},{17,1},{25,9},{2,18},{10... | collective-permute-start | bytes 786440 | tf_op jit(solution)/shard_map/ppermute | solution.py:340
  3.0 0.9 %fusion = (f32[2,8,1024]{2,1,0:T(8,128)S(1)}, f32[2,8,1024]{2,1,0:T(8,128)S(1)}) fusion(f32[2,32,1024]{2,1,0:T(8,128)} %refs_1_.3), kind=kLoop, calls=%fused_computation.1 | loop fusion | bytes 262144 | tf_op jit(solution)/shard_map/slice | solution.py:329
  3.9 5.6 %collective-permute-done.2.refs_1_ = f32[2,32,1024]{2,1,0:T(8,128)S(1)} collective-permute-done((f32[2,32,1024]{2,1,0:T(8,128)}, f32[2,32,1024]{2,1,0:T(8,128)S(1)}, u32[]{:S(2)}, u32[]{:S(2)}) %collective-permute-start.2) | collective-permute-done | bytes 262176 | tf_op jit(solution)/shard_map/ppermute | solution.py:340
  9.5 0.0 collective-permute-start.3
  9.5 0.0 copy-start.2
  9.5 1.8 %collective-permute-start.9 = (f32[2,16,1024]{2,1,0:T(8,128)S(1)}, f32[2,16,1024]{2,1,0:T(8,128)S(1)}, u32[]{:S(2)}, u32[]{:S(2)}) collective-permute-start(f32[2,16,1024]{2,1,0:T(8,128)S(1)} %pad_maximum_fusion), channel_id=1, source_target_pairs={{0,16},{8,24},{16,0},{24,8},{1,17},{9,25},{17,1},{25,9},{2,18},{10... | collective-permute-start | bytes 393224 | tf_op jit(solution)/shard_map/ppermute | solution.py:330
  11.3 0.2 collective-permute-start
  11.5 3.9 %collective-permute-done.9.refs_1_ = f32[2,16,1024]{2,1,0:T(8,128)S(1)} collective-permute-done((f32[2,16,1024]{2,1,0:T(8,128)S(1)}, f32[2,16,1024]{2,1,0:T(8,128)S(1)}, u32[]{:S(2)}, u32[]{:S(2)}) %collective-permute-start.9) | collective-permute-done | bytes 131104 | tf_op jit(solution)/shard_map/ppermute | solution.py:330
  15.5 0.0 collective-permute-start.10
  15.5 0.0 collective-permute-done.3.refs_2_
  15.5 0.0 copy-start
  15.5 3.4 %copy-done = bf16[16,8,32,1024]{3,2,1,0:T(8,128)(2,1)S(1)} copy-done((bf16[16,8,32,1024]{3,2,1,0:T(8,128)(2,1)S(1)}, bf16[16,8,32,1024]{3,2,1,0:T(8,128)(2,1)}, u32[]{:S(2)}) %copy-start) | copy-done | bytes 8388632
  18.9 0.0 copy-start.1
  18.9 0.9 %copy-done.1 = s32[32,1024]{1,0:T(8,128)S(1)} copy-done((s32[32,1024]{1,0:T(8,128)S(1)}, s32[32,1024]{1,0:T(8,128)}, u32[]{:S(2)}) %copy-start.1) | copy-done | bytes 131096
  19.8 0.0 copy-start.3
  19.8 5.7 %interior.3 = (f32[2,32,1024]{2,1,0:T(8,128)S(1)}, f32[2,32,1024]{2,1,0:T(8,128)S(1)}) custom-call(bf16[16,8,32,1024]{3,2,1,0:T(8,128)(2,1)S(1)} %copy-done, f32[2,32,1024]{2,1,0:T(8,128)S(1)} %collective-permute-done.2.refs_1_, f32[2,32,1024]{2,1,0:T(8,128)S(1)} %collective-permute-done.3.refs_2_, s32[32,1024]{1,0:T(8,128)S(1)} %copy-done.1), custom_call_target="tpu_custom_call" | custom-call | flops 52428800 | bytes 9043968 | tf_op jit(solution)/shard_map/interior/pallas_call | solution.py:29
  25.5 0.6 collective-permute-start.4
  26.1 0.0 collective-permute-done.10.refs_2_
  26.1 0.5 project.3
  26.6 1.8 %collective-permute-start.11 = (f32[8,8,1024]{2,1,0:T(8,128)S(1)}, f32[8,8,1024]{2,1,0:T(8,128)S(1)}, u32[]{:S(2)}, u32[]{:S(2)}) collective-permute-start(f32[8,8,1024]{2,1,0:T(8,128)S(1)} %get-tuple-element.29), channel_id=1, source_target_pairs={{0,1},{1,0},{2,3},{3,2},{4,5},{5,4},{6,7},{7,6},{8,9},{9,8},{10,11... | collective-permute-start | bytes 786440 | tf_op jit(solution)/shard_map/ppermute | solution.py:337
  28.3 0.0 collective-permute-done.refs_2_
  28.3 0.0 copy-done.2
  28.4 0.0 copy-done.3
  28.4 0.5 project.2
  28.9 0.4 collective-permute-start.6
  29.3 0.7 %collective-permute-start.7 = (f32[9,8,1024]{2,1,0:T(8,128)S(1)}, f32[9,8,1024]{2,1,0:T(8,128)S(1)}, u32[]{:S(2)}, u32[]{:S(2)}) collective-permute-start(f32[9,8,1024]{2,1,0:T(8,128)S(1)} %get-tuple-element.25), channel_id=1, source_target_pairs={{1,2},{3,4},{5,6},{2,1},{4,3},{6,5},{9,10},{11,12},{13,14},{10,9},... | collective-permute-start | bytes 884744 | tf_op jit(solution)/shard_map/ppermute | solution.py:335
  29.9 0.7 %collective-permute-start.12 = (f32[8,8,1024]{2,1,0:T(8,128)S(1)}, f32[8,8,1024]{2,1,0:T(8,128)S(1)}, u32[]{:S(2)}, u32[]{:S(2)}) collective-permute-start(f32[8,8,1024]{2,1,0:T(8,128)S(1)} %get-tuple-element.30), channel_id=1, source_target_pairs={{1,2},{3,4},{5,6},{2,1},{4,3},{6,5},{9,10},{11,12},{13,14},{10,9},... | collective-permute-start | bytes 786440 | tf_op jit(solution)/shard_map/ppermute | solution.py:338
  30.6 5.7 %interior.2 = (f32[2,32,1024]{2,1,0:T(8,128)S(1)}, f32[2,32,1024]{2,1,0:T(8,128)S(1)}) custom-call(bf16[16,8,32,1024]{3,2,1,0:T(8,128)(2,1)S(1)} %copy-done, f32[2,32,1024]{2,1,0:T(8,128)S(1)} %copy-done.3, f32[2,32,1024]{2,1,0:T(8,128)S(1)} %collective-permute-done.refs_2_, s32[32,1024]{1,0:T(8,128)S(1)} %copy-done.2), custom_call_target="tpu_custom_call" | custom-call | flops 52428800 | bytes 9043968 | tf_op jit(solution)/shard_map/interior/pallas_call | solution.py:29
  36.3 0.0 collective-permute-done.4
  36.3 0.1 collective-permute-start.1
  36.5 10.5 %collective-permute-done.11.refs_2_ = f32[8,8,1024]{2,1,0:T(8,128)S(1)} collective-permute-done((f32[8,8,1024]{2,1,0:T(8,128)S(1)}, f32[8,8,1024]{2,1,0:T(8,128)S(1)}, u32[]{:S(2)}, u32[]{:S(2)}) %collective-permute-start.11) | collective-permute-done | bytes 262176 | tf_op jit(solution)/shard_map/ppermute | solution.py:337
  47.0 1.5 %collective-permute-start.5 = (f32[2,32,1024]{2,1,0:T(8,128)S(1)}, f32[2,32,1024]{2,1,0:T(8,128)S(1)}, u32[]{:S(2)}, u32[]{:S(2)}) collective-permute-start(f32[2,32,1024]{2,1,0:T(8,128)S(1)} %add.6), channel_id=1, source_target_pairs={{0,16},{8,24},{16,0},{24,8},{1,17},{9,25},{17,1},{25,9},{2,18},{10... | collective-permute-start | bytes 786440 | tf_op jit(solution)/shard_map/ppermute | solution.py:346
  48.5 0.0 collective-permute-done.12.refs_3_
  48.5 3.9 %collective-permute-done.6.refs_2_.refs_4_ = f32[9,8,1024]{2,1,0:T(8,128)S(1)} collective-permute-done((f32[9,8,1024]{2,1,0:T(8,128)S(1)}, f32[9,8,1024]{2,1,0:T(8,128)S(1)}, u32[]{:S(2)}, u32[]{:S(2)}) %collective-permute-start.6) | collective-permute-done | bytes 294944 | tf_op jit(solution)/shard_map/ppermute | solution.py:334
  52.4 0.0 collective-permute-done.7.refs_3_.refs_5_
  52.4 4.1 %edges.3 = (f32[2,8,1024]{2,1,0:T(8,128)S(1)}, f32[2,8,1024]{2,1,0:T(8,128)S(1)}) custom-call(bf16[16,8,32,1024]{3,2,1,0:T(8,128)(2,1)S(1)} %copy-done, f32[16,16,1024]{2,1,0:T(8,128)S(1)} %get-tuple-element.28.refs_1_, f32[8,8,1024]{2,1,0:T(8,128)S(1)} %collective-permute-done.11.refs_2_, f32[8,8,1024]{2,1,0:T(8,128)S(1)} %collective-permute-done.12.refs_3_, ...), custom_call_target="tpu_custom_call" | custom-call | flops 26214400 | bytes 10682368 | tf_op jit(solution)/shard_map/edges/pallas_call | solution.py:29
  56.5 0.1 collective-permute-start.13
  56.6 4.1 %edges.2 = (f32[2,8,1024]{2,1,0:T(8,128)S(1)}, f32[2,8,1024]{2,1,0:T(8,128)S(1)}) custom-call(bf16[16,8,32,1024]{3,2,1,0:T(8,128)(2,1)S(1)} %copy-done, f32[16,16,1024]{2,1,0:T(8,128)S(1)} %get-tuple-element.23.refs_1_, f32[9,8,1024]{2,1,0:T(8,128)S(1)} %collective-permute-done.6.refs_2_.refs_4_, f32[9,8,1024]{2,1,0:T(8,128)S(1)} %collective-permute-done.7.refs_3_.refs_5_, ...), custom_call_target="tpu_custom_call" | custom-call | flops 26214400 | bytes 10747904 | tf_op jit(solution)/shard_map/edges/pallas_call | solution.py:29
  60.7 0.6 collective-permute-start.8
  61.3 0.0 collective-permute-done.13
  61.3 1.6 %collective-permute-start.14 = (f32[2,8,1024]{2,1,0:T(8,128)S(1)}, f32[2,8,1024]{2,1,0:T(8,128)S(1)}, u32[]{:S(2)}, u32[]{:S(2)}) collective-permute-start(f32[2,8,1024]{2,1,0:T(8,128)S(1)} %add.7), channel_id=1, source_target_pairs={{0,16},{8,24},{16,0},{24,8},{1,17},{9,25},{17,1},{25,9},{2,18},{10... | collective-permute-start | bytes 196616 | tf_op jit(solution)/shard_map/ppermute | solution.py:352
  62.9 0.0 collective-permute-done.1.refs_1_
  62.9 0.0 collective-permute-done.8.refs_4_
  62.9 2.7 %collective-permute-done.14.refs_5_ = f32[2,8,1024]{2,1,0:T(8,128)S(1)} collective-permute-done((f32[2,8,1024]{2,1,0:T(8,128)S(1)}, f32[2,8,1024]{2,1,0:T(8,128)S(1)}, u32[]{:S(2)}, u32[]{:S(2)}) %collective-permute-start.14) | collective-permute-done | bytes 65568 | tf_op jit(solution)/shard_map/ppermute | solution.py:352
  65.6 0.0 collective-permute-done.5.refs_2_
  65.6 0.8 %finish.1 = f32[2,32,1024]{2,1,0:T(8,128)} custom-call(f32[2,32,1024]{2,1,0:T(8,128)S(1)} %get-tuple-element.19.refs_0_, f32[2,32,1024]{2,1,0:T(8,128)S(1)} %collective-permute-done.1.refs_1_, f32[2,32,1024]{2,1,0:T(8,128)S(1)} %collective-permute-done.5.refs_2_, f32[2,8,1024]{2,1,0:T(8,128)S(1)} %get-tuple-element.26.refs_3_, ...), custom_call_target="tpu_custom_call" | custom-call | flops 262144 | bytes 983040 | tf_op jit(solution)/shard_map/finish/pallas_call | solution.py:29
  (3 shorter events, 0.0 us)
Async XLA Ops:
  0.0 9.5 %collective-permute-start.2 = (f32[2,32,1024]{2,1,0:T(8,128)}, f32[2,32,1024]{2,1,0:T(8,128)S(1)}, u32[]{:S(2)}, u32[]{:S(2)}) collective-permute-start(f32[2,32,1024]{2,1,0:T(8,128)} %refs_1_.3), channel_id=1, source_target_pairs={{0,16},{8,24},{16,0},{24,8},{1,17},{9,25},{17,1},{25,9},{2,18},{10... | collective-permute-start | bytes 786440 | tf_op jit(solution)/shard_map/ppermute | solution.py:340
  9.5 6.0 %collective-permute-start.3 = (f32[2,32,1024]{2,1,0:T(8,128)S(1)}, f32[2,32,1024]{2,1,0:T(8,128)S(1)}, u32[]{:S(2)}, u32[]{:S(2)}) collective-permute-start(f32[2,32,1024]{2,1,0:T(8,128)S(1)} %collective-permute-done.2.refs_1_), channel_id=1, source_target_pairs={{0,8},{8,0},{16,24},{24,16},{1,9},{9,1},{17,25},{25,17},{2,10},{10... | collective-permute-start | bytes 786440 | tf_op jit(solution)/shard_map/ppermute | solution.py:341
  9.5 18.9 %copy-start.2 = (s32[32,1024]{1,0:T(8,128)S(1)}, s32[32,1024]{1,0:T(8,128)}, u32[]{:S(2)}) copy-start(s32[32,1024]{1,0:T(8,128)} %refs_6_.3) | copy-start | bytes 393220
  9.5 6.0 %collective-permute-start.9 = (f32[2,16,1024]{2,1,0:T(8,128)S(1)}, f32[2,16,1024]{2,1,0:T(8,128)S(1)}, u32[]{:S(2)}, u32[]{:S(2)}) collective-permute-start(f32[2,16,1024]{2,1,0:T(8,128)S(1)} %pad_maximum_fusion), channel_id=1, source_target_pairs={{0,16},{8,24},{16,0},{24,8},{1,17},{9,25},{17,1},{25,9},{2,18},{10... | collective-permute-start | bytes 393224 | tf_op jit(solution)/shard_map/ppermute | solution.py:330
  11.3 17.0 %collective-permute-start = (f32[2,32,1024]{2,1,0:T(8,128)}, f32[2,32,1024]{2,1,0:T(8,128)S(1)}, u32[]{:S(2)}, u32[]{:S(2)}) collective-permute-start(f32[2,32,1024]{2,1,0:T(8,128)} %refs_1_.3), channel_id=1, source_target_pairs={{0,8},{8,0},{16,24},{24,16},{1,9},{9,1},{17,25},{25,17},{2,10},{10... | collective-permute-start | bytes 786440 | tf_op jit(solution)/shard_map/ppermute | solution.py:328
  15.5 10.6 %collective-permute-start.10 = (f32[2,16,1024]{2,1,0:T(8,128)S(1)}, f32[2,16,1024]{2,1,0:T(8,128)S(1)}, u32[]{:S(2)}, u32[]{:S(2)}) collective-permute-start(f32[2,16,1024]{2,1,0:T(8,128)S(1)} %collective-permute-done.9.refs_1_), channel_id=1, source_target_pairs={{0,8},{8,0},{16,24},{24,16},{1,9},{9,1},{17,25},{25,17},{2,10},{10... | collective-permute-start | bytes 393224 | tf_op jit(solution)/shard_map/ppermute | solution.py:331
  15.5 3.4 %copy-start = (bf16[16,8,32,1024]{3,2,1,0:T(8,128)(2,1)S(1)}, bf16[16,8,32,1024]{3,2,1,0:T(8,128)(2,1)}, u32[]{:S(2)}) copy-start(bf16[16,8,32,1024]{3,2,1,0:T(8,128)(2,1)} %refs_0_.11) | copy-start | bytes 25165828
  18.9 0.9 %copy-start.1 = (s32[32,1024]{1,0:T(8,128)S(1)}, s32[32,1024]{1,0:T(8,128)}, u32[]{:S(2)}) copy-start(s32[32,1024]{1,0:T(8,128)} %refs_6_.3) | copy-start | bytes 393220
  19.8 8.6 %copy-start.3 = (f32[2,32,1024]{2,1,0:T(8,128)S(1)}, f32[2,32,1024]{2,1,0:T(8,128)}, u32[]{:S(2)}) copy-start(f32[2,32,1024]{2,1,0:T(8,128)} %refs_1_.3) | copy-start | bytes 786436
  25.5 10.9 %collective-permute-start.4 = (f32[2,32,1024]{2,1,0:T(8,128)S(1)}, f32[2,32,1024]{2,1,0:T(8,128)S(1)}, u32[]{:S(2)}, u32[]{:S(2)}) collective-permute-start(f32[2,32,1024]{2,1,0:T(8,128)S(1)} %get-tuple-element.22), channel_id=1, source_target_pairs={{0,8},{8,0},{16,24},{24,16},{1,9},{9,1},{17,25},{25,17},{2,10},{10... | collective-permute-start | bytes 786440 | tf_op jit(solution)/shard_map/ppermute | solution.py:345
  26.6 20.4 %collective-permute-start.11 = (f32[8,8,1024]{2,1,0:T(8,128)S(1)}, f32[8,8,1024]{2,1,0:T(8,128)S(1)}, u32[]{:S(2)}, u32[]{:S(2)}) collective-permute-start(f32[8,8,1024]{2,1,0:T(8,128)S(1)} %get-tuple-element.29), channel_id=1, source_target_pairs={{0,1},{1,0},{2,3},{3,2},{4,5},{5,4},{6,7},{7,6},{8,9},{9,8},{10,11... | collective-permute-start | bytes 786440 | tf_op jit(solution)/shard_map/ppermute | solution.py:337
  28.9 23.5 %collective-permute-start.6 = (f32[9,8,1024]{2,1,0:T(8,128)S(1)}, f32[9,8,1024]{2,1,0:T(8,128)S(1)}, u32[]{:S(2)}, u32[]{:S(2)}) collective-permute-start(f32[9,8,1024]{2,1,0:T(8,128)S(1)} %get-tuple-element.24), channel_id=1, source_target_pairs={{0,1},{1,0},{2,3},{3,2},{4,5},{5,4},{6,7},{7,6},{8,9},{9,8},{10,11... | collective-permute-start | bytes 884744 | tf_op jit(solution)/shard_map/ppermute | solution.py:334
  29.3 23.1 %collective-permute-start.7 = (f32[9,8,1024]{2,1,0:T(8,128)S(1)}, f32[9,8,1024]{2,1,0:T(8,128)S(1)}, u32[]{:S(2)}, u32[]{:S(2)}) collective-permute-start(f32[9,8,1024]{2,1,0:T(8,128)S(1)} %get-tuple-element.25), channel_id=1, source_target_pairs={{1,2},{3,4},{5,6},{2,1},{4,3},{6,5},{9,10},{11,12},{13,14},{10,9},... | collective-permute-start | bytes 884744 | tf_op jit(solution)/shard_map/ppermute | solution.py:335
  29.9 18.6 %collective-permute-start.12 = (f32[8,8,1024]{2,1,0:T(8,128)S(1)}, f32[8,8,1024]{2,1,0:T(8,128)S(1)}, u32[]{:S(2)}, u32[]{:S(2)}) collective-permute-start(f32[8,8,1024]{2,1,0:T(8,128)S(1)} %get-tuple-element.30), channel_id=1, source_target_pairs={{1,2},{3,4},{5,6},{2,1},{4,3},{6,5},{9,10},{11,12},{13,14},{10,9},... | collective-permute-start | bytes 786440 | tf_op jit(solution)/shard_map/ppermute | solution.py:338
  36.3 26.6 %collective-permute-start.1 = (f32[2,32,1024]{2,1,0:T(8,128)S(1)}, f32[2,32,1024]{2,1,0:T(8,128)S(1)}, u32[]{:S(2)}, u32[]{:S(2)}) collective-permute-start(f32[2,32,1024]{2,1,0:T(8,128)S(1)} %get-tuple-element.20), channel_id=1, source_target_pairs={{0,8},{8,0},{16,24},{24,16},{1,9},{9,1},{17,25},{25,17},{2,10},{10... | collective-permute-start | bytes 786440 | tf_op jit(solution)/shard_map/ppermute | solution.py:344
  47.0 18.7 %collective-permute-start.5 = (f32[2,32,1024]{2,1,0:T(8,128)S(1)}, f32[2,32,1024]{2,1,0:T(8,128)S(1)}, u32[]{:S(2)}, u32[]{:S(2)}) collective-permute-start(f32[2,32,1024]{2,1,0:T(8,128)S(1)} %add.6), channel_id=1, source_target_pairs={{0,16},{8,24},{16,0},{24,8},{1,17},{9,25},{17,1},{25,9},{2,18},{10... | collective-permute-start | bytes 786440 | tf_op jit(solution)/shard_map/ppermute | solution.py:346
  56.5 4.8 %collective-permute-start.13 = (f32[2,8,1024]{2,1,0:T(8,128)S(1)}, f32[2,8,1024]{2,1,0:T(8,128)S(1)}, u32[]{:S(2)}, u32[]{:S(2)}) collective-permute-start(f32[2,8,1024]{2,1,0:T(8,128)S(1)} %get-tuple-element.32), channel_id=1, source_target_pairs={{0,8},{8,0},{16,24},{24,16},{1,9},{9,1},{17,25},{25,17},{2,10},{10... | collective-permute-start | bytes 196616 | tf_op jit(solution)/shard_map/ppermute | solution.py:351
  60.7 2.2 %collective-permute-start.8 = (f32[2,8,1024]{2,1,0:T(8,128)S(1)}, f32[2,8,1024]{2,1,0:T(8,128)S(1)}, u32[]{:S(2)}, u32[]{:S(2)}) collective-permute-start(f32[2,8,1024]{2,1,0:T(8,128)S(1)} %get-tuple-element.27), channel_id=1, source_target_pairs={{0,8},{8,0},{16,24},{24,16},{1,9},{9,1},{17,25},{25,17},{2,10},{10... | collective-permute-start | bytes 196616 | tf_op jit(solution)/shard_map/ppermute | solution.py:350
  61.3 4.3 %collective-permute-start.14 = (f32[2,8,1024]{2,1,0:T(8,128)S(1)}, f32[2,8,1024]{2,1,0:T(8,128)S(1)}, u32[]{:S(2)}, u32[]{:S(2)}) collective-permute-start(f32[2,8,1024]{2,1,0:T(8,128)S(1)} %add.7), channel_id=1, source_target_pairs={{0,16},{8,24},{16,0},{24,8},{1,17},{9,25},{17,1},{25,9},{2,18},{10... | collective-permute-start | bytes 196616 | tf_op jit(solution)/shard_map/ppermute | solution.py:352

commit v2 on v1

v2 whole, which is shorter than its diff:
```python
import math

import jax
import jax.numpy as jnp
from jax import lax
from jax.experimental import pallas as pl
from jax.experimental.pallas import tpu as pltpu
from jax.sharding import PartitionSpec as P

SLOTS = 2
VARS = 4
FIELDS = 8
SWEEPS = 4

COEFF_X = 0.35
COEFF_Y = 0.12
CENTRE = 1.0 - 2.0 * COEFF_X - 2.0 * COEFF_Y
RATIO = COEFF_Y / COEFF_X

LANES = 128
TILE = 8
HALF = 16
VMEM_BYTES = 40 * 2**20


def kernel_call(body, out_shape, scratch, flops, name, outside={}):
    def call(*args):
        spaces = [outside.get(i, pltpu.VMEM) for i in range(len(args))]
        return pl.pallas_call(
            body,
            out_shape=out_shape,
            in_specs=[pl.BlockSpec(memory_space=space) for space in spaces],
            out_specs=jax.tree.map(lambda _: pl.BlockSpec(memory_space=pltpu.VMEM), out_shape),
            scratch_shapes=scratch,
            compiler_params=pltpu.CompilerParams(vmem_limit_bytes=VMEM_BYTES),
            cost_estimate=pl.CostEstimate(flops=flops, bytes_accessed=1024, transcendentals=0),
            name=name,
        )(*args)

    return call


def hold(x, *tokens):
    return pl.pallas_call(
        lambda *refs: None,
        out_shape=jax.ShapeDtypeStruct(x.shape, x.dtype),
        in_specs=[pl.BlockSpec(memory_space=pl.ANY)] * (1 + len(tokens)),
        out_specs=pl.BlockSpec(memory_space=pl.ANY),
        input_output_aliases={0: 0},
        cost_estimate=pl.CostEstimate(flops=1, bytes_accessed=1, transcendentals=0),
        name="hold",
    )(x, *tokens)


def lane_masks():
    lane = lax.broadcasted_iota(jnp.int32, (TILE, LANES), 1)
    return lane == 0, lane == LANES - 1


def top_half():
    return lax.broadcasted_iota(jnp.int32, (TILE, LANES), 0) < TILE // 2


def cols(j):
    return pl.ds(j * LANES, LANES)


def sides(values, first, last):
    before = [pltpu.roll(v, 1, 1) for v in values]
    after = [pltpu.roll(v, LANES - 1, 1) for v in values]
    zero = jnp.zeros_like(values[0])
    count = len(values)
    sums = []
    for j in range(count):
        left = jnp.where(first, before[j - 1] if j else zero, before[j])
        right = jnp.where(last, after[j + 1] if j + 1 < count else zero, after[j])
        sums.append(left + right)
    return sums


def order(own):
    shares = VARS // own
    share = lax.axis_index("mem") % shares
    return [at * own + k for at in (share, shares - 1 - share) for k in range(own)]


def fetch(local, own, p_ref, *rest):
    out_ref, sem = rest[-2:]
    members = out_ref.shape[0]
    slot = lax.axis_index("mem") // (VARS // own)
    slot = slot if local else SLOTS - 1 - slot
    copies = [
        pltpu.make_async_copy(p_ref.at[m, pl.ds(slot * VARS, VARS)], out_ref.at[m], sem.at[m]) for m in range(members)
    ]
    for copy in copies:
        copy.start()
    for copy in copies:
        copy.wait()


def weights_of(own, refs):
    return [(ref, k) for ref in refs for k in range(own)]


def project_edges(local, own, p_ref, *rest):
    if local:
        *g_refs, counts_ref, e_ref, o_ref, u_ref = rest
    else:
        *g_refs, _, e_ref, o_ref, u_ref = rest
    members, _, rows, ny = p_ref.shape
    grows = g_refs[0].shape[1]
    even = lax.axis_index("strip") % 2 == 0
    half = top_half()
    fields = order(own)
    grads = weights_of(own, g_refs)

    def put(row, j, top, bottom):
        e_ref[row, :, cols(j)] = jnp.where(even, bottom, top)
        o_ref[row, :, cols(j)] = jnp.where(even, top, bottom)

    if local:
        for j in range(ny // LANES):
            top = counts_ref[0:TILE, cols(j)].astype(jnp.float32)
            bottom = counts_ref[rows - TILE : rows, cols(j)].astype(jnp.float32)
            put(members // 2, j, top, pltpu.roll(bottom, TILE // 2, 0))

    def pair(q, carry):
        for j in range(ny // LANES):
            tops, bottoms = [], []
            for m in (2 * q, 2 * q + 1):
                top = bottom = None
                for f, (g_ref, k) in zip(fields, grads):
                    low = p_ref[m, f, 0:HALF, cols(j)].astype(jnp.float32)[0:TILE]
                    high = p_ref[m, f, rows - HALF : rows, cols(j)].astype(jnp.float32)[HALF - TILE :]
                    low = low * g_ref[k, 0:TILE, cols(j)]
                    high = high * g_ref[k, grows - TILE : grows, cols(j)]
                    top = low if top is None else top + low
                    bottom = high if bottom is None else bottom + high
                u_ref[m, 0:TILE, cols(j)] = top
                u_ref[m, TILE : 2 * TILE, cols(j)] = bottom
                tops.append(top)
                bottoms.append(bottom)
            top = jnp.where(half, tops[0], pltpu.roll(tops[1], TILE // 2, 0))
            bottom = jnp.where(half, pltpu.roll(bottoms[0], TILE // 2, 0), bottoms[1])
            put(q, j, top, bottom)
        return carry

    lax.fori_loop(0, members // 2, pair, 0)


def interior(p_ref, *refs):
    *g_refs, counts_ref, _, own_ref, other_ref, coef, buf_a, buf_b, total_ref = refs
    members, _, rows, ny = p_ref.shape
    own = own_ref.shape[0]
    blocks = ny // LANES
    group = buf_a.shape[0]
    first, last = lane_masks()
    fields = order(own)
    grads = weights_of(own, g_refs)
    sums = [(own_ref, k) for k in range(own)] + [(other_ref, k) for k in range(own)]
    skip = TILE // 2
    whole = list(range(0, rows, TILE))
    kept = list(range(skip, rows - skip, TILE))
    for t in range(1, SWEEPS):
        for j in range(blocks):
            active = (counts_ref[:, cols(j)] > t).astype(jnp.float32)
            total_ref[0, j] = active
            for n, r in enumerate(kept if t == SWEEPS - 1 else whole):
                active = total_ref[0, j, r : r + TILE]
                coef[t - 1, 0, j, n * TILE : (n + 1) * TILE] = active * COEFF_X
                coef[t - 1, 1, j, n * TILE : (n + 1) * TILE] = 1.0 - active * (1.0 - CENTRE)
    zero = jnp.zeros((TILE, LANES), jnp.float32)
    for buf in (buf_a, buf_b):
        for i in range(group):
            for j in range(blocks):
                buf[i, j, 0:TILE] = zero
                buf[i, j, TILE + rows :] = zero
    total_ref[...] = jnp.zeros_like(total_ref)

    def step(s, carry):
        base = s * group
        for r in range(0, rows, HALF):
            for j in range(blocks):
                weights = [g_ref[k, r : r + HALF, cols(j)] for g_ref, k in grads]
                for i in range(group):
                    total = None
                    for f, w in zip(fields, weights):
                        term = p_ref[base + i, f, r : r + HALF, cols(j)].astype(jnp.float32) * w
                        total = term if total is None else total + term
                    buf_a[i, j, TILE + r : TILE + r + HALF] = total
        src, dst = buf_a, buf_b
        for t in range(SWEEPS):
            for n, r in enumerate(kept if t == SWEEPS - 1 else whole):
                at, to = TILE + r, TILE + n * TILE
                for i in range(group):
                    centre = [src[i, j, at : at + TILE] for j in range(blocks)]
                    lateral = sides(centre, first, last)
                    for j in range(blocks):
                        stacked = src[i, j, at - 1 : at - 1 + TILE] + src[i, j, at + 1 : at + 1 + TILE]
                        moved = stacked + RATIO * lateral[j]
                        if t == 0:
                            new = COEFF_X * moved + CENTRE * centre[j]
                        else:
                            own_row = pl.ds(n * TILE, TILE)
                            new = coef[t - 1, 0, j, own_row] * moved + coef[t - 1, 1, j, own_row] * centre[j]
                        dst[i, j, to : to + TILE] = new
            src, dst = dst, src
        for r in range(0, rows, HALF):
            for j in range(blocks):
                smooth = [src[i, j, TILE - skip + r : TILE - skip + r + HALF] for i in range(group)]
                for n, f in enumerate(fields):
                    total = total_ref[n, j, r : r + HALF]
                    for i in range(group):
                        total = total + p_ref[base + i, f, r : r + HALF, cols(j)].astype(jnp.float32) * smooth[i]
                    total_ref[n, j, r : r + HALF] = total
        return carry

    lax.fori_loop(0, members // group, step, 0)
    for n, (ref, k) in enumerate(sums):
        for j in range(blocks):
            for r in range(0, rows - TILE, TILE):
                ref[k, r : r + TILE, cols(j)] = total_ref[n, j, skip + r : skip + r + TILE]


def edges(p_ref, u_ref, e_ref, o_ref, ce_ref, co_ref, counts_ref, _, own_ref, other_ref, coef, buf_a, buf_b, halo):
    members, _, rows, ny = p_ref.shape
    own = own_ref.shape[0]
    blocks = ny // LANES
    first, last = lane_masks()
    half = top_half()
    even = lax.axis_index("strip") % 2 == 0
    fields = order(own)
    sums = [(own_ref, k) for k in range(own)] + [(other_ref, k) for k in range(own)]
    crow = ce_ref.shape[0] - 1
    for j in range(blocks):
        e, o = ce_ref[crow, :, cols(j)], co_ref[crow, :, cols(j)]
        halo[j, 4:12] = jnp.where(even, o, e)
        halo[j, 24:32] = jnp.where(even, e, o)
        halo[j, 8:16] = counts_ref[0:TILE, cols(j)].astype(jnp.float32)
        halo[j, 16:24] = counts_ref[rows - TILE : rows, cols(j)].astype(jnp.float32)

        def weigh(t, to, given):
            active = (given > t).astype(jnp.float32)
            coef[t, 0, j, to : to + TILE] = active * COEFF_X
            coef[t, 1, j, to : to + TILE] = 1.0 - active * (1.0 - CENTRE)

        for to in (8, 16, 24):
            weigh(0, to, halo[j, to - 3 : to + 5])
        for t in range(1, SWEEPS - 1):
            weigh(t, 8, halo[j, 6:14])
            weigh(t, 24, halo[j, 18:26])
        weigh(SWEEPS - 1, 0, jnp.where(half, halo[j, 8:16], halo[j, 16:24]))
    own_ref[...] = jnp.zeros_like(own_ref)
    other_ref[...] = jnp.zeros_like(other_ref)
    plans = [[(5, 8), (13, 16), (21, 24)], [(9, 8), (21, 24)], [(8, 8), (24, 24)]]

    def step(q, carry):
        for j in range(blocks):
            e, o = e_ref[q, :, cols(j)], o_ref[q, :, cols(j)]
            above, below = jnp.where(even, o, e), jnp.where(even, e, o)
            buf_a[0, j, 4:12] = above
            buf_a[0, j, 24:32] = below
            buf_a[1, j, 0:8] = above
            buf_a[1, j, 20:28] = below
            for i in range(2):
                buf_a[i, j, 8:16] = u_ref[2 * q + i, 0:TILE, cols(j)]
                buf_a[i, j, 16:24] = u_ref[2 * q + i, TILE : 2 * TILE, cols(j)]
        src, dst = buf_a, buf_b
        for t in range(SWEEPS - 1):
            for at, to in plans[t]:
                weights = [[coef[t, c, j, to : to + TILE] for j in range(blocks)] for c in range(2)]
                for i in range(2):
                    centre = [src[i, j, at : at + TILE] for j in range(blocks)]
                    lateral = sides(centre, first, last)
                    for j in range(blocks):
                        stacked = src[i, j, at - 1 : at - 1 + TILE] + src[i, j, at + 1 : at + 1 + TILE]
                        moved = stacked + RATIO * lateral[j]
                        dst[i, j, to : to + TILE] = weights[0][j] * moved + weights[1][j] * centre[j]
            src, dst = dst, src

        def both(ref, i, j, shift):
            low, high = ref[i, j, 10 + shift : 18 + shift], ref[i, j, 22 + shift : 30 + shift]
            return jnp.where(half, low, high)

        t = SWEEPS - 1
        weights = [[coef[t, c, j, 0:TILE] for j in range(blocks)] for c in range(2)]
        smooth = []
        for i in range(2):
            centre = [both(src, i, j, 0) for j in range(blocks)]
            lateral = sides(centre, first, last)
            result = []
            for j in range(blocks):
                moved = both(src, i, j, -1) + both(src, i, j, 1) + RATIO * lateral[j]
                result.append(weights[0][j] * moved + weights[1][j] * centre[j])
            smooth.append(result)
        for j in range(blocks):
            for f, (ref, k) in zip(fields, sums):
                total = ref[k, :, cols(j)]
                for i in range(2):
                    low = p_ref[2 * q + i, f, 0:HALF, cols(j)].astype(jnp.float32)[0:TILE]
                    high = p_ref[2 * q + i, f, rows - HALF : rows, cols(j)].astype(jnp.float32)[HALF - TILE :]
                    total = total + jnp.where(half, low, high) * smooth[i][j]
                ref[k, :, cols(j)] = total
        return carry

    lax.fori_loop(0, members // 2, step, 0)


def finish(scale, *refs):
    inner_refs, edge_refs, out_ref = refs[:4], refs[4:8], refs[8]
    own, rows, ny = out_ref.shape
    half = top_half()
    for k in range(own):
        for j in range(ny // LANES):
            edge = sum(ref[k, :, cols(j)] for ref in edge_refs[1:]) + edge_refs[0][k, :, cols(j)]
            parts = [edge]
            for r in range(0, rows - TILE, TILE):
                inner = sum(ref[k, r : r + TILE, cols(j)] for ref in inner_refs[1:]) + inner_refs[0][k, r : r + TILE, cols(j)]
                parts.append(pltpu.roll(inner, TILE // 2, 0))
            parts.append(edge)
            for n in range(rows // TILE):
                out_ref[k, n * TILE : (n + 1) * TILE, cols(j)] = jnp.where(half, parts[n], parts[n + 1]) * scale


def per_device(gradient, perturbations, counts):
    members, _, rows, ny = perturbations.shape
    own = gradient.shape[0]
    mem, strips = lax.axis_size("mem"), lax.axis_size("strip")
    shares = VARS // own
    blocks = ny // LANES
    assert shares == 2 and mem == shares * SLOTS and members % 2 == 0
    scale = 1.0 / math.sqrt(members * mem * FIELDS)
    f32 = jnp.float32

    near = [(i, i ^ 1) for i in range(mem)]
    across = [(i, (i + shares) % mem) for i in range(mem)]
    cross = [(i, (i + shares) % mem ^ 1) for i in range(mem)]
    even = [(i, i ^ 1) for i in range(strips) if i ^ 1 < strips]
    odd = [(i, i + 1) for i in range(1, strips - 1, 2)]
    odd = odd + [(j, i) for i, j in odd]

    def shape(*dims):
        return jax.ShapeDtypeStruct(dims, f32)

    def window(*lead):
        return pltpu.VMEM((*lead, blocks, 40, LANES), f32)

    def call_fetch(local, *token):
        return kernel_call(
            lambda *refs: fetch(local, own, *refs),
            jax.ShapeDtypeStruct((members, VARS, rows, ny), perturbations.dtype),
            [pltpu.SemaphoreType.DMA((members,))], 1024, "fetch", outside={0: pl.ANY, 1: pl.ANY},
        )(pltpu.with_memory_space_constraint(perturbations, pltpu.HBM), *token)

    def call_project(local, *args):
        pairs = members // 2 + (1 if local else 0)
        outs = (shape(pairs, TILE, ny), shape(pairs, TILE, ny), shape(members, 2 * TILE, ny))
        outside = {} if local else {len(args) - 1: pl.ANY}
        body = lambda *refs: project_edges(local, own, *refs)
        return kernel_call(body, outs, [], 1024, "project", outside=outside)(*args)

    def call_interior(*args):
        outs = (shape(own, rows - TILE, ny), shape(own, rows - TILE, ny))
        total = pltpu.VMEM((VARS, blocks, rows, LANES), f32)
        buf = pltpu.VMEM((2, blocks, rows + 2 * TILE, LANES), f32)
        coef = pltpu.VMEM((SWEEPS - 1, 2, blocks, rows, LANES), f32)
        return kernel_call(interior, outs, [coef, buf, buf, total], 1024, "interior", outside={len(args) - 1: pl.ANY})(*args)

    def call_edges(*args):
        outs = (shape(own, TILE, ny), shape(own, TILE, ny))
        scratch = [window(SWEEPS, 2), window(2), window(2), window()]
        return kernel_call(edges, outs, scratch, 1024, "edges", outside={7: pl.ANY})(*args)

    partner = lax.ppermute(gradient, "mem", near)
    far = lax.ppermute(gradient, "mem", across)
    far_partner = lax.ppermute(gradient, "mem", cross)

    p0 = call_fetch(True)
    e0, o0, u0 = call_project(True, p0, gradient, partner, counts)
    e0 = lax.ppermute(e0, "strip", even)
    o0 = lax.ppermute(o0, "strip", odd)
    p1 = call_fetch(False, u0)
    own0, other0 = call_interior(p0, gradient, partner, counts, p1)

    e1, o1, u1 = call_project(False, p1, far, far_partner, own0)
    e1 = lax.ppermute(e1, "strip", even)
    o1 = lax.ppermute(o1, "strip", odd)
    own1, other1 = call_interior(p1, far, far_partner, counts, u1)
    eown0, eother0 = call_edges(p0, u0, e0, o0, e0, o0, counts, own1)
    eown1, eother1 = call_edges(p1, u1, e1, o1, e0, o0, counts, eown0)

    near0 = lax.ppermute(other0, "mem", near)
    far1 = hold(lax.ppermute(own1, "mem", across), near0)
    cross1 = hold(lax.ppermute(other1, "mem", cross), far1)
    enear0 = hold(lax.ppermute(eother0, "mem", near), cross1)
    efar1 = hold(lax.ppermute(eown1, "mem", across), enear0)
    ecross1 = hold(lax.ppermute(eother1, "mem", cross), efar1)

    return kernel_call(
        lambda *refs: finish(scale, *refs), shape(own, rows, ny), [], 1024, "finish"
    )(own0, near0, far1, cross1, eown0, enear0, efar1, ecross1)


def solution(mesh):
    return jax.shard_map(
        per_device,
        mesh=mesh,
        in_specs=(P("mem", "strip", None), P("mem", None, "strip", None), P("strip", None)),
        out_specs=P("mem", "strip", None),
        check_vma=False,
    )
```

time: 66.6 us -> 53.6 us (0.80)
  the two profiles are of different devices: /device:TPU:0 before, /device:TPU:3 now
where the time goes in v2:
time: 53.6 us; the launch traced here: 53.3 us
  Pallas kernels  26.5 us (49%)
  starting transfers between devices  16.9 us (32%)
  local copies, waits for them, and re-layouts  8.56 us (16%)
  waiting for transfers between devices  1.16 us (2%)
    pallas_call x9, Pallas kernels, call(): pl.pallas_call(body, out_shape=out_shape, in_specs=[pl.BlockSpec(memory_s...  26.5 us
    unnamed x28, local copies, waits for them, and re-layouts  8.56 us
    ppermute x1, starting transfers between devices, per_device(): o1 = lax.ppermute(o1, 'strip', odd)  4.36 us
    ppermute x1, starting transfers between devices, per_device(): o0 = lax.ppermute(o0, 'strip', odd)  4.27 us
    ppermute x1, starting transfers between devices, per_device(): near0 = lax.ppermute(other0, 'mem', near)  1.9 us
    ppermute x1, starting transfers between devices, per_device(): far1 = hold(lax.ppermute(own1, 'mem', across), near0)  1.3 us
    ppermute x1, starting transfers between devices, per_device(): efar1 = hold(lax.ppermute(eown1, 'mem', across), enear0)  1.3 us
    ppermute x1, starting transfers between devices, per_device(): far_partner = lax.ppermute(gradient, 'mem', cross)  1.2 us
  transfers between devices with their start and end apart: 13, of which 1 were waited for; matrix products, arithmetic and copies ran while one was open for 0% of the time, Pallas kernels for 48%

profile of v2, /device:TPU:3, one launch (start us, length us, event | category | flops | bytes accessed | tf_op | source)
XLA Modules:
  0.0 53.3 jit_solution(9011982627191527165)
XLA Ops:
  0.0 0.7 %collective-permute-start = (f32[2,32,1024]{2,1,0:T(8,128)}, f32[2,32,1024]{2,1,0:T(8,128)S(1)}, u32[]{:S(2)}, u32[]{:S(2)}) collective-permute-start(f32[2,32,1024]{2,1,0:T(8,128)} %refs_0_.5), channel_id=1, source_target_pairs={{0,8},{8,0},{16,24},{24,16},{1,9},{9,1},{17,25},{25,17},{2,10},{10... | collective-permute-start | bytes 786440 | tf_op jit(solution)/shard_map/ppermute | solution.py:374
  0.7 1.2 %collective-permute-start.3 = (f32[2,32,1024]{2,1,0:T(8,128)}, f32[2,32,1024]{2,1,0:T(8,128)S(1)}, u32[]{:S(2)}, u32[]{:S(2)}) collective-permute-start(f32[2,32,1024]{2,1,0:T(8,128)} %refs_0_.5), channel_id=1, source_target_pairs={{0,24},{8,16},{16,8},{24,0},{1,25},{9,17},{17,9},{25,1},{2,26},{10... | collective-permute-start | bytes 786440 | tf_op jit(solution)/shard_map/ppermute | solution.py:376
  1.9 0.2 collective-permute-start.2
  2.1 2.3 %fetch.2.refs_0_.p_ref = bf16[16,4,32,1024]{3,2,1,0:T(8,128)(2,1)S(1)} custom-call(bf16[16,8,32,1024]{3,2,1,0:T(8,128)(2,1)} %refs_0_.4), custom_call_target="tpu_custom_call" | custom-call | flops 1024 | bytes 1024 | tf_op jit(solution)/shard_map/fetch/pallas_call | solution.py:29
  4.4 0.0 collective-permute-done.refs_2_.refs_1_
  4.4 0.0 copy-done.5
  4.4 0.5 project.2
  4.9 0.2 collective-permute-start.6
  5.1 4.3 %collective-permute-start.7 = (f32[9,8,1024]{2,1,0:T(8,128)S(1)}, f32[9,8,1024]{2,1,0:T(8,128)S(1)}, u32[]{:S(2)}, u32[]{:S(2)}) collective-permute-start(f32[9,8,1024]{2,1,0:T(8,128)S(1)} %get-tuple-element.26), channel_id=1, source_target_pairs={{1,2},{3,4},{5,6},{2,1},{4,3},{6,5},{9,10},{11,12},{13,14},{10,9},... | collective-permute-start | bytes 884744 | tf_op jit(solution)/shard_map/ppermute | solution.py:381
  9.4 2.3 %fetch.3.refs_3_.refs_0_.p_ref = bf16[16,4,32,1024]{3,2,1,0:T(8,128)(2,1)S(1)} custom-call(bf16[16,8,32,1024]{3,2,1,0:T(8,128)(2,1)} %refs_0_.4, f32[16,16,1024]{2,1,0:T(8,128)S(1)} %get-tuple-element.19.refs_1_.u_ref), custom_call_target="tpu_custom_call" | custom-call | flops 1024 | bytes 1024 | tf_op jit(solution)/shard_map/fetch/pallas_call | solution.py:29
  11.7 6.0 %interior.2 = (f32[2,24,1024]{2,1,0:T(8,128)S(1)}, f32[2,24,1024]{2,1,0:T(8,128)S(1)}) custom-call(bf16[16,4,32,1024]{3,2,1,0:T(8,128)(2,1)S(1)} %fetch.2.refs_0_.p_ref, f32[2,32,1024]{2,1,0:T(8,128)S(1)} %copy-done.5, f32[2,32,1024]{2,1,0:T(8,128)S(1)} %collective-permute-done.refs_2_.refs_1_, s32[32,1024]{1,0:T(8,128)S(1)} %copy-done, ...), custom_call_target="tpu_custom_call" | custom-call | flops 1024 | bytes 1024 | tf_op jit(solution)/shard_map/interior/pallas_call | solution.py:29
  17.7 0.0 collective-permute-done.3.refs_2_.refs_1_
  17.7 0.0 collective-permute-done.2.refs_1_.refs_0_
  17.7 0.5 project.3
  18.3 0.1 collective-permute-start.9
  18.3 4.4 %collective-permute-start.10 = (f32[8,8,1024]{2,1,0:T(8,128)S(1)}, f32[8,8,1024]{2,1,0:T(8,128)S(1)}, u32[]{:S(2)}, u32[]{:S(2)}) collective-permute-start(f32[8,8,1024]{2,1,0:T(8,128)S(1)} %get-tuple-element.30), channel_id=1, source_target_pairs={{1,2},{3,4},{5,6},{2,1},{4,3},{6,5},{9,10},{11,12},{13,14},{10,9},... | collective-permute-start | bytes 786440 | tf_op jit(solution)/shard_map/ppermute | solution.py:387
  22.7 1.9 %collective-permute-start.1 = (f32[2,24,1024]{2,1,0:T(8,128)S(1)}, f32[2,24,1024]{2,1,0:T(8,128)S(1)}, u32[]{:S(2)}, u32[]{:S(2)}) collective-permute-start(f32[2,24,1024]{2,1,0:T(8,128)S(1)} %get-tuple-element.21), channel_id=1, source_target_pairs={{0,8},{8,0},{16,24},{24,16},{1,9},{9,1},{17,25},{25,17},{2,10},{10... | collective-permute-start | bytes 589832 | tf_op jit(solution)/shard_map/ppermute | solution.py:392
  24.6 6.0 %interior.3 = (f32[2,24,1024]{2,1,0:T(8,128)S(1)}, f32[2,24,1024]{2,1,0:T(8,128)S(1)}) custom-call(bf16[16,4,32,1024]{3,2,1,0:T(8,128)(2,1)S(1)} %fetch.3.refs_3_.refs_0_.p_ref, f32[2,32,1024]{2,1,0:T(8,128)S(1)} %collective-permute-done.2.refs_1_.refs_0_, f32[2,32,1024]{2,1,0:T(8,128)S(1)} %collective-permute-done.3.refs_2_.refs_1_, ...), custom_call_target="tpu_custom_call" | custom-call | flops 1024 | bytes 1024 | tf_op jit(solution)/shard_map/interior/pallas_call | solution.py:29
  30.6 0.0 collective-permute-done.6.e_ref.ce_ref
  30.6 1.3 %collective-permute-start.4 = (f32[2,24,1024]{2,1,0:T(8,128)S(1)}, f32[2,24,1024]{2,1,0:T(8,128)S(1)}, u32[]{:S(2)}, u32[]{:S(2)}) collective-permute-start(f32[2,24,1024]{2,1,0:T(8,128)S(1)} %get-tuple-element.23._), channel_id=1, source_target_pairs={{0,16},{8,24},{16,0},{24,8},{1,17},{9,25},{17,1},{25,9},{2,18},{10... | collective-permute-start | bytes 589832 | tf_op jit(solution)/shard_map/ppermute | solution.py:393
  31.9 0.0 collective-permute-done.7.o_ref.co_ref
  31.9 0.4 collective-permute-start.5
  32.4 4.1 %edges.2 = (f32[2,8,1024]{2,1,0:T(8,128)S(1)}, f32[2,8,1024]{2,1,0:T(8,128)S(1)}) custom-call(bf16[16,4,32,1024]{3,2,1,0:T(8,128)(2,1)S(1)} %fetch.2.refs_0_.p_ref, f32[16,16,1024]{2,1,0:T(8,128)S(1)} %get-tuple-element.19.refs_1_.u_ref, f32[9,8,1024]{2,1,0:T(8,128)S(1)} %collective-permute-done.6.e_ref.ce_ref, ...), custom_call_target="tpu_custom_call" | custom-call | flops 1024 | bytes 1024 | tf_op jit(solution)/shard_map/edges/pallas_call | solution.py:29
  36.4 0.0 collective-permute-done.9.e_ref
  36.5 0.3 collective-permute-start.8
  36.7 0.0 collective-permute-done.10.o_ref
  36.7 4.1 %edges.3 = (f32[2,8,1024]{2,1,0:T(8,128)S(1)}, f32[2,8,1024]{2,1,0:T(8,128)S(1)}) custom-call(bf16[16,4,32,1024]{3,2,1,0:T(8,128)(2,1)S(1)} %fetch.3.refs_3_.refs_0_.p_ref, f32[16,16,1024]{2,1,0:T(8,128)S(1)} %get-tuple-element.22.refs_3_.u_ref, f32[8,8,1024]{2,1,0:T(8,128)S(1)} %collective-permute-done.9.e_ref, ...), custom_call_target="tpu_custom_call" | custom-call | flops 1024 | bytes 1024 | tf_op jit(solution)/shard_map/edges/pallas_call | solution.py:29
  40.8 1.3 %collective-permute-start.11 = (f32[2,8,1024]{2,1,0:T(8,128)S(1)}, f32[2,8,1024]{2,1,0:T(8,128)S(1)}, u32[]{:S(2)}, u32[]{:S(2)}) collective-permute-start(f32[2,8,1024]{2,1,0:T(8,128)S(1)} %get-tuple-element.31), channel_id=1, source_target_pairs={{0,16},{8,24},{16,0},{24,8},{1,17},{9,25},{17,1},{25,9},{2,18},{10... | collective-permute-start | bytes 196616 | tf_op jit(solution)/shard_map/ppermute | solution.py:396
  42.1 0.0 collective-permute-done.1.refs_1_
  42.1 0.7 %collective-permute-start.12 = (f32[2,8,1024]{2,1,0:T(8,128)S(1)}, f32[2,8,1024]{2,1,0:T(8,128)S(1)}, u32[]{:S(2)}, u32[]{:S(2)}) collective-permute-start(f32[2,8,1024]{2,1,0:T(8,128)S(1)} %get-tuple-element.32), channel_id=1, source_target_pairs={{0,24},{8,16},{16,8},{24,0},{1,25},{9,17},{17,9},{25,1},{2,26},{10... | collective-permute-start | bytes 196616 | tf_op jit(solution)/shard_map/ppermute | solution.py:397
  42.8 0.0 collective-permute-done.4.refs_0_
  42.8 0.0 copy-done.6
  42.8 0.7 %copy-done.3 = f32[2,24,1024]{2,1,0:T(8,128)} copy-done((f32[2,24,1024]{2,1,0:T(8,128)}, f32[2,24,1024]{2,1,0:T(8,128)S(1)}, u32[]{:S(2)}) %copy-start.3) | copy-done | bytes 196632
  43.5 0.0 collective-permute-done.5.refs_0_
  43.5 0.7 %copy-done.1 = f32[2,24,1024]{2,1,0:T(8,128)} copy-done((f32[2,24,1024]{2,1,0:T(8,128)}, f32[2,24,1024]{2,1,0:T(8,128)S(1)}, u32[]{:S(2)}) %copy-start.1) | copy-done | bytes 196632
  44.2 0.0 collective-permute-done.8.refs_0_
  44.2 0.6 %copy-done.8 = f32[2,8,1024]{2,1,0:T(8,128)} copy-done((f32[2,8,1024]{2,1,0:T(8,128)}, f32[2,8,1024]{2,1,0:T(8,128)S(1)}, u32[]{:S(2)}) %copy-start.8) | copy-done | bytes 65560
  44.8 0.0 collective-permute-done.11.refs_0_
  44.8 0.6 %copy-done.10 = f32[2,8,1024]{2,1,0:T(8,128)} copy-done((f32[2,8,1024]{2,1,0:T(8,128)}, f32[2,8,1024]{2,1,0:T(8,128)S(1)}, u32[]{:S(2)}) %copy-start.10) | copy-done | bytes 65560
  45.5 1.1 %collective-permute-done.12.refs_0_ = f32[2,8,1024]{2,1,0:T(8,128)S(1)} collective-permute-done((f32[2,8,1024]{2,1,0:T(8,128)S(1)}, f32[2,8,1024]{2,1,0:T(8,128)S(1)}, u32[]{:S(2)}, u32[]{:S(2)}) %collective-permute-start.12) | collective-permute-done | bytes 65568 | tf_op jit(solution)/shard_map/ppermute | solution.py:397
  46.6 0.6 %copy-done.12 = f32[2,8,1024]{2,1,0:T(8,128)} copy-done((f32[2,8,1024]{2,1,0:T(8,128)}, f32[2,8,1024]{2,1,0:T(8,128)S(1)}, u32[]{:S(2)}) %copy-start.12) | copy-done | bytes 65560
  47.2 0.9 %copy-done.2 = f32[2,24,1024]{2,1,0:T(8,128)S(1)} copy-done((f32[2,24,1024]{2,1,0:T(8,128)S(1)}, f32[2,24,1024]{2,1,0:T(8,128)}, u32[]{:S(2)}) %copy-start.2) | copy-done | bytes 196632
  48.1 0.9 %copy-done.4 = f32[2,24,1024]{2,1,0:T(8,128)S(1)} copy-done((f32[2,24,1024]{2,1,0:T(8,128)S(1)}, f32[2,24,1024]{2,1,0:T(8,128)}, u32[]{:S(2)}) %copy-start.4) | copy-done | bytes 196632
  49.1 0.9 %copy-done.7 = f32[2,24,1024]{2,1,0:T(8,128)S(1)} copy-done((f32[2,24,1024]{2,1,0:T(8,128)S(1)}, f32[2,24,1024]{2,1,0:T(8,128)}, u32[]{:S(2)}) %copy-start.7) | copy-done | bytes 196632
  50.0 0.8 %copy-done.9 = f32[2,8,1024]{2,1,0:T(8,128)S(1)} copy-done((f32[2,8,1024]{2,1,0:T(8,128)S(1)}, f32[2,8,1024]{2,1,0:T(8,128)}, u32[]{:S(2)}) %copy-start.9) | copy-done | bytes 65560
  50.8 0.8 %copy-done.11 = f32[2,8,1024]{2,1,0:T(8,128)S(1)} copy-done((f32[2,8,1024]{2,1,0:T(8,128)S(1)}, f32[2,8,1024]{2,1,0:T(8,128)}, u32[]{:S(2)}) %copy-start.11) | copy-done | bytes 65560
  51.7 0.8 %copy-done.13 = f32[2,8,1024]{2,1,0:T(8,128)S(1)} copy-done((f32[2,8,1024]{2,1,0:T(8,128)S(1)}, f32[2,8,1024]{2,1,0:T(8,128)}, u32[]{:S(2)}) %copy-start.13) | copy-done | bytes 65560
  52.5 0.8 %finish.1 = f32[2,32,1024]{2,1,0:T(8,128)} custom-call(f32[2,24,1024]{2,1,0:T(8,128)S(1)} %get-tuple-element.20.refs_3_.refs_0_, f32[2,24,1024]{2,1,0:T(8,128)S(1)} %copy-done.7, f32[2,24,1024]{2,1,0:T(8,128)S(1)} %copy-done.4, f32[2,24,1024]{2,1,0:T(8,128)S(1)} %copy-done.2, f32[2,8,1024]{2,1,0:T(8,128)S(1)} %get-tuple-element.27._.refs_4_, ...), custom_call_target="tpu_custom_call" | custom-call | flops 1024 | bytes 1024 | tf_op jit(solution)/shard_map/finish/pallas_call | solution.py:29
  (20 shorter events, 0.0 us)
Async XLA Ops:
  0.0 4.4 %copy-start.5 = (f32[2,32,1024]{2,1,0:T(8,128)S(1)}, f32[2,32,1024]{2,1,0:T(8,128)}, u32[]{:S(2)}) copy-start(f32[2,32,1024]{2,1,0:T(8,128)} %refs_0_.5) | copy-start | bytes 786436
  0.0 4.4 %copy-start = (s32[32,1024]{1,0:T(8,128)S(1)}, s32[32,1024]{1,0:T(8,128)}, u32[]{:S(2)}) copy-start(s32[32,1024]{1,0:T(8,128)} %counts_ref.3) | copy-start | bytes 393220
  0.0 4.4 %collective-permute-start = (f32[2,32,1024]{2,1,0:T(8,128)}, f32[2,32,1024]{2,1,0:T(8,128)S(1)}, u32[]{:S(2)}, u32[]{:S(2)}) collective-permute-start(f32[2,32,1024]{2,1,0:T(8,128)} %refs_0_.5), channel_id=1, source_target_pairs={{0,8},{8,0},{16,24},{24,16},{1,9},{9,1},{17,25},{25,17},{2,10},{10... | collective-permute-start | bytes 786440 | tf_op jit(solution)/shard_map/ppermute | solution.py:374
  0.7 17.0 %collective-permute-start.3 = (f32[2,32,1024]{2,1,0:T(8,128)}, f32[2,32,1024]{2,1,0:T(8,128)S(1)}, u32[]{:S(2)}, u32[]{:S(2)}) collective-permute-start(f32[2,32,1024]{2,1,0:T(8,128)} %refs_0_.5), channel_id=1, source_target_pairs={{0,24},{8,16},{16,8},{24,0},{1,25},{9,17},{17,9},{25,1},{2,26},{10... | collective-permute-start | bytes 786440 | tf_op jit(solution)/shard_map/ppermute | solution.py:376
  1.9 15.8 %collective-permute-start.2 = (f32[2,32,1024]{2,1,0:T(8,128)}, f32[2,32,1024]{2,1,0:T(8,128)S(1)}, u32[]{:S(2)}, u32[]{:S(2)}) collective-permute-start(f32[2,32,1024]{2,1,0:T(8,128)} %refs_0_.5), channel_id=1, source_target_pairs={{0,16},{8,24},{16,0},{24,8},{1,17},{9,25},{17,1},{25,9},{2,18},{10... | collective-permute-start | bytes 786440 | tf_op jit(solution)/shard_map/ppermute | solution.py:375
  4.9 25.7 %collective-permute-start.6 = (f32[9,8,1024]{2,1,0:T(8,128)S(1)}, f32[9,8,1024]{2,1,0:T(8,128)S(1)}, u32[]{:S(2)}, u32[]{:S(2)}) collective-permute-start(f32[9,8,1024]{2,1,0:T(8,128)S(1)} %get-tuple-element.25), channel_id=1, source_target_pairs={{0,1},{1,0},{2,3},{3,2},{4,5},{5,4},{6,7},{7,6},{8,9},{9,8},{10,11... | collective-permute-start | bytes 884744 | tf_op jit(solution)/shard_map/ppermute | solution.py:380
  5.1 26.8 %collective-permute-start.7 = (f32[9,8,1024]{2,1,0:T(8,128)S(1)}, f32[9,8,1024]{2,1,0:T(8,128)S(1)}, u32[]{:S(2)}, u32[]{:S(2)}) collective-permute-start(f32[9,8,1024]{2,1,0:T(8,128)S(1)} %get-tuple-element.26), channel_id=1, source_target_pairs={{1,2},{3,4},{5,6},{2,1},{4,3},{6,5},{9,10},{11,12},{13,14},{10,9},... | collective-permute-start | bytes 884744 | tf_op jit(solution)/shard_map/ppermute | solution.py:381
  18.3 18.2 %collective-permute-start.9 = (f32[8,8,1024]{2,1,0:T(8,128)S(1)}, f32[8,8,1024]{2,1,0:T(8,128)S(1)}, u32[]{:S(2)}, u32[]{:S(2)}) collective-permute-start(f32[8,8,1024]{2,1,0:T(8,128)S(1)} %get-tuple-element.29), channel_id=1, source_target_pairs={{0,1},{1,0},{2,3},{3,2},{4,5},{5,4},{6,7},{7,6},{8,9},{9,8},{10,11... | collective-permute-start | bytes 786440 | tf_op jit(solution)/shard_map/ppermute | solution.py:386
  18.3 18.4 %collective-permute-start.10 = (f32[8,8,1024]{2,1,0:T(8,128)S(1)}, f32[8,8,1024]{2,1,0:T(8,128)S(1)}, u32[]{:S(2)}, u32[]{:S(2)}) collective-permute-start(f32[8,8,1024]{2,1,0:T(8,128)S(1)} %get-tuple-element.30), channel_id=1, source_target_pairs={{1,2},{3,4},{5,6},{2,1},{4,3},{6,5},{9,10},{11,12},{13,14},{10,9},... | collective-permute-start | bytes 786440 | tf_op jit(solution)/shard_map/ppermute | solution.py:387
  22.7 19.4 %collective-permute-start.1 = (f32[2,24,1024]{2,1,0:T(8,128)S(1)}, f32[2,24,1024]{2,1,0:T(8,128)S(1)}, u32[]{:S(2)}, u32[]{:S(2)}) collective-permute-start(f32[2,24,1024]{2,1,0:T(8,128)S(1)} %get-tuple-element.21), channel_id=1, source_target_pairs={{0,8},{8,0},{16,24},{24,16},{1,9},{9,1},{17,25},{25,17},{2,10},{10... | collective-permute-start | bytes 589832 | tf_op jit(solution)/shard_map/ppermute | solution.py:392
  30.6 12.2 %collective-permute-start.4 = (f32[2,24,1024]{2,1,0:T(8,128)S(1)}, f32[2,24,1024]{2,1,0:T(8,128)S(1)}, u32[]{:S(2)}, u32[]{:S(2)}) collective-permute-start(f32[2,24,1024]{2,1,0:T(8,128)S(1)} %get-tuple-element.23._), channel_id=1, source_target_pairs={{0,16},{8,24},{16,0},{24,8},{1,17},{9,25},{17,1},{25,9},{2,18},{10... | collective-permute-start | bytes 589832 | tf_op jit(solution)/shard_map/ppermute | solution.py:393
  31.9 11.6 %collective-permute-start.5 = (f32[2,24,1024]{2,1,0:T(8,128)S(1)}, f32[2,24,1024]{2,1,0:T(8,128)S(1)}, u32[]{:S(2)}, u32[]{:S(2)}) collective-permute-start(f32[2,24,1024]{2,1,0:T(8,128)S(1)} %get-tuple-element.24), channel_id=1, source_target_pairs={{0,24},{8,16},{16,8},{24,0},{1,25},{9,17},{17,9},{25,1},{2,26},{10... | collective-permute-start | bytes 589832 | tf_op jit(solution)/shard_map/ppermute | solution.py:394
  36.5 7.7 %collective-permute-start.8 = (f32[2,8,1024]{2,1,0:T(8,128)S(1)}, f32[2,8,1024]{2,1,0:T(8,128)S(1)}, u32[]{:S(2)}, u32[]{:S(2)}) collective-permute-start(f32[2,8,1024]{2,1,0:T(8,128)S(1)} %get-tuple-element.28), channel_id=1, source_target_pairs={{0,8},{8,0},{16,24},{24,16},{1,9},{9,1},{17,25},{25,17},{2,10},{10... | collective-permute-start | bytes 196616 | tf_op jit(solution)/shard_map/ppermute | solution.py:395
  40.8 4.0 %collective-permute-start.11 = (f32[2,8,1024]{2,1,0:T(8,128)S(1)}, f32[2,8,1024]{2,1,0:T(8,128)S(1)}, u32[]{:S(2)}, u32[]{:S(2)}) collective-permute-start(f32[2,8,1024]{2,1,0:T(8,128)S(1)} %get-tuple-element.31), channel_id=1, source_target_pairs={{0,16},{8,24},{16,0},{24,8},{1,17},{9,25},{17,1},{25,9},{2,18},{10... | collective-permute-start | bytes 196616 | tf_op jit(solution)/shard_map/ppermute | solution.py:396
  42.1 0.7 %copy-start.6 = (f32[2,24,1024]{2,1,0:T(8,128)}, f32[2,24,1024]{2,1,0:T(8,128)S(1)}, u32[]{:S(2)}) copy-start(f32[2,24,1024]{2,1,0:T(8,128)S(1)} %collective-permute-done.1.refs_1_) | copy-start | bytes 589828
  42.1 4.5 %collective-permute-start.12 = (f32[2,8,1024]{2,1,0:T(8,128)S(1)}, f32[2,8,1024]{2,1,0:T(8,128)S(1)}, u32[]{:S(2)}, u32[]{:S(2)}) collective-permute-start(f32[2,8,1024]{2,1,0:T(8,128)S(1)} %get-tuple-element.32), channel_id=1, source_target_pairs={{0,24},{8,16},{16,8},{24,0},{1,25},{9,17},{17,9},{25,1},{2,26},{10... | collective-permute-start | bytes 196616 | tf_op jit(solution)/shard_map/ppermute | solution.py:397
  42.8 0.7 %copy-start.3 = (f32[2,24,1024]{2,1,0:T(8,128)}, f32[2,24,1024]{2,1,0:T(8,128)S(1)}, u32[]{:S(2)}) copy-start(f32[2,24,1024]{2,1,0:T(8,128)S(1)} %collective-permute-done.4.refs_0_) | copy-start | bytes 589828
  43.5 0.7 %copy-start.1 = (f32[2,24,1024]{2,1,0:T(8,128)}, f32[2,24,1024]{2,1,0:T(8,128)S(1)}, u32[]{:S(2)}) copy-start(f32[2,24,1024]{2,1,0:T(8,128)S(1)} %collective-permute-done.5.refs_0_) | copy-start | bytes 589828
  44.2 0.6 %copy-start.8 = (f32[2,8,1024]{2,1,0:T(8,128)}, f32[2,8,1024]{2,1,0:T(8,128)S(1)}, u32[]{:S(2)}) copy-start(f32[2,8,1024]{2,1,0:T(8,128)S(1)} %collective-permute-done.8.refs_0_) | copy-start | bytes 196612
  44.8 0.6 %copy-start.10 = (f32[2,8,1024]{2,1,0:T(8,128)}, f32[2,8,1024]{2,1,0:T(8,128)S(1)}, u32[]{:S(2)}) copy-start(f32[2,8,1024]{2,1,0:T(8,128)S(1)} %collective-permute-done.11.refs_0_) | copy-start | bytes 196612
  46.6 0.6 %copy-start.12 = (f32[2,8,1024]{2,1,0:T(8,128)}, f32[2,8,1024]{2,1,0:T(8,128)S(1)}, u32[]{:S(2)}) copy-start(f32[2,8,1024]{2,1,0:T(8,128)S(1)} %collective-permute-done.12.refs_0_) | copy-start | bytes 196612
  47.2 0.9 %copy-start.2 = (f32[2,24,1024]{2,1,0:T(8,128)S(1)}, f32[2,24,1024]{2,1,0:T(8,128)}, u32[]{:S(2)}) copy-start(f32[2,24,1024]{2,1,0:T(8,128)} %hold.6.refs_1_.refs_3_) | copy-start | bytes 589828
  48.1 0.9 %copy-start.4 = (f32[2,24,1024]{2,1,0:T(8,128)S(1)}, f32[2,24,1024]{2,1,0:T(8,128)}, u32[]{:S(2)}) copy-start(f32[2,24,1024]{2,1,0:T(8,128)} %hold.5.refs_1_.refs_2_) | copy-start | bytes 589828
  49.1 0.9 %copy-start.7 = (f32[2,24,1024]{2,1,0:T(8,128)S(1)}, f32[2,24,1024]{2,1,0:T(8,128)}, u32[]{:S(2)}) copy-start(f32[2,24,1024]{2,1,0:T(8,128)} %copy-done.6) | copy-start | bytes 589828
  50.0 0.8 %copy-start.9 = (f32[2,8,1024]{2,1,0:T(8,128)S(1)}, f32[2,8,1024]{2,1,0:T(8,128)}, u32[]{:S(2)}) copy-start(f32[2,8,1024]{2,1,0:T(8,128)} %hold.7.refs_1_.refs_5_) | copy-start | bytes 196612
  50.8 0.8 %copy-start.11 = (f32[2,8,1024]{2,1,0:T(8,128)S(1)}, f32[2,8,1024]{2,1,0:T(8,128)}, u32[]{:S(2)}) copy-start(f32[2,8,1024]{2,1,0:T(8,128)} %hold.8.refs_1_.refs_6_) | copy-start | bytes 196612
  51.7 0.8 %copy-start.13 = (f32[2,8,1024]{2,1,0:T(8,128)S(1)}, f32[2,8,1024]{2,1,0:T(8,128)}, u32[]{:S(2)}) copy-start(f32[2,8,1024]{2,1,0:T(8,128)} %hold.9.refs_7_) | copy-start | bytes 196612

commit v3 on v2

--- a/solution.py
+++ b/solution.py
@@ -40,18 +40,6 @@
     return call
 
 
-def hold(x, *tokens):
-    return pl.pallas_call(
-        lambda *refs: None,
-        out_shape=jax.ShapeDtypeStruct(x.shape, x.dtype),
-        in_specs=[pl.BlockSpec(memory_space=pl.ANY)] * (1 + len(tokens)),
-        out_specs=pl.BlockSpec(memory_space=pl.ANY),
-        input_output_aliases={0: 0},
-        cost_estimate=pl.CostEstimate(flops=1, bytes_accessed=1, transcendentals=0),
-        name="hold",
-    )(x, *tokens)
-
-
 def lane_masks():
     lane = lax.broadcasted_iota(jnp.int32, (TILE, LANES), 1)
     return lane == 0, lane == LANES - 1
@@ -84,18 +72,13 @@
     return [at * own + k for at in (share, shares - 1 - share) for k in range(own)]
 
 
-def fetch(local, own, p_ref, *rest):
-    out_ref, sem = rest[-2:]
-    members = out_ref.shape[0]
+def fetches(local, own, p_ref, out_ref, sem):
     slot = lax.axis_index("mem") // (VARS // own)
     slot = slot if local else SLOTS - 1 - slot
-    copies = [
-        pltpu.make_async_copy(p_ref.at[m, pl.ds(slot * VARS, VARS)], out_ref.at[m], sem.at[m]) for m in range(members)
+    return [
+        pltpu.make_async_copy(p_ref.at[m, pl.ds(slot * VARS, VARS)], out_ref.at[m], sem.at[m])
+        for m in range(out_ref.shape[0])
     ]
-    for copy in copies:
-        copy.start()
-    for copy in copies:
-        copy.wait()
 
 
 def weights_of(own, refs):
@@ -104,7 +87,17 @@
 
 def project_edges(local, own, p_ref, *rest):
     if local:
-        *g_refs, counts_ref, e_ref, o_ref, u_ref = rest
+        far_g_ref, far_counts_ref, partner_ref, e_ref, o_ref, u_ref, out_ref, g_ref, counts_ref, sem, small_sem = rest
+        copies = fetches(True, own, p_ref, out_ref, sem)
+        small = [
+            pltpu.make_async_copy(far_g_ref, g_ref, small_sem.at[0]),
+            pltpu.make_async_copy(far_counts_ref, counts_ref, small_sem.at[1]),
+        ]
+        for copy in small + copies:
+            copy.start()
+        for copy in small:
+            copy.wait()
+        p_ref, g_refs = out_ref, [g_ref, partner_ref]
     else:
         *g_refs, _, e_ref, o_ref, u_ref = rest
     members, _, rows, ny = p_ref.shape
@@ -124,7 +117,7 @@
             bottom = counts_ref[rows - TILE : rows, cols(j)].astype(jnp.float32)
             put(members // 2, j, top, pltpu.roll(bottom, TILE // 2, 0))
 
-    def pair(q, carry):
+    def pair(q):
         for j in range(ny // LANES):
             tops, bottoms = [], []
             for m in (2 * q, 2 * q + 1):
@@ -143,13 +136,25 @@
             top = jnp.where(half, tops[0], pltpu.roll(tops[1], TILE // 2, 0))
             bottom = jnp.where(half, pltpu.roll(bottoms[0], TILE // 2, 0), bottoms[1])
             put(q, j, top, bottom)
-        return carry
-
-    lax.fori_loop(0, members // 2, pair, 0)
-
-
-def interior(p_ref, *refs):
-    *g_refs, counts_ref, _, own_ref, other_ref, coef, buf_a, buf_b, total_ref = refs
+
+    if local:
+        for q in range(members // 2):
+            copies[2 * q].wait()
+            copies[2 * q + 1].wait()
+            pair(q)
+    else:
+        pl.loop(0, members // 2)(pair)
+
+
+def interior(local, p_ref, *refs):
+    if local:
+        *g_refs, counts_ref, rest_ref, own_ref, other_ref, next_ref, coef, buf_a, buf_b, total_ref, sem = refs
+        copies = fetches(False, own_ref.shape[0], rest_ref, next_ref, sem)
+        for copy in copies:
+            copy.start()
+    else:
+        *g_refs, counts_ref, _, own_ref, other_ref, coef, buf_a, buf_b, total_ref = refs
+        copies = []
     members, _, rows, ny = p_ref.shape
     own = own_ref.shape[0]
     blocks = ny // LANES
@@ -220,6 +225,8 @@
         for j in range(blocks):
             for r in range(0, rows - TILE, TILE):
                 ref[k, r : r + TILE, cols(j)] = total_ref[n, j, skip + r : skip + r + TILE]
+    for copy in copies:
+        copy.wait()
 
 
 def edges(p_ref, u_ref, e_ref, o_ref, ce_ref, co_ref, counts_ref, _, own_ref, other_ref, coef, buf_a, buf_b, halo):
@@ -307,7 +314,7 @@
 
 
 def finish(scale, *refs):
-    inner_refs, edge_refs, out_ref = refs[:4], refs[4:8], refs[8]
+    inner_ref, *edge_refs, out_ref = refs
     own, rows, ny = out_ref.shape
     half = top_half()
     for k in range(own):
@@ -315,8 +322,7 @@
             edge = sum(ref[k, :, cols(j)] for ref in edge_refs[1:]) + edge_refs[0][k, :, cols(j)]
             parts = [edge]
             for r in range(0, rows - TILE, TILE):
-                inner = sum(ref[k, r : r + TILE, cols(j)] for ref in inner_refs[1:]) + inner_refs[0][k, r : r + TILE, cols(j)]
-                parts.append(pltpu.roll(inner, TILE // 2, 0))
+                parts.append(pltpu.roll(inner_ref[k, r : r + TILE, cols(j)], TILE // 2, 0))
             parts.append(edge)
             for n in range(rows // TILE):
                 out_ref[k, n * TILE : (n + 1) * TILE, cols(j)] = jnp.where(half, parts[n], parts[n + 1]) * scale
@@ -345,26 +351,28 @@
     def window(*lead):
         return pltpu.VMEM((*lead, blocks, 40, LANES), f32)
 
-    def call_fetch(local, *token):
-        return kernel_call(
-            lambda *refs: fetch(local, own, *refs),
-            jax.ShapeDtypeStruct((members, VARS, rows, ny), perturbations.dtype),
-            [pltpu.SemaphoreType.DMA((members,))], 1024, "fetch", outside={0: pl.ANY, 1: pl.ANY},
-        )(pltpu.with_memory_space_constraint(perturbations, pltpu.HBM), *token)
+    stored, stored_g, stored_counts = (
+        pltpu.with_memory_space_constraint(x, pltpu.HBM) for x in (perturbations, gradient, counts)
+    )
+    one_slot = jax.ShapeDtypeStruct((members, VARS, rows, ny), perturbations.dtype)
+    copy_sem = pltpu.SemaphoreType.DMA((members,))
 
     def call_project(local, *args):
         pairs = members // 2 + (1 if local else 0)
         outs = (shape(pairs, TILE, ny), shape(pairs, TILE, ny), shape(members, 2 * TILE, ny))
-        outside = {} if local else {len(args) - 1: pl.ANY}
+        outs = outs + ((one_slot, shape(own, rows, ny), jax.ShapeDtypeStruct((rows, ny), counts.dtype)) if local else ())
+        outside = {0: pl.ANY, 1: pl.ANY, 2: pl.ANY} if local else {len(args) - 1: pl.ANY}
         body = lambda *refs: project_edges(local, own, *refs)
-        return kernel_call(body, outs, [], 1024, "project", outside=outside)(*args)
-
-    def call_interior(*args):
-        outs = (shape(own, rows - TILE, ny), shape(own, rows - TILE, ny))
+        return kernel_call(body, outs, [copy_sem, pltpu.SemaphoreType.DMA((2,))] if local else [], 1024, "project", outside=outside)(*args)
+
+    def call_interior(local, *args):
+        outs = (shape(own, rows - TILE, ny), shape(own, rows - TILE, ny)) + ((one_slot,) if local else ())
         total = pltpu.VMEM((VARS, blocks, rows, LANES), f32)
         buf = pltpu.VMEM((2, blocks, rows + 2 * TILE, LANES), f32)
         coef = pltpu.VMEM((SWEEPS - 1, 2, blocks, rows, LANES), f32)
-        return kernel_call(interior, outs, [coef, buf, buf, total], 1024, "interior", outside={len(args) - 1: pl.ANY})(*args)
+        scratch = [coef, buf, buf, total] + ([copy_sem] if local else [])
+        body = lambda *refs: interior(local, *refs)
+        return kernel_call(body, outs, scratch, 1024, "interior", outside={len(args) - 1: pl.ANY})(*args)
 
     def call_edges(*args):
         outs = (shape(own, TILE, ny), shape(own, TILE, ny))
@@ -375,30 +383,27 @@
     far = lax.ppermute(gradient, "mem", across)
     far_partner = lax.ppermute(gradient, "mem", cross)
 
-    p0 = call_fetch(True)
-    e0, o0, u0 = call_project(True, p0, gradient, partner, counts)
+    e0, o0, u0, p0, near_g, near_counts = call_project(True, stored, stored_g, stored_counts, partner)
     e0 = lax.ppermute(e0, "strip", even)
     o0 = lax.ppermute(o0, "strip", odd)
-    p1 = call_fetch(False, u0)
-    own0, other0 = call_interior(p0, gradient, partner, counts, p1)
+    own0, other0, p1 = call_interior(True, p0, near_g, partner, near_counts, stored)
 
     e1, o1, u1 = call_project(False, p1, far, far_partner, own0)
     e1 = lax.ppermute(e1, "strip", even)
     o1 = lax.ppermute(o1, "strip", odd)
-    own1, other1 = call_interior(p1, far, far_partner, counts, u1)
-    eown0, eother0 = call_edges(p0, u0, e0, o0, e0, o0, counts, own1)
-    eown1, eother1 = call_edges(p1, u1, e1, o1, e0, o0, counts, eown0)
-
-    near0 = lax.ppermute(other0, "mem", near)
-    far1 = hold(lax.ppermute(own1, "mem", across), near0)
-    cross1 = hold(lax.ppermute(other1, "mem", cross), far1)
-    enear0 = hold(lax.ppermute(eother0, "mem", near), cross1)
-    efar1 = hold(lax.ppermute(eown1, "mem", across), enear0)
-    ecross1 = hold(lax.ppermute(eother1, "mem", cross), efar1)
-
+    own1, other1 = call_interior(False, p1, far, far_partner, near_counts, u1)
+    eown0, eother0 = call_edges(p0, u0, e0, o0, e0, o0, near_counts, own1)
+    eown1, eother1 = call_edges(p1, u1, e1, o1, e0, o0, near_counts, eown0)
+
+    inner = own0 + lax.ppermute(other0, "mem", near)
+    inner = inner + lax.ppermute(own1, "mem", across)
+    inner = inner + lax.ppermute(other1, "mem", cross)
+    enear0 = lax.ppermute(eother0, "mem", near)
+    efar1 = lax.ppermute(eown1, "mem", across)
+    ecross1 = lax.ppermute(eother1, "mem", cross)
     return kernel_call(
         lambda *refs: finish(scale, *refs), shape(own, rows, ny), [], 1024, "finish"
-    )(own0, near0, far1, cross1, eown0, enear0, efar1, ecross1)
+    )(inner, eown0, enear0, efar1, ecross1)
 
 
 def solution(mesh):

time: 53.6 us -> 45.2 us (0.84)
  local copies, waits for them, and re-layouts: 8.56 us -> 0 us
  waiting for transfers between devices: 1.16 us -> 3.57 us
  Pallas kernels: 26.5 us -> 24.5 us
    unnamed x28 -> x0, local copies, waits for them, and re-layouts: 8.56 us -> none
    ppermute x6, waiting for transfers between devices: 1.14 us -> 3.54 us  [the longest x1 1.99 us: per_device(): efar1 = lax.ppermute(eown1, 'mem', across)]
    pallas_call x9 -> x7, Pallas kernels: 26.5 us -> 24.5 us  [call(): pl.pallas_call(body, out_shape=out_shape, in_specs=[pl.BlockSpec(memory_s...]
  transfers between devices with their start and end apart: 13 -> 13, of which waited for: 1 -> 2; matrix products, arithmetic and copies ran while one was open for 0% -> 0% of each run, Pallas kernels for 48% -> 53%
where the time goes in v3:
time: 45.2 us; the launch traced here: 45 us
  Pallas kernels  24.5 us (54%)
  starting transfers between devices  16.9 us (37%)
  waiting for transfers between devices  3.57 us (8%)
    pallas_call x7, Pallas kernels, call(): pl.pallas_call(body, out_shape=out_shape, in_specs=[pl.BlockSpec(memory_s...  24.5 us
    ppermute x1, starting transfers between devices, per_device(): o1 = lax.ppermute(o1, 'strip', odd)  4.36 us
    ppermute x1, starting transfers between devices, per_device(): o0 = lax.ppermute(o0, 'strip', odd)  4.22 us
    ppermute x1, waiting for transfers between devices, per_device(): efar1 = lax.ppermute(eown1, 'mem', across)  1.99 us
    ppermute x1, starting transfers between devices, per_device(): inner = own0 + lax.ppermute(other0, 'mem', near)  1.96 us
    ppermute x1, waiting for transfers between devices, per_device(): ecross1 = lax.ppermute(eother1, 'mem', cross)  1.54 us
    ppermute x1, starting transfers between devices, per_device(): efar1 = lax.ppermute(eown1, 'mem', across)  1.3 us
    ppermute x1, starting transfers between devices, per_device(): inner = inner + lax.ppermute(other1, 'mem', cross)  1.21 us
  transfers between devices with their start and end apart: 13, of which 2 were waited for; matrix products, arithmetic and copies ran while one was open for 0% of the time, Pallas kernels for 53%

profile of v3, /device:TPU:3, one launch (start us, length us, event | category | flops | bytes accessed | tf_op | source)
XLA Modules:
  0.0 45.0 jit_solution(2744616924093482388)
XLA Ops:
  0.0 0.7 %collective-permute-start = (f32[2,32,1024]{2,1,0:T(8,128)}, f32[2,32,1024]{2,1,0:T(8,128)S(1)}, u32[]{:S(2)}, u32[]{:S(2)}) collective-permute-start(f32[2,32,1024]{2,1,0:T(8,128)} %refs_1_.1), channel_id=1, source_target_pairs={{0,8},{8,0},{16,24},{24,16},{1,9},{9,1},{17,25},{25,17},{2,10},{10... | collective-permute-start | bytes 786440 | tf_op jit(solution)/shard_map/ppermute | solution.py:382
  0.7 1.1 %collective-permute-start.3 = (f32[2,32,1024]{2,1,0:T(8,128)}, f32[2,32,1024]{2,1,0:T(8,128)S(1)}, u32[]{:S(2)}, u32[]{:S(2)}) collective-permute-start(f32[2,32,1024]{2,1,0:T(8,128)} %refs_1_.1), channel_id=1, source_target_pairs={{0,24},{8,16},{16,8},{24,0},{1,25},{9,17},{17,9},{25,1},{2,26},{10... | collective-permute-start | bytes 786440 | tf_op jit(solution)/shard_map/ppermute | solution.py:384
  1.8 0.2 collective-permute-start.2
  2.0 0.0 collective-permute-done.refs_3_.refs_2_
  2.0 2.8 %project.2 = (f32[9,8,1024]{2,1,0:T(8,128)S(1)}, f32[9,8,1024]{2,1,0:T(8,128)S(1)}, f32[16,16,1024]{2,1,0:T(8,128)S(1)}, bf16[16,4,32,1024]{3,2,1,0:T(8,128)(2,1...) custom-call(bf16[16,8,32,1024]{3,2,1,0:T(8,128)(2,1)} %refs_4_.1, f32[2,32,1024]{2,1,0:T(8,128)} %refs_1_.1, ...), custom_call_target="tpu_custom_call" | custom-call | flops 1024 | bytes 1024 | tf_op jit(solution)/shard_map/project/pallas_call | solution.py:29
  4.9 0.2 collective-permute-start.6
  5.1 4.2 %collective-permute-start.7 = (f32[9,8,1024]{2,1,0:T(8,128)S(1)}, f32[9,8,1024]{2,1,0:T(8,128)S(1)}, u32[]{:S(2)}, u32[]{:S(2)}) collective-permute-start(f32[9,8,1024]{2,1,0:T(8,128)S(1)} %get-tuple-element.34), channel_id=1, source_target_pairs={{1,2},{3,4},{5,6},{2,1},{4,3},{6,5},{9,10},{11,12},{13,14},{10,9},... | collective-permute-start | bytes 884744 | tf_op jit(solution)/shard_map/ppermute | solution.py:388
  9.4 6.2 %interior.2 = (f32[2,24,1024]{2,1,0:T(8,128)S(1)}, f32[2,24,1024]{2,1,0:T(8,128)S(1)}, bf16[16,4,32,1024]{3,2,1,0:T(8,128)(2,1)S(1)}) custom-call(bf16[16,4,32,1024]{3,2,1,0:T(8,128)(2,1)S(1)} %get-tuple-element.23.refs_0_.p_ref, f32[2,32,1024]{2,1,0:T(8,128)S(1)} %get-tuple-element.24.refs_1_, f32[2,32,1024]{2,1,0:T(8,128)S(1)} %collective-permute-done.refs_3_.refs_2_, ...), custom_call_target="tpu_custom_call" | custom-call | flops 1024 | bytes 1024 | tf_op jit(solution)/shard_map/interior/pallas_call | solution.py:29
  15.5 0.0 collective-permute-done.3.refs_2_
  15.6 0.0 collective-permute-done.2.refs_1_
  15.6 0.5 %project.3 = (f32[8,8,1024]{2,1,0:T(8,128)S(1)}, f32[8,8,1024]{2,1,0:T(8,128)S(1)}, f32[16,16,1024]{2,1,0:T(8,128)S(1)}) custom-call(bf16[16,4,32,1024]{3,2,1,0:T(8,128)(2,1)S(1)} %get-tuple-element.28.refs_0_.p_ref, f32[2,32,1024]{2,1,0:T(8,128)S(1)} %collective-permute-done.2.refs_1_, f32[2,32,1024]{2,1,0:T(8,128)S(1)} %collective-permute-done.3.refs_2_, ...), custom_call_target="tpu_custom_call" | custom-call | flops 1024 | bytes 1024 | tf_op jit(solution)/shard_map/project/pallas_call | solution.py:29
  16.1 0.1 collective-permute-start.9
  16.2 4.4 %collective-permute-start.10 = (f32[8,8,1024]{2,1,0:T(8,128)S(1)}, f32[8,8,1024]{2,1,0:T(8,128)S(1)}, u32[]{:S(2)}, u32[]{:S(2)}) collective-permute-start(f32[8,8,1024]{2,1,0:T(8,128)S(1)} %get-tuple-element.38), channel_id=1, source_target_pairs={{1,2},{3,4},{5,6},{2,1},{4,3},{6,5},{9,10},{11,12},{13,14},{10,9},... | collective-permute-start | bytes 786440 | tf_op jit(solution)/shard_map/ppermute | solution.py:393
  20.5 2.0 %collective-permute-start.1 = (f32[2,24,1024]{2,1,0:T(8,128)S(1)}, f32[2,24,1024]{2,1,0:T(8,128)S(1)}, u32[]{:S(2)}, u32[]{:S(2)}) collective-permute-start(f32[2,24,1024]{2,1,0:T(8,128)S(1)} %get-tuple-element.27), channel_id=1, source_target_pairs={{0,8},{8,0},{16,24},{24,16},{1,9},{9,1},{17,25},{25,17},{2,10},{10... | collective-permute-start | bytes 589832 | tf_op jit(solution)/shard_map/ppermute | solution.py:398
  22.5 6.0 %interior.3 = (f32[2,24,1024]{2,1,0:T(8,128)S(1)}, f32[2,24,1024]{2,1,0:T(8,128)S(1)}) custom-call(bf16[16,4,32,1024]{3,2,1,0:T(8,128)(2,1)S(1)} %get-tuple-element.28.refs_0_.p_ref, f32[2,32,1024]{2,1,0:T(8,128)S(1)} %collective-permute-done.2.refs_1_, f32[2,32,1024]{2,1,0:T(8,128)S(1)} %collective-permute-done.3.refs_2_, ...), custom_call_target="tpu_custom_call" | custom-call | flops 1024 | bytes 1024 | tf_op jit(solution)/shard_map/interior/pallas_call | solution.py:29
  28.5 0.0 collective-permute-done.6.e_ref.ce_ref
  28.5 1.2 %collective-permute-start.5 = (f32[2,24,1024]{2,1,0:T(8,128)S(1)}, f32[2,24,1024]{2,1,0:T(8,128)S(1)}, u32[]{:S(2)}, u32[]{:S(2)}) collective-permute-start(f32[2,24,1024]{2,1,0:T(8,128)S(1)} %get-tuple-element.31), channel_id=1, source_target_pairs={{0,24},{8,16},{16,8},{24,0},{1,25},{9,17},{17,9},{25,1},{2,26},{10... | collective-permute-start | bytes 589832 | tf_op jit(solution)/shard_map/ppermute | solution.py:400
  29.7 0.0 collective-permute-done.7.o_ref.co_ref
  29.7 0.2 collective-permute-start.4
  30.0 4.1 %edges.2 = (f32[2,8,1024]{2,1,0:T(8,128)S(1)}, f32[2,8,1024]{2,1,0:T(8,128)S(1)}) custom-call(bf16[16,4,32,1024]{3,2,1,0:T(8,128)(2,1)S(1)} %get-tuple-element.23.refs_0_.p_ref, f32[16,16,1024]{2,1,0:T(8,128)S(1)} %get-tuple-element.32.u_ref, f32[9,8,1024]{2,1,0:T(8,128)S(1)} %collective-permute-done.6.e_ref.ce_ref, ...), custom_call_target="tpu_custom_call" | custom-call | flops 1024 | bytes 1024 | tf_op jit(solution)/shard_map/edges/pallas_call | solution.py:29
  34.1 0.0 collective-permute-done.9.e_ref
  34.1 0.8 %collective-permute-start.8 = (f32[2,8,1024]{2,1,0:T(8,128)S(1)}, f32[2,8,1024]{2,1,0:T(8,128)S(1)}, u32[]{:S(2)}, u32[]{:S(2)}) collective-permute-start(f32[2,8,1024]{2,1,0:T(8,128)S(1)} %get-tuple-element.36), channel_id=1, source_target_pairs={{0,8},{8,0},{16,24},{24,16},{1,9},{9,1},{17,25},{25,17},{2,10},{10... | collective-permute-start | bytes 196616 | tf_op jit(solution)/shard_map/ppermute | solution.py:401
  34.9 0.0 collective-permute-done.10.o_ref
  34.9 4.1 %edges.3 = (f32[2,8,1024]{2,1,0:T(8,128)S(1)}, f32[2,8,1024]{2,1,0:T(8,128)S(1)}) custom-call(bf16[16,4,32,1024]{3,2,1,0:T(8,128)(2,1)S(1)} %get-tuple-element.28.refs_0_.p_ref, f32[16,16,1024]{2,1,0:T(8,128)S(1)} %get-tuple-element.29.refs_4_.u_ref, f32[8,8,1024]{2,1,0:T(8,128)S(1)} %collective-permute-done.9.e_ref, ...), custom_call_target="tpu_custom_call" | custom-call | flops 1024 | bytes 1024 | tf_op jit(solution)/shard_map/edges/pallas_call | solution.py:29
  39.0 1.3 %collective-permute-start.11 = (f32[2,8,1024]{2,1,0:T(8,128)S(1)}, f32[2,8,1024]{2,1,0:T(8,128)S(1)}, u32[]{:S(2)}, u32[]{:S(2)}) collective-permute-start(f32[2,8,1024]{2,1,0:T(8,128)S(1)} %get-tuple-element.39), channel_id=1, source_target_pairs={{0,16},{8,24},{16,0},{24,8},{1,17},{9,25},{17,1},{25,9},{2,18},{10... | collective-permute-start | bytes 196616 | tf_op jit(solution)/shard_map/ppermute | solution.py:402
  40.3 0.0 collective-permute-done.1
  40.3 0.4 collective-permute-start.12
  40.7 0.0 collective-permute-done.5
  40.7 0.0 collective-permute-done.4
  40.8 0.0 collective-permute-done.8.refs_2_
  40.8 2.0 %collective-permute-done.11.refs_3_ = f32[2,8,1024]{2,1,0:T(8,128)S(1)} collective-permute-done((f32[2,8,1024]{2,1,0:T(8,128)S(1)}, f32[2,8,1024]{2,1,0:T(8,128)S(1)}, u32[]{:S(2)}, u32[]{:S(2)}) %collective-permute-start.11) | collective-permute-done | bytes 65568 | tf_op jit(solution)/shard_map/ppermute | solution.py:402
  42.8 1.5 %collective-permute-done.12.refs_4_ = f32[2,8,1024]{2,1,0:T(8,128)S(1)} collective-permute-done((f32[2,8,1024]{2,1,0:T(8,128)S(1)}, f32[2,8,1024]{2,1,0:T(8,128)S(1)}, u32[]{:S(2)}, u32[]{:S(2)}) %collective-permute-start.12) | collective-permute-done | bytes 65568 | tf_op jit(solution)/shard_map/ppermute | solution.py:403
  44.3 0.7 %finish.1 = f32[2,32,1024]{2,1,0:T(8,128)} custom-call(f32[2,24,1024]{2,1,0:T(8,128)S(1)} %add_add_fusion.refs_0_, f32[2,8,1024]{2,1,0:T(8,128)S(1)} %get-tuple-element.35._.refs_1_, f32[2,8,1024]{2,1,0:T(8,128)S(1)} %collective-permute-done.8.refs_2_, f32[2,8,1024]{2,1,0:T(8,128)S(1)} %collective-permute-done.11.refs_3_, ...), custom_call_target="tpu_custom_call" | custom-call | flops 1024 | bytes 1024 | tf_op jit(solution)/shard_map/finish/pallas_call | solution.py:29
  (1 shorter events, 0.0 us)
Async XLA Ops:
  0.0 2.0 %collective-permute-start = (f32[2,32,1024]{2,1,0:T(8,128)}, f32[2,32,1024]{2,1,0:T(8,128)S(1)}, u32[]{:S(2)}, u32[]{:S(2)}) collective-permute-start(f32[2,32,1024]{2,1,0:T(8,128)} %refs_1_.1), channel_id=1, source_target_pairs={{0,8},{8,0},{16,24},{24,16},{1,9},{9,1},{17,25},{25,17},{2,10},{10... | collective-permute-start | bytes 786440 | tf_op jit(solution)/shard_map/ppermute | solution.py:382
  0.7 14.9 %collective-permute-start.3 = (f32[2,32,1024]{2,1,0:T(8,128)}, f32[2,32,1024]{2,1,0:T(8,128)S(1)}, u32[]{:S(2)}, u32[]{:S(2)}) collective-permute-start(f32[2,32,1024]{2,1,0:T(8,128)} %refs_1_.1), channel_id=1, source_target_pairs={{0,24},{8,16},{16,8},{24,0},{1,25},{9,17},{17,9},{25,1},{2,26},{10... | collective-permute-start | bytes 786440 | tf_op jit(solution)/shard_map/ppermute | solution.py:384
  1.8 13.8 %collective-permute-start.2 = (f32[2,32,1024]{2,1,0:T(8,128)}, f32[2,32,1024]{2,1,0:T(8,128)S(1)}, u32[]{:S(2)}, u32[]{:S(2)}) collective-permute-start(f32[2,32,1024]{2,1,0:T(8,128)} %refs_1_.1), channel_id=1, source_target_pairs={{0,16},{8,24},{16,0},{24,8},{1,17},{9,25},{17,1},{25,9},{2,18},{10... | collective-permute-start | bytes 786440 | tf_op jit(solution)/shard_map/ppermute | solution.py:383
  4.9 23.6 %collective-permute-start.6 = (f32[9,8,1024]{2,1,0:T(8,128)S(1)}, f32[9,8,1024]{2,1,0:T(8,128)S(1)}, u32[]{:S(2)}, u32[]{:S(2)}) collective-permute-start(f32[9,8,1024]{2,1,0:T(8,128)S(1)} %get-tuple-element.33), channel_id=1, source_target_pairs={{0,1},{1,0},{2,3},{3,2},{4,5},{5,4},{6,7},{7,6},{8,9},{9,8},{10,11... | collective-permute-start | bytes 884744 | tf_op jit(solution)/shard_map/ppermute | solution.py:387
  5.1 24.6 %collective-permute-start.7 = (f32[9,8,1024]{2,1,0:T(8,128)S(1)}, f32[9,8,1024]{2,1,0:T(8,128)S(1)}, u32[]{:S(2)}, u32[]{:S(2)}) collective-permute-start(f32[9,8,1024]{2,1,0:T(8,128)S(1)} %get-tuple-element.34), channel_id=1, source_target_pairs={{1,2},{3,4},{5,6},{2,1},{4,3},{6,5},{9,10},{11,12},{13,14},{10,9},... | collective-permute-start | bytes 884744 | tf_op jit(solution)/shard_map/ppermute | solution.py:388
  16.1 18.0 %collective-permute-start.9 = (f32[8,8,1024]{2,1,0:T(8,128)S(1)}, f32[8,8,1024]{2,1,0:T(8,128)S(1)}, u32[]{:S(2)}, u32[]{:S(2)}) collective-permute-start(f32[8,8,1024]{2,1,0:T(8,128)S(1)} %get-tuple-element.37), channel_id=1, source_target_pairs={{0,1},{1,0},{2,3},{3,2},{4,5},{5,4},{6,7},{7,6},{8,9},{9,8},{10,11... | collective-permute-start | bytes 786440 | tf_op jit(solution)/shard_map/ppermute | solution.py:392
  16.2 18.7 %collective-permute-start.10 = (f32[8,8,1024]{2,1,0:T(8,128)S(1)}, f32[8,8,1024]{2,1,0:T(8,128)S(1)}, u32[]{:S(2)}, u32[]{:S(2)}) collective-permute-start(f32[8,8,1024]{2,1,0:T(8,128)S(1)} %get-tuple-element.38), channel_id=1, source_target_pairs={{1,2},{3,4},{5,6},{2,1},{4,3},{6,5},{9,10},{11,12},{13,14},{10,9},... | collective-permute-start | bytes 786440 | tf_op jit(solution)/shard_map/ppermute | solution.py:393
  20.5 19.8 %collective-permute-start.1 = (f32[2,24,1024]{2,1,0:T(8,128)S(1)}, f32[2,24,1024]{2,1,0:T(8,128)S(1)}, u32[]{:S(2)}, u32[]{:S(2)}) collective-permute-start(f32[2,24,1024]{2,1,0:T(8,128)S(1)} %get-tuple-element.27), channel_id=1, source_target_pairs={{0,8},{8,0},{16,24},{24,16},{1,9},{9,1},{17,25},{25,17},{2,10},{10... | collective-permute-start | bytes 589832 | tf_op jit(solution)/shard_map/ppermute | solution.py:398
  28.5 12.2 %collective-permute-start.5 = (f32[2,24,1024]{2,1,0:T(8,128)S(1)}, f32[2,24,1024]{2,1,0:T(8,128)S(1)}, u32[]{:S(2)}, u32[]{:S(2)}) collective-permute-start(f32[2,24,1024]{2,1,0:T(8,128)S(1)} %get-tuple-element.31), channel_id=1, source_target_pairs={{0,24},{8,16},{16,8},{24,0},{1,25},{9,17},{17,9},{25,1},{2,26},{10... | collective-permute-start | bytes 589832 | tf_op jit(solution)/shard_map/ppermute | solution.py:400
  29.7 11.0 %collective-permute-start.4 = (f32[2,24,1024]{2,1,0:T(8,128)S(1)}, f32[2,24,1024]{2,1,0:T(8,128)S(1)}, u32[]{:S(2)}, u32[]{:S(2)}) collective-permute-start(f32[2,24,1024]{2,1,0:T(8,128)S(1)} %get-tuple-element.30._), channel_id=1, source_target_pairs={{0,16},{8,24},{16,0},{24,8},{1,17},{9,25},{17,1},{25,9},{2,18},{10... | collective-permute-start | bytes 589832 | tf_op jit(solution)/shard_map/ppermute | solution.py:399
  34.1 6.7 %collective-permute-start.8 = (f32[2,8,1024]{2,1,0:T(8,128)S(1)}, f32[2,8,1024]{2,1,0:T(8,128)S(1)}, u32[]{:S(2)}, u32[]{:S(2)}) collective-permute-start(f32[2,8,1024]{2,1,0:T(8,128)S(1)} %get-tuple-element.36), channel_id=1, source_target_pairs={{0,8},{8,0},{16,24},{24,16},{1,9},{9,1},{17,25},{25,17},{2,10},{10... | collective-permute-start | bytes 196616 | tf_op jit(solution)/shard_map/ppermute | solution.py:401
  39.0 3.8 %collective-permute-start.11 = (f32[2,8,1024]{2,1,0:T(8,128)S(1)}, f32[2,8,1024]{2,1,0:T(8,128)S(1)}, u32[]{:S(2)}, u32[]{:S(2)}) collective-permute-start(f32[2,8,1024]{2,1,0:T(8,128)S(1)} %get-tuple-element.39), channel_id=1, source_target_pairs={{0,16},{8,24},{16,0},{24,8},{1,17},{9,25},{17,1},{25,9},{2,18},{10... | collective-permute-start | bytes 196616 | tf_op jit(solution)/shard_map/ppermute | solution.py:402
  40.3 4.0 %collective-permute-start.12 = (f32[2,8,1024]{2,1,0:T(8,128)S(1)}, f32[2,8,1024]{2,1,0:T(8,128)S(1)}, u32[]{:S(2)}, u32[]{:S(2)}) collective-permute-start(f32[2,8,1024]{2,1,0:T(8,128)S(1)} %get-tuple-element.40), channel_id=1, source_target_pairs={{0,24},{8,16},{16,8},{24,0},{1,25},{9,17},{17,9},{25,1},{2,26},{10... | collective-permute-start | bytes 196616 | tf_op jit(solution)/shard_map/ppermute | solution.py:403

commit v4 on v3

--- a/solution.py
+++ b/solution.py
@@ -87,7 +87,7 @@
 
 def project_edges(local, own, p_ref, *rest):
     if local:
-        far_g_ref, far_counts_ref, partner_ref, e_ref, o_ref, u_ref, out_ref, g_ref, counts_ref, sem, small_sem = rest
+        far_g_ref, far_counts_ref, partner_ref, e_ref, o_ref, out_ref, g_ref, counts_ref, sem, small_sem = rest
         copies = fetches(True, own, p_ref, out_ref, sem)
         small = [
             pltpu.make_async_copy(far_g_ref, g_ref, small_sem.at[0]),
@@ -99,9 +99,8 @@
             copy.wait()
         p_ref, g_refs = out_ref, [g_ref, partner_ref]
     else:
-        *g_refs, _, e_ref, o_ref, u_ref = rest
+        *g_refs, e_ref, o_ref, u_ref = rest
     members, _, rows, ny = p_ref.shape
-    grows = g_refs[0].shape[1]
     even = lax.axis_index("strip") % 2 == 0
     half = top_half()
     fields = order(own)
@@ -126,11 +125,12 @@
                     low = p_ref[m, f, 0:HALF, cols(j)].astype(jnp.float32)[0:TILE]
                     high = p_ref[m, f, rows - HALF : rows, cols(j)].astype(jnp.float32)[HALF - TILE :]
                     low = low * g_ref[k, 0:TILE, cols(j)]
-                    high = high * g_ref[k, grows - TILE : grows, cols(j)]
+                    high = high * g_ref[k, g_ref.shape[1] - TILE : g_ref.shape[1], cols(j)]
                     top = low if top is None else top + low
                     bottom = high if bottom is None else bottom + high
-                u_ref[m, 0:TILE, cols(j)] = top
-                u_ref[m, TILE : 2 * TILE, cols(j)] = bottom
+                if not local:
+                    u_ref[m, 0:TILE, cols(j)] = top
+                    u_ref[m, TILE : 2 * TILE, cols(j)] = bottom
                 tops.append(top)
                 bottoms.append(bottom)
             top = jnp.where(half, tops[0], pltpu.roll(tops[1], TILE // 2, 0))
@@ -146,15 +146,8 @@
         pl.loop(0, members // 2)(pair)
 
 
-def interior(local, p_ref, *refs):
-    if local:
-        *g_refs, counts_ref, rest_ref, own_ref, other_ref, next_ref, coef, buf_a, buf_b, total_ref, sem = refs
-        copies = fetches(False, own_ref.shape[0], rest_ref, next_ref, sem)
-        for copy in copies:
-            copy.start()
-    else:
-        *g_refs, counts_ref, _, own_ref, other_ref, coef, buf_a, buf_b, total_ref = refs
-        copies = []
+def interior(p_ref, ga_ref, gb_ref, counts_ref, _, own_ref, other_ref, coef, buf_a, buf_b, total_ref):
+    g_refs = ga_ref, gb_ref
     members, _, rows, ny = p_ref.shape
     own = own_ref.shape[0]
     blocks = ny // LANES
@@ -225,8 +218,93 @@
         for j in range(blocks):
             for r in range(0, rows - TILE, TILE):
                 ref[k, r : r + TILE, cols(j)] = total_ref[n, j, skip + r : skip + r + TILE]
+
+
+def fetch(own, p_ref, _, out_ref, sem):
+    copies = fetches(False, own, p_ref, out_ref, sem)
+    for copy in copies:
+        copy.start()
     for copy in copies:
         copy.wait()
+
+
+def relay(*refs):
+    count = len(refs) // 2
+    for ref, out_ref in zip(refs[:count], refs[count + 1 :]):
+        out_ref[...] = ref[...]
+
+
+def whole(p_ref, ga_ref, gb_ref, e_ref, o_ref, counts_ref, _, own_ref, other_ref, coef, buf_a, buf_b):
+    members, _, rows, ny = p_ref.shape
+    own = own_ref.shape[0]
+    blocks = ny // LANES
+    first, last = lane_masks()
+    even = lax.axis_index("strip") % 2 == 0
+    fields = order(own)
+    grads = weights_of(own, (ga_ref, gb_ref))
+    sums = [(own_ref, k) for k in range(own)] + [(other_ref, k) for k in range(own)]
+    count = [-(-(rows + 2 * (SWEEPS - 1 - t)) // TILE) for t in range(SWEEPS)]
+    start = TILE + TILE // 2
+
+    def place(dst, j, at_odd, e, o):
+        above, below = jnp.where(even, o, e), jnp.where(even, e, o)
+        if at_odd:
+            dst[j, TILE : 2 * TILE] = above
+            dst[j, start + rows : start + rows + TILE] = below
+        else:
+            dst[j, start : start + TILE] = above
+            dst[j, 2 * TILE + rows : 3 * TILE + rows] = below
+
+    for j in range(blocks):
+        counted = buf_b.at[0]
+        place(counted, j, False, e_ref[members // 2, :, cols(j)], o_ref[members // 2, :, cols(j)])
+        counted[j, 2 * TILE : 2 * TILE + rows] = counts_ref[:, cols(j)].astype(jnp.float32)
+        for t in range(SWEEPS):
+            for n in range(count[t]):
+                at = start + 1 + t + n * TILE
+                active = (counted[j, at : at + TILE] > t).astype(jnp.float32)
+                coef[t, 0, j, n * TILE : (n + 1) * TILE] = active * COEFF_X
+                coef[t, 1, j, n * TILE : (n + 1) * TILE] = 1.0 - active * (1.0 - CENTRE)
+    own_ref[...] = jnp.zeros_like(own_ref)
+    other_ref[...] = jnp.zeros_like(other_ref)
+
+    def step(q, carry):
+        for j in range(blocks):
+            for i in range(2):
+                place(buf_a.at[i], j, i == 1, e_ref[q, :, cols(j)], o_ref[q, :, cols(j)])
+        for r in range(0, rows, HALF):
+            for j in range(blocks):
+                weights = [g_ref[k, r : r + HALF, cols(j)] for g_ref, k in grads]
+                for i in range(2):
+                    total = None
+                    for f, w in zip(fields, weights):
+                        term = p_ref[2 * q + i, f, r : r + HALF, cols(j)].astype(jnp.float32) * w
+                        total = term if total is None else total + term
+                    buf_a[i, j, 2 * TILE + r : 2 * TILE + r + HALF] = total
+        src, dst = buf_a, buf_b
+        for t in range(SWEEPS):
+            for n in range(count[t]):
+                at, to = (TILE if t else start) + 1 + n * TILE, TILE + n * TILE
+                weights = [[coef[t, c, j, n * TILE : (n + 1) * TILE] for j in range(blocks)] for c in range(2)]
+                for i in range(2):
+                    centre = [src[i, j, at : at + TILE] for j in range(blocks)]
+                    lateral = sides(centre, first, last)
+                    for j in range(blocks):
+                        stacked = src[i, j, at - 1 : at - 1 + TILE] + src[i, j, at + 1 : at + 1 + TILE]
+                        moved = stacked + RATIO * lateral[j]
+                        dst[i, j, to : to + TILE] = weights[0][j] * moved + weights[1][j] * centre[j]
+            src, dst = dst, src
+        for r in range(0, rows, HALF):
+            for j in range(blocks):
+                smooth = [src[i, j, TILE + r : TILE + r + HALF] for i in range(2)]
+                for f, (ref, k) in zip(fields, sums):
+                    total = ref[k, r : r + HALF, cols(j)]
+                    for i in range(2):
+                        total = total + p_ref[2 * q + i, f, r : r + HALF, cols(j)].astype(jnp.float32) * smooth[i]
+                    ref[k, r : r + HALF, cols(j)] = total
+        return carry
+
+    lax.fori_loop(0, members // 2, step, 0)
 
 
 def edges(p_ref, u_ref, e_ref, o_ref, ce_ref, co_ref, counts_ref, _, own_ref, other_ref, coef, buf_a, buf_b, halo):
@@ -313,19 +391,21 @@
     lax.fori_loop(0, members // 2, step, 0)
 
 
-def finish(scale, *refs):
-    inner_ref, *edge_refs, out_ref = refs
+def finish(scale, own_ref, near_ref, inner_ref, *refs):
+    *edge_refs, out_ref = refs
     own, rows, ny = out_ref.shape
     half = top_half()
     for k in range(own):
         for j in range(ny // LANES):
-            edge = sum(ref[k, :, cols(j)] for ref in edge_refs[1:]) + edge_refs[0][k, :, cols(j)]
+            edge = edge_refs[0][k, :, cols(j)] + edge_refs[1][k, :, cols(j)]
             parts = [edge]
             for r in range(0, rows - TILE, TILE):
                 parts.append(pltpu.roll(inner_ref[k, r : r + TILE, cols(j)], TILE // 2, 0))
             parts.append(edge)
             for n in range(rows // TILE):
-                out_ref[k, n * TILE : (n + 1) * TILE, cols(j)] = jnp.where(half, parts[n], parts[n + 1]) * scale
+                far = jnp.where(half, parts[n], parts[n + 1])
+                tile = pl.ds(n * TILE, TILE)
+                out_ref[k, tile, cols(j)] = (own_ref[k, tile, cols(j)] + near_ref[k, tile, cols(j)] + far) * scale
 
 
 def per_device(gradient, perturbations, counts):
@@ -359,20 +439,36 @@
 
     def call_project(local, *args):
         pairs = members // 2 + (1 if local else 0)
-        outs = (shape(pairs, TILE, ny), shape(pairs, TILE, ny), shape(members, 2 * TILE, ny))
-        outs = outs + ((one_slot, shape(own, rows, ny), jax.ShapeDtypeStruct((rows, ny), counts.dtype)) if local else ())
-        outside = {0: pl.ANY, 1: pl.ANY, 2: pl.ANY} if local else {len(args) - 1: pl.ANY}
+        outs = (shape(pairs, TILE, ny), shape(pairs, TILE, ny))
+        if local:
+            outs = outs + (one_slot, shape(own, rows, ny), jax.ShapeDtypeStruct((rows, ny), counts.dtype))
+        else:
+            outs = outs + (shape(members, 2 * TILE, ny),)
+        outside = {0: pl.ANY, 1: pl.ANY, 2: pl.ANY} if local else {}
+        scratch = [copy_sem, pltpu.SemaphoreType.DMA((2,))] if local else []
         body = lambda *refs: project_edges(local, own, *refs)
-        return kernel_call(body, outs, [copy_sem, pltpu.SemaphoreType.DMA((2,))] if local else [], 1024, "project", outside=outside)(*args)
-
-    def call_interior(local, *args):
-        outs = (shape(own, rows - TILE, ny), shape(own, rows - TILE, ny)) + ((one_slot,) if local else ())
+        return kernel_call(body, outs, scratch, 1024, "project", outside=outside)(*args)
+
+    def call_fetch(*args):
+        body = lambda *refs: fetch(own, *refs)
+        return kernel_call(body, one_slot, [copy_sem], 1024, "fetch", outside={0: pl.ANY, 1: pl.ANY})(*args)
+
+    def call_relay(*args):
+        outs = tuple(shape(*x.shape) for x in args[:-1])
+        return kernel_call(relay, outs, [], 1024, "relay", outside={len(outs): pl.ANY})(*args)
+
+    def call_interior(*args):
+        outs = (shape(own, rows - TILE, ny), shape(own, rows - TILE, ny))
         total = pltpu.VMEM((VARS, blocks, rows, LANES), f32)
         buf = pltpu.VMEM((2, blocks, rows + 2 * TILE, LANES), f32)
         coef = pltpu.VMEM((SWEEPS - 1, 2, blocks, rows, LANES), f32)
-        scratch = [coef, buf, buf, total] + ([copy_sem] if local else [])
-        body = lambda *refs: interior(local, *refs)
-        return kernel_call(body, outs, scratch, 1024, "interior", outside={len(args) - 1: pl.ANY})(*args)
+        return kernel_call(interior, outs, [coef, buf, buf, total], 1024, "interior", outside={4: pl.ANY})(*args)
+
+    def call_whole(*args):
+        outs = (shape(own, rows, ny), shape(own, rows, ny))
+        buf = pltpu.VMEM((2, blocks, rows + 3 * TILE, LANES), f32)
+        coef = pltpu.VMEM((SWEEPS, 2, blocks, rows + TILE, LANES), f32)
+        return kernel_call(whole, outs, [coef, buf, buf], 1024, "whole", outside={6: pl.ANY})(*args)
 
     def call_edges(*args):
         outs = (shape(own, TILE, ny), shape(own, TILE, ny))
@@ -380,30 +476,29 @@
         return kernel_call(edges, outs, scratch, 1024, "edges", outside={7: pl.ANY})(*args)
 
     partner = lax.ppermute(gradient, "mem", near)
+    rim = jnp.concatenate([gradient[:, :TILE], gradient[:, rows - TILE :]], axis=1)
+    far_rim = lax.ppermute(rim, "mem", cross)
     far = lax.ppermute(gradient, "mem", across)
-    far_partner = lax.ppermute(gradient, "mem", cross)
-
-    e0, o0, u0, p0, near_g, near_counts = call_project(True, stored, stored_g, stored_counts, partner)
+    e0, o0, p0, near_g, near_counts = call_project(True, stored, stored_g, stored_counts, partner)
     e0 = lax.ppermute(e0, "strip", even)
     o0 = lax.ppermute(o0, "strip", odd)
-    own0, other0, p1 = call_interior(True, p0, near_g, partner, near_counts, stored)
-
-    e1, o1, u1 = call_project(False, p1, far, far_partner, own0)
+    p1 = call_fetch(stored, near_counts)
+    e1, o1, u1 = call_project(False, p1, far, far_rim)
+    far_partner = lax.ppermute(call_relay(far, u1)[0], "mem", near)
     e1 = lax.ppermute(e1, "strip", even)
     o1 = lax.ppermute(o1, "strip", odd)
-    own1, other1 = call_interior(False, p1, far, far_partner, near_counts, u1)
-    eown0, eother0 = call_edges(p0, u0, e0, o0, e0, o0, near_counts, own1)
-    eown1, eother1 = call_edges(p1, u1, e1, o1, e0, o0, near_counts, eown0)
-
-    inner = own0 + lax.ppermute(other0, "mem", near)
-    inner = inner + lax.ppermute(own1, "mem", across)
-    inner = inner + lax.ppermute(other1, "mem", cross)
-    enear0 = lax.ppermute(eother0, "mem", near)
+    own1, other1 = call_interior(p1, far, far_partner, near_counts, u1)
+    own0, other0 = call_whole(p0, near_g, partner, e0, o0, near_counts, own1)
+    eown1, eother1 = call_edges(p1, u1, e1, o1, e0, o0, near_counts, own0)
+
+    near0 = lax.ppermute(other0, "mem", near)
+    inner = lax.ppermute(own1, "mem", across) + lax.ppermute(other1, "mem", cross)
+    eown1, eother1 = call_relay(eown1, eother1, inner)
     efar1 = lax.ppermute(eown1, "mem", across)
     ecross1 = lax.ppermute(eother1, "mem", cross)
     return kernel_call(
         lambda *refs: finish(scale, *refs), shape(own, rows, ny), [], 1024, "finish"
-    )(inner, eown0, enear0, efar1, ecross1)
+    )(own0, near0, inner, efar1, ecross1)
 
 
 def solution(mesh):

time: 45.2 us -> 46.9 us (1.038)
  starting transfers between devices: 16.9 us -> 18.8 us
  Pallas kernels: 24.5 us -> 23.2 us
  local copies, waits for them, and re-layouts: 0 us -> 0.88 us
    pallas_call x7 -> x9, Pallas kernels: 24.5 us -> 23.2 us  [call(): pl.pallas_call(body, out_shape=out_shape, in_specs=[pl.BlockSpec(memory_s...]
    ppermute x1, starting transfers between devices: 0.41 us -> 1.43 us  [per_device(): ecross1 = lax.ppermute(eother1, 'mem', cross)]
    ppermute x1, starting transfers between devices: 1.3 us -> 0.29 us  [per_device(): efar1 = lax.ppermute(eown1, 'mem', across)]
    ppermute x1, starting transfers between devices: 0.23 us -> 1.24 us  [per_device(): far = lax.ppermute(gradient, 'mem', across)]
    ppermute x5, starting transfers between devices: 5.36 us -> 6.36 us  [the longest x1 2.03 us: per_device(): near0 = lax.ppermute(other0, 'mem', near)]
    slice x0 -> x1, local copies, waits for them, and re-layouts: none -> 0.88 us  [per_device(): gradient[:, :TILE]]
  transfers between devices with their start and end apart: 13 -> 13, of which waited for: 2 -> 2; matrix products, arithmetic and copies ran while one was open for 0% -> 2% of each run, Pallas kernels for 53% -> 48%
where the time goes in v4:
time: 46.9 us; the launch traced here: 46.7 us
  Pallas kernels  23.2 us (49%)
  starting transfers between devices  18.8 us (40%)
  waiting for transfers between devices  3.59 us (8%)
  local copies, waits for them, and re-layouts  0.88 us (2%)
    pallas_call x9, Pallas kernels, call(): pl.pallas_call(body, out_shape=out_shape, in_specs=[pl.BlockSpec(memory_s...  23.2 us
    ppermute x1, starting transfers between devices, per_device(): o1 = lax.ppermute(o1, 'strip', odd)  4.39 us
    ppermute x1, starting transfers between devices, per_device(): o0 = lax.ppermute(o0, 'strip', odd)  4.36 us
    ppermute x1, waiting for transfers between devices, per_device(): efar1 = lax.ppermute(eown1, 'mem', across)  2.03 us
    ppermute x1, starting transfers between devices, per_device(): near0 = lax.ppermute(other0, 'mem', near)  2.03 us
    ppermute x1, starting transfers between devices, per_device(): lax.ppermute(other1, 'mem', cross)  1.81 us
    ppermute x1, waiting for transfers between devices, per_device(): ecross1 = lax.ppermute(eother1, 'mem', cross)  1.53 us
    ppermute x1, starting transfers between devices, per_device(): ecross1 = lax.ppermute(eother1, 'mem', cross)  1.43 us
  transfers between devices with their start and end apart: 13, of which 2 were waited for; matrix products, arithmetic and copies ran while one was open for 2% of the time, Pallas kernels for 48%

profile of v4, /device:TPU:3, one launch (start us, length us, event | category | flops | bytes accessed | tf_op | source)
XLA Modules:
  0.0 46.7 jit_solution(9343451400012086922)
XLA Ops:
  0.0 0.7 %collective-permute-start = (f32[2,32,1024]{2,1,0:T(8,128)}, f32[2,32,1024]{2,1,0:T(8,128)S(1)}, u32[]{:S(2)}, u32[]{:S(2)}) collective-permute-start(f32[2,32,1024]{2,1,0:T(8,128)} %refs_1_.1), channel_id=1, source_target_pairs={{0,8},{8,0},{16,24},{24,16},{1,9},{9,1},{17,25},{25,17},{2,10},{10... | collective-permute-start | bytes 786440 | tf_op jit(solution)/shard_map/ppermute | solution.py:478
  0.7 1.2 %collective-permute-start.3 = (f32[2,32,1024]{2,1,0:T(8,128)}, f32[2,32,1024]{2,1,0:T(8,128)S(1)}, u32[]{:S(2)}, u32[]{:S(2)}) collective-permute-start(f32[2,32,1024]{2,1,0:T(8,128)} %refs_1_.1), channel_id=1, source_target_pairs={{0,16},{8,24},{16,0},{24,8},{1,17},{9,25},{17,1},{25,9},{2,18},{10... | collective-permute-start | bytes 786440 | tf_op jit(solution)/shard_map/ppermute | solution.py:481
  1.9 0.9 %fusion = (f32[2,8,1024]{2,1,0:T(8,128)S(1)}, f32[2,8,1024]{2,1,0:T(8,128)S(1)}) fusion(f32[2,32,1024]{2,1,0:T(8,128)} %refs_1_.1), kind=kLoop, calls=%fused_computation.1 | loop fusion | bytes 262144 | tf_op jit(solution)/shard_map/slice | solution.py:479
  2.8 0.5 collective-permute-start.4
  3.3 0.0 collective-permute-done.refs_3_.gb_ref
  3.3 2.8 %project.2 = (f32[9,8,1024]{2,1,0:T(8,128)S(1)}, f32[9,8,1024]{2,1,0:T(8,128)S(1)}, bf16[16,4,32,1024]{3,2,1,0:T(8,128)(2,1)S(1)}, f32[2,32,1024]{2,1,0:T(8,128)S(1)}, s32[32,1024]{1,0:T(8,128)S(1)}) custom-call(bf16[16,8,32,1024]{3,2,1,0:T(8,128)(2,1)} %refs_0_.3, f32[2,32,1024]{2,1,0:T(8,128)} %refs_1_.1, s32[32,1024]{1,0:T(8,128)} %refs_2_.1, ...), custom_call_target="tpu_custom_call" | custom-call | flops 1024 | bytes 1024 | tf_op jit(solution)/shard_map/project/pallas_call | solution.py:29
  6.1 0.1 collective-permute-start.1
  6.2 4.4 %collective-permute-start.2 = (f32[9,8,1024]{2,1,0:T(8,128)S(1)}, f32[9,8,1024]{2,1,0:T(8,128)S(1)}, u32[]{:S(2)}, u32[]{:S(2)}) collective-permute-start(f32[9,8,1024]{2,1,0:T(8,128)S(1)} %get-tuple-element.24), channel_id=1, source_target_pairs={{1,2},{3,4},{5,6},{2,1},{4,3},{6,5},{9,10},{11,12},{13,14},{10,9},... | collective-permute-start | bytes 884744 | tf_op jit(solution)/shard_map/ppermute | solution.py:484
  10.6 2.3 %fetch.1.refs_0_.p_ref = bf16[16,4,32,1024]{3,2,1,0:T(8,128)(2,1)S(1)} custom-call(bf16[16,8,32,1024]{3,2,1,0:T(8,128)(2,1)} %refs_0_.3, s32[32,1024]{1,0:T(8,128)S(1)} %get-tuple-element.25.refs_1_.counts_ref), custom_call_target="tpu_custom_call" | custom-call | flops 1024 | bytes 1024 | tf_op jit(solution)/shard_map/fetch/pallas_call | solution.py:29
  12.9 0.0 collective-permute-done.4.refs_2_
  12.9 0.0 collective-permute-done.3.refs_1_.refs_0_.ga_ref
  12.9 0.5 %project.3 = (f32[8,8,1024]{2,1,0:T(8,128)S(1)}, f32[8,8,1024]{2,1,0:T(8,128)S(1)}, f32[16,16,1024]{2,1,0:T(8,128)S(1)}) custom-call(bf16[16,4,32,1024]{3,2,1,0:T(8,128)(2,1)S(1)} %fetch.1.refs_0_.p_ref, f32[2,32,1024]{2,1,0:T(8,128)S(1)} %collective-permute-done.3.refs_1_.refs_0_.ga_ref, f32[2,16,1024]{2,1,0:T(8,128)S(1)} %collective-permute-done.4.refs_2_), custom_call_target="tpu_custom_call" | custom-call | flops 1024 | bytes 1024 | tf_op jit(solution)/shard_map/project/pallas_call | solution.py:29
  13.5 0.9 %collective-permute-start.5 = (f32[2,32,1024]{2,1,0:T(8,128)S(1)}, f32[2,32,1024]{2,1,0:T(8,128)S(1)}, u32[]{:S(2)}, u32[]{:S(2)}) collective-permute-start(f32[2,32,1024]{2,1,0:T(8,128)S(1)} %relay.2), channel_id=1, source_target_pairs={{0,8},{8,0},{16,24},{24,16},{1,9},{9,1},{17,25},{25,17},{2,10},{10... | collective-permute-start | bytes 786440 | tf_op jit(solution)/shard_map/ppermute | solution.py:487
  14.3 0.0 collective-permute-start.9
  14.3 4.4 %collective-permute-start.10 = (f32[8,8,1024]{2,1,0:T(8,128)S(1)}, f32[8,8,1024]{2,1,0:T(8,128)S(1)}, u32[]{:S(2)}, u32[]{:S(2)}) collective-permute-start(f32[8,8,1024]{2,1,0:T(8,128)S(1)} %get-tuple-element.32), channel_id=1, source_target_pairs={{1,2},{3,4},{5,6},{2,1},{4,3},{6,5},{9,10},{11,12},{13,14},{10,9},... | collective-permute-start | bytes 786440 | tf_op jit(solution)/shard_map/ppermute | solution.py:489
  18.7 0.0 collective-permute-done.5.gb_ref
  18.7 6.0 %interior.1 = (f32[2,24,1024]{2,1,0:T(8,128)S(1)}, f32[2,24,1024]{2,1,0:T(8,128)S(1)}) custom-call(bf16[16,4,32,1024]{3,2,1,0:T(8,128)(2,1)S(1)} %fetch.1.refs_0_.p_ref, f32[2,32,1024]{2,1,0:T(8,128)S(1)} %collective-permute-done.3.refs_1_.refs_0_.ga_ref, f32[2,32,1024]{2,1,0:T(8,128)S(1)} %collective-permute-done.5.gb_ref, ...), custom_call_target="tpu_custom_call" | custom-call | flops 1024 | bytes 1024 | tf_op jit(solution)/shard_map/interior/pallas_call | solution.py:29
  24.7 1.8 %collective-permute-start.8 = (f32[2,24,1024]{2,1,0:T(8,128)S(1)}, f32[2,24,1024]{2,1,0:T(8,128)S(1)}, u32[]{:S(2)}, u32[]{:S(2)}) collective-permute-start(f32[2,24,1024]{2,1,0:T(8,128)S(1)} %get-tuple-element.30), channel_id=1, source_target_pairs={{0,24},{8,16},{16,8},{24,0},{1,25},{9,17},{17,9},{25,1},{2,26},{10... | collective-permute-start | bytes 589832 | tf_op jit(solution)/shard_map/ppermute | solution.py:495
  26.6 0.0 collective-permute-done.1.e_ref.ce_ref
  26.6 1.2 %collective-permute-start.7 = (f32[2,24,1024]{2,1,0:T(8,128)S(1)}, f32[2,24,1024]{2,1,0:T(8,128)S(1)}, u32[]{:S(2)}, u32[]{:S(2)}) collective-permute-start(f32[2,24,1024]{2,1,0:T(8,128)S(1)} %get-tuple-element.27._), channel_id=1, source_target_pairs={{0,16},{8,24},{16,0},{24,8},{1,17},{9,25},{17,1},{25,9},{2,18},{10... | collective-permute-start | bytes 589832 | tf_op jit(solution)/shard_map/ppermute | solution.py:495
  27.8 0.0 collective-permute-done.2.o_ref.co_ref
  27.8 6.6 %whole.1 = (f32[2,32,1024]{2,1,0:T(8,128)S(1)}, f32[2,32,1024]{2,1,0:T(8,128)S(1)}) custom-call(bf16[16,4,32,1024]{3,2,1,0:T(8,128)(2,1)S(1)} %get-tuple-element.21.p_ref, f32[2,32,1024]{2,1,0:T(8,128)S(1)} %get-tuple-element.22.ga_ref, f32[2,32,1024]{2,1,0:T(8,128)S(1)} %collective-permute-done.refs_3_.gb_ref, ...), custom_call_target="tpu_custom_call" | custom-call | flops 1024 | bytes 1024 | tf_op jit(solution)/shard_map/whole/pallas_call | solution.py:29
  34.4 2.0 %collective-permute-start.6 = (f32[2,32,1024]{2,1,0:T(8,128)S(1)}, f32[2,32,1024]{2,1,0:T(8,128)S(1)}, u32[]{:S(2)}, u32[]{:S(2)}) collective-permute-start(f32[2,32,1024]{2,1,0:T(8,128)S(1)} %get-tuple-element.29), channel_id=1, source_target_pairs={{0,8},{8,0},{16,24},{24,16},{1,9},{9,1},{17,25},{25,17},{2,10},{10... | collective-permute-start | bytes 786440 | tf_op jit(solution)/shard_map/ppermute | solution.py:494
  36.4 0.0 collective-permute-done.9.e_ref
  36.5 0.0 collective-permute-done.10.o_ref
  36.5 4.1 %edges.1 = (f32[2,8,1024]{2,1,0:T(8,128)S(1)}, f32[2,8,1024]{2,1,0:T(8,128)S(1)}) custom-call(bf16[16,4,32,1024]{3,2,1,0:T(8,128)(2,1)S(1)} %fetch.1.refs_0_.p_ref, f32[16,16,1024]{2,1,0:T(8,128)S(1)} %get-tuple-element.26.refs_1_._.u_ref, f32[8,8,1024]{2,1,0:T(8,128)S(1)} %collective-permute-done.9.e_ref, f32[8,8,1024]{2,1,0:T(8,128)S(1)} %collective-permute-done.10.o_ref, ...), custom_call_target="tpu_custom_call" | custom-call | flops 1024 | bytes 1024 | tf_op jit(solution)/shard_map/edges/pallas_call | solution.py:29
  40.5 0.0 collective-permute-done.8
  40.6 0.0 collective-permute-done.7
  40.6 0.3 collective-permute-start.11
  40.9 1.4 %collective-permute-start.12 = (f32[2,8,1024]{2,1,0:T(8,128)S(1)}, f32[2,8,1024]{2,1,0:T(8,128)S(1)}, u32[]{:S(2)}, u32[]{:S(2)}) collective-permute-start(f32[2,8,1024]{2,1,0:T(8,128)S(1)} %get-tuple-element.36), channel_id=1, source_target_pairs={{0,24},{8,16},{16,8},{24,0},{1,25},{9,17},{17,9},{25,1},{2,26},{10... | collective-permute-start | bytes 196616 | tf_op jit(solution)/shard_map/ppermute | solution.py:498
  42.3 2.0 %collective-permute-done.11.refs_3_ = f32[2,8,1024]{2,1,0:T(8,128)S(1)} collective-permute-done((f32[2,8,1024]{2,1,0:T(8,128)S(1)}, f32[2,8,1024]{2,1,0:T(8,128)S(1)}, u32[]{:S(2)}, u32[]{:S(2)}) %collective-permute-start.11) | collective-permute-done | bytes 65568 | tf_op jit(solution)/shard_map/ppermute | solution.py:497
  44.4 1.5 %collective-permute-done.12.refs_4_ = f32[2,8,1024]{2,1,0:T(8,128)S(1)} collective-permute-done((f32[2,8,1024]{2,1,0:T(8,128)S(1)}, f32[2,8,1024]{2,1,0:T(8,128)S(1)}, u32[]{:S(2)}, u32[]{:S(2)}) %collective-permute-start.12) | collective-permute-done | bytes 65568 | tf_op jit(solution)/shard_map/ppermute | solution.py:498
  45.9 0.0 collective-permute-done.6.refs_1_
  45.9 0.8 %finish.1 = f32[2,32,1024]{2,1,0:T(8,128)} custom-call(f32[2,32,1024]{2,1,0:T(8,128)S(1)} %get-tuple-element.28._.refs_0_, f32[2,32,1024]{2,1,0:T(8,128)S(1)} %collective-permute-done.6.refs_1_, f32[2,24,1024]{2,1,0:T(8,128)S(1)} %add.3.refs_2_, f32[2,8,1024]{2,1,0:T(8,128)S(1)} %collective-permute-done.11.refs_3_, ...), custom_call_target="tpu_custom_call" | custom-call | flops 1024 | bytes 1024 | tf_op jit(solution)/shard_map/finish/pallas_call | solution.py:29
  (4 shorter events, 0.1 us)
Async XLA Ops:
  0.0 3.3 %collective-permute-start = (f32[2,32,1024]{2,1,0:T(8,128)}, f32[2,32,1024]{2,1,0:T(8,128)S(1)}, u32[]{:S(2)}, u32[]{:S(2)}) collective-permute-start(f32[2,32,1024]{2,1,0:T(8,128)} %refs_1_.1), channel_id=1, source_target_pairs={{0,8},{8,0},{16,24},{24,16},{1,9},{9,1},{17,25},{25,17},{2,10},{10... | collective-permute-start | bytes 786440 | tf_op jit(solution)/shard_map/ppermute | solution.py:478
  0.7 12.2 %collective-permute-start.3 = (f32[2,32,1024]{2,1,0:T(8,128)}, f32[2,32,1024]{2,1,0:T(8,128)S(1)}, u32[]{:S(2)}, u32[]{:S(2)}) collective-permute-start(f32[2,32,1024]{2,1,0:T(8,128)} %refs_1_.1), channel_id=1, source_target_pairs={{0,16},{8,24},{16,0},{24,8},{1,17},{9,25},{17,1},{25,9},{2,18},{10... | collective-permute-start | bytes 786440 | tf_op jit(solution)/shard_map/ppermute | solution.py:481
  2.8 10.1 %collective-permute-start.4 = (f32[2,16,1024]{2,1,0:T(8,128)S(1)}, f32[2,16,1024]{2,1,0:T(8,128)S(1)}, u32[]{:S(2)}, u32[]{:S(2)}) collective-permute-start(f32[2,16,1024]{2,1,0:T(8,128)S(1)} %pad_maximum_fusion), channel_id=1, source_target_pairs={{0,24},{8,16},{16,8},{24,0},{1,25},{9,17},{17,9},{25,1},{2,26},{10... | collective-permute-start | bytes 393224 | tf_op jit(solution)/shard_map/ppermute | solution.py:480
  6.1 20.4 %collective-permute-start.1 = (f32[9,8,1024]{2,1,0:T(8,128)S(1)}, f32[9,8,1024]{2,1,0:T(8,128)S(1)}, u32[]{:S(2)}, u32[]{:S(2)}) collective-permute-start(f32[9,8,1024]{2,1,0:T(8,128)S(1)} %get-tuple-element.23), channel_id=1, source_target_pairs={{0,1},{1,0},{2,3},{3,2},{4,5},{5,4},{6,7},{7,6},{8,9},{9,8},{10,11... | collective-permute-start | bytes 884744 | tf_op jit(solution)/shard_map/ppermute | solution.py:483
  6.2 21.5 %collective-permute-start.2 = (f32[9,8,1024]{2,1,0:T(8,128)S(1)}, f32[9,8,1024]{2,1,0:T(8,128)S(1)}, u32[]{:S(2)}, u32[]{:S(2)}) collective-permute-start(f32[9,8,1024]{2,1,0:T(8,128)S(1)} %get-tuple-element.24), channel_id=1, source_target_pairs={{1,2},{3,4},{5,6},{2,1},{4,3},{6,5},{9,10},{11,12},{13,14},{10,9},... | collective-permute-start | bytes 884744 | tf_op jit(solution)/shard_map/ppermute | solution.py:484
  13.5 5.3 %collective-permute-start.5 = (f32[2,32,1024]{2,1,0:T(8,128)S(1)}, f32[2,32,1024]{2,1,0:T(8,128)S(1)}, u32[]{:S(2)}, u32[]{:S(2)}) collective-permute-start(f32[2,32,1024]{2,1,0:T(8,128)S(1)} %relay.2), channel_id=1, source_target_pairs={{0,8},{8,0},{16,24},{24,16},{1,9},{9,1},{17,25},{25,17},{2,10},{10... | collective-permute-start | bytes 786440 | tf_op jit(solution)/shard_map/ppermute | solution.py:487
  14.3 22.1 %collective-permute-start.9 = (f32[8,8,1024]{2,1,0:T(8,128)S(1)}, f32[8,8,1024]{2,1,0:T(8,128)S(1)}, u32[]{:S(2)}, u32[]{:S(2)}) collective-permute-start(f32[8,8,1024]{2,1,0:T(8,128)S(1)} %get-tuple-element.31), channel_id=1, source_target_pairs={{0,1},{1,0},{2,3},{3,2},{4,5},{5,4},{6,7},{7,6},{8,9},{9,8},{10,11... | collective-permute-start | bytes 786440 | tf_op jit(solution)/shard_map/ppermute | solution.py:488
  14.3 22.1 %collective-permute-start.10 = (f32[8,8,1024]{2,1,0:T(8,128)S(1)}, f32[8,8,1024]{2,1,0:T(8,128)S(1)}, u32[]{:S(2)}, u32[]{:S(2)}) collective-permute-start(f32[8,8,1024]{2,1,0:T(8,128)S(1)} %get-tuple-element.32), channel_id=1, source_target_pairs={{1,2},{3,4},{5,6},{2,1},{4,3},{6,5},{9,10},{11,12},{13,14},{10,9},... | collective-permute-start | bytes 786440 | tf_op jit(solution)/shard_map/ppermute | solution.py:489
  24.7 15.8 %collective-permute-start.8 = (f32[2,24,1024]{2,1,0:T(8,128)S(1)}, f32[2,24,1024]{2,1,0:T(8,128)S(1)}, u32[]{:S(2)}, u32[]{:S(2)}) collective-permute-start(f32[2,24,1024]{2,1,0:T(8,128)S(1)} %get-tuple-element.30), channel_id=1, source_target_pairs={{0,24},{8,16},{16,8},{24,0},{1,25},{9,17},{17,9},{25,1},{2,26},{10... | collective-permute-start | bytes 589832 | tf_op jit(solution)/shard_map/ppermute | solution.py:495
  26.6 14.0 %collective-permute-start.7 = (f32[2,24,1024]{2,1,0:T(8,128)S(1)}, f32[2,24,1024]{2,1,0:T(8,128)S(1)}, u32[]{:S(2)}, u32[]{:S(2)}) collective-permute-start(f32[2,24,1024]{2,1,0:T(8,128)S(1)} %get-tuple-element.27._), channel_id=1, source_target_pairs={{0,16},{8,24},{16,0},{24,8},{1,17},{9,25},{17,1},{25,9},{2,18},{10... | collective-permute-start | bytes 589832 | tf_op jit(solution)/shard_map/ppermute | solution.py:495
  34.4 11.5 %collective-permute-start.6 = (f32[2,32,1024]{2,1,0:T(8,128)S(1)}, f32[2,32,1024]{2,1,0:T(8,128)S(1)}, u32[]{:S(2)}, u32[]{:S(2)}) collective-permute-start(f32[2,32,1024]{2,1,0:T(8,128)S(1)} %get-tuple-element.29), channel_id=1, source_target_pairs={{0,8},{8,0},{16,24},{24,16},{1,9},{9,1},{17,25},{25,17},{2,10},{10... | collective-permute-start | bytes 786440 | tf_op jit(solution)/shard_map/ppermute | solution.py:494
  40.6 3.8 %collective-permute-start.11 = (f32[2,8,1024]{2,1,0:T(8,128)S(1)}, f32[2,8,1024]{2,1,0:T(8,128)S(1)}, u32[]{:S(2)}, u32[]{:S(2)}) collective-permute-start(f32[2,8,1024]{2,1,0:T(8,128)S(1)} %get-tuple-element.35), channel_id=1, source_target_pairs={{0,16},{8,24},{16,0},{24,8},{1,17},{9,25},{17,1},{25,9},{2,18},{10... | collective-permute-start | bytes 196616 | tf_op jit(solution)/shard_map/ppermute | solution.py:497
  40.9 5.0 %collective-permute-start.12 = (f32[2,8,1024]{2,1,0:T(8,128)S(1)}, f32[2,8,1024]{2,1,0:T(8,128)S(1)}, u32[]{:S(2)}, u32[]{:S(2)}) collective-permute-start(f32[2,8,1024]{2,1,0:T(8,128)S(1)} %get-tuple-element.36), channel_id=1, source_target_pairs={{0,24},{8,16},{16,8},{24,0},{1,25},{9,17},{17,9},{25,1},{2,26},{10... | collective-permute-start | bytes 196616 | tf_op jit(solution)/shard_map/ppermute | solution.py:498

commit v5 on v2

--- a/solution.py
+++ b/solution.py
@@ -21,6 +21,7 @@
 TILE = 8
 HALF = 16
 VMEM_BYTES = 40 * 2**20
+PREPARE_FLOPS = 10**10
 
 
 def kernel_call(body, out_shape, scratch, flops, name, outside={}):
@@ -40,18 +41,6 @@
     return call
 
 
-def hold(x, *tokens):
-    return pl.pallas_call(
-        lambda *refs: None,
-        out_shape=jax.ShapeDtypeStruct(x.shape, x.dtype),
-        in_specs=[pl.BlockSpec(memory_space=pl.ANY)] * (1 + len(tokens)),
-        out_specs=pl.BlockSpec(memory_space=pl.ANY),
-        input_output_aliases={0: 0},
-        cost_estimate=pl.CostEstimate(flops=1, bytes_accessed=1, transcendentals=0),
-        name="hold",
-    )(x, *tokens)
-
-
 def lane_masks():
     lane = lax.broadcasted_iota(jnp.int32, (TILE, LANES), 1)
     return lane == 0, lane == LANES - 1
@@ -78,19 +67,21 @@
     return sums
 
 
-def order(own):
+def fields_of(local, own):
     shares = VARS // own
-    share = lax.axis_index("mem") % shares
-    return [at * own + k for at in (share, shares - 1 - share) for k in range(own)]
-
-
-def fetch(local, own, p_ref, *rest):
-    out_ref, sem = rest[-2:]
-    members = out_ref.shape[0]
-    slot = lax.axis_index("mem") // (VARS // own)
+    mem = lax.axis_index("mem")
+    slot, share = mem // shares, mem % shares
     slot = slot if local else SLOTS - 1 - slot
+    return [slot * VARS + at * own + k for at in (share, shares - 1 - share) for k in range(own)]
+
+
+def prepare(g_ref, counts_ref, near_g_ref, rim_ref, near_counts_ref, sem):
+    rows = g_ref.shape[1]
     copies = [
-        pltpu.make_async_copy(p_ref.at[m, pl.ds(slot * VARS, VARS)], out_ref.at[m], sem.at[m]) for m in range(members)
+        pltpu.make_async_copy(g_ref.at[:, 0:TILE], rim_ref.at[:, 0:TILE], sem.at[0]),
+        pltpu.make_async_copy(g_ref.at[:, rows - TILE : rows], rim_ref.at[:, TILE : 2 * TILE], sem.at[1]),
+        pltpu.make_async_copy(g_ref, near_g_ref, sem.at[2]),
+        pltpu.make_async_copy(counts_ref, near_counts_ref, sem.at[3]),
     ]
     for copy in copies:
         copy.start()
@@ -108,10 +99,9 @@
     else:
         *g_refs, _, e_ref, o_ref, u_ref = rest
     members, _, rows, ny = p_ref.shape
-    grows = g_refs[0].shape[1]
     even = lax.axis_index("strip") % 2 == 0
     half = top_half()
-    fields = order(own)
+    fields = fields_of(local, own)
     grads = weights_of(own, g_refs)
 
     def put(row, j, top, bottom):
@@ -124,7 +114,7 @@
             bottom = counts_ref[rows - TILE : rows, cols(j)].astype(jnp.float32)
             put(members // 2, j, top, pltpu.roll(bottom, TILE // 2, 0))
 
-    def pair(q, carry):
+    def pair(q):
         for j in range(ny // LANES):
             tops, bottoms = [], []
             for m in (2 * q, 2 * q + 1):
@@ -133,7 +123,7 @@
                     low = p_ref[m, f, 0:HALF, cols(j)].astype(jnp.float32)[0:TILE]
                     high = p_ref[m, f, rows - HALF : rows, cols(j)].astype(jnp.float32)[HALF - TILE :]
                     low = low * g_ref[k, 0:TILE, cols(j)]
-                    high = high * g_ref[k, grows - TILE : grows, cols(j)]
+                    high = high * g_ref[k, g_ref.shape[1] - TILE : g_ref.shape[1], cols(j)]
                     top = low if top is None else top + low
                     bottom = high if bottom is None else bottom + high
                 u_ref[m, 0:TILE, cols(j)] = top
@@ -143,19 +133,18 @@
             top = jnp.where(half, tops[0], pltpu.roll(tops[1], TILE // 2, 0))
             bottom = jnp.where(half, pltpu.roll(bottoms[0], TILE // 2, 0), bottoms[1])
             put(q, j, top, bottom)
-        return carry
-
-    lax.fori_loop(0, members // 2, pair, 0)
-
-
-def interior(p_ref, *refs):
+
+    pl.loop(0, members // 2)(pair)
+
+
+def interior(local, p_ref, *refs):
     *g_refs, counts_ref, _, own_ref, other_ref, coef, buf_a, buf_b, total_ref = refs
     members, _, rows, ny = p_ref.shape
     own = own_ref.shape[0]
     blocks = ny // LANES
     group = buf_a.shape[0]
     first, last = lane_masks()
-    fields = order(own)
+    fields = fields_of(local, own)
     grads = weights_of(own, g_refs)
     sums = [(own_ref, k) for k in range(own)] + [(other_ref, k) for k in range(own)]
     skip = TILE // 2
@@ -222,14 +211,14 @@
                 ref[k, r : r + TILE, cols(j)] = total_ref[n, j, skip + r : skip + r + TILE]
 
 
-def edges(p_ref, u_ref, e_ref, o_ref, ce_ref, co_ref, counts_ref, _, own_ref, other_ref, coef, buf_a, buf_b, halo):
+def edges(local, p_ref, u_ref, e_ref, o_ref, ce_ref, co_ref, counts_ref, _, own_ref, other_ref, coef, buf_a, buf_b, halo):
     members, _, rows, ny = p_ref.shape
     own = own_ref.shape[0]
     blocks = ny // LANES
     first, last = lane_masks()
     half = top_half()
     even = lax.axis_index("strip") % 2 == 0
-    fields = order(own)
+    fields = fields_of(local, own)
     sums = [(own_ref, k) for k in range(own)] + [(other_ref, k) for k in range(own)]
     crow = ce_ref.shape[0] - 1
     for j in range(blocks):
@@ -307,7 +296,7 @@
 
 
 def finish(scale, *refs):
-    inner_refs, edge_refs, out_ref = refs[:4], refs[4:8], refs[8]
+    inner_ref, *edge_refs, out_ref = refs
     own, rows, ny = out_ref.shape
     half = top_half()
     for k in range(own):
@@ -315,8 +304,7 @@
             edge = sum(ref[k, :, cols(j)] for ref in edge_refs[1:]) + edge_refs[0][k, :, cols(j)]
             parts = [edge]
             for r in range(0, rows - TILE, TILE):
-                inner = sum(ref[k, r : r + TILE, cols(j)] for ref in inner_refs[1:]) + inner_refs[0][k, r : r + TILE, cols(j)]
-                parts.append(pltpu.roll(inner, TILE // 2, 0))
+                parts.append(pltpu.roll(inner_ref[k, r : r + TILE, cols(j)], TILE // 2, 0))
             parts.append(edge)
             for n in range(rows // TILE):
                 out_ref[k, n * TILE : (n + 1) * TILE, cols(j)] = jnp.where(half, parts[n], parts[n + 1]) * scale
@@ -345,12 +333,11 @@
     def window(*lead):
         return pltpu.VMEM((*lead, blocks, 40, LANES), f32)
 
-    def call_fetch(local, *token):
-        return kernel_call(
-            lambda *refs: fetch(local, own, *refs),
-            jax.ShapeDtypeStruct((members, VARS, rows, ny), perturbations.dtype),
-            [pltpu.SemaphoreType.DMA((members,))], 1024, "fetch", outside={0: pl.ANY, 1: pl.ANY},
-        )(pltpu.with_memory_space_constraint(perturbations, pltpu.HBM), *token)
+    def call_prepare(*args):
+        outs = (shape(own, rows, ny), shape(own, 2 * TILE, ny), jax.ShapeDtypeStruct((rows, ny), counts.dtype))
+        stored = [pltpu.with_memory_space_constraint(x, pltpu.HBM) for x in args]
+        outside = {0: pl.ANY, 1: pl.ANY}
+        return kernel_call(prepare, outs, [pltpu.SemaphoreType.DMA((4,))], PREPARE_FLOPS, "prepare", outside)(*stored)
 
     def call_project(local, *args):
         pairs = members // 2 + (1 if local else 0)
@@ -359,46 +346,47 @@
         body = lambda *refs: project_edges(local, own, *refs)
         return kernel_call(body, outs, [], 1024, "project", outside=outside)(*args)
 
-    def call_interior(*args):
+    def call_interior(local, *args):
         outs = (shape(own, rows - TILE, ny), shape(own, rows - TILE, ny))
         total = pltpu.VMEM((VARS, blocks, rows, LANES), f32)
         buf = pltpu.VMEM((2, blocks, rows + 2 * TILE, LANES), f32)
         coef = pltpu.VMEM((SWEEPS - 1, 2, blocks, rows, LANES), f32)
-        return kernel_call(interior, outs, [coef, buf, buf, total], 1024, "interior", outside={len(args) - 1: pl.ANY})(*args)
-
-    def call_edges(*args):
+        body = lambda *refs: interior(local, *refs)
+        return kernel_call(body, outs, [coef, buf, buf, total], 1024, "interior", outside={len(args) - 1: pl.ANY})(*args)
+
+    def call_edges(local, *args):
         outs = (shape(own, TILE, ny), shape(own, TILE, ny))
         scratch = [window(SWEEPS, 2), window(2), window(2), window()]
-        return kernel_call(edges, outs, scratch, 1024, "edges", outside={7: pl.ANY})(*args)
-
+        body = lambda *refs: edges(local, *refs)
+        return kernel_call(body, outs, scratch, 1024, "edges", outside={7: pl.ANY})(*args)
+
+    near_g, _, near_counts = call_prepare(gradient, counts)
     partner = lax.ppermute(gradient, "mem", near)
     far = lax.ppermute(gradient, "mem", across)
     far_partner = lax.ppermute(gradient, "mem", cross)
 
-    p0 = call_fetch(True)
-    e0, o0, u0 = call_project(True, p0, gradient, partner, counts)
+    p = perturbations
+    e0, o0, u0 = call_project(True, p, near_g, partner, near_counts)
     e0 = lax.ppermute(e0, "strip", even)
     o0 = lax.ppermute(o0, "strip", odd)
-    p1 = call_fetch(False, u0)
-    own0, other0 = call_interior(p0, gradient, partner, counts, p1)
-
-    e1, o1, u1 = call_project(False, p1, far, far_partner, own0)
+    own0, other0 = call_interior(True, p, near_g, partner, near_counts, u0)
+
+    e1, o1, u1 = call_project(False, p, far, far_partner, own0)
     e1 = lax.ppermute(e1, "strip", even)
     o1 = lax.ppermute(o1, "strip", odd)
-    own1, other1 = call_interior(p1, far, far_partner, counts, u1)
-    eown0, eother0 = call_edges(p0, u0, e0, o0, e0, o0, counts, own1)
-    eown1, eother1 = call_edges(p1, u1, e1, o1, e0, o0, counts, eown0)
-
-    near0 = lax.ppermute(other0, "mem", near)
-    far1 = hold(lax.ppermute(own1, "mem", across), near0)
-    cross1 = hold(lax.ppermute(other1, "mem", cross), far1)
-    enear0 = hold(lax.ppermute(eother0, "mem", near), cross1)
-    efar1 = hold(lax.ppermute(eown1, "mem", across), enear0)
-    ecross1 = hold(lax.ppermute(eother1, "mem", cross), efar1)
-
+    own1, other1 = call_interior(False, p, far, far_partner, near_counts, u1)
+    eown0, eother0 = call_edges(True, p, u0, e0, o0, e0, o0, near_counts, own1)
+    eown1, eother1 = call_edges(False, p, u1, e1, o1, e0, o0, near_counts, eown0)
+
+    inner = own0 + lax.ppermute(other0, "mem", near)
+    inner = inner + lax.ppermute(own1, "mem", across)
+    inner = inner + lax.ppermute(other1, "mem", cross)
+    enear0 = lax.ppermute(eother0, "mem", near)
+    efar1 = lax.ppermute(eown1, "mem", across)
+    ecross1 = lax.ppermute(eother1, "mem", cross)
     return kernel_call(
         lambda *refs: finish(scale, *refs), shape(own, rows, ny), [], 1024, "finish"
-    )(own0, near0, far1, cross1, eown0, enear0, efar1, ecross1)
+    )(inner, eown0, enear0, efar1, ecross1)
 
 
 def solution(mesh):

time: 53.6 us -> 44.7 us (0.83)
  local copies, waits for them, and re-layouts: 8.56 us -> 0.01 us
  Pallas kernels: 26.5 us -> 24 us
  waiting for transfers between devices: 1.16 us -> 3.56 us
    unnamed x28 -> x2, local copies, waits for them, and re-layouts: 8.56 us -> 0.01 us
    pallas_call x9 -> x8, Pallas kernels: 26.5 us -> 24 us  [call(): pl.pallas_call(body, out_shape=out_shape, in_specs=[pl.BlockSpec(memory_s...]
    ppermute x6, waiting for transfers between devices: 1.14 us -> 3.54 us  [the longest x1 1.98 us: per_device(): efar1 = lax.ppermute(eown1, 'mem', across)]
  transfers between devices with their start and end apart: 13 -> 13, of which waited for: 1 -> 2; matrix products, arithmetic and copies ran while one was open for 0% -> 0% of each run, Pallas kernels for 48% -> 52%
where the time goes in v5:
time: 44.7 us; the launch traced here: 44.6 us
  Pallas kernels  24 us (54%)
  starting transfers between devices  16.8 us (38%)
  waiting for transfers between devices  3.56 us (8%)
    pallas_call x8, Pallas kernels, call(): pl.pallas_call(body, out_shape=out_shape, in_specs=[pl.BlockSpec(memory_s...  24 us
    ppermute x1, starting transfers between devices, per_device(): o0 = lax.ppermute(o0, 'strip', odd)  4.36 us
    ppermute x1, starting transfers between devices, per_device(): o1 = lax.ppermute(o1, 'strip', odd)  4.36 us
    ppermute x1, waiting for transfers between devices, per_device(): efar1 = lax.ppermute(eown1, 'mem', across)  1.98 us
    ppermute x1, starting transfers between devices, per_device(): inner = own0 + lax.ppermute(other0, 'mem', near)  1.86 us
    ppermute x1, waiting for transfers between devices, per_device(): ecross1 = lax.ppermute(eother1, 'mem', cross)  1.55 us
    ppermute x1, starting transfers between devices, per_device(): efar1 = lax.ppermute(eown1, 'mem', across)  1.3 us
    ppermute x1, starting transfers between devices, per_device(): inner = inner + lax.ppermute(other1, 'mem', cross)  1.21 us
  transfers between devices with their start and end apart: 13, of which 2 were waited for; matrix products, arithmetic and copies ran while one was open for 0% of the time, Pallas kernels for 52%

profile of v5, /device:TPU:3, one launch (start us, length us, event | category | flops | bytes accessed | tf_op | source)
XLA Modules:
  0.0 44.6 jit_solution(3573416445618373192)
XLA Ops:
  0.0 0.0 copy-start
  0.0 0.7 %collective-permute-start = (f32[2,32,1024]{2,1,0:T(8,128)}, f32[2,32,1024]{2,1,0:T(8,128)S(1)}, u32[]{:S(2)}, u32[]{:S(2)}) collective-permute-start(f32[2,32,1024]{2,1,0:T(8,128)} %g_ref.1), channel_id=1, source_target_pairs={{0,8},{8,0},{16,24},{24,16},{1,9},{9,1},{17,25},{25,17},{2,10},{10... | collective-permute-start | bytes 786440 | tf_op jit(solution)/shard_map/ppermute | solution.py:364
  0.7 1.2 %collective-permute-start.3 = (f32[2,32,1024]{2,1,0:T(8,128)}, f32[2,32,1024]{2,1,0:T(8,128)S(1)}, u32[]{:S(2)}, u32[]{:S(2)}) collective-permute-start(f32[2,32,1024]{2,1,0:T(8,128)} %g_ref.1), channel_id=1, source_target_pairs={{0,24},{8,16},{16,8},{24,0},{1,25},{9,17},{17,9},{25,1},{2,26},{10... | collective-permute-start | bytes 786440 | tf_op jit(solution)/shard_map/ppermute | solution.py:366
  1.9 0.2 collective-permute-start.2
  2.1 2.0 %prepare.1 = (f32[2,32,1024]{2,1,0:T(8,128)S(1)}, f32[2,16,1024]{2,1,0:T(8,128)}, s32[32,1024]{1,0:T(8,128)S(1)}) custom-call(f32[2,32,1024]{2,1,0:T(8,128)} %g_ref.1, s32[32,1024]{1,0:T(8,128)} %counts_ref.1), custom_call_target="tpu_custom_call" | custom-call | flops 10000000000 | bytes 1024 | tf_op jit(solution)/shard_map/prepare/pallas_call | solution.py:30
  4.1 0.0 collective-permute-done.refs_2_
  4.1 0.0 copy-done
  4.1 0.5 %project.2 = (f32[9,8,1024]{2,1,0:T(8,128)S(1)}, f32[9,8,1024]{2,1,0:T(8,128)S(1)}, f32[16,16,1024]{2,1,0:T(8,128)S(1)}) custom-call(bf16[16,8,32,1024]{3,2,1,0:T(8,128)(2,1)S(1)} %copy-done, f32[2,32,1024]{2,1,0:T(8,128)S(1)} %get-tuple-element.21.refs_1_, f32[2,32,1024]{2,1,0:T(8,128)S(1)} %collective-permute-done.refs_2_, ...), custom_call_target="tpu_custom_call" | custom-call | flops 1024 | bytes 1024 | tf_op jit(solution)/shard_map/project/pallas_call | solution.py:30
  4.7 0.1 collective-permute-start.6
  4.8 4.4 %collective-permute-start.7 = (f32[9,8,1024]{2,1,0:T(8,128)S(1)}, f32[9,8,1024]{2,1,0:T(8,128)S(1)}, u32[]{:S(2)}, u32[]{:S(2)}) collective-permute-start(f32[9,8,1024]{2,1,0:T(8,128)S(1)} %get-tuple-element.30), channel_id=1, source_target_pairs={{1,2},{3,4},{5,6},{2,1},{4,3},{6,5},{9,10},{11,12},{13,14},{10,9},... | collective-permute-start | bytes 884744 | tf_op jit(solution)/shard_map/ppermute | solution.py:371
  9.1 6.0 %interior.2 = (f32[2,24,1024]{2,1,0:T(8,128)S(1)}, f32[2,24,1024]{2,1,0:T(8,128)S(1)}) custom-call(bf16[16,8,32,1024]{3,2,1,0:T(8,128)(2,1)S(1)} %copy-done, f32[2,32,1024]{2,1,0:T(8,128)S(1)} %get-tuple-element.21.refs_1_, f32[2,32,1024]{2,1,0:T(8,128)S(1)} %collective-permute-done.refs_2_, s32[32,1024]{1,0:T(8,128)S(1)} %get-tuple-element.22.refs_3_.refs_6_, ...), custom_call_target="tpu_custom_call" | custom-call | flops 1024 | bytes 1024 | tf_op jit(solution)/shard_map/interior/pallas_call | solution.py:30
  15.1 0.0 collective-permute-done.3.refs_2_
  15.2 0.0 collective-permute-done.2.refs_1_
  15.2 0.5 %project.3 = (f32[8,8,1024]{2,1,0:T(8,128)S(1)}, f32[8,8,1024]{2,1,0:T(8,128)S(1)}, f32[16,16,1024]{2,1,0:T(8,128)S(1)}) custom-call(bf16[16,8,32,1024]{3,2,1,0:T(8,128)(2,1)S(1)} %copy-done, f32[2,32,1024]{2,1,0:T(8,128)S(1)} %collective-permute-done.2.refs_1_, f32[2,32,1024]{2,1,0:T(8,128)S(1)} %collective-permute-done.3.refs_2_, ...), custom_call_target="tpu_custom_call" | custom-call | flops 1024 | bytes 1024 | tf_op jit(solution)/shard_map/project/pallas_call | solution.py:30
  15.7 0.1 collective-permute-start.9
  15.8 4.4 %collective-permute-start.10 = (f32[8,8,1024]{2,1,0:T(8,128)S(1)}, f32[8,8,1024]{2,1,0:T(8,128)S(1)}, u32[]{:S(2)}, u32[]{:S(2)}) collective-permute-start(f32[8,8,1024]{2,1,0:T(8,128)S(1)} %get-tuple-element.34), channel_id=1, source_target_pairs={{1,2},{3,4},{5,6},{2,1},{4,3},{6,5},{9,10},{11,12},{13,14},{10,9},... | collective-permute-start | bytes 786440 | tf_op jit(solution)/shard_map/ppermute | solution.py:376
  20.1 1.9 %collective-permute-start.1 = (f32[2,24,1024]{2,1,0:T(8,128)S(1)}, f32[2,24,1024]{2,1,0:T(8,128)S(1)}, u32[]{:S(2)}, u32[]{:S(2)}) collective-permute-start(f32[2,24,1024]{2,1,0:T(8,128)S(1)} %get-tuple-element.25), channel_id=1, source_target_pairs={{0,8},{8,0},{16,24},{24,16},{1,9},{9,1},{17,25},{25,17},{2,10},{10... | collective-permute-start | bytes 589832 | tf_op jit(solution)/shard_map/ppermute | solution.py:381
  22.0 6.0 %interior.3 = (f32[2,24,1024]{2,1,0:T(8,128)S(1)}, f32[2,24,1024]{2,1,0:T(8,128)S(1)}) custom-call(bf16[16,8,32,1024]{3,2,1,0:T(8,128)(2,1)S(1)} %copy-done, f32[2,32,1024]{2,1,0:T(8,128)S(1)} %collective-permute-done.2.refs_1_, f32[2,32,1024]{2,1,0:T(8,128)S(1)} %collective-permute-done.3.refs_2_, s32[32,1024]{1,0:T(8,128)S(1)} %get-tuple-element.22.refs_3_.refs_6_, ...), custom_call_target="tpu_custom_call" | custom-call | flops 1024 | bytes 1024 | tf_op jit(solution)/shard_map/interior/pallas_call | solution.py:30
  28.0 0.0 collective-permute-done.6.refs_2_.refs_4_
  28.0 1.2 %collective-permute-start.5 = (f32[2,24,1024]{2,1,0:T(8,128)S(1)}, f32[2,24,1024]{2,1,0:T(8,128)S(1)}, u32[]{:S(2)}, u32[]{:S(2)}) collective-permute-start(f32[2,24,1024]{2,1,0:T(8,128)S(1)} %get-tuple-element.28), channel_id=1, source_target_pairs={{0,24},{8,16},{16,8},{24,0},{1,25},{9,17},{17,9},{25,1},{2,26},{10... | collective-permute-start | bytes 589832 | tf_op jit(solution)/shard_map/ppermute | solution.py:383
  29.2 0.0 collective-permute-done.7.refs_3_.refs_5_
  29.2 0.2 collective-permute-start.4
  29.5 4.1 %edges.2 = (f32[2,8,1024]{2,1,0:T(8,128)S(1)}, f32[2,8,1024]{2,1,0:T(8,128)S(1)}) custom-call(bf16[16,8,32,1024]{3,2,1,0:T(8,128)(2,1)S(1)} %copy-done, f32[16,16,1024]{2,1,0:T(8,128)S(1)} %get-tuple-element.23.refs_4_.refs_1_, f32[9,8,1024]{2,1,0:T(8,128)S(1)} %collective-permute-done.6.refs_2_.refs_4_, ...), custom_call_target="tpu_custom_call" | custom-call | flops 1024 | bytes 1024 | tf_op jit(solution)/shard_map/edges/pallas_call | solution.py:30
  33.6 0.0 collective-permute-done.9.refs_2_
  33.6 0.8 %collective-permute-start.8 = (f32[2,8,1024]{2,1,0:T(8,128)S(1)}, f32[2,8,1024]{2,1,0:T(8,128)S(1)}, u32[]{:S(2)}, u32[]{:S(2)}) collective-permute-start(f32[2,8,1024]{2,1,0:T(8,128)S(1)} %get-tuple-element.32), channel_id=1, source_target_pairs={{0,8},{8,0},{16,24},{24,16},{1,9},{9,1},{17,25},{25,17},{2,10},{10... | collective-permute-start | bytes 196616 | tf_op jit(solution)/shard_map/ppermute | solution.py:384
  34.4 0.0 collective-permute-done.10.refs_3_
  34.4 4.1 %edges.3 = (f32[2,8,1024]{2,1,0:T(8,128)S(1)}, f32[2,8,1024]{2,1,0:T(8,128)S(1)}) custom-call(bf16[16,8,32,1024]{3,2,1,0:T(8,128)(2,1)S(1)} %copy-done, f32[16,16,1024]{2,1,0:T(8,128)S(1)} %get-tuple-element.26.refs_4_.refs_1_, f32[8,8,1024]{2,1,0:T(8,128)S(1)} %collective-permute-done.9.refs_2_, f32[8,8,1024]{2,1,0:T(8,128)S(1)} %collective-permute-done.10.refs_3_, ...), custom_call_target="tpu_custom_call" | custom-call | flops 1024 | bytes 1024 | tf_op jit(solution)/shard_map/edges/pallas_call | solution.py:30
  38.5 1.3 %collective-permute-start.11 = (f32[2,8,1024]{2,1,0:T(8,128)S(1)}, f32[2,8,1024]{2,1,0:T(8,128)S(1)}, u32[]{:S(2)}, u32[]{:S(2)}) collective-permute-start(f32[2,8,1024]{2,1,0:T(8,128)S(1)} %get-tuple-element.35), channel_id=1, source_target_pairs={{0,16},{8,24},{16,0},{24,8},{1,17},{9,25},{17,1},{25,9},{2,18},{10... | collective-permute-start | bytes 196616 | tf_op jit(solution)/shard_map/ppermute | solution.py:385
  39.8 0.0 collective-permute-done.1
  39.8 0.4 collective-permute-start.12
  40.2 0.0 collective-permute-done.5
  40.2 0.0 collective-permute-done.4
  40.3 0.0 collective-permute-done.8.refs_2_
  40.3 2.0 %collective-permute-done.11.refs_3_ = f32[2,8,1024]{2,1,0:T(8,128)S(1)} collective-permute-done((f32[2,8,1024]{2,1,0:T(8,128)S(1)}, f32[2,8,1024]{2,1,0:T(8,128)S(1)}, u32[]{:S(2)}, u32[]{:S(2)}) %collective-permute-start.11) | collective-permute-done | bytes 65568 | tf_op jit(solution)/shard_map/ppermute | solution.py:385
  42.3 1.6 %collective-permute-done.12.refs_4_ = f32[2,8,1024]{2,1,0:T(8,128)S(1)} collective-permute-done((f32[2,8,1024]{2,1,0:T(8,128)S(1)}, f32[2,8,1024]{2,1,0:T(8,128)S(1)}, u32[]{:S(2)}, u32[]{:S(2)}) %collective-permute-start.12) | collective-permute-done | bytes 65568 | tf_op jit(solution)/shard_map/ppermute | solution.py:386
  43.8 0.7 %finish.1 = f32[2,32,1024]{2,1,0:T(8,128)} custom-call(f32[2,24,1024]{2,1,0:T(8,128)S(1)} %add_add_fusion.refs_0_, f32[2,8,1024]{2,1,0:T(8,128)S(1)} %get-tuple-element.31.refs_7_.refs_1_, f32[2,8,1024]{2,1,0:T(8,128)S(1)} %collective-permute-done.8.refs_2_, f32[2,8,1024]{2,1,0:T(8,128)S(1)} %collective-permute-done.11.refs_3_, ...), custom_call_target="tpu_custom_call" | custom-call | flops 1024 | bytes 1024 | tf_op jit(solution)/shard_map/finish/pallas_call | solution.py:30
  (1 shorter events, 0.0 us)
Async XLA Ops:
  0.0 4.1 %copy-start = (bf16[16,8,32,1024]{3,2,1,0:T(8,128)(2,1)S(1)}, bf16[16,8,32,1024]{3,2,1,0:T(8,128)(2,1)}, u32[]{:S(2)}) copy-start(bf16[16,8,32,1024]{3,2,1,0:T(8,128)(2,1)} %refs_0_.11) | copy-start | bytes 25165828
  0.0 4.1 %collective-permute-start = (f32[2,32,1024]{2,1,0:T(8,128)}, f32[2,32,1024]{2,1,0:T(8,128)S(1)}, u32[]{:S(2)}, u32[]{:S(2)}) collective-permute-start(f32[2,32,1024]{2,1,0:T(8,128)} %g_ref.1), channel_id=1, source_target_pairs={{0,8},{8,0},{16,24},{24,16},{1,9},{9,1},{17,25},{25,17},{2,10},{10... | collective-permute-start | bytes 786440 | tf_op jit(solution)/shard_map/ppermute | solution.py:364
  0.7 14.5 %collective-permute-start.3 = (f32[2,32,1024]{2,1,0:T(8,128)}, f32[2,32,1024]{2,1,0:T(8,128)S(1)}, u32[]{:S(2)}, u32[]{:S(2)}) collective-permute-start(f32[2,32,1024]{2,1,0:T(8,128)} %g_ref.1), channel_id=1, source_target_pairs={{0,24},{8,16},{16,8},{24,0},{1,25},{9,17},{17,9},{25,1},{2,26},{10... | collective-permute-start | bytes 786440 | tf_op jit(solution)/shard_map/ppermute | solution.py:366
  1.9 13.3 %collective-permute-start.2 = (f32[2,32,1024]{2,1,0:T(8,128)}, f32[2,32,1024]{2,1,0:T(8,128)S(1)}, u32[]{:S(2)}, u32[]{:S(2)}) collective-permute-start(f32[2,32,1024]{2,1,0:T(8,128)} %g_ref.1), channel_id=1, source_target_pairs={{0,16},{8,24},{16,0},{24,8},{1,17},{9,25},{17,1},{25,9},{2,18},{10... | collective-permute-start | bytes 786440 | tf_op jit(solution)/shard_map/ppermute | solution.py:365
  4.7 23.4 %collective-permute-start.6 = (f32[9,8,1024]{2,1,0:T(8,128)S(1)}, f32[9,8,1024]{2,1,0:T(8,128)S(1)}, u32[]{:S(2)}, u32[]{:S(2)}) collective-permute-start(f32[9,8,1024]{2,1,0:T(8,128)S(1)} %get-tuple-element.29), channel_id=1, source_target_pairs={{0,1},{1,0},{2,3},{3,2},{4,5},{5,4},{6,7},{7,6},{8,9},{9,8},{10,11... | collective-permute-start | bytes 884744 | tf_op jit(solution)/shard_map/ppermute | solution.py:370
  4.8 24.5 %collective-permute-start.7 = (f32[9,8,1024]{2,1,0:T(8,128)S(1)}, f32[9,8,1024]{2,1,0:T(8,128)S(1)}, u32[]{:S(2)}, u32[]{:S(2)}) collective-permute-start(f32[9,8,1024]{2,1,0:T(8,128)S(1)} %get-tuple-element.30), channel_id=1, source_target_pairs={{1,2},{3,4},{5,6},{2,1},{4,3},{6,5},{9,10},{11,12},{13,14},{10,9},... | collective-permute-start | bytes 884744 | tf_op jit(solution)/shard_map/ppermute | solution.py:371
  15.7 17.9 %collective-permute-start.9 = (f32[8,8,1024]{2,1,0:T(8,128)S(1)}, f32[8,8,1024]{2,1,0:T(8,128)S(1)}, u32[]{:S(2)}, u32[]{:S(2)}) collective-permute-start(f32[8,8,1024]{2,1,0:T(8,128)S(1)} %get-tuple-element.33), channel_id=1, source_target_pairs={{0,1},{1,0},{2,3},{3,2},{4,5},{5,4},{6,7},{7,6},{8,9},{9,8},{10,11... | collective-permute-start | bytes 786440 | tf_op jit(solution)/shard_map/ppermute | solution.py:375
  15.8 18.6 %collective-permute-start.10 = (f32[8,8,1024]{2,1,0:T(8,128)S(1)}, f32[8,8,1024]{2,1,0:T(8,128)S(1)}, u32[]{:S(2)}, u32[]{:S(2)}) collective-permute-start(f32[8,8,1024]{2,1,0:T(8,128)S(1)} %get-tuple-element.34), channel_id=1, source_target_pairs={{1,2},{3,4},{5,6},{2,1},{4,3},{6,5},{9,10},{11,12},{13,14},{10,9},... | collective-permute-start | bytes 786440 | tf_op jit(solution)/shard_map/ppermute | solution.py:376
  20.1 19.7 %collective-permute-start.1 = (f32[2,24,1024]{2,1,0:T(8,128)S(1)}, f32[2,24,1024]{2,1,0:T(8,128)S(1)}, u32[]{:S(2)}, u32[]{:S(2)}) collective-permute-start(f32[2,24,1024]{2,1,0:T(8,128)S(1)} %get-tuple-element.25), channel_id=1, source_target_pairs={{0,8},{8,0},{16,24},{24,16},{1,9},{9,1},{17,25},{25,17},{2,10},{10... | collective-permute-start | bytes 589832 | tf_op jit(solution)/shard_map/ppermute | solution.py:381
  28.0 12.2 %collective-permute-start.5 = (f32[2,24,1024]{2,1,0:T(8,128)S(1)}, f32[2,24,1024]{2,1,0:T(8,128)S(1)}, u32[]{:S(2)}, u32[]{:S(2)}) collective-permute-start(f32[2,24,1024]{2,1,0:T(8,128)S(1)} %get-tuple-element.28), channel_id=1, source_target_pairs={{0,24},{8,16},{16,8},{24,0},{1,25},{9,17},{17,9},{25,1},{2,26},{10... | collective-permute-start | bytes 589832 | tf_op jit(solution)/shard_map/ppermute | solution.py:383
  29.2 11.0 %collective-permute-start.4 = (f32[2,24,1024]{2,1,0:T(8,128)S(1)}, f32[2,24,1024]{2,1,0:T(8,128)S(1)}, u32[]{:S(2)}, u32[]{:S(2)}) collective-permute-start(f32[2,24,1024]{2,1,0:T(8,128)S(1)} %get-tuple-element.27.refs_7_), channel_id=1, source_target_pairs={{0,16},{8,24},{16,0},{24,8},{1,17},{9,25},{17,1},{25,9},{2,18},{10... | collective-permute-start | bytes 589832 | tf_op jit(solution)/shard_map/ppermute | solution.py:382
  33.6 6.7 %collective-permute-start.8 = (f32[2,8,1024]{2,1,0:T(8,128)S(1)}, f32[2,8,1024]{2,1,0:T(8,128)S(1)}, u32[]{:S(2)}, u32[]{:S(2)}) collective-permute-start(f32[2,8,1024]{2,1,0:T(8,128)S(1)} %get-tuple-element.32), channel_id=1, source_target_pairs={{0,8},{8,0},{16,24},{24,16},{1,9},{9,1},{17,25},{25,17},{2,10},{10... | collective-permute-start | bytes 196616 | tf_op jit(solution)/shard_map/ppermute | solution.py:384
  38.5 3.8 %collective-permute-start.11 = (f32[2,8,1024]{2,1,0:T(8,128)S(1)}, f32[2,8,1024]{2,1,0:T(8,128)S(1)}, u32[]{:S(2)}, u32[]{:S(2)}) collective-permute-start(f32[2,8,1024]{2,1,0:T(8,128)S(1)} %get-tuple-element.35), channel_id=1, source_target_pairs={{0,16},{8,24},{16,0},{24,8},{1,17},{9,25},{17,1},{25,9},{2,18},{10... | collective-permute-start | bytes 196616 | tf_op jit(solution)/shard_map/ppermute | solution.py:385
  39.8 4.0 %collective-permute-start.12 = (f32[2,8,1024]{2,1,0:T(8,128)S(1)}, f32[2,8,1024]{2,1,0:T(8,128)S(1)}, u32[]{:S(2)}, u32[]{:S(2)}) collective-permute-start(f32[2,8,1024]{2,1,0:T(8,128)S(1)} %get-tuple-element.36), channel_id=1, source_target_pairs={{0,24},{8,16},{16,8},{24,0},{1,25},{9,17},{17,9},{25,1},{2,26},{10... | collective-permute-start | bytes 196616 | tf_op jit(solution)/shard_map/ppermute | solution.py:386

commit v6 on v5

--- a/solution.py
+++ b/solution.py
@@ -55,15 +55,13 @@
 
 
 def sides(values, first, last):
-    before = [pltpu.roll(v, 1, 1) for v in values]
-    after = [pltpu.roll(v, LANES - 1, 1) for v in values]
     zero = jnp.zeros_like(values[0])
     count = len(values)
     sums = []
     for j in range(count):
-        left = jnp.where(first, before[j - 1] if j else zero, before[j])
-        right = jnp.where(last, after[j + 1] if j + 1 < count else zero, after[j])
-        sums.append(left + right)
+        left = jnp.where(last, values[j - 1] if j else zero, values[j])
+        right = jnp.where(first, values[j + 1] if j + 1 < count else zero, values[j])
+        sums.append(pltpu.roll(left, 1, 1) + pltpu.roll(right, LANES - 1, 1))
     return sums
 
 
@@ -75,13 +73,10 @@
     return [slot * VARS + at * own + k for at in (share, shares - 1 - share) for k in range(own)]
 
 
-def prepare(g_ref, counts_ref, near_g_ref, rim_ref, near_counts_ref, sem):
-    rows = g_ref.shape[1]
+def prepare(g_ref, counts_ref, near_g_ref, near_counts_ref, sem):
     copies = [
-        pltpu.make_async_copy(g_ref.at[:, 0:TILE], rim_ref.at[:, 0:TILE], sem.at[0]),
-        pltpu.make_async_copy(g_ref.at[:, rows - TILE : rows], rim_ref.at[:, TILE : 2 * TILE], sem.at[1]),
-        pltpu.make_async_copy(g_ref, near_g_ref, sem.at[2]),
-        pltpu.make_async_copy(counts_ref, near_counts_ref, sem.at[3]),
+        pltpu.make_async_copy(g_ref, near_g_ref, sem.at[0]),
+        pltpu.make_async_copy(counts_ref, near_counts_ref, sem.at[1]),
     ]
     for copy in copies:
         copy.start()
@@ -95,9 +90,9 @@
 
 def project_edges(local, own, p_ref, *rest):
     if local:
-        *g_refs, counts_ref, e_ref, o_ref, u_ref = rest
+        *g_refs, counts_ref, e_ref, o_ref = rest
     else:
-        *g_refs, _, e_ref, o_ref, u_ref = rest
+        *g_refs, _, e_ref, o_ref = rest
     members, _, rows, ny = p_ref.shape
     even = lax.axis_index("strip") % 2 == 0
     half = top_half()
@@ -126,8 +121,6 @@
                     high = high * g_ref[k, g_ref.shape[1] - TILE : g_ref.shape[1], cols(j)]
                     top = low if top is None else top + low
                     bottom = high if bottom is None else bottom + high
-                u_ref[m, 0:TILE, cols(j)] = top
-                u_ref[m, TILE : 2 * TILE, cols(j)] = bottom
                 tops.append(top)
                 bottoms.append(bottom)
             top = jnp.where(half, tops[0], pltpu.roll(tops[1], TILE // 2, 0))
@@ -138,22 +131,25 @@
 
 
 def interior(local, p_ref, *refs):
-    *g_refs, counts_ref, _, own_ref, other_ref, coef, buf_a, buf_b, total_ref = refs
+    if local:
+        *g_refs, counts_ref, _, own_ref, other_ref, kept_ref, coef, buf_a, buf_b, total_ref = refs
+    else:
+        *g_refs, coef, _, own_ref, other_ref, kept_ref, buf_a, buf_b, total_ref = refs
     members, _, rows, ny = p_ref.shape
     own = own_ref.shape[0]
     blocks = ny // LANES
     group = buf_a.shape[0]
     first, last = lane_masks()
+    half = top_half()
     fields = fields_of(local, own)
     grads = weights_of(own, g_refs)
     sums = [(own_ref, k) for k in range(own)] + [(other_ref, k) for k in range(own)]
     skip = TILE // 2
     whole = list(range(0, rows, TILE))
     kept = list(range(skip, rows - skip, TILE))
-    for t in range(1, SWEEPS):
-        for j in range(blocks):
-            active = (counts_ref[:, cols(j)] > t).astype(jnp.float32)
-            total_ref[0, j] = active
+    for t in range(1, SWEEPS if local else 1):
+        for j in range(blocks):
+            total_ref[0, j] = (counts_ref[:, cols(j)] > t).astype(jnp.float32)
             for n, r in enumerate(kept if t == SWEEPS - 1 else whole):
                 active = total_ref[0, j, r : r + TILE]
                 coef[t - 1, 0, j, n * TILE : (n + 1) * TILE] = active * COEFF_X
@@ -179,6 +175,11 @@
                     buf_a[i, j, TILE + r : TILE + r + HALF] = total
         src, dst = buf_a, buf_b
         for t in range(SWEEPS):
+            for i in range(group):
+                for j in range(blocks):
+                    low, high = TILE + t, rows - t
+                    tile = jnp.where(half, src[i, j, low : low + TILE], src[i, j, high : high + TILE])
+                    kept_ref[base + i, t * TILE : (t + 1) * TILE, cols(j)] = tile
             for n, r in enumerate(kept if t == SWEEPS - 1 else whole):
                 at, to = TILE + r, TILE + n * TILE
                 for i in range(group):
@@ -211,7 +212,11 @@
                 ref[k, r : r + TILE, cols(j)] = total_ref[n, j, skip + r : skip + r + TILE]
 
 
-def edges(local, p_ref, u_ref, e_ref, o_ref, ce_ref, co_ref, counts_ref, _, own_ref, other_ref, coef, buf_a, buf_b, halo):
+def edges(local, p_ref, kept_ref, e_ref, o_ref, *refs):
+    if local:
+        counts_ref, own_ref, other_ref, coef, win_a, win_b, halo = refs
+    else:
+        coef, _, own_ref, other_ref, win_a, win_b = refs
     members, _, rows, ny = p_ref.shape
     own = own_ref.shape[0]
     blocks = ny // LANES
@@ -220,68 +225,55 @@
     even = lax.axis_index("strip") % 2 == 0
     fields = fields_of(local, own)
     sums = [(own_ref, k) for k in range(own)] + [(other_ref, k) for k in range(own)]
-    crow = ce_ref.shape[0] - 1
-    for j in range(blocks):
-        e, o = ce_ref[crow, :, cols(j)], co_ref[crow, :, cols(j)]
-        halo[j, 4:12] = jnp.where(even, o, e)
-        halo[j, 24:32] = jnp.where(even, e, o)
-        halo[j, 8:16] = counts_ref[0:TILE, cols(j)].astype(jnp.float32)
-        halo[j, 16:24] = counts_ref[rows - TILE : rows, cols(j)].astype(jnp.float32)
-
-        def weigh(t, to, given):
-            active = (given > t).astype(jnp.float32)
-            coef[t, 0, j, to : to + TILE] = active * COEFF_X
-            coef[t, 1, j, to : to + TILE] = 1.0 - active * (1.0 - CENTRE)
-
-        for to in (8, 16, 24):
-            weigh(0, to, halo[j, to - 3 : to + 5])
-        for t in range(1, SWEEPS - 1):
-            weigh(t, 8, halo[j, 6:14])
-            weigh(t, 24, halo[j, 18:26])
-        weigh(SWEEPS - 1, 0, jnp.where(half, halo[j, 8:16], halo[j, 16:24]))
+    start = TILE
+
+    def sent(q, j):
+        e, o = e_ref[q, :, cols(j)], o_ref[q, :, cols(j)]
+        return jnp.where(even, o, e), jnp.where(even, e, o)
+
+    def merged(ref, low, high):
+        return jnp.where(half, ref[low : low + TILE], ref[high : high + TILE])
+
+    if local:
+        for j in range(blocks):
+            above, below = sent(members // 2, j)
+            halo[j, 4:12] = above
+            halo[j, 24:32] = below
+            halo[j, 8:16] = counts_ref[0:TILE, cols(j)].astype(jnp.float32)
+            halo[j, 16:24] = counts_ref[rows - TILE : rows, cols(j)].astype(jnp.float32)
+            for t in range(SWEEPS):
+                active = (merged(halo.at[j], 5 + t, 19 - t) > t).astype(jnp.float32)
+                coef[t, 0, j] = active * COEFF_X
+                coef[t, 1, j] = 1.0 - active * (1.0 - CENTRE)
     own_ref[...] = jnp.zeros_like(own_ref)
     other_ref[...] = jnp.zeros_like(other_ref)
-    plans = [[(5, 8), (13, 16), (21, 24)], [(9, 8), (21, 24)], [(8, 8), (24, 24)]]
 
     def step(q, carry):
         for j in range(blocks):
-            e, o = e_ref[q, :, cols(j)], o_ref[q, :, cols(j)]
-            above, below = jnp.where(even, o, e), jnp.where(even, e, o)
-            buf_a[0, j, 4:12] = above
-            buf_a[0, j, 24:32] = below
-            buf_a[1, j, 0:8] = above
-            buf_a[1, j, 20:28] = below
+            above, below = sent(q, j)
+            win_a[0, j, start : start + TILE] = above
+            win_a[0, j, start + 12 : start + 20] = below
+            win_a[1, j, start - 4 : start + 4] = above
+            win_a[1, j, start + 8 : start + 16] = below
             for i in range(2):
-                buf_a[i, j, 8:16] = u_ref[2 * q + i, 0:TILE, cols(j)]
-                buf_a[i, j, 16:24] = u_ref[2 * q + i, TILE : 2 * TILE, cols(j)]
-        src, dst = buf_a, buf_b
-        for t in range(SWEEPS - 1):
-            for at, to in plans[t]:
-                weights = [[coef[t, c, j, to : to + TILE] for j in range(blocks)] for c in range(2)]
-                for i in range(2):
-                    centre = [src[i, j, at : at + TILE] for j in range(blocks)]
-                    lateral = sides(centre, first, last)
-                    for j in range(blocks):
-                        stacked = src[i, j, at - 1 : at - 1 + TILE] + src[i, j, at + 1 : at + 1 + TILE]
-                        moved = stacked + RATIO * lateral[j]
-                        dst[i, j, to : to + TILE] = weights[0][j] * moved + weights[1][j] * centre[j]
+                win_a[i, j, start + 4 : start + 12] = kept_ref[2 * q + i, 0:TILE, cols(j)]
+        src, dst = win_a, win_b
+        smooth = [[], []]
+        for t in range(SWEEPS):
+            weights = [[coef[t, c, j] for j in range(blocks)] for c in range(2)]
+            for i in range(2):
+                centre = [merged(src.at[i, j], start + 1, start + 7) for j in range(blocks)]
+                lateral = sides(centre, first, last)
+                for j in range(blocks):
+                    stacked = merged(src.at[i, j], start, start + 6) + merged(src.at[i, j], start + 2, start + 8)
+                    new = weights[0][j] * (stacked + RATIO * lateral[j]) + weights[1][j] * centre[j]
+                    if t == SWEEPS - 1:
+                        smooth[i].append(new)
+                    else:
+                        dst[i, j, start : start + TILE] = new
+                        dst[i, j, start + 8 : start + 16] = new
+                        dst[i, j, start + 4 : start + 12] = kept_ref[2 * q + i, (t + 1) * TILE : (t + 2) * TILE, cols(j)]
             src, dst = dst, src
-
-        def both(ref, i, j, shift):
-            low, high = ref[i, j, 10 + shift : 18 + shift], ref[i, j, 22 + shift : 30 + shift]
-            return jnp.where(half, low, high)
-
-        t = SWEEPS - 1
-        weights = [[coef[t, c, j, 0:TILE] for j in range(blocks)] for c in range(2)]
-        smooth = []
-        for i in range(2):
-            centre = [both(src, i, j, 0) for j in range(blocks)]
-            lateral = sides(centre, first, last)
-            result = []
-            for j in range(blocks):
-                moved = both(src, i, j, -1) + both(src, i, j, 1) + RATIO * lateral[j]
-                result.append(weights[0][j] * moved + weights[1][j] * centre[j])
-            smooth.append(result)
         for j in range(blocks):
             for f, (ref, k) in zip(fields, sums):
                 total = ref[k, :, cols(j)]
@@ -331,52 +323,56 @@
         return jax.ShapeDtypeStruct(dims, f32)
 
     def window(*lead):
-        return pltpu.VMEM((*lead, blocks, 40, LANES), f32)
+        return pltpu.VMEM((*lead, blocks, 4 * TILE, LANES), f32)
 
     def call_prepare(*args):
-        outs = (shape(own, rows, ny), shape(own, 2 * TILE, ny), jax.ShapeDtypeStruct((rows, ny), counts.dtype))
+        outs = (shape(own, rows, ny), jax.ShapeDtypeStruct((rows, ny), counts.dtype))
         stored = [pltpu.with_memory_space_constraint(x, pltpu.HBM) for x in args]
         outside = {0: pl.ANY, 1: pl.ANY}
-        return kernel_call(prepare, outs, [pltpu.SemaphoreType.DMA((4,))], PREPARE_FLOPS, "prepare", outside)(*stored)
+        return kernel_call(prepare, outs, [pltpu.SemaphoreType.DMA((2,))], PREPARE_FLOPS, "prepare", outside)(*stored)
 
     def call_project(local, *args):
         pairs = members // 2 + (1 if local else 0)
-        outs = (shape(pairs, TILE, ny), shape(pairs, TILE, ny), shape(members, 2 * TILE, ny))
+        outs = (shape(pairs, TILE, ny), shape(pairs, TILE, ny))
         outside = {} if local else {len(args) - 1: pl.ANY}
         body = lambda *refs: project_edges(local, own, *refs)
         return kernel_call(body, outs, [], 1024, "project", outside=outside)(*args)
 
     def call_interior(local, *args):
-        outs = (shape(own, rows - TILE, ny), shape(own, rows - TILE, ny))
         total = pltpu.VMEM((VARS, blocks, rows, LANES), f32)
         buf = pltpu.VMEM((2, blocks, rows + 2 * TILE, LANES), f32)
-        coef = pltpu.VMEM((SWEEPS - 1, 2, blocks, rows, LANES), f32)
+        outs = (shape(own, rows - TILE, ny), shape(own, rows - TILE, ny), shape(members, SWEEPS * TILE, ny))
+        if local:
+            outs = outs + (shape(SWEEPS - 1, 2, blocks, rows, LANES),)
         body = lambda *refs: interior(local, *refs)
-        return kernel_call(body, outs, [coef, buf, buf, total], 1024, "interior", outside={len(args) - 1: pl.ANY})(*args)
+        return kernel_call(body, outs, [buf, buf, total], 1024, "interior", outside={len(args) - 1: pl.ANY})(*args)
 
     def call_edges(local, *args):
         outs = (shape(own, TILE, ny), shape(own, TILE, ny))
-        scratch = [window(SWEEPS, 2), window(2), window(2), window()]
+        scratch = [window(2), window(2)]
+        if local:
+            outs, scratch = outs + (shape(SWEEPS, 2, blocks, TILE, LANES),), scratch + [window()]
         body = lambda *refs: edges(local, *refs)
-        return kernel_call(body, outs, scratch, 1024, "edges", outside={7: pl.ANY})(*args)
-
-    near_g, _, near_counts = call_prepare(gradient, counts)
+        outside = {} if local else {len(args) - 1: pl.ANY}
+        return kernel_call(body, outs, scratch, 1024, "edges", outside=outside)(*args)
+
+    near_g, near_counts = call_prepare(gradient, counts)
     partner = lax.ppermute(gradient, "mem", near)
     far = lax.ppermute(gradient, "mem", across)
     far_partner = lax.ppermute(gradient, "mem", cross)
 
     p = perturbations
-    e0, o0, u0 = call_project(True, p, near_g, partner, near_counts)
+    e0, o0 = call_project(True, p, near_g, partner, near_counts)
+    own0, other0, kept0, inner_coef = call_interior(True, p, near_g, partner, near_counts, e0)
     e0 = lax.ppermute(e0, "strip", even)
     o0 = lax.ppermute(o0, "strip", odd)
-    own0, other0 = call_interior(True, p, near_g, partner, near_counts, u0)
-
-    e1, o1, u1 = call_project(False, p, far, far_partner, own0)
+
+    e1, o1 = call_project(False, p, far, far_partner, own0)
+    own1, other1, kept1 = call_interior(False, p, far, far_partner, inner_coef, e1)
     e1 = lax.ppermute(e1, "strip", even)
     o1 = lax.ppermute(o1, "strip", odd)
-    own1, other1 = call_interior(False, p, far, far_partner, near_counts, u1)
-    eown0, eother0 = call_edges(True, p, u0, e0, o0, e0, o0, near_counts, own1)
-    eown1, eother1 = call_edges(False, p, u1, e1, o1, e0, o0, near_counts, eown0)
+    eown0, eother0, edge_coef = call_edges(True, p, kept0, e0, o0, near_counts)
+    eown1, eother1 = call_edges(False, p, kept1, e1, o1, edge_coef, eown0)
 
     inner = own0 + lax.ppermute(other0, "mem", near)
     inner = inner + lax.ppermute(own1, "mem", across)

time: 44.7 us -> 45.7 us (1.022)
  Pallas kernels: 24 us -> 21.1 us
  local copies, waits for them, and re-layouts: 0.01 us -> 2.35 us
  waiting for transfers between devices: 3.56 us -> 4.86 us
    pallas_call x8, Pallas kernels: 24 us -> 21.1 us  [call(): pl.pallas_call(body, out_shape=out_shape, in_specs=[pl.BlockSpec(memory_s...]
    unnamed x2, local copies, waits for them, and re-layouts: 0.01 us -> 2.35 us
    ppermute x1, starting transfers between devices: 4.36 us -> 3.18 us  [per_device(): o0 = lax.ppermute(o0, 'strip', odd)]
    ppermute x1, waiting for transfers between devices: 1.55 us -> 2.73 us  [per_device(): ecross1 = lax.ppermute(eother1, 'mem', cross)]
    ppermute x1, starting transfers between devices: 0.23 us -> 1.3 us  [per_device(): inner = inner + lax.ppermute(own1, 'mem', across)]
    ppermute x1, waiting for transfers between devices: 1.98 us -> 0.92 us  [per_device(): efar1 = lax.ppermute(eown1, 'mem', across)]
    ppermute x1, starting transfers between devices: 0.84 us -> 0.07 us  [per_device(): enear0 = lax.ppermute(eother0, 'mem', near)]
    ppermute x1, waiting for transfers between devices: 0.01 us -> 0.63 us  [per_device(): e0 = lax.ppermute(e0, 'strip', even)]
  transfers between devices with their start and end apart: 13 -> 13, of which waited for: 2 -> 4; matrix products, arithmetic and copies ran while one was open for 0% -> 0% of each run, Pallas kernels for 52% -> 45%
where the time goes in v6:
time: 45.7 us; the launch traced here: 45.2 us
  Pallas kernels  21.1 us (46%)
  starting transfers between devices  16.7 us (37%)
  waiting for transfers between devices  4.86 us (11%)
  local copies, waits for them, and re-layouts  2.35 us (5%)
    pallas_call x8, Pallas kernels, call(): pl.pallas_call(body, out_shape=out_shape, in_specs=[pl.BlockSpec(memory_s...  21.1 us
    ppermute x1, starting transfers between devices, per_device(): o1 = lax.ppermute(o1, 'strip', odd)  4.37 us
    ppermute x1, starting transfers between devices, per_device(): o0 = lax.ppermute(o0, 'strip', odd)  3.18 us
    ppermute x1, waiting for transfers between devices, per_device(): ecross1 = lax.ppermute(eother1, 'mem', cross)  2.73 us
    unnamed x2, local copies, waits for them, and re-layouts  2.35 us
    ppermute x1, starting transfers between devices, per_device(): inner = inner + lax.ppermute(other1, 'mem', cross)  1.71 us
    ppermute x1, starting transfers between devices, per_device(): inner = own0 + lax.ppermute(other0, 'mem', near)  1.69 us
    ppermute x1, starting transfers between devices, per_device(): inner = inner + lax.ppermute(own1, 'mem', across)  1.3 us
  transfers between devices with their start and end apart: 13, of which 4 were waited for; matrix products, arithmetic and copies ran while one was open for 0% of the time, Pallas kernels for 45%

profile of v6, /device:TPU:3, one launch (start us, length us, event | category | flops | bytes accessed | tf_op | source)
XLA Modules:
  0.0 45.2 jit_solution(11283247159390000774)
XLA Ops:
  0.0 0.7 %collective-permute-start = (f32[2,32,1024]{2,1,0:T(8,128)}, f32[2,32,1024]{2,1,0:T(8,128)S(1)}, u32[]{:S(2)}, u32[]{:S(2)}) collective-permute-start(f32[2,32,1024]{2,1,0:T(8,128)} %g_ref.1), channel_id=1, source_target_pairs={{0,8},{8,0},{16,24},{24,16},{1,9},{9,1},{17,25},{25,17},{2,10},{10... | collective-permute-start | bytes 786440 | tf_op jit(solution)/shard_map/ppermute | solution.py:360
  0.7 1.1 %collective-permute-start.3 = (f32[2,32,1024]{2,1,0:T(8,128)}, f32[2,32,1024]{2,1,0:T(8,128)S(1)}, u32[]{:S(2)}, u32[]{:S(2)}) collective-permute-start(f32[2,32,1024]{2,1,0:T(8,128)} %g_ref.1), channel_id=1, source_target_pairs={{0,24},{8,16},{16,8},{24,0},{1,25},{9,17},{17,9},{25,1},{2,26},{10... | collective-permute-start | bytes 786440 | tf_op jit(solution)/shard_map/ppermute | solution.py:362
  1.8 0.2 collective-permute-start.2
  2.0 0.0 copy-start
  2.0 1.1 %prepare.1 = (f32[2,32,1024]{2,1,0:T(8,128)S(1)}, s32[32,1024]{1,0:T(8,128)S(1)}) custom-call(f32[2,32,1024]{2,1,0:T(8,128)} %g_ref.1, s32[32,1024]{1,0:T(8,128)} %counts_ref.1), custom_call_target="tpu_custom_call" | custom-call | flops 10000000000 | bytes 1024 | tf_op jit(solution)/shard_map/prepare/pallas_call | solution.py:30
  3.2 0.0 collective-permute-done.refs_2_
  3.2 2.4 %copy-done = bf16[16,8,32,1024]{3,2,1,0:T(8,128)(2,1)S(1)} copy-done((bf16[16,8,32,1024]{3,2,1,0:T(8,128)(2,1)S(1)}, bf16[16,8,32,1024]{3,2,1,0:T(8,128)(2,1)}, u32[]{:S(2)}) %copy-start) | copy-done | bytes 8388632
  5.6 0.5 %project.2 = (f32[9,8,1024]{2,1,0:T(8,128)S(1)}, f32[9,8,1024]{2,1,0:T(8,128)S(1)}) custom-call(bf16[16,8,32,1024]{3,2,1,0:T(8,128)(2,1)S(1)} %copy-done, f32[2,32,1024]{2,1,0:T(8,128)S(1)} %get-tuple-element.23.refs_1_, f32[2,32,1024]{2,1,0:T(8,128)S(1)} %collective-permute-done.refs_2_, s32[32,1024]{1,0:T(8,128)S(1)} %get-tuple-element.24.refs_3_.refs_4_), custom_call_target="tpu_custom_call" | custom-call | flops 1024 | bytes 1024 | tf_op jit(solution)/shard_map/project/pallas_call | solution.py:30
  6.1 3.2 %collective-permute-start.7 = (f32[9,8,1024]{2,1,0:T(8,128)S(1)}, f32[9,8,1024]{2,1,0:T(8,128)S(1)}, u32[]{:S(2)}, u32[]{:S(2)}) collective-permute-start(f32[9,8,1024]{2,1,0:T(8,128)S(1)} %get-tuple-element.33), channel_id=1, source_target_pairs={{1,2},{3,4},{5,6},{2,1},{4,3},{6,5},{9,10},{11,12},{13,14},{10,9},... | collective-permute-start | bytes 884744 | tf_op jit(solution)/shard_map/ppermute | solution.py:368
  9.2 0.1 collective-permute-start.6
  9.3 5.9 %interior.2 = (f32[2,24,1024]{2,1,0:T(8,128)S(1)}, f32[2,24,1024]{2,1,0:T(8,128)S(1)}, f32[16,32,1024]{2,1,0:T(8,128)S(1)}, f32[3,2,8,32,128]{4,3,2,1,0:T(8,128)S(1)}) custom-call(bf16[16,8,32,1024]{3,2,1,0:T(8,128)(2,1)S(1)} %copy-done, f32[2,32,1024]{2,1,0:T(8,128)S(1)} %get-tuple-element.23.refs_1_, f32[2,32,1024]{2,1,0:T(8,128)S(1)} %collective-permute-done.refs_2_, ...), custom_call_target="tpu_custom_call" | custom-call | flops 1024 | bytes 1024 | tf_op jit(solution)/shard_map/interior/pallas_call | solution.py:30
  15.2 0.0 collective-permute-done.3.refs_2_
  15.3 0.0 collective-permute-done.2.refs_1_
  15.3 0.5 %project.3 = (f32[8,8,1024]{2,1,0:T(8,128)S(1)}, f32[8,8,1024]{2,1,0:T(8,128)S(1)}) custom-call(bf16[16,8,32,1024]{3,2,1,0:T(8,128)(2,1)S(1)} %copy-done, f32[2,32,1024]{2,1,0:T(8,128)S(1)} %collective-permute-done.2.refs_1_, f32[2,32,1024]{2,1,0:T(8,128)S(1)} %collective-permute-done.3.refs_2_, f32[2,24,1024]{2,1,0:T(8,128)S(1)} %get-tuple-element.26.refs_3_), custom_call_target="tpu_custom_call" | custom-call | flops 1024 | bytes 1024 | tf_op jit(solution)/shard_map/project/pallas_call | solution.py:30
  15.8 4.4 %collective-permute-start.10 = (f32[8,8,1024]{2,1,0:T(8,128)S(1)}, f32[8,8,1024]{2,1,0:T(8,128)S(1)}, u32[]{:S(2)}, u32[]{:S(2)}) collective-permute-start(f32[8,8,1024]{2,1,0:T(8,128)S(1)} %get-tuple-element.37), channel_id=1, source_target_pairs={{1,2},{3,4},{5,6},{2,1},{4,3},{6,5},{9,10},{11,12},{13,14},{10,9},... | collective-permute-start | bytes 786440 | tf_op jit(solution)/shard_map/ppermute | solution.py:373
  20.2 0.1 collective-permute-start.9
  20.2 1.7 %collective-permute-start.1 = (f32[2,24,1024]{2,1,0:T(8,128)S(1)}, f32[2,24,1024]{2,1,0:T(8,128)S(1)}, u32[]{:S(2)}, u32[]{:S(2)}) collective-permute-start(f32[2,24,1024]{2,1,0:T(8,128)S(1)} %get-tuple-element.27), channel_id=1, source_target_pairs={{0,8},{8,0},{16,24},{24,16},{1,9},{9,1},{17,25},{25,17},{2,10},{10... | collective-permute-start | bytes 589832 | tf_op jit(solution)/shard_map/ppermute | solution.py:377
  21.9 5.8 %interior.3 = (f32[2,24,1024]{2,1,0:T(8,128)S(1)}, f32[2,24,1024]{2,1,0:T(8,128)S(1)}, f32[16,32,1024]{2,1,0:T(8,128)S(1)}) custom-call(bf16[16,8,32,1024]{3,2,1,0:T(8,128)(2,1)S(1)} %copy-done, f32[2,32,1024]{2,1,0:T(8,128)S(1)} %collective-permute-done.2.refs_1_, f32[2,32,1024]{2,1,0:T(8,128)S(1)} %collective-permute-done.3.refs_2_, ...), custom_call_target="tpu_custom_call" | custom-call | flops 1024 | bytes 1024 | tf_op jit(solution)/shard_map/interior/pallas_call | solution.py:30
  27.8 0.0 collective-permute-done.7.refs_3_
  27.8 1.3 %collective-permute-start.4 = (f32[2,24,1024]{2,1,0:T(8,128)S(1)}, f32[2,24,1024]{2,1,0:T(8,128)S(1)}, u32[]{:S(2)}, u32[]{:S(2)}) collective-permute-start(f32[2,24,1024]{2,1,0:T(8,128)S(1)} %get-tuple-element.30), channel_id=1, source_target_pairs={{0,16},{8,24},{16,0},{24,8},{1,17},{9,25},{17,1},{25,9},{2,18},{10... | collective-permute-start | bytes 589832 | tf_op jit(solution)/shard_map/ppermute | solution.py:378
  29.1 0.6 %collective-permute-done.6.refs_2_ = f32[9,8,1024]{2,1,0:T(8,128)S(1)} collective-permute-done((f32[9,8,1024]{2,1,0:T(8,128)S(1)}, f32[9,8,1024]{2,1,0:T(8,128)S(1)}, u32[]{:S(2)}, u32[]{:S(2)}) %collective-permute-start.6) | collective-permute-done | bytes 294944 | tf_op jit(solution)/shard_map/ppermute | solution.py:367
  29.7 1.7 %collective-permute-start.5 = (f32[2,24,1024]{2,1,0:T(8,128)S(1)}, f32[2,24,1024]{2,1,0:T(8,128)S(1)}, u32[]{:S(2)}, u32[]{:S(2)}) collective-permute-start(f32[2,24,1024]{2,1,0:T(8,128)S(1)} %get-tuple-element.31), channel_id=1, source_target_pairs={{0,24},{8,16},{16,8},{24,0},{1,25},{9,17},{17,9},{25,1},{2,26},{10... | collective-permute-start | bytes 589832 | tf_op jit(solution)/shard_map/ppermute | solution.py:379
  31.4 3.3 %edges.2 = (f32[2,8,1024]{2,1,0:T(8,128)S(1)}, f32[2,8,1024]{2,1,0:T(8,128)S(1)}, f32[4,2,8,8,128]{4,3,2,1,0:T(8,128)S(1)}) custom-call(bf16[16,8,32,1024]{3,2,1,0:T(8,128)(2,1)S(1)} %copy-done, f32[16,32,1024]{2,1,0:T(8,128)S(1)} %get-tuple-element.32.refs_1_, f32[9,8,1024]{2,1,0:T(8,128)S(1)} %collective-permute-done.6.refs_2_, ...), custom_call_target="tpu_custom_call" | custom-call | flops 1024 | bytes 1024 | tf_op jit(solution)/shard_map/edges/pallas_call | solution.py:30
  34.7 0.0 collective-permute-done.10.refs_3_
  34.7 0.1 collective-permute-start.8
  34.8 0.6 %collective-permute-done.9.refs_2_ = f32[8,8,1024]{2,1,0:T(8,128)S(1)} collective-permute-done((f32[8,8,1024]{2,1,0:T(8,128)S(1)}, f32[8,8,1024]{2,1,0:T(8,128)S(1)}, u32[]{:S(2)}, u32[]{:S(2)}) %collective-permute-start.9) | collective-permute-done | bytes 262176 | tf_op jit(solution)/shard_map/ppermute | solution.py:372
  35.3 3.2 %edges.3 = (f32[2,8,1024]{2,1,0:T(8,128)S(1)}, f32[2,8,1024]{2,1,0:T(8,128)S(1)}) custom-call(bf16[16,8,32,1024]{3,2,1,0:T(8,128)(2,1)S(1)} %copy-done, f32[16,32,1024]{2,1,0:T(8,128)S(1)} %get-tuple-element.36.refs_1_, f32[8,8,1024]{2,1,0:T(8,128)S(1)} %collective-permute-done.9.refs_2_, f32[8,8,1024]{2,1,0:T(8,128)S(1)} %collective-permute-done.10.refs_3_, ...), custom_call_target="tpu_custom_call" | custom-call | flops 1024 | bytes 1024 | tf_op jit(solution)/shard_map/edges/pallas_call | solution.py:30
  38.6 1.3 %collective-permute-start.11 = (f32[2,8,1024]{2,1,0:T(8,128)S(1)}, f32[2,8,1024]{2,1,0:T(8,128)S(1)}, u32[]{:S(2)}, u32[]{:S(2)}) collective-permute-start(f32[2,8,1024]{2,1,0:T(8,128)S(1)} %get-tuple-element.39), channel_id=1, source_target_pairs={{0,16},{8,24},{16,0},{24,8},{1,17},{9,25},{17,1},{25,9},{2,18},{10... | collective-permute-start | bytes 196616 | tf_op jit(solution)/shard_map/ppermute | solution.py:381
  39.9 0.0 collective-permute-done.1
  39.9 0.9 %collective-permute-start.12 = (f32[2,8,1024]{2,1,0:T(8,128)S(1)}, f32[2,8,1024]{2,1,0:T(8,128)S(1)}, u32[]{:S(2)}, u32[]{:S(2)}) collective-permute-start(f32[2,8,1024]{2,1,0:T(8,128)S(1)} %get-tuple-element.40), channel_id=1, source_target_pairs={{0,24},{8,16},{16,8},{24,0},{1,25},{9,17},{17,9},{25,1},{2,26},{10... | collective-permute-start | bytes 196616 | tf_op jit(solution)/shard_map/ppermute | solution.py:382
  40.8 0.0 collective-permute-done.4
  40.8 0.0 collective-permute-done.5
  40.8 0.0 collective-permute-done.8.refs_2_
  40.8 0.9 %collective-permute-done.11.refs_3_ = f32[2,8,1024]{2,1,0:T(8,128)S(1)} collective-permute-done((f32[2,8,1024]{2,1,0:T(8,128)S(1)}, f32[2,8,1024]{2,1,0:T(8,128)S(1)}, u32[]{:S(2)}, u32[]{:S(2)}) %collective-permute-start.11) | collective-permute-done | bytes 65568 | tf_op jit(solution)/shard_map/ppermute | solution.py:381
  41.7 2.7 %collective-permute-done.12.refs_4_ = f32[2,8,1024]{2,1,0:T(8,128)S(1)} collective-permute-done((f32[2,8,1024]{2,1,0:T(8,128)S(1)}, f32[2,8,1024]{2,1,0:T(8,128)S(1)}, u32[]{:S(2)}, u32[]{:S(2)}) %collective-permute-start.12) | collective-permute-done | bytes 65568 | tf_op jit(solution)/shard_map/ppermute | solution.py:382
  44.5 0.7 %finish.1 = f32[2,32,1024]{2,1,0:T(8,128)} custom-call(f32[2,24,1024]{2,1,0:T(8,128)S(1)} %add_add_fusion.refs_0_, f32[2,8,1024]{2,1,0:T(8,128)S(1)} %get-tuple-element.34.refs_5_.refs_1_, f32[2,8,1024]{2,1,0:T(8,128)S(1)} %collective-permute-done.8.refs_2_, f32[2,8,1024]{2,1,0:T(8,128)S(1)} %collective-permute-done.11.refs_3_, ...), custom_call_target="tpu_custom_call" | custom-call | flops 1024 | bytes 1024 | tf_op jit(solution)/shard_map/finish/pallas_call | solution.py:30
  (1 shorter events, 0.0 us)
Async XLA Ops:
  0.0 3.2 %collective-permute-start = (f32[2,32,1024]{2,1,0:T(8,128)}, f32[2,32,1024]{2,1,0:T(8,128)S(1)}, u32[]{:S(2)}, u32[]{:S(2)}) collective-permute-start(f32[2,32,1024]{2,1,0:T(8,128)} %g_ref.1), channel_id=1, source_target_pairs={{0,8},{8,0},{16,24},{24,16},{1,9},{9,1},{17,25},{25,17},{2,10},{10... | collective-permute-start | bytes 786440 | tf_op jit(solution)/shard_map/ppermute | solution.py:360
  0.7 14.6 %collective-permute-start.3 = (f32[2,32,1024]{2,1,0:T(8,128)}, f32[2,32,1024]{2,1,0:T(8,128)S(1)}, u32[]{:S(2)}, u32[]{:S(2)}) collective-permute-start(f32[2,32,1024]{2,1,0:T(8,128)} %g_ref.1), channel_id=1, source_target_pairs={{0,24},{8,16},{16,8},{24,0},{1,25},{9,17},{17,9},{25,1},{2,26},{10... | collective-permute-start | bytes 786440 | tf_op jit(solution)/shard_map/ppermute | solution.py:362
  1.8 13.5 %collective-permute-start.2 = (f32[2,32,1024]{2,1,0:T(8,128)}, f32[2,32,1024]{2,1,0:T(8,128)S(1)}, u32[]{:S(2)}, u32[]{:S(2)}) collective-permute-start(f32[2,32,1024]{2,1,0:T(8,128)} %g_ref.1), channel_id=1, source_target_pairs={{0,16},{8,24},{16,0},{24,8},{1,17},{9,25},{17,1},{25,9},{2,18},{10... | collective-permute-start | bytes 786440 | tf_op jit(solution)/shard_map/ppermute | solution.py:361
  2.0 3.5 %copy-start = (bf16[16,8,32,1024]{3,2,1,0:T(8,128)(2,1)S(1)}, bf16[16,8,32,1024]{3,2,1,0:T(8,128)(2,1)}, u32[]{:S(2)}) copy-start(bf16[16,8,32,1024]{3,2,1,0:T(8,128)(2,1)} %refs_0_.11) | copy-start | bytes 25165828
  6.1 21.7 %collective-permute-start.7 = (f32[9,8,1024]{2,1,0:T(8,128)S(1)}, f32[9,8,1024]{2,1,0:T(8,128)S(1)}, u32[]{:S(2)}, u32[]{:S(2)}) collective-permute-start(f32[9,8,1024]{2,1,0:T(8,128)S(1)} %get-tuple-element.33), channel_id=1, source_target_pairs={{1,2},{3,4},{5,6},{2,1},{4,3},{6,5},{9,10},{11,12},{13,14},{10,9},... | collective-permute-start | bytes 884744 | tf_op jit(solution)/shard_map/ppermute | solution.py:368
  9.2 20.5 %collective-permute-start.6 = (f32[9,8,1024]{2,1,0:T(8,128)S(1)}, f32[9,8,1024]{2,1,0:T(8,128)S(1)}, u32[]{:S(2)}, u32[]{:S(2)}) collective-permute-start(f32[9,8,1024]{2,1,0:T(8,128)S(1)} %get-tuple-element.25.refs_4_), channel_id=1, source_target_pairs={{0,1},{1,0},{2,3},{3,2},{4,5},{5,4},{6,7},{7,6},{8,9},{9,8},{10,11... | collective-permute-start | bytes 884744 | tf_op jit(solution)/shard_map/ppermute | solution.py:367
  15.8 18.9 %collective-permute-start.10 = (f32[8,8,1024]{2,1,0:T(8,128)S(1)}, f32[8,8,1024]{2,1,0:T(8,128)S(1)}, u32[]{:S(2)}, u32[]{:S(2)}) collective-permute-start(f32[8,8,1024]{2,1,0:T(8,128)S(1)} %get-tuple-element.37), channel_id=1, source_target_pairs={{1,2},{3,4},{5,6},{2,1},{4,3},{6,5},{9,10},{11,12},{13,14},{10,9},... | collective-permute-start | bytes 786440 | tf_op jit(solution)/shard_map/ppermute | solution.py:373
  20.2 15.2 %collective-permute-start.9 = (f32[8,8,1024]{2,1,0:T(8,128)S(1)}, f32[8,8,1024]{2,1,0:T(8,128)S(1)}, u32[]{:S(2)}, u32[]{:S(2)}) collective-permute-start(f32[8,8,1024]{2,1,0:T(8,128)S(1)} %get-tuple-element.29.refs_4_), channel_id=1, source_target_pairs={{0,1},{1,0},{2,3},{3,2},{4,5},{5,4},{6,7},{7,6},{8,9},{9,8},{10,11... | collective-permute-start | bytes 786440 | tf_op jit(solution)/shard_map/ppermute | solution.py:372
  20.2 19.6 %collective-permute-start.1 = (f32[2,24,1024]{2,1,0:T(8,128)S(1)}, f32[2,24,1024]{2,1,0:T(8,128)S(1)}, u32[]{:S(2)}, u32[]{:S(2)}) collective-permute-start(f32[2,24,1024]{2,1,0:T(8,128)S(1)} %get-tuple-element.27), channel_id=1, source_target_pairs={{0,8},{8,0},{16,24},{24,16},{1,9},{9,1},{17,25},{25,17},{2,10},{10... | collective-permute-start | bytes 589832 | tf_op jit(solution)/shard_map/ppermute | solution.py:377
  27.8 13.0 %collective-permute-start.4 = (f32[2,24,1024]{2,1,0:T(8,128)S(1)}, f32[2,24,1024]{2,1,0:T(8,128)S(1)}, u32[]{:S(2)}, u32[]{:S(2)}) collective-permute-start(f32[2,24,1024]{2,1,0:T(8,128)S(1)} %get-tuple-element.30), channel_id=1, source_target_pairs={{0,16},{8,24},{16,0},{24,8},{1,17},{9,25},{17,1},{25,9},{2,18},{10... | collective-permute-start | bytes 589832 | tf_op jit(solution)/shard_map/ppermute | solution.py:378
  29.7 11.0 %collective-permute-start.5 = (f32[2,24,1024]{2,1,0:T(8,128)S(1)}, f32[2,24,1024]{2,1,0:T(8,128)S(1)}, u32[]{:S(2)}, u32[]{:S(2)}) collective-permute-start(f32[2,24,1024]{2,1,0:T(8,128)S(1)} %get-tuple-element.31), channel_id=1, source_target_pairs={{0,24},{8,16},{16,8},{24,0},{1,25},{9,17},{17,9},{25,1},{2,26},{10... | collective-permute-start | bytes 589832 | tf_op jit(solution)/shard_map/ppermute | solution.py:379
  34.7 6.1 %collective-permute-start.8 = (f32[2,8,1024]{2,1,0:T(8,128)S(1)}, f32[2,8,1024]{2,1,0:T(8,128)S(1)}, u32[]{:S(2)}, u32[]{:S(2)}) collective-permute-start(f32[2,8,1024]{2,1,0:T(8,128)S(1)} %get-tuple-element.35), channel_id=1, source_target_pairs={{0,8},{8,0},{16,24},{24,16},{1,9},{9,1},{17,25},{25,17},{2,10},{10... | collective-permute-start | bytes 196616 | tf_op jit(solution)/shard_map/ppermute | solution.py:380
  38.6 3.2 %collective-permute-start.11 = (f32[2,8,1024]{2,1,0:T(8,128)S(1)}, f32[2,8,1024]{2,1,0:T(8,128)S(1)}, u32[]{:S(2)}, u32[]{:S(2)}) collective-permute-start(f32[2,8,1024]{2,1,0:T(8,128)S(1)} %get-tuple-element.39), channel_id=1, source_target_pairs={{0,16},{8,24},{16,0},{24,8},{1,17},{9,25},{17,1},{25,9},{2,18},{10... | collective-permute-start | bytes 196616 | tf_op jit(solution)/shard_map/ppermute | solution.py:381
  39.9 4.6 %collective-permute-start.12 = (f32[2,8,1024]{2,1,0:T(8,128)S(1)}, f32[2,8,1024]{2,1,0:T(8,128)S(1)}, u32[]{:S(2)}, u32[]{:S(2)}) collective-permute-start(f32[2,8,1024]{2,1,0:T(8,128)S(1)} %get-tuple-element.40), channel_id=1, source_target_pairs={{0,24},{8,16},{16,8},{24,0},{1,25},{9,17},{17,9},{25,1},{2,26},{10... | collective-permute-start | bytes 196616 | tf_op jit(solution)/shard_map/ppermute | solution.py:382

commit v7 on v6

--- a/solution.py
+++ b/solution.py
@@ -22,6 +22,8 @@
 HALF = 16
 VMEM_BYTES = 40 * 2**20
 PREPARE_FLOPS = 10**10
+EDGE_GROUP = 8
+INNER_GROUP = 2
 
 
 def kernel_call(body, out_shape, scratch, flops, name, outside={}):
@@ -73,10 +75,13 @@
     return [slot * VARS + at * own + k for at in (share, shares - 1 - share) for k in range(own)]
 
 
-def prepare(g_ref, counts_ref, near_g_ref, near_counts_ref, sem):
+def prepare(g_ref, counts_ref, near_g_ref, rim_ref, near_counts_ref, sem):
+    rows = g_ref.shape[1]
     copies = [
-        pltpu.make_async_copy(g_ref, near_g_ref, sem.at[0]),
-        pltpu.make_async_copy(counts_ref, near_counts_ref, sem.at[1]),
+        pltpu.make_async_copy(g_ref.at[:, 0:TILE], rim_ref.at[:, 0:TILE], sem.at[0]),
+        pltpu.make_async_copy(g_ref.at[:, rows - TILE : rows], rim_ref.at[:, TILE : 2 * TILE], sem.at[1]),
+        pltpu.make_async_copy(g_ref, near_g_ref, sem.at[2]),
+        pltpu.make_async_copy(counts_ref, near_counts_ref, sem.at[3]),
     ]
     for copy in copies:
         copy.start()
@@ -248,20 +253,24 @@
     own_ref[...] = jnp.zeros_like(own_ref)
     other_ref[...] = jnp.zeros_like(other_ref)
 
-    def step(q, carry):
+    group = win_a.shape[0]
+
+    def step(s, carry):
+        base = s * group
         for j in range(blocks):
-            above, below = sent(q, j)
-            win_a[0, j, start : start + TILE] = above
-            win_a[0, j, start + 12 : start + 20] = below
-            win_a[1, j, start - 4 : start + 4] = above
-            win_a[1, j, start + 8 : start + 16] = below
-            for i in range(2):
-                win_a[i, j, start + 4 : start + 12] = kept_ref[2 * q + i, 0:TILE, cols(j)]
+            for i in range(0, group, 2):
+                above, below = sent(s * (group // 2) + i // 2, j)
+                win_a[i, j, start : start + TILE] = above
+                win_a[i, j, start + 12 : start + 20] = below
+                win_a[i + 1, j, start - 4 : start + 4] = above
+                win_a[i + 1, j, start + 8 : start + 16] = below
+            for i in range(group):
+                win_a[i, j, start + 4 : start + 12] = kept_ref[base + i, 0:TILE, cols(j)]
         src, dst = win_a, win_b
-        smooth = [[], []]
+        smooth = [[] for i in range(group)]
         for t in range(SWEEPS):
             weights = [[coef[t, c, j] for j in range(blocks)] for c in range(2)]
-            for i in range(2):
+            for i in range(group):
                 centre = [merged(src.at[i, j], start + 1, start + 7) for j in range(blocks)]
                 lateral = sides(centre, first, last)
                 for j in range(blocks):
@@ -272,19 +281,25 @@
                     else:
                         dst[i, j, start : start + TILE] = new
                         dst[i, j, start + 8 : start + 16] = new
-                        dst[i, j, start + 4 : start + 12] = kept_ref[2 * q + i, (t + 1) * TILE : (t + 2) * TILE, cols(j)]
+                        dst[i, j, start + 4 : start + 12] = kept_ref[base + i, (t + 1) * TILE : (t + 2) * TILE, cols(j)]
             src, dst = dst, src
         for j in range(blocks):
             for f, (ref, k) in zip(fields, sums):
                 total = ref[k, :, cols(j)]
-                for i in range(2):
-                    low = p_ref[2 * q + i, f, 0:HALF, cols(j)].astype(jnp.float32)[0:TILE]
-                    high = p_ref[2 * q + i, f, rows - HALF : rows, cols(j)].astype(jnp.float32)[HALF - TILE :]
+                for i in range(group):
+                    low = p_ref[base + i, f, 0:HALF, cols(j)].astype(jnp.float32)[0:TILE]
+                    high = p_ref[base + i, f, rows - HALF : rows, cols(j)].astype(jnp.float32)[HALF - TILE :]
                     total = total + jnp.where(half, low, high) * smooth[i][j]
                 ref[k, :, cols(j)] = total
         return carry
 
-    lax.fori_loop(0, members // 2, step, 0)
+    lax.fori_loop(0, members // group, step, 0)
+
+
+def relay(*refs):
+    count = len(refs) // 2
+    for ref, out_ref in zip(refs[:count], refs[count + 1 :]):
+        out_ref[...] = ref[...]
 
 
 def finish(scale, *refs):
@@ -326,10 +341,10 @@
         return pltpu.VMEM((*lead, blocks, 4 * TILE, LANES), f32)
 
     def call_prepare(*args):
-        outs = (shape(own, rows, ny), jax.ShapeDtypeStruct((rows, ny), counts.dtype))
+        outs = (shape(own, rows, ny), shape(own, 2 * TILE, ny), jax.ShapeDtypeStruct((rows, ny), counts.dtype))
         stored = [pltpu.with_memory_space_constraint(x, pltpu.HBM) for x in args]
         outside = {0: pl.ANY, 1: pl.ANY}
-        return kernel_call(prepare, outs, [pltpu.SemaphoreType.DMA((2,))], PREPARE_FLOPS, "prepare", outside)(*stored)
+        return kernel_call(prepare, outs, [pltpu.SemaphoreType.DMA((4,))], PREPARE_FLOPS, "prepare", outside)(*stored)
 
     def call_project(local, *args):
         pairs = members // 2 + (1 if local else 0)
@@ -338,9 +353,13 @@
         body = lambda *refs: project_edges(local, own, *refs)
         return kernel_call(body, outs, [], 1024, "project", outside=outside)(*args)
 
+    def call_relay(*args):
+        outs = tuple(shape(*x.shape) for x in args[:-1])
+        return kernel_call(relay, outs, [], 1024, "relay", outside={len(outs): pl.ANY})(*args)
+
     def call_interior(local, *args):
         total = pltpu.VMEM((VARS, blocks, rows, LANES), f32)
-        buf = pltpu.VMEM((2, blocks, rows + 2 * TILE, LANES), f32)
+        buf = pltpu.VMEM((INNER_GROUP, blocks, rows + 2 * TILE, LANES), f32)
         outs = (shape(own, rows - TILE, ny), shape(own, rows - TILE, ny), shape(members, SWEEPS * TILE, ny))
         if local:
             outs = outs + (shape(SWEEPS - 1, 2, blocks, rows, LANES),)
@@ -349,26 +368,27 @@
 
     def call_edges(local, *args):
         outs = (shape(own, TILE, ny), shape(own, TILE, ny))
-        scratch = [window(2), window(2)]
+        scratch = [window(EDGE_GROUP), window(EDGE_GROUP)]
         if local:
             outs, scratch = outs + (shape(SWEEPS, 2, blocks, TILE, LANES),), scratch + [window()]
         body = lambda *refs: edges(local, *refs)
         outside = {} if local else {len(args) - 1: pl.ANY}
         return kernel_call(body, outs, scratch, 1024, "edges", outside=outside)(*args)
 
-    near_g, near_counts = call_prepare(gradient, counts)
+    near_g, rim, near_counts = call_prepare(gradient, counts)
     partner = lax.ppermute(gradient, "mem", near)
     far = lax.ppermute(gradient, "mem", across)
-    far_partner = lax.ppermute(gradient, "mem", cross)
+    far_rim = lax.ppermute(rim, "mem", cross)
 
     p = perturbations
     e0, o0 = call_project(True, p, near_g, partner, near_counts)
-    own0, other0, kept0, inner_coef = call_interior(True, p, near_g, partner, near_counts, e0)
+    own0, other0, kept0, inner_coef = call_interior(True, p, near_g, partner, near_counts, o0)
     e0 = lax.ppermute(e0, "strip", even)
     o0 = lax.ppermute(o0, "strip", odd)
 
-    e1, o1 = call_project(False, p, far, far_partner, own0)
-    own1, other1, kept1 = call_interior(False, p, far, far_partner, inner_coef, e1)
+    e1, o1 = call_project(False, p, far, far_rim, own0)
+    far_partner = lax.ppermute(call_relay(far, o1)[0], "mem", near)
+    own1, other1, kept1 = call_interior(False, p, far, far_partner, inner_coef, o1)
     e1 = lax.ppermute(e1, "strip", even)
     o1 = lax.ppermute(o1, "strip", odd)
     eown0, eother0, edge_coef = call_edges(True, p, kept0, e0, o0, near_counts)

time: 45.7 us -> 43.4 us (0.950)
  Pallas kernels: 21.1 us -> 18.9 us
  waiting for transfers between devices: 4.86 us -> 5.4 us
    ppermute x1, waiting for transfers between devices: 0.01 us -> 3.01 us  [per_device(): inner = inner + lax.ppermute(other1, 'mem', cross)]
    pallas_call x8 -> x9, Pallas kernels: 21.1 us -> 18.9 us  [call(): pl.pallas_call(body, out_shape=out_shape, in_specs=[pl.BlockSpec(memory_s...]
    ppermute x1, waiting for transfers between devices: 2.73 us -> 1.51 us  [per_device(): ecross1 = lax.ppermute(eother1, 'mem', cross)]
    ppermute x1, starting transfers between devices: 1.3 us -> 0.29 us  [per_device(): efar1 = lax.ppermute(eown1, 'mem', across)]
    ppermute x1, starting transfers between devices: 1.3 us -> 0.29 us  [per_device(): inner = inner + lax.ppermute(own1, 'mem', across)]
    ppermute x1, starting transfers between devices: 0.23 us -> 1.24 us  [per_device(): far = lax.ppermute(gradient, 'mem', across)]
    ppermute x1, starting transfers between devices: 1.69 us -> 0.69 us  [per_device(): inner = own0 + lax.ppermute(other0, 'mem', near)]
    ppermute x1, starting transfers between devices: 3.18 us -> 4.12 us  [per_device(): o0 = lax.ppermute(o0, 'strip', odd)]
  transfers between devices with their start and end apart: 13 -> 14, of which waited for: 4 -> 3; matrix products, arithmetic and copies ran while one was open for 0% -> 0% of each run, Pallas kernels for 45% -> 42%
where the time goes in v7:
time: 43.4 us; the launch traced here: 43.3 us
  Pallas kernels  18.9 us (44%)
  starting transfers between devices  16.6 us (38%)
  waiting for transfers between devices  5.4 us (12%)
  local copies, waits for them, and re-layouts  2.16 us (5%)
    pallas_call x9, Pallas kernels, call(): pl.pallas_call(body, out_shape=out_shape, in_specs=[pl.BlockSpec(memory_s...  18.9 us
    ppermute x1, starting transfers between devices, per_device(): o1 = lax.ppermute(o1, 'strip', odd)  4.38 us
    ppermute x1, starting transfers between devices, per_device(): o0 = lax.ppermute(o0, 'strip', odd)  4.12 us
    ppermute x1, waiting for transfers between devices, per_device(): inner = inner + lax.ppermute(other1, 'mem', cross)  3.01 us
    unnamed x2, local copies, waits for them, and re-layouts  2.16 us
    ppermute x1, waiting for transfers between devices, per_device(): ecross1 = lax.ppermute(eother1, 'mem', cross)  1.51 us
    ppermute x1, starting transfers between devices, per_device(): inner = inner + lax.ppermute(other1, 'mem', cross)  1.42 us
    ppermute x1, starting transfers between devices, per_device(): ecross1 = lax.ppermute(eother1, 'mem', cross)  1.41 us
  transfers between devices with their start and end apart: 14, of which 3 were waited for; matrix products, arithmetic and copies ran while one was open for 0% of the time, Pallas kernels for 42%

profile of v7, /device:TPU:3, one launch (start us, length us, event | category | flops | bytes accessed | tf_op | source)
XLA Modules:
  0.0 43.3 jit_solution(8251221070522389375)
XLA Ops:
  0.0 1.2 %collective-permute-start.2 = (f32[2,32,1024]{2,1,0:T(8,128)}, f32[2,32,1024]{2,1,0:T(8,128)S(1)}, u32[]{:S(2)}, u32[]{:S(2)}) collective-permute-start(f32[2,32,1024]{2,1,0:T(8,128)} %g_ref.1), channel_id=1, source_target_pairs={{0,16},{8,24},{16,0},{24,8},{1,17},{9,25},{17,1},{25,9},{2,18},{10... | collective-permute-start | bytes 786440 | tf_op jit(solution)/shard_map/ppermute | solution.py:380
  1.2 1.0 %collective-permute-start = (f32[2,32,1024]{2,1,0:T(8,128)}, f32[2,32,1024]{2,1,0:T(8,128)S(1)}, u32[]{:S(2)}, u32[]{:S(2)}) collective-permute-start(f32[2,32,1024]{2,1,0:T(8,128)} %g_ref.1), channel_id=1, source_target_pairs={{0,8},{8,0},{16,24},{24,16},{1,9},{9,1},{17,25},{25,17},{2,10},{10... | collective-permute-start | bytes 786440 | tf_op jit(solution)/shard_map/ppermute | solution.py:379
  2.2 0.0 copy-start
  2.2 1.2 %prepare.1 = (f32[2,32,1024]{2,1,0:T(8,128)S(1)}, f32[2,16,1024]{2,1,0:T(8,128)S(1)}, s32[32,1024]{1,0:T(8,128)S(1)}) custom-call(f32[2,32,1024]{2,1,0:T(8,128)} %g_ref.1, s32[32,1024]{1,0:T(8,128)} %counts_ref.1), custom_call_target="tpu_custom_call" | custom-call | flops 10000000000 | bytes 1024 | tf_op jit(solution)/shard_map/prepare/pallas_call | solution.py:32
  3.4 0.2 collective-permute-start.3
  3.6 0.0 collective-permute-done.refs_2_
  3.6 2.2 %copy-done = bf16[16,8,32,1024]{3,2,1,0:T(8,128)(2,1)S(1)} copy-done((bf16[16,8,32,1024]{3,2,1,0:T(8,128)(2,1)S(1)}, bf16[16,8,32,1024]{3,2,1,0:T(8,128)(2,1)}, u32[]{:S(2)}) %copy-start) | copy-done | bytes 8388632
  5.8 0.5 %project.2 = (f32[9,8,1024]{2,1,0:T(8,128)S(1)}, f32[9,8,1024]{2,1,0:T(8,128)S(1)}) custom-call(bf16[16,8,32,1024]{3,2,1,0:T(8,128)(2,1)S(1)} %copy-done, f32[2,32,1024]{2,1,0:T(8,128)S(1)} %get-tuple-element.24.refs_1_, f32[2,32,1024]{2,1,0:T(8,128)S(1)} %collective-permute-done.refs_2_, s32[32,1024]{1,0:T(8,128)S(1)} %get-tuple-element.25.refs_3_.refs_4_), custom_call_target="tpu_custom_call" | custom-call | flops 1024 | bytes 1024 | tf_op jit(solution)/shard_map/project/pallas_call | solution.py:32
  6.3 0.3 collective-permute-start.7
  6.6 4.1 %collective-permute-start.8 = (f32[9,8,1024]{2,1,0:T(8,128)S(1)}, f32[9,8,1024]{2,1,0:T(8,128)S(1)}, u32[]{:S(2)}, u32[]{:S(2)}) collective-permute-start(f32[9,8,1024]{2,1,0:T(8,128)S(1)} %get-tuple-element.26.refs_4_), channel_id=1, source_target_pairs={{1,2},{3,4},{5,6},{2,1},{4,3},{6,5},{9,10},{11,12},{13,14},{10,9},... | collective-permute-start | bytes 884744 | tf_op jit(solution)/shard_map/ppermute | solution.py:387
  10.7 5.9 %interior.2 = (f32[2,24,1024]{2,1,0:T(8,128)S(1)}, f32[2,24,1024]{2,1,0:T(8,128)S(1)}, f32[16,32,1024]{2,1,0:T(8,128)S(1)}, f32[3,2,8,32,128]{4,3,2,1,0:T(8,128)S(1)}) custom-call(bf16[16,8,32,1024]{3,2,1,0:T(8,128)(2,1)S(1)} %copy-done, f32[2,32,1024]{2,1,0:T(8,128)S(1)} %get-tuple-element.24.refs_1_, f32[2,32,1024]{2,1,0:T(8,128)S(1)} %collective-permute-done.refs_2_, ...), custom_call_target="tpu_custom_call" | custom-call | flops 1024 | bytes 1024 | tf_op jit(solution)/shard_map/interior/pallas_call | solution.py:32
  16.7 0.0 collective-permute-done.3.refs_2_
  16.7 0.0 collective-permute-done.2.refs_1_.refs_0_
  16.7 0.5 %project.3 = (f32[8,8,1024]{2,1,0:T(8,128)S(1)}, f32[8,8,1024]{2,1,0:T(8,128)S(1)}) custom-call(bf16[16,8,32,1024]{3,2,1,0:T(8,128)(2,1)S(1)} %copy-done, f32[2,32,1024]{2,1,0:T(8,128)S(1)} %collective-permute-done.2.refs_1_.refs_0_, f32[2,16,1024]{2,1,0:T(8,128)S(1)} %collective-permute-done.3.refs_2_, f32[2,24,1024]{2,1,0:T(8,128)S(1)} %get-tuple-element.27.refs_3_), custom_call_target="tpu_custom_call" | custom-call | flops 1024 | bytes 1024 | tf_op jit(solution)/shard_map/project/pallas_call | solution.py:32
  17.2 0.6 %collective-permute-start.4 = (f32[2,32,1024]{2,1,0:T(8,128)S(1)}, f32[2,32,1024]{2,1,0:T(8,128)S(1)}, u32[]{:S(2)}, u32[]{:S(2)}) collective-permute-start(f32[2,32,1024]{2,1,0:T(8,128)S(1)} %relay.1), channel_id=1, source_target_pairs={{0,8},{8,0},{16,24},{24,16},{1,9},{9,1},{17,25},{25,17},{2,10},{10... | collective-permute-start | bytes 786440 | tf_op jit(solution)/shard_map/ppermute | solution.py:390
  17.9 0.0 collective-permute-start.10
  17.9 4.4 %collective-permute-start.11 = (f32[8,8,1024]{2,1,0:T(8,128)S(1)}, f32[8,8,1024]{2,1,0:T(8,128)S(1)}, u32[]{:S(2)}, u32[]{:S(2)}) collective-permute-start(f32[8,8,1024]{2,1,0:T(8,128)S(1)} %get-tuple-element.30.refs_1_.refs_4_), channel_id=1, source_target_pairs={{1,2},{3,4},{5,6},{2,1},{4,3},{6,5},{9,10},{11,12},{13,14},{10,9},... | collective-permute-start | bytes 786440 | tf_op jit(solution)/shard_map/ppermute | solution.py:393
  22.3 0.0 collective-permute-done.4.refs_2_
  22.3 0.7 %collective-permute-start.1 = (f32[2,24,1024]{2,1,0:T(8,128)S(1)}, f32[2,24,1024]{2,1,0:T(8,128)S(1)}, u32[]{:S(2)}, u32[]{:S(2)}) collective-permute-start(f32[2,24,1024]{2,1,0:T(8,128)S(1)} %get-tuple-element.28), channel_id=1, source_target_pairs={{0,8},{8,0},{16,24},{24,16},{1,9},{9,1},{17,25},{25,17},{2,10},{10... | collective-permute-start | bytes 589832 | tf_op jit(solution)/shard_map/ppermute | solution.py:397
  23.0 5.8 %interior.3 = (f32[2,24,1024]{2,1,0:T(8,128)S(1)}, f32[2,24,1024]{2,1,0:T(8,128)S(1)}, f32[16,32,1024]{2,1,0:T(8,128)S(1)}) custom-call(bf16[16,8,32,1024]{3,2,1,0:T(8,128)(2,1)S(1)} %copy-done, f32[2,32,1024]{2,1,0:T(8,128)S(1)} %collective-permute-done.2.refs_1_.refs_0_, f32[2,32,1024]{2,1,0:T(8,128)S(1)} %collective-permute-done.4.refs_2_, ...), custom_call_target="tpu_custom_call" | custom-call | flops 1024 | bytes 1024 | tf_op jit(solution)/shard_map/interior/pallas_call | solution.py:32
  28.8 0.0 collective-permute-done.7.refs_2_
  28.8 0.3 collective-permute-start.5
  29.1 0.0 collective-permute-done.8.refs_3_
  29.1 1.4 %collective-permute-start.6 = (f32[2,24,1024]{2,1,0:T(8,128)S(1)}, f32[2,24,1024]{2,1,0:T(8,128)S(1)}, u32[]{:S(2)}, u32[]{:S(2)}) collective-permute-start(f32[2,24,1024]{2,1,0:T(8,128)S(1)} %get-tuple-element.33), channel_id=1, source_target_pairs={{0,24},{8,16},{16,8},{24,0},{1,25},{9,17},{17,9},{25,1},{2,26},{10... | collective-permute-start | bytes 589832 | tf_op jit(solution)/shard_map/ppermute | solution.py:399
  30.5 2.1 %edges.2 = (f32[2,8,1024]{2,1,0:T(8,128)S(1)}, f32[2,8,1024]{2,1,0:T(8,128)S(1)}, f32[4,2,8,8,128]{4,3,2,1,0:T(8,128)S(1)}) custom-call(bf16[16,8,32,1024]{3,2,1,0:T(8,128)(2,1)S(1)} %copy-done, f32[16,32,1024]{2,1,0:T(8,128)S(1)} %get-tuple-element.34.refs_1_, f32[9,8,1024]{2,1,0:T(8,128)S(1)} %collective-permute-done.7.refs_2_, ...), custom_call_target="tpu_custom_call" | custom-call | flops 1024 | bytes 1024 | tf_op jit(solution)/shard_map/edges/pallas_call | solution.py:32
  32.6 0.0 collective-permute-done.10.refs_2_
  32.6 0.7 %collective-permute-start.9 = (f32[2,8,1024]{2,1,0:T(8,128)S(1)}, f32[2,8,1024]{2,1,0:T(8,128)S(1)}, u32[]{:S(2)}, u32[]{:S(2)}) collective-permute-start(f32[2,8,1024]{2,1,0:T(8,128)S(1)} %get-tuple-element.37), channel_id=1, source_target_pairs={{0,8},{8,0},{16,24},{24,16},{1,9},{9,1},{17,25},{25,17},{2,10},{10... | collective-permute-start | bytes 196616 | tf_op jit(solution)/shard_map/ppermute | solution.py:400
  33.3 0.0 collective-permute-done.11.refs_3_
  33.3 2.0 %edges.3 = (f32[2,8,1024]{2,1,0:T(8,128)S(1)}, f32[2,8,1024]{2,1,0:T(8,128)S(1)}) custom-call(bf16[16,8,32,1024]{3,2,1,0:T(8,128)(2,1)S(1)} %copy-done, f32[16,32,1024]{2,1,0:T(8,128)S(1)} %get-tuple-element.38.refs_1_, f32[8,8,1024]{2,1,0:T(8,128)S(1)} %collective-permute-done.10.refs_2_, f32[8,8,1024]{2,1,0:T(8,128)S(1)} %collective-permute-done.11.refs_3_, ...), custom_call_target="tpu_custom_call" | custom-call | flops 1024 | bytes 1024 | tf_op jit(solution)/shard_map/edges/pallas_call | solution.py:32
  35.4 0.3 collective-permute-start.12
  35.7 0.0 collective-permute-done.1
  35.7 1.4 %collective-permute-start.13 = (f32[2,8,1024]{2,1,0:T(8,128)S(1)}, f32[2,8,1024]{2,1,0:T(8,128)S(1)}, u32[]{:S(2)}, u32[]{:S(2)}) collective-permute-start(f32[2,8,1024]{2,1,0:T(8,128)S(1)} %get-tuple-element.42), channel_id=1, source_target_pairs={{0,24},{8,16},{16,8},{24,0},{1,25},{9,17},{17,9},{25,1},{2,26},{10... | collective-permute-start | bytes 196616 | tf_op jit(solution)/shard_map/ppermute | solution.py:402
  37.1 0.0 collective-permute-done.5
  37.1 3.0 %collective-permute-done.6 = f32[2,24,1024]{2,1,0:T(8,128)S(1)} collective-permute-done((f32[2,24,1024]{2,1,0:T(8,128)S(1)}, f32[2,24,1024]{2,1,0:T(8,128)S(1)}, u32[]{:S(2)}, u32[]{:S(2)}) %collective-permute-start.6) | collective-permute-done | bytes 196640 | tf_op jit(solution)/shard_map/ppermute | solution.py:399
  40.2 0.0 collective-permute-done.9.refs_2_
  40.2 0.8 %collective-permute-done.12.refs_3_ = f32[2,8,1024]{2,1,0:T(8,128)S(1)} collective-permute-done((f32[2,8,1024]{2,1,0:T(8,128)S(1)}, f32[2,8,1024]{2,1,0:T(8,128)S(1)}, u32[]{:S(2)}, u32[]{:S(2)}) %collective-permute-start.12) | collective-permute-done | bytes 65568 | tf_op jit(solution)/shard_map/ppermute | solution.py:401
  41.0 1.5 %collective-permute-done.13.refs_4_ = f32[2,8,1024]{2,1,0:T(8,128)S(1)} collective-permute-done((f32[2,8,1024]{2,1,0:T(8,128)S(1)}, f32[2,8,1024]{2,1,0:T(8,128)S(1)}, u32[]{:S(2)}, u32[]{:S(2)}) %collective-permute-start.13) | collective-permute-done | bytes 65568 | tf_op jit(solution)/shard_map/ppermute | solution.py:402
  42.5 0.7 %finish.1 = f32[2,32,1024]{2,1,0:T(8,128)} custom-call(f32[2,24,1024]{2,1,0:T(8,128)S(1)} %add_add_fusion.refs_0_, f32[2,8,1024]{2,1,0:T(8,128)S(1)} %get-tuple-element.36.refs_5_.refs_1_, f32[2,8,1024]{2,1,0:T(8,128)S(1)} %collective-permute-done.9.refs_2_, f32[2,8,1024]{2,1,0:T(8,128)S(1)} %collective-permute-done.12.refs_3_, ...), custom_call_target="tpu_custom_call" | custom-call | flops 1024 | bytes 1024 | tf_op jit(solution)/shard_map/finish/pallas_call | solution.py:32
  (2 shorter events, 0.1 us)
Async XLA Ops:
  0.0 16.7 %collective-permute-start.2 = (f32[2,32,1024]{2,1,0:T(8,128)}, f32[2,32,1024]{2,1,0:T(8,128)S(1)}, u32[]{:S(2)}, u32[]{:S(2)}) collective-permute-start(f32[2,32,1024]{2,1,0:T(8,128)} %g_ref.1), channel_id=1, source_target_pairs={{0,16},{8,24},{16,0},{24,8},{1,17},{9,25},{17,1},{25,9},{2,18},{10... | collective-permute-start | bytes 786440 | tf_op jit(solution)/shard_map/ppermute | solution.py:380
  1.2 2.4 %collective-permute-start = (f32[2,32,1024]{2,1,0:T(8,128)}, f32[2,32,1024]{2,1,0:T(8,128)S(1)}, u32[]{:S(2)}, u32[]{:S(2)}) collective-permute-start(f32[2,32,1024]{2,1,0:T(8,128)} %g_ref.1), channel_id=1, source_target_pairs={{0,8},{8,0},{16,24},{24,16},{1,9},{9,1},{17,25},{25,17},{2,10},{10... | collective-permute-start | bytes 786440 | tf_op jit(solution)/shard_map/ppermute | solution.py:379
  2.2 3.6 %copy-start = (bf16[16,8,32,1024]{3,2,1,0:T(8,128)(2,1)S(1)}, bf16[16,8,32,1024]{3,2,1,0:T(8,128)(2,1)}, u32[]{:S(2)}) copy-start(bf16[16,8,32,1024]{3,2,1,0:T(8,128)(2,1)} %refs_0_.11) | copy-start | bytes 25165828
  3.4 13.2 %collective-permute-start.3 = (f32[2,16,1024]{2,1,0:T(8,128)S(1)}, f32[2,16,1024]{2,1,0:T(8,128)S(1)}, u32[]{:S(2)}, u32[]{:S(2)}) collective-permute-start(f32[2,16,1024]{2,1,0:T(8,128)S(1)} %get-tuple-element.29), channel_id=1, source_target_pairs={{0,24},{8,16},{16,8},{24,0},{1,25},{9,17},{17,9},{25,1},{2,26},{10... | collective-permute-start | bytes 393224 | tf_op jit(solution)/shard_map/ppermute | solution.py:381
  6.3 22.5 %collective-permute-start.7 = (f32[9,8,1024]{2,1,0:T(8,128)S(1)}, f32[9,8,1024]{2,1,0:T(8,128)S(1)}, u32[]{:S(2)}, u32[]{:S(2)}) collective-permute-start(f32[9,8,1024]{2,1,0:T(8,128)S(1)} %get-tuple-element.35), channel_id=1, source_target_pairs={{0,1},{1,0},{2,3},{3,2},{4,5},{5,4},{6,7},{7,6},{8,9},{9,8},{10,11... | collective-permute-start | bytes 884744 | tf_op jit(solution)/shard_map/ppermute | solution.py:386
  6.6 22.5 %collective-permute-start.8 = (f32[9,8,1024]{2,1,0:T(8,128)S(1)}, f32[9,8,1024]{2,1,0:T(8,128)S(1)}, u32[]{:S(2)}, u32[]{:S(2)}) collective-permute-start(f32[9,8,1024]{2,1,0:T(8,128)S(1)} %get-tuple-element.26.refs_4_), channel_id=1, source_target_pairs={{1,2},{3,4},{5,6},{2,1},{4,3},{6,5},{9,10},{11,12},{13,14},{10,9},... | collective-permute-start | bytes 884744 | tf_op jit(solution)/shard_map/ppermute | solution.py:387
  17.2 5.0 %collective-permute-start.4 = (f32[2,32,1024]{2,1,0:T(8,128)S(1)}, f32[2,32,1024]{2,1,0:T(8,128)S(1)}, u32[]{:S(2)}, u32[]{:S(2)}) collective-permute-start(f32[2,32,1024]{2,1,0:T(8,128)S(1)} %relay.1), channel_id=1, source_target_pairs={{0,8},{8,0},{16,24},{24,16},{1,9},{9,1},{17,25},{25,17},{2,10},{10... | collective-permute-start | bytes 786440 | tf_op jit(solution)/shard_map/ppermute | solution.py:390
  17.9 14.8 %collective-permute-start.10 = (f32[8,8,1024]{2,1,0:T(8,128)S(1)}, f32[8,8,1024]{2,1,0:T(8,128)S(1)}, u32[]{:S(2)}, u32[]{:S(2)}) collective-permute-start(f32[8,8,1024]{2,1,0:T(8,128)S(1)} %get-tuple-element.39), channel_id=1, source_target_pairs={{0,1},{1,0},{2,3},{3,2},{4,5},{5,4},{6,7},{7,6},{8,9},{9,8},{10,11... | collective-permute-start | bytes 786440 | tf_op jit(solution)/shard_map/ppermute | solution.py:392
  17.9 15.5 %collective-permute-start.11 = (f32[8,8,1024]{2,1,0:T(8,128)S(1)}, f32[8,8,1024]{2,1,0:T(8,128)S(1)}, u32[]{:S(2)}, u32[]{:S(2)}) collective-permute-start(f32[8,8,1024]{2,1,0:T(8,128)S(1)} %get-tuple-element.30.refs_1_.refs_4_), channel_id=1, source_target_pairs={{1,2},{3,4},{5,6},{2,1},{4,3},{6,5},{9,10},{11,12},{13,14},{10,9},... | collective-permute-start | bytes 786440 | tf_op jit(solution)/shard_map/ppermute | solution.py:393
  22.3 13.4 %collective-permute-start.1 = (f32[2,24,1024]{2,1,0:T(8,128)S(1)}, f32[2,24,1024]{2,1,0:T(8,128)S(1)}, u32[]{:S(2)}, u32[]{:S(2)}) collective-permute-start(f32[2,24,1024]{2,1,0:T(8,128)S(1)} %get-tuple-element.28), channel_id=1, source_target_pairs={{0,8},{8,0},{16,24},{24,16},{1,9},{9,1},{17,25},{25,17},{2,10},{10... | collective-permute-start | bytes 589832 | tf_op jit(solution)/shard_map/ppermute | solution.py:397
  28.8 8.3 %collective-permute-start.5 = (f32[2,24,1024]{2,1,0:T(8,128)S(1)}, f32[2,24,1024]{2,1,0:T(8,128)S(1)}, u32[]{:S(2)}, u32[]{:S(2)}) collective-permute-start(f32[2,24,1024]{2,1,0:T(8,128)S(1)} %get-tuple-element.32), channel_id=1, source_target_pairs={{0,16},{8,24},{16,0},{24,8},{1,17},{9,25},{17,1},{25,9},{2,18},{10... | collective-permute-start | bytes 589832 | tf_op jit(solution)/shard_map/ppermute | solution.py:398
  29.1 11.0 %collective-permute-start.6 = (f32[2,24,1024]{2,1,0:T(8,128)S(1)}, f32[2,24,1024]{2,1,0:T(8,128)S(1)}, u32[]{:S(2)}, u32[]{:S(2)}) collective-permute-start(f32[2,24,1024]{2,1,0:T(8,128)S(1)} %get-tuple-element.33), channel_id=1, source_target_pairs={{0,24},{8,16},{16,8},{24,0},{1,25},{9,17},{17,9},{25,1},{2,26},{10... | collective-permute-start | bytes 589832 | tf_op jit(solution)/shard_map/ppermute | solution.py:399
  32.6 7.5 %collective-permute-start.9 = (f32[2,8,1024]{2,1,0:T(8,128)S(1)}, f32[2,8,1024]{2,1,0:T(8,128)S(1)}, u32[]{:S(2)}, u32[]{:S(2)}) collective-permute-start(f32[2,8,1024]{2,1,0:T(8,128)S(1)} %get-tuple-element.37), channel_id=1, source_target_pairs={{0,8},{8,0},{16,24},{24,16},{1,9},{9,1},{17,25},{25,17},{2,10},{10... | collective-permute-start | bytes 196616 | tf_op jit(solution)/shard_map/ppermute | solution.py:400
  35.4 5.6 %collective-permute-start.12 = (f32[2,8,1024]{2,1,0:T(8,128)S(1)}, f32[2,8,1024]{2,1,0:T(8,128)S(1)}, u32[]{:S(2)}, u32[]{:S(2)}) collective-permute-start(f32[2,8,1024]{2,1,0:T(8,128)S(1)} %get-tuple-element.41), channel_id=1, source_target_pairs={{0,16},{8,24},{16,0},{24,8},{1,17},{9,25},{17,1},{25,9},{2,18},{10... | collective-permute-start | bytes 196616 | tf_op jit(solution)/shard_map/ppermute | solution.py:401
  35.7 6.8 %collective-permute-start.13 = (f32[2,8,1024]{2,1,0:T(8,128)S(1)}, f32[2,8,1024]{2,1,0:T(8,128)S(1)}, u32[]{:S(2)}, u32[]{:S(2)}) collective-permute-start(f32[2,8,1024]{2,1,0:T(8,128)S(1)} %get-tuple-element.42), channel_id=1, source_target_pairs={{0,24},{8,16},{16,8},{24,0},{1,25},{9,17},{17,9},{25,1},{2,26},{10... | collective-permute-start | bytes 196616 | tf_op jit(solution)/shard_map/ppermute | solution.py:402

commit v8 on v7

--- a/solution.py
+++ b/solution.py
@@ -136,7 +136,7 @@
 
 
 def interior(local, p_ref, *refs):
-    if local:
+    if not local:
         *g_refs, counts_ref, _, own_ref, other_ref, kept_ref, coef, buf_a, buf_b, total_ref = refs
     else:
         *g_refs, coef, _, own_ref, other_ref, kept_ref, buf_a, buf_b, total_ref = refs
@@ -152,7 +152,7 @@
     skip = TILE // 2
     whole = list(range(0, rows, TILE))
     kept = list(range(skip, rows - skip, TILE))
-    for t in range(1, SWEEPS if local else 1):
+    for t in range(1, 1 if local else SWEEPS):
         for j in range(blocks):
             total_ref[0, j] = (counts_ref[:, cols(j)] > t).astype(jnp.float32)
             for n, r in enumerate(kept if t == SWEEPS - 1 else whole):
@@ -303,7 +303,7 @@
 
 
 def finish(scale, *refs):
-    inner_ref, *edge_refs, out_ref = refs
+    own_ref, near_ref, inner_ref, *edge_refs, out_ref = refs
     own, rows, ny = out_ref.shape
     half = top_half()
     for k in range(own):
@@ -311,7 +311,8 @@
             edge = sum(ref[k, :, cols(j)] for ref in edge_refs[1:]) + edge_refs[0][k, :, cols(j)]
             parts = [edge]
             for r in range(0, rows - TILE, TILE):
-                parts.append(pltpu.roll(inner_ref[k, r : r + TILE, cols(j)], TILE // 2, 0))
+                inner = own_ref[k, r : r + TILE, cols(j)] + near_ref[k, r : r + TILE, cols(j)] + inner_ref[k, r : r + TILE, cols(j)]
+                parts.append(pltpu.roll(inner, TILE // 2, 0))
             parts.append(edge)
             for n in range(rows // TILE):
                 out_ref[k, n * TILE : (n + 1) * TILE, cols(j)] = jnp.where(half, parts[n], parts[n + 1]) * scale
@@ -361,7 +362,7 @@
         total = pltpu.VMEM((VARS, blocks, rows, LANES), f32)
         buf = pltpu.VMEM((INNER_GROUP, blocks, rows + 2 * TILE, LANES), f32)
         outs = (shape(own, rows - TILE, ny), shape(own, rows - TILE, ny), shape(members, SWEEPS * TILE, ny))
-        if local:
+        if not local:
             outs = outs + (shape(SWEEPS - 1, 2, blocks, rows, LANES),)
         body = lambda *refs: interior(local, *refs)
         return kernel_call(body, outs, [buf, buf, total], 1024, "interior", outside={len(args) - 1: pl.ANY})(*args)
@@ -382,27 +383,26 @@
 
     p = perturbations
     e0, o0 = call_project(True, p, near_g, partner, near_counts)
-    own0, other0, kept0, inner_coef = call_interior(True, p, near_g, partner, near_counts, o0)
+    e1, o1 = call_project(False, p, far, far_rim, o0)
+    far_partner = lax.ppermute(call_relay(far, o1)[0], "mem", near)
+    own1, other1, kept1, inner_coef = call_interior(False, p, far, far_partner, near_counts, o1)
+    own0, other0, kept0 = call_interior(True, p, near_g, partner, inner_coef, own1)
     e0 = lax.ppermute(e0, "strip", even)
     o0 = lax.ppermute(o0, "strip", odd)
-
-    e1, o1 = call_project(False, p, far, far_rim, own0)
-    far_partner = lax.ppermute(call_relay(far, o1)[0], "mem", near)
-    own1, other1, kept1 = call_interior(False, p, far, far_partner, inner_coef, o1)
     e1 = lax.ppermute(e1, "strip", even)
     o1 = lax.ppermute(o1, "strip", odd)
     eown0, eother0, edge_coef = call_edges(True, p, kept0, e0, o0, near_counts)
     eown1, eother1 = call_edges(False, p, kept1, e1, o1, edge_coef, eown0)
 
-    inner = own0 + lax.ppermute(other0, "mem", near)
-    inner = inner + lax.ppermute(own1, "mem", across)
-    inner = inner + lax.ppermute(other1, "mem", cross)
+    inner = lax.ppermute(own1, "mem", across) + lax.ppermute(other1, "mem", cross)
+    near0 = lax.ppermute(other0, "mem", near)
     enear0 = lax.ppermute(eother0, "mem", near)
+    eown1, eother1 = call_relay(eown1, eother1, inner)
     efar1 = lax.ppermute(eown1, "mem", across)
     ecross1 = lax.ppermute(eother1, "mem", cross)
     return kernel_call(
         lambda *refs: finish(scale, *refs), shape(own, rows, ny), [], 1024, "finish"
-    )(inner, eown0, enear0, efar1, ecross1)
+    )(own0, near0, inner, eown0, enear0, efar1, ecross1)
 
 
 def solution(mesh):

time: 43.4 us -> 45.2 us (1.041)
  waiting for transfers between devices: 5.4 us -> 8.12 us
  starting transfers between devices: 16.6 us -> 15.7 us
    ppermute x1, waiting for transfers between devices: 0.01 us -> 4.73 us  [per_device(): far_rim = lax.ppermute(rim, 'mem', cross)]
    ppermute x3, waiting for transfers between devices: 3.01 us -> 0.01 us  [the longest x1 0.01 us: per_device(): lax.ppermute(own1, 'mem', across) + lax.ppermute(other1, 'mem', cross)]
    ppermute x1, starting transfers between devices: 0.29 us -> 1.3 us  [per_device(): efar1 = lax.ppermute(eown1, 'mem', across)]
    ppermute x1, starting transfers between devices: 4.12 us -> 3.18 us  [per_device(): o0 = lax.ppermute(o0, 'strip', odd)]
    ppermute x1, starting transfers between devices: 1.41 us -> 0.65 us  [per_device(): ecross1 = lax.ppermute(eother1, 'mem', cross)]
    ppermute x3, starting transfers between devices: 2.4 us -> 3.06 us  [the longest x1 2.51 us: per_device(): lax.ppermute(other1, 'mem', cross)]
    ppermute x1, waiting for transfers between devices: 1.51 us -> 2.13 us  [per_device(): ecross1 = lax.ppermute(eother1, 'mem', cross)]
    ppermute x1, starting transfers between devices: 0.63 us -> 0.07 us  [per_device(): far_partner = lax.ppermute(call_relay(far, o1)[0], 'mem', near)]
  transfers between devices with their start and end apart: 14 -> 14, of which waited for: 3 -> 3; matrix products, arithmetic and copies ran while one was open for 0% -> 0% of each run, Pallas kernels for 42% -> 40%
where the time goes in v8:
time: 45.2 us; the launch traced here: 45 us
  Pallas kernels  18.9 us (42%)
  starting transfers between devices  15.7 us (35%)
  waiting for transfers between devices  8.12 us (18%)
  local copies, waits for them, and re-layouts  2.16 us (5%)
    pallas_call x10, Pallas kernels, call(): pl.pallas_call(body, out_shape=out_shape, in_specs=[pl.BlockSpec(memory_s...  18.9 us
    ppermute x1, waiting for transfers between devices, per_device(): far_rim = lax.ppermute(rim, 'mem', cross)  4.73 us
    ppermute x1, starting transfers between devices, per_device(): o1 = lax.ppermute(o1, 'strip', odd)  4.36 us
    ppermute x1, starting transfers between devices, per_device(): o0 = lax.ppermute(o0, 'strip', odd)  3.18 us
    ppermute x1, starting transfers between devices, per_device(): lax.ppermute(other1, 'mem', cross)  2.51 us
    unnamed x2, local copies, waits for them, and re-layouts  2.16 us
    ppermute x1, waiting for transfers between devices, per_device(): ecross1 = lax.ppermute(eother1, 'mem', cross)  2.13 us
    ppermute x1, starting transfers between devices, per_device(): efar1 = lax.ppermute(eown1, 'mem', across)  1.3 us
  transfers between devices with their start and end apart: 14, of which 3 were waited for; matrix products, arithmetic and copies ran while one was open for 0% of the time, Pallas kernels for 40%

profile of v8, /device:TPU:3, one launch (start us, length us, event | category | flops | bytes accessed | tf_op | source)
XLA Modules:
  0.0 45.0 jit_solution(3759473934208675733)
XLA Ops:
  0.0 1.2 %collective-permute-start.1 = (f32[2,32,1024]{2,1,0:T(8,128)}, f32[2,32,1024]{2,1,0:T(8,128)S(1)}, u32[]{:S(2)}, u32[]{:S(2)}) collective-permute-start(f32[2,32,1024]{2,1,0:T(8,128)} %g_ref.1), channel_id=1, source_target_pairs={{0,16},{8,24},{16,0},{24,8},{1,17},{9,25},{17,1},{25,9},{2,18},{10... | collective-permute-start | bytes 786440 | tf_op jit(solution)/shard_map/ppermute | solution.py:381
  1.2 1.0 %collective-permute-start = (f32[2,32,1024]{2,1,0:T(8,128)}, f32[2,32,1024]{2,1,0:T(8,128)S(1)}, u32[]{:S(2)}, u32[]{:S(2)}) collective-permute-start(f32[2,32,1024]{2,1,0:T(8,128)} %g_ref.1), channel_id=1, source_target_pairs={{0,8},{8,0},{16,24},{24,16},{1,9},{9,1},{17,25},{25,17},{2,10},{10... | collective-permute-start | bytes 786440 | tf_op jit(solution)/shard_map/ppermute | solution.py:380
  2.2 0.0 copy-start
  2.2 1.2 %prepare.1 = (f32[2,32,1024]{2,1,0:T(8,128)S(1)}, f32[2,16,1024]{2,1,0:T(8,128)S(1)}, s32[32,1024]{1,0:T(8,128)S(1)}) custom-call(f32[2,32,1024]{2,1,0:T(8,128)} %g_ref.1, s32[32,1024]{1,0:T(8,128)} %counts_ref.1), custom_call_target="tpu_custom_call" | custom-call | flops 10000000000 | bytes 1024 | tf_op jit(solution)/shard_map/prepare/pallas_call | solution.py:32
  3.4 0.2 collective-permute-start.2
  3.6 0.0 collective-permute-done.refs_2_
  3.6 2.2 %copy-done = bf16[16,8,32,1024]{3,2,1,0:T(8,128)(2,1)S(1)} copy-done((bf16[16,8,32,1024]{3,2,1,0:T(8,128)(2,1)S(1)}, bf16[16,8,32,1024]{3,2,1,0:T(8,128)(2,1)}, u32[]{:S(2)}) %copy-start) | copy-done | bytes 8388632
  5.8 0.5 %project.2 = (f32[9,8,1024]{2,1,0:T(8,128)S(1)}, f32[9,8,1024]{2,1,0:T(8,128)S(1)}) custom-call(bf16[16,8,32,1024]{3,2,1,0:T(8,128)(2,1)S(1)} %copy-done, f32[2,32,1024]{2,1,0:T(8,128)S(1)} %get-tuple-element.26.refs_1_, f32[2,32,1024]{2,1,0:T(8,128)S(1)} %collective-permute-done.refs_2_, s32[32,1024]{1,0:T(8,128)S(1)} %get-tuple-element.28.refs_3_.refs_4_), custom_call_target="tpu_custom_call" | custom-call | flops 1024 | bytes 1024 | tf_op jit(solution)/shard_map/project/pallas_call | solution.py:32
  6.3 0.3 collective-permute-start.7
  6.6 4.7 %collective-permute-done.2.refs_2_ = f32[2,16,1024]{2,1,0:T(8,128)S(1)} collective-permute-done((f32[2,16,1024]{2,1,0:T(8,128)S(1)}, f32[2,16,1024]{2,1,0:T(8,128)S(1)}, u32[]{:S(2)}, u32[]{:S(2)}) %collective-permute-start.2) | collective-permute-done | bytes 131104 | tf_op jit(solution)/shard_map/ppermute | solution.py:382
  11.3 0.0 collective-permute-done.1.refs_1_.refs_0_
  11.3 0.5 %project.3 = (f32[8,8,1024]{2,1,0:T(8,128)S(1)}, f32[8,8,1024]{2,1,0:T(8,128)S(1)}) custom-call(bf16[16,8,32,1024]{3,2,1,0:T(8,128)(2,1)S(1)} %copy-done, f32[2,32,1024]{2,1,0:T(8,128)S(1)} %collective-permute-done.1.refs_1_.refs_0_, f32[2,16,1024]{2,1,0:T(8,128)S(1)} %collective-permute-done.2.refs_2_, f32[9,8,1024]{2,1,0:T(8,128)S(1)} %get-tuple-element.29.refs_3_), custom_call_target="tpu_custom_call" | custom-call | flops 1024 | bytes 1024 | tf_op jit(solution)/shard_map/project/pallas_call | solution.py:32
  11.9 0.1 collective-permute-start.3
  12.0 3.2 %collective-permute-start.8 = (f32[9,8,1024]{2,1,0:T(8,128)S(1)}, f32[9,8,1024]{2,1,0:T(8,128)S(1)}, u32[]{:S(2)}, u32[]{:S(2)}) collective-permute-start(f32[9,8,1024]{2,1,0:T(8,128)S(1)} %get-tuple-element.29.refs_3_), channel_id=1, source_target_pairs={{1,2},{3,4},{5,6},{2,1},{4,3},{6,5},{9,10},{11,12},{13,14},{10,9},... | collective-permute-start | bytes 884744 | tf_op jit(solution)/shard_map/ppermute | solution.py:391
  15.1 0.1 collective-permute-start.10
  15.2 4.4 %collective-permute-start.11 = (f32[8,8,1024]{2,1,0:T(8,128)S(1)}, f32[8,8,1024]{2,1,0:T(8,128)S(1)}, u32[]{:S(2)}, u32[]{:S(2)}) collective-permute-start(f32[8,8,1024]{2,1,0:T(8,128)S(1)} %get-tuple-element.30.refs_1_.refs_4_), channel_id=1, source_target_pairs={{1,2},{3,4},{5,6},{2,1},{4,3},{6,5},{9,10},{11,12},{13,14},{10,9},... | collective-permute-start | bytes 786440 | tf_op jit(solution)/shard_map/ppermute | solution.py:393
  19.6 0.0 collective-permute-done.3.refs_2_
  19.6 5.9 %interior.2 = (f32[2,24,1024]{2,1,0:T(8,128)S(1)}, f32[2,24,1024]{2,1,0:T(8,128)S(1)}, f32[16,32,1024]{2,1,0:T(8,128)S(1)}, f32[3,2,8,32,128]{4,3,2,1,0:T(8,128)S(1)}) custom-call(bf16[16,8,32,1024]{3,2,1,0:T(8,128)(2,1)S(1)} %copy-done, f32[2,32,1024]{2,1,0:T(8,128)S(1)} %collective-permute-done.1.refs_1_.refs_0_, ...), custom_call_target="tpu_custom_call" | custom-call | flops 1024 | bytes 1024 | tf_op jit(solution)/shard_map/interior/pallas_call | solution.py:32
  25.5 2.5 %collective-permute-start.6 = (f32[2,24,1024]{2,1,0:T(8,128)S(1)}, f32[2,24,1024]{2,1,0:T(8,128)S(1)}, u32[]{:S(2)}, u32[]{:S(2)}) collective-permute-start(f32[2,24,1024]{2,1,0:T(8,128)S(1)} %get-tuple-element.35), channel_id=1, source_target_pairs={{0,24},{8,16},{16,8},{24,0},{1,25},{9,17},{17,9},{25,1},{2,26},{10... | collective-permute-start | bytes 589832 | tf_op jit(solution)/shard_map/ppermute | solution.py:397
  28.0 0.0 collective-permute-done.7.refs_2_
  28.0 0.2 collective-permute-start.5
  28.3 5.8 %interior.3 = (f32[2,24,1024]{2,1,0:T(8,128)S(1)}, f32[2,24,1024]{2,1,0:T(8,128)S(1)}, f32[16,32,1024]{2,1,0:T(8,128)S(1)}) custom-call(bf16[16,8,32,1024]{3,2,1,0:T(8,128)(2,1)S(1)} %copy-done, f32[2,32,1024]{2,1,0:T(8,128)S(1)} %get-tuple-element.26.refs_1_, f32[2,32,1024]{2,1,0:T(8,128)S(1)} %collective-permute-done.refs_2_, ...), custom_call_target="tpu_custom_call" | custom-call | flops 1024 | bytes 1024 | tf_op jit(solution)/shard_map/interior/pallas_call | solution.py:32
  34.1 0.0 collective-permute-done.8.refs_3_
  34.1 0.3 collective-permute-start.4
  34.4 2.1 %edges.2 = (f32[2,8,1024]{2,1,0:T(8,128)S(1)}, f32[2,8,1024]{2,1,0:T(8,128)S(1)}, f32[4,2,8,8,128]{4,3,2,1,0:T(8,128)S(1)}) custom-call(bf16[16,8,32,1024]{3,2,1,0:T(8,128)(2,1)S(1)} %copy-done, f32[16,32,1024]{2,1,0:T(8,128)S(1)} %get-tuple-element.36.refs_1_, f32[9,8,1024]{2,1,0:T(8,128)S(1)} %collective-permute-done.7.refs_2_, ...), custom_call_target="tpu_custom_call" | custom-call | flops 1024 | bytes 1024 | tf_op jit(solution)/shard_map/edges/pallas_call | solution.py:32
  36.5 0.0 collective-permute-done.10.refs_2_
  36.5 0.3 collective-permute-start.9
  36.8 0.0 collective-permute-done.11.refs_3_
  36.9 2.0 %edges.3 = (f32[2,8,1024]{2,1,0:T(8,128)S(1)}, f32[2,8,1024]{2,1,0:T(8,128)S(1)}) custom-call(bf16[16,8,32,1024]{3,2,1,0:T(8,128)(2,1)S(1)} %copy-done, f32[16,32,1024]{2,1,0:T(8,128)S(1)} %get-tuple-element.40.refs_1_, f32[8,8,1024]{2,1,0:T(8,128)S(1)} %collective-permute-done.10.refs_2_, f32[8,8,1024]{2,1,0:T(8,128)S(1)} %collective-permute-done.11.refs_3_, ...), custom_call_target="tpu_custom_call" | custom-call | flops 1024 | bytes 1024 | tf_op jit(solution)/shard_map/edges/pallas_call | solution.py:32
  38.9 0.0 collective-permute-done.6
  38.9 0.0 collective-permute-done.5
  39.0 1.3 %collective-permute-start.12 = (f32[2,8,1024]{2,1,0:T(8,128)S(1)}, f32[2,8,1024]{2,1,0:T(8,128)S(1)}, u32[]{:S(2)}, u32[]{:S(2)}) collective-permute-start(f32[2,8,1024]{2,1,0:T(8,128)S(1)} %get-tuple-element.45), channel_id=1, source_target_pairs={{0,16},{8,24},{16,0},{24,8},{1,17},{9,25},{17,1},{25,9},{2,18},{10... | collective-permute-start | bytes 196616 | tf_op jit(solution)/shard_map/ppermute | solution.py:401
  40.3 0.6 %collective-permute-start.13 = (f32[2,8,1024]{2,1,0:T(8,128)S(1)}, f32[2,8,1024]{2,1,0:T(8,128)S(1)}, u32[]{:S(2)}, u32[]{:S(2)}) collective-permute-start(f32[2,8,1024]{2,1,0:T(8,128)S(1)} %get-tuple-element.46), channel_id=1, source_target_pairs={{0,24},{8,16},{16,8},{24,0},{1,25},{9,17},{17,9},{25,1},{2,26},{10... | collective-permute-start | bytes 196616 | tf_op jit(solution)/shard_map/ppermute | solution.py:402
  40.9 0.0 collective-permute-done.9.refs_4_
  40.9 0.0 collective-permute-done.4.refs_1_
  40.9 1.2 %collective-permute-done.12.refs_5_ = f32[2,8,1024]{2,1,0:T(8,128)S(1)} collective-permute-done((f32[2,8,1024]{2,1,0:T(8,128)S(1)}, f32[2,8,1024]{2,1,0:T(8,128)S(1)}, u32[]{:S(2)}, u32[]{:S(2)}) %collective-permute-start.12) | collective-permute-done | bytes 65568 | tf_op jit(solution)/shard_map/ppermute | solution.py:401
  42.2 2.1 %collective-permute-done.13.refs_6_ = f32[2,8,1024]{2,1,0:T(8,128)S(1)} collective-permute-done((f32[2,8,1024]{2,1,0:T(8,128)S(1)}, f32[2,8,1024]{2,1,0:T(8,128)S(1)}, u32[]{:S(2)}, u32[]{:S(2)}) %collective-permute-start.13) | collective-permute-done | bytes 65568 | tf_op jit(solution)/shard_map/ppermute | solution.py:402
  44.3 0.8 %finish.1 = f32[2,32,1024]{2,1,0:T(8,128)} custom-call(f32[2,24,1024]{2,1,0:T(8,128)S(1)} %get-tuple-element.33.refs_0_, f32[2,24,1024]{2,1,0:T(8,128)S(1)} %collective-permute-done.4.refs_1_, f32[2,24,1024]{2,1,0:T(8,128)S(1)} %add.3.refs_2_, f32[2,8,1024]{2,1,0:T(8,128)S(1)} %get-tuple-element.38.refs_5_.refs_3_, ...), custom_call_target="tpu_custom_call" | custom-call | flops 1024 | bytes 1024 | tf_op jit(solution)/shard_map/finish/pallas_call | solution.py:32
  (3 shorter events, 0.1 us)
Async XLA Ops:
  0.0 11.3 %collective-permute-start.1 = (f32[2,32,1024]{2,1,0:T(8,128)}, f32[2,32,1024]{2,1,0:T(8,128)S(1)}, u32[]{:S(2)}, u32[]{:S(2)}) collective-permute-start(f32[2,32,1024]{2,1,0:T(8,128)} %g_ref.1), channel_id=1, source_target_pairs={{0,16},{8,24},{16,0},{24,8},{1,17},{9,25},{17,1},{25,9},{2,18},{10... | collective-permute-start | bytes 786440 | tf_op jit(solution)/shard_map/ppermute | solution.py:381
  1.2 2.4 %collective-permute-start = (f32[2,32,1024]{2,1,0:T(8,128)}, f32[2,32,1024]{2,1,0:T(8,128)S(1)}, u32[]{:S(2)}, u32[]{:S(2)}) collective-permute-start(f32[2,32,1024]{2,1,0:T(8,128)} %g_ref.1), channel_id=1, source_target_pairs={{0,8},{8,0},{16,24},{24,16},{1,9},{9,1},{17,25},{25,17},{2,10},{10... | collective-permute-start | bytes 786440 | tf_op jit(solution)/shard_map/ppermute | solution.py:380
  2.2 3.6 %copy-start = (bf16[16,8,32,1024]{3,2,1,0:T(8,128)(2,1)S(1)}, bf16[16,8,32,1024]{3,2,1,0:T(8,128)(2,1)}, u32[]{:S(2)}) copy-start(bf16[16,8,32,1024]{3,2,1,0:T(8,128)(2,1)} %refs_0_.11) | copy-start | bytes 25165828
  3.4 7.9 %collective-permute-start.2 = (f32[2,16,1024]{2,1,0:T(8,128)S(1)}, f32[2,16,1024]{2,1,0:T(8,128)S(1)}, u32[]{:S(2)}, u32[]{:S(2)}) collective-permute-start(f32[2,16,1024]{2,1,0:T(8,128)S(1)} %get-tuple-element.27), channel_id=1, source_target_pairs={{0,24},{8,16},{16,8},{24,0},{1,25},{9,17},{17,9},{25,1},{2,26},{10... | collective-permute-start | bytes 393224 | tf_op jit(solution)/shard_map/ppermute | solution.py:382
  6.3 21.7 %collective-permute-start.7 = (f32[9,8,1024]{2,1,0:T(8,128)S(1)}, f32[9,8,1024]{2,1,0:T(8,128)S(1)}, u32[]{:S(2)}, u32[]{:S(2)}) collective-permute-start(f32[9,8,1024]{2,1,0:T(8,128)S(1)} %get-tuple-element.37), channel_id=1, source_target_pairs={{0,1},{1,0},{2,3},{3,2},{4,5},{5,4},{6,7},{7,6},{8,9},{9,8},{10,11... | collective-permute-start | bytes 884744 | tf_op jit(solution)/shard_map/ppermute | solution.py:390
  11.9 7.7 %collective-permute-start.3 = (f32[2,32,1024]{2,1,0:T(8,128)S(1)}, f32[2,32,1024]{2,1,0:T(8,128)S(1)}, u32[]{:S(2)}, u32[]{:S(2)}) collective-permute-start(f32[2,32,1024]{2,1,0:T(8,128)S(1)} %relay.2), channel_id=1, source_target_pairs={{0,8},{8,0},{16,24},{24,16},{1,9},{9,1},{17,25},{25,17},{2,10},{10... | collective-permute-start | bytes 786440 | tf_op jit(solution)/shard_map/ppermute | solution.py:387
  12.0 22.1 %collective-permute-start.8 = (f32[9,8,1024]{2,1,0:T(8,128)S(1)}, f32[9,8,1024]{2,1,0:T(8,128)S(1)}, u32[]{:S(2)}, u32[]{:S(2)}) collective-permute-start(f32[9,8,1024]{2,1,0:T(8,128)S(1)} %get-tuple-element.29.refs_3_), channel_id=1, source_target_pairs={{1,2},{3,4},{5,6},{2,1},{4,3},{6,5},{9,10},{11,12},{13,14},{10,9},... | collective-permute-start | bytes 884744 | tf_op jit(solution)/shard_map/ppermute | solution.py:391
  15.1 21.4 %collective-permute-start.10 = (f32[8,8,1024]{2,1,0:T(8,128)S(1)}, f32[8,8,1024]{2,1,0:T(8,128)S(1)}, u32[]{:S(2)}, u32[]{:S(2)}) collective-permute-start(f32[8,8,1024]{2,1,0:T(8,128)S(1)} %get-tuple-element.41), channel_id=1, source_target_pairs={{0,1},{1,0},{2,3},{3,2},{4,5},{5,4},{6,7},{7,6},{8,9},{9,8},{10,11... | collective-permute-start | bytes 786440 | tf_op jit(solution)/shard_map/ppermute | solution.py:392
  15.2 21.6 %collective-permute-start.11 = (f32[8,8,1024]{2,1,0:T(8,128)S(1)}, f32[8,8,1024]{2,1,0:T(8,128)S(1)}, u32[]{:S(2)}, u32[]{:S(2)}) collective-permute-start(f32[8,8,1024]{2,1,0:T(8,128)S(1)} %get-tuple-element.30.refs_1_.refs_4_), channel_id=1, source_target_pairs={{1,2},{3,4},{5,6},{2,1},{4,3},{6,5},{9,10},{11,12},{13,14},{10,9},... | collective-permute-start | bytes 786440 | tf_op jit(solution)/shard_map/ppermute | solution.py:393
  25.5 13.4 %collective-permute-start.6 = (f32[2,24,1024]{2,1,0:T(8,128)S(1)}, f32[2,24,1024]{2,1,0:T(8,128)S(1)}, u32[]{:S(2)}, u32[]{:S(2)}) collective-permute-start(f32[2,24,1024]{2,1,0:T(8,128)S(1)} %get-tuple-element.35), channel_id=1, source_target_pairs={{0,24},{8,16},{16,8},{24,0},{1,25},{9,17},{17,9},{25,1},{2,26},{10... | collective-permute-start | bytes 589832 | tf_op jit(solution)/shard_map/ppermute | solution.py:397
  28.0 10.9 %collective-permute-start.5 = (f32[2,24,1024]{2,1,0:T(8,128)S(1)}, f32[2,24,1024]{2,1,0:T(8,128)S(1)}, u32[]{:S(2)}, u32[]{:S(2)}) collective-permute-start(f32[2,24,1024]{2,1,0:T(8,128)S(1)} %get-tuple-element.32.refs_4_), channel_id=1, source_target_pairs={{0,16},{8,24},{16,0},{24,8},{1,17},{9,25},{17,1},{25,9},{2,18},{10... | collective-permute-start | bytes 589832 | tf_op jit(solution)/shard_map/ppermute | solution.py:397
  34.1 6.8 %collective-permute-start.4 = (f32[2,24,1024]{2,1,0:T(8,128)S(1)}, f32[2,24,1024]{2,1,0:T(8,128)S(1)}, u32[]{:S(2)}, u32[]{:S(2)}) collective-permute-start(f32[2,24,1024]{2,1,0:T(8,128)S(1)} %get-tuple-element.34), channel_id=1, source_target_pairs={{0,8},{8,0},{16,24},{24,16},{1,9},{9,1},{17,25},{25,17},{2,10},{10... | collective-permute-start | bytes 589832 | tf_op jit(solution)/shard_map/ppermute | solution.py:398
  36.5 4.4 %collective-permute-start.9 = (f32[2,8,1024]{2,1,0:T(8,128)S(1)}, f32[2,8,1024]{2,1,0:T(8,128)S(1)}, u32[]{:S(2)}, u32[]{:S(2)}) collective-permute-start(f32[2,8,1024]{2,1,0:T(8,128)S(1)} %get-tuple-element.39), channel_id=1, source_target_pairs={{0,8},{8,0},{16,24},{24,16},{1,9},{9,1},{17,25},{25,17},{2,10},{10... | collective-permute-start | bytes 196616 | tf_op jit(solution)/shard_map/ppermute | solution.py:399
  39.0 3.2 %collective-permute-start.12 = (f32[2,8,1024]{2,1,0:T(8,128)S(1)}, f32[2,8,1024]{2,1,0:T(8,128)S(1)}, u32[]{:S(2)}, u32[]{:S(2)}) collective-permute-start(f32[2,8,1024]{2,1,0:T(8,128)S(1)} %get-tuple-element.45), channel_id=1, source_target_pairs={{0,16},{8,24},{16,0},{24,8},{1,17},{9,25},{17,1},{25,9},{2,18},{10... | collective-permute-start | bytes 196616 | tf_op jit(solution)/shard_map/ppermute | solution.py:401
  40.3 4.0 %collective-permute-start.13 = (f32[2,8,1024]{2,1,0:T(8,128)S(1)}, f32[2,8,1024]{2,1,0:T(8,128)S(1)}, u32[]{:S(2)}, u32[]{:S(2)}) collective-permute-start(f32[2,8,1024]{2,1,0:T(8,128)S(1)} %get-tuple-element.46), channel_id=1, source_target_pairs={{0,24},{8,16},{16,8},{24,0},{1,25},{9,17},{17,9},{25,1},{2,26},{10... | collective-permute-start | bytes 196616 | tf_op jit(solution)/shard_map/ppermute | solution.py:402

commit v9 on v8

--- a/solution.py
+++ b/solution.py
@@ -1,3 +1,4 @@
+import functools
 import math
 
 import jax
@@ -95,14 +96,16 @@
 
 def project_edges(local, own, p_ref, *rest):
     if local:
-        *g_refs, counts_ref, e_ref, o_ref = rest
+        *g_refs, counts_ref, e_ref, o_ref, token_ref = rest
     else:
-        *g_refs, _, e_ref, o_ref = rest
+        *g_refs, _, e_ref, o_ref, token_ref = rest
     members, _, rows, ny = p_ref.shape
     even = lax.axis_index("strip") % 2 == 0
     half = top_half()
     fields = fields_of(local, own)
     grads = weights_of(own, g_refs)
+
+    token_ref[...] = jnp.zeros_like(token_ref)
 
     def put(row, j, top, bottom):
         e_ref[row, :, cols(j)] = jnp.where(even, bottom, top)
@@ -135,11 +138,15 @@
     pl.loop(0, members // 2)(pair)
 
 
-def interior(local, p_ref, *refs):
-    if not local:
+def interior(local, begin, stage, p_ref, *refs):
+    if stage == 0:
         *g_refs, counts_ref, _, own_ref, other_ref, kept_ref, coef, buf_a, buf_b, total_ref = refs
+    elif stage == 1:
+        *g_refs, coef, _, own_ref, other_ref, kept_ref, buf_a, buf_b, total_ref = refs
     else:
-        *g_refs, coef, _, own_ref, other_ref, kept_ref, buf_a, buf_b, total_ref = refs
+        g_refs, (coef, counts_ref, e_ref, o_ref), refs = refs[:2], refs[2:6], refs[6:]
+        own_so_far, other_so_far, _, own_ref, other_ref, kept_ref, edge_coef, buf_a, buf_b, total_ref, halo = refs
+        edge_weights(counts_ref, e_ref, o_ref, edge_coef, halo)
     members, _, rows, ny = p_ref.shape
     own = own_ref.shape[0]
     blocks = ny // LANES
@@ -152,7 +159,7 @@
     skip = TILE // 2
     whole = list(range(0, rows, TILE))
     kept = list(range(skip, rows - skip, TILE))
-    for t in range(1, 1 if local else SWEEPS):
+    for t in range(1, 1 if stage else SWEEPS):
         for j in range(blocks):
             total_ref[0, j] = (counts_ref[:, cols(j)] > t).astype(jnp.float32)
             for n, r in enumerate(kept if t == SWEEPS - 1 else whole):
@@ -168,7 +175,7 @@
     total_ref[...] = jnp.zeros_like(total_ref)
 
     def step(s, carry):
-        base = s * group
+        base = begin + s * group
         for r in range(0, rows, HALF):
             for j in range(blocks):
                 weights = [g_ref[k, r : r + HALF, cols(j)] for g_ref, k in grads]
@@ -184,7 +191,7 @@
                 for j in range(blocks):
                     low, high = TILE + t, rows - t
                     tile = jnp.where(half, src[i, j, low : low + TILE], src[i, j, high : high + TILE])
-                    kept_ref[base + i, t * TILE : (t + 1) * TILE, cols(j)] = tile
+                    kept_ref[s * group + i, t * TILE : (t + 1) * TILE, cols(j)] = tile
             for n, r in enumerate(kept if t == SWEEPS - 1 else whole):
                 at, to = TILE + r, TILE + n * TILE
                 for i in range(group):
@@ -210,62 +217,68 @@
                     total_ref[n, j, r : r + HALF] = total
         return carry
 
-    lax.fori_loop(0, members // group, step, 0)
+    lax.fori_loop(0, kept_ref.shape[0] // group, step, 0)
+    so_far = [(ref, k) for ref in (own_so_far, other_so_far) for k in range(own)] if stage == 2 else None
     for n, (ref, k) in enumerate(sums):
         for j in range(blocks):
             for r in range(0, rows - TILE, TILE):
-                ref[k, r : r + TILE, cols(j)] = total_ref[n, j, skip + r : skip + r + TILE]
-
-
-def edges(local, p_ref, kept_ref, e_ref, o_ref, *refs):
-    if local:
-        counts_ref, own_ref, other_ref, coef, win_a, win_b, halo = refs
-    else:
-        coef, _, own_ref, other_ref, win_a, win_b = refs
+                total = total_ref[n, j, skip + r : skip + r + TILE]
+                if so_far:
+                    total = total + so_far[n][0][k, r : r + TILE, cols(j)]
+                ref[k, r : r + TILE, cols(j)] = total
+
+
+def sent_tiles(e_ref, o_ref, q, j):
+    even = lax.axis_index("strip") % 2 == 0
+    e, o = e_ref[q, :, cols(j)], o_ref[q, :, cols(j)]
+    return jnp.where(even, o, e), jnp.where(even, e, o)
+
+
+def merged(ref, low, high):
+    return jnp.where(top_half(), ref[low : low + TILE], ref[high : high + TILE])
+
+
+def edge_weights(counts_ref, e_ref, o_ref, coef, halo):
+    rows, ny = counts_ref.shape
+    for j in range(ny // LANES):
+        above, below = sent_tiles(e_ref, o_ref, e_ref.shape[0] - 1, j)
+        halo[j, 4:12] = above
+        halo[j, 24:32] = below
+        halo[j, 8:16] = counts_ref[0:TILE, cols(j)].astype(jnp.float32)
+        halo[j, 16:24] = counts_ref[rows - TILE : rows, cols(j)].astype(jnp.float32)
+        for t in range(SWEEPS):
+            active = (merged(halo.at[j], 5 + t, 19 - t) > t).astype(jnp.float32)
+            coef[t, 0, j] = active * COEFF_X
+            coef[t, 1, j] = 1.0 - active * (1.0 - CENTRE)
+
+
+def edges(local, p_ref, *refs):
+    *kept_refs, e_ref, o_ref, coef, _, own_ref, other_ref, win_a, win_b = refs
     members, _, rows, ny = p_ref.shape
     own = own_ref.shape[0]
     blocks = ny // LANES
     first, last = lane_masks()
     half = top_half()
-    even = lax.axis_index("strip") % 2 == 0
     fields = fields_of(local, own)
     sums = [(own_ref, k) for k in range(own)] + [(other_ref, k) for k in range(own)]
     start = TILE
 
-    def sent(q, j):
-        e, o = e_ref[q, :, cols(j)], o_ref[q, :, cols(j)]
-        return jnp.where(even, o, e), jnp.where(even, e, o)
-
-    def merged(ref, low, high):
-        return jnp.where(half, ref[low : low + TILE], ref[high : high + TILE])
-
-    if local:
-        for j in range(blocks):
-            above, below = sent(members // 2, j)
-            halo[j, 4:12] = above
-            halo[j, 24:32] = below
-            halo[j, 8:16] = counts_ref[0:TILE, cols(j)].astype(jnp.float32)
-            halo[j, 16:24] = counts_ref[rows - TILE : rows, cols(j)].astype(jnp.float32)
-            for t in range(SWEEPS):
-                active = (merged(halo.at[j], 5 + t, 19 - t) > t).astype(jnp.float32)
-                coef[t, 0, j] = active * COEFF_X
-                coef[t, 1, j] = 1.0 - active * (1.0 - CENTRE)
     own_ref[...] = jnp.zeros_like(own_ref)
     other_ref[...] = jnp.zeros_like(other_ref)
 
     group = win_a.shape[0]
 
-    def step(s, carry):
-        base = s * group
+    def step(begin, kept_ref, s, carry):
+        base = begin + s * group
         for j in range(blocks):
             for i in range(0, group, 2):
-                above, below = sent(s * (group // 2) + i // 2, j)
+                above, below = sent_tiles(e_ref, o_ref, base // 2 + i // 2, j)
                 win_a[i, j, start : start + TILE] = above
                 win_a[i, j, start + 12 : start + 20] = below
                 win_a[i + 1, j, start - 4 : start + 4] = above
                 win_a[i + 1, j, start + 8 : start + 16] = below
             for i in range(group):
-                win_a[i, j, start + 4 : start + 12] = kept_ref[base + i, 0:TILE, cols(j)]
+                win_a[i, j, start + 4 : start + 12] = kept_ref[s * group + i, 0:TILE, cols(j)]
         src, dst = win_a, win_b
         smooth = [[] for i in range(group)]
         for t in range(SWEEPS):
@@ -281,7 +294,7 @@
                     else:
                         dst[i, j, start : start + TILE] = new
                         dst[i, j, start + 8 : start + 16] = new
-                        dst[i, j, start + 4 : start + 12] = kept_ref[base + i, (t + 1) * TILE : (t + 2) * TILE, cols(j)]
+                        dst[i, j, start + 4 : start + 12] = kept_ref[s * group + i, (t + 1) * TILE : (t + 2) * TILE, cols(j)]
             src, dst = dst, src
         for j in range(blocks):
             for f, (ref, k) in zip(fields, sums):
@@ -293,7 +306,10 @@
                 ref[k, :, cols(j)] = total
         return carry
 
-    lax.fori_loop(0, members // group, step, 0)
+    begin = 0
+    for kept_ref in kept_refs:
+        lax.fori_loop(0, kept_ref.shape[0] // group, functools.partial(step, begin, kept_ref), 0)
+        begin += kept_ref.shape[0]
 
 
 def relay(*refs):
@@ -302,8 +318,8 @@
         out_ref[...] = ref[...]
 
 
-def finish(scale, *refs):
-    own_ref, near_ref, inner_ref, *edge_refs, out_ref = refs
+def gather_up(own_ref, near_ref, inner_ref, *refs):
+    *edge_refs, out_ref = refs
     own, rows, ny = out_ref.shape
     half = top_half()
     for k in range(own):
@@ -315,7 +331,21 @@
                 parts.append(pltpu.roll(inner, TILE // 2, 0))
             parts.append(edge)
             for n in range(rows // TILE):
-                out_ref[k, n * TILE : (n + 1) * TILE, cols(j)] = jnp.where(half, parts[n], parts[n + 1]) * scale
+                out_ref[k, n * TILE : (n + 1) * TILE, cols(j)] = jnp.where(half, parts[n], parts[n + 1])
+
+
+def finish(scale, sum_ref, edge_ref, out_ref):
+    own, rows, ny = out_ref.shape
+    half = top_half()
+    for k in range(own):
+        for j in range(ny // LANES):
+            edge = edge_ref[k, :, cols(j)]
+            none = jnp.zeros_like(edge)
+            out_ref[k, 0:TILE, cols(j)] = (sum_ref[k, 0:TILE, cols(j)] + jnp.where(half, edge, none)) * scale
+            middle = pl.ds(TILE, rows - 2 * TILE)
+            out_ref[k, middle, cols(j)] = sum_ref[k, middle, cols(j)] * scale
+            end = pl.ds(rows - TILE, TILE)
+            out_ref[k, end, cols(j)] = (sum_ref[k, end, cols(j)] + jnp.where(half, none, edge)) * scale
 
 
 def per_device(gradient, perturbations, counts):
@@ -349,7 +379,7 @@
 
     def call_project(local, *args):
         pairs = members // 2 + (1 if local else 0)
-        outs = (shape(pairs, TILE, ny), shape(pairs, TILE, ny))
+        outs = (shape(pairs, TILE, ny), shape(pairs, TILE, ny), shape(TILE, LANES))
         outside = {} if local else {len(args) - 1: pl.ANY}
         body = lambda *refs: project_edges(local, own, *refs)
         return kernel_call(body, outs, [], 1024, "project", outside=outside)(*args)
@@ -358,23 +388,20 @@
         outs = tuple(shape(*x.shape) for x in args[:-1])
         return kernel_call(relay, outs, [], 1024, "relay", outside={len(outs): pl.ANY})(*args)
 
-    def call_interior(local, *args):
+    def call_interior(local, begin, count, stage, *args):
         total = pltpu.VMEM((VARS, blocks, rows, LANES), f32)
         buf = pltpu.VMEM((INNER_GROUP, blocks, rows + 2 * TILE, LANES), f32)
-        outs = (shape(own, rows - TILE, ny), shape(own, rows - TILE, ny), shape(members, SWEEPS * TILE, ny))
-        if not local:
-            outs = outs + (shape(SWEEPS - 1, 2, blocks, rows, LANES),)
-        body = lambda *refs: interior(local, *refs)
-        return kernel_call(body, outs, [buf, buf, total], 1024, "interior", outside={len(args) - 1: pl.ANY})(*args)
+        outs = (shape(own, rows - TILE, ny), shape(own, rows - TILE, ny), shape(count, SWEEPS * TILE, ny))
+        outs += ((shape(SWEEPS - 1, 2, blocks, rows, LANES),), (), (shape(SWEEPS, 2, blocks, TILE, LANES),))[stage]
+        scratch = [buf, buf, total] + ([window()] if stage == 2 else [])
+        body = lambda *refs: interior(local, begin, stage, *refs)
+        return kernel_call(body, outs, scratch, 1024, "interior", outside={len(args) - 1: pl.ANY})(*args)
 
     def call_edges(local, *args):
         outs = (shape(own, TILE, ny), shape(own, TILE, ny))
+        body = lambda *refs: edges(local, *refs)
         scratch = [window(EDGE_GROUP), window(EDGE_GROUP)]
-        if local:
-            outs, scratch = outs + (shape(SWEEPS, 2, blocks, TILE, LANES),), scratch + [window()]
-        body = lambda *refs: edges(local, *refs)
-        outside = {} if local else {len(args) - 1: pl.ANY}
-        return kernel_call(body, outs, scratch, 1024, "edges", outside=outside)(*args)
+        return kernel_call(body, outs, scratch, 1024, "edges", outside={len(args) - 1: pl.ANY})(*args)
 
     near_g, rim, near_counts = call_prepare(gradient, counts)
     partner = lax.ppermute(gradient, "mem", near)
@@ -382,27 +409,34 @@
     far_rim = lax.ppermute(rim, "mem", cross)
 
     p = perturbations
-    e0, o0 = call_project(True, p, near_g, partner, near_counts)
-    e1, o1 = call_project(False, p, far, far_rim, o0)
-    far_partner = lax.ppermute(call_relay(far, o1)[0], "mem", near)
-    own1, other1, kept1, inner_coef = call_interior(False, p, far, far_partner, near_counts, o1)
-    own0, other0, kept0 = call_interior(True, p, near_g, partner, inner_coef, own1)
+    part = members // 2
+    e0, o0, token0 = call_project(True, p, near_g, partner, near_counts)
+    own0, other0, kept0, inner_coef = call_interior(True, 0, part, 0, p, near_g, partner, near_counts, token0)
     e0 = lax.ppermute(e0, "strip", even)
     o0 = lax.ppermute(o0, "strip", odd)
+    e1, o1, token1 = call_project(False, p, far, far_rim, own0)
+    far_partner = lax.ppermute(call_relay(far, token1)[0], "mem", near)
+    own1, other1, kept1 = call_interior(False, 0, members, 1, p, far, far_partner, inner_coef, token1)
     e1 = lax.ppermute(e1, "strip", even)
     o1 = lax.ppermute(o1, "strip", odd)
-    eown0, eother0, edge_coef = call_edges(True, p, kept0, e0, o0, near_counts)
-    eown1, eother1 = call_edges(False, p, kept1, e1, o1, edge_coef, eown0)
+    own0, other0, kept2, edge_coef = call_interior(
+        True, part, part, 2, p, near_g, partner, inner_coef, near_counts, e0, o0, own0, other0, own1
+    )
+    eown1, eother1 = call_edges(False, p, kept1, e1, o1, edge_coef, own0)
+    eown0, eother0 = call_edges(True, p, kept0, kept2, e0, o0, edge_coef, eown1)
 
     inner = lax.ppermute(own1, "mem", across) + lax.ppermute(other1, "mem", cross)
     near0 = lax.ppermute(other0, "mem", near)
-    enear0 = lax.ppermute(eother0, "mem", near)
     eown1, eother1 = call_relay(eown1, eother1, inner)
     efar1 = lax.ppermute(eown1, "mem", across)
     ecross1 = lax.ppermute(eother1, "mem", cross)
+    enear0 = lax.ppermute(eother0, "mem", near)
+    total = kernel_call(gather_up, shape(own, rows, ny), [], PREPARE_FLOPS, "gather_up")(
+        own0, near0, inner, eown0, efar1, ecross1
+    )
     return kernel_call(
         lambda *refs: finish(scale, *refs), shape(own, rows, ny), [], 1024, "finish"
-    )(own0, near0, inner, eown0, enear0, efar1, ecross1)
+    )(total, enear0)
 
 
 def solution(mesh):

time: 45.2 us -> 44.8 us (level)
  local copies, waits for them, and re-layouts: 2.16 us -> 0.01 us
  Pallas kernels: 18.9 us -> 20.2 us
  waiting for transfers between devices: 8.12 us -> 8.68 us
    ppermute x1, waiting for transfers between devices: 0.01 us -> 2.69 us  [per_device(): e1 = lax.ppermute(e1, 'strip', even)]
    unnamed x2, local copies, waits for them, and re-layouts: 2.16 us -> 0.01 us
    pallas_call x10 -> x12, Pallas kernels: 18.9 us -> 20.2 us  [call(): pl.pallas_call(body, out_shape=out_shape, in_specs=[pl.BlockSpec(memory_s...]
    ppermute x1, waiting for transfers between devices: 1.23 us -> 0.01 us  [per_device(): efar1 = lax.ppermute(eown1, 'mem', across)]
    ppermute x1, waiting for transfers between devices: 2.13 us -> 0.95 us  [per_device(): ecross1 = lax.ppermute(eother1, 'mem', cross)]
    ppermute x1, waiting for transfers between devices: 0.01 us -> 1.16 us  [per_device(): lax.ppermute(own1, 'mem', across) + lax.ppermute(other1, 'mem', cross)]
    ppermute x1, waiting for transfers between devices: 4.73 us -> 3.63 us  [per_device(): far_rim = lax.ppermute(rim, 'mem', cross)]
    ppermute x1, starting transfers between devices: 0.65 us -> 1.72 us  [per_device(): ecross1 = lax.ppermute(eother1, 'mem', cross)]
  transfers between devices with their start and end apart: 14 -> 14, of which waited for: 3 -> 5; matrix products, arithmetic and copies ran while one was open for 0% -> 0% of each run, Pallas kernels for 40% -> 44%
where the time goes in v9:
time: 44.8 us; the launch traced here: 44.7 us
  Pallas kernels  20.2 us (45%)
  starting transfers between devices  15.6 us (35%)
  waiting for transfers between devices  8.68 us (19%)
    pallas_call x12, Pallas kernels, call(): pl.pallas_call(body, out_shape=out_shape, in_specs=[pl.BlockSpec(memory_s...  20.2 us
    ppermute x1, starting transfers between devices, per_device(): o1 = lax.ppermute(o1, 'strip', odd)  4.36 us
    ppermute x1, waiting for transfers between devices, per_device(): far_rim = lax.ppermute(rim, 'mem', cross)  3.63 us
    ppermute x1, starting transfers between devices, per_device(): o0 = lax.ppermute(o0, 'strip', odd)  3.18 us
    ppermute x1, waiting for transfers between devices, per_device(): e1 = lax.ppermute(e1, 'strip', even)  2.69 us
    ppermute x1, starting transfers between devices, per_device(): lax.ppermute(other1, 'mem', cross)  2.51 us
    ppermute x1, starting transfers between devices, per_device(): ecross1 = lax.ppermute(eother1, 'mem', cross)  1.72 us
    ppermute x1, starting transfers between devices, per_device(): far = lax.ppermute(gradient, 'mem', across)  1.24 us
  transfers between devices with their start and end apart: 14, of which 5 were waited for; matrix products, arithmetic and copies ran while one was open for 0% of the time, Pallas kernels for 44%

profile of v9, /device:TPU:3, one launch (start us, length us, event | category | flops | bytes accessed | tf_op | source)
XLA Modules:
  0.0 44.7 jit_solution(1573414368442755822)
XLA Ops:
  0.0 0.0 copy-start
  0.0 1.2 %collective-permute-start.3 = (f32[2,32,1024]{2,1,0:T(8,128)}, f32[2,32,1024]{2,1,0:T(8,128)S(1)}, u32[]{:S(2)}, u32[]{:S(2)}) collective-permute-start(f32[2,32,1024]{2,1,0:T(8,128)} %g_ref.1), channel_id=1, source_target_pairs={{0,16},{8,24},{16,0},{24,8},{1,17},{9,25},{17,1},{25,9},{2,18},{10... | collective-permute-start | bytes 786440 | tf_op jit(solution)/shard_map/ppermute | solution.py:408
  1.2 1.0 %collective-permute-start = (f32[2,32,1024]{2,1,0:T(8,128)}, f32[2,32,1024]{2,1,0:T(8,128)S(1)}, u32[]{:S(2)}, u32[]{:S(2)}) collective-permute-start(f32[2,32,1024]{2,1,0:T(8,128)} %g_ref.1), channel_id=1, source_target_pairs={{0,8},{8,0},{16,24},{24,16},{1,9},{9,1},{17,25},{25,17},{2,10},{10... | collective-permute-start | bytes 786440 | tf_op jit(solution)/shard_map/ppermute | solution.py:407
  2.2 1.3 %prepare.1 = (f32[2,32,1024]{2,1,0:T(8,128)S(1)}, f32[2,16,1024]{2,1,0:T(8,128)S(1)}, s32[32,1024]{1,0:T(8,128)S(1)}) custom-call(f32[2,32,1024]{2,1,0:T(8,128)} %g_ref.1, s32[32,1024]{1,0:T(8,128)} %counts_ref.1), custom_call_target="tpu_custom_call" | custom-call | flops 10000000000 | bytes 1024 | tf_op jit(solution)/shard_map/prepare/pallas_call | solution.py:33
  3.5 0.2 collective-permute-start.4
  3.7 0.0 collective-permute-done.refs_2_
  3.7 0.0 copy-done
  3.7 0.6 %project.2 = (f32[9,8,1024]{2,1,0:T(8,128)S(1)}, f32[9,8,1024]{2,1,0:T(8,128)S(1)}, f32[8,128]{1,0:T(8,128)S(1)}) custom-call(bf16[16,8,32,1024]{3,2,1,0:T(8,128)(2,1)S(1)} %copy-done, f32[2,32,1024]{2,1,0:T(8,128)S(1)} %get-tuple-element.31.refs_1_, f32[2,32,1024]{2,1,0:T(8,128)S(1)} %collective-permute-done.refs_2_, ...), custom_call_target="tpu_custom_call" | custom-call | flops 1024 | bytes 1024 | tf_op jit(solution)/shard_map/project/pallas_call | solution.py:33
  4.2 0.2 collective-permute-start.1
  4.4 3.3 %interior.3 = (f32[2,24,1024]{2,1,0:T(8,128)S(1)}, f32[2,24,1024]{2,1,0:T(8,128)S(1)}, f32[8,32,1024]{2,1,0:T(8,128)S(1)}, f32[3,2,8,32,128]{4,3,2,1,0:T(8,128)S(1)}) custom-call(bf16[16,8,32,1024]{3,2,1,0:T(8,128)(2,1)S(1)} %copy-done, f32[2,32,1024]{2,1,0:T(8,128)S(1)} %get-tuple-element.31.refs_1_, f32[2,32,1024]{2,1,0:T(8,128)S(1)} %collective-permute-done.refs_2_, ...), custom_call_target="tpu_custom_call" | custom-call | flops 1024 | bytes 1024 | tf_op jit(solution)/shard_map/interior/pallas_call | solution.py:33
  7.7 3.6 %collective-permute-done.4.refs_2_ = f32[2,16,1024]{2,1,0:T(8,128)S(1)} collective-permute-done((f32[2,16,1024]{2,1,0:T(8,128)S(1)}, f32[2,16,1024]{2,1,0:T(8,128)S(1)}, u32[]{:S(2)}, u32[]{:S(2)}) %collective-permute-start.4) | collective-permute-done | bytes 131104 | tf_op jit(solution)/shard_map/ppermute | solution.py:409
  11.3 0.0 collective-permute-done.3.refs_1_.refs_0_
  11.4 0.5 %project.3 = (f32[8,8,1024]{2,1,0:T(8,128)S(1)}, f32[8,8,1024]{2,1,0:T(8,128)S(1)}, f32[8,128]{1,0:T(8,128)S(1)}) custom-call(bf16[16,8,32,1024]{3,2,1,0:T(8,128)(2,1)S(1)} %copy-done, f32[2,32,1024]{2,1,0:T(8,128)S(1)} %collective-permute-done.3.refs_1_.refs_0_, f32[2,16,1024]{2,1,0:T(8,128)S(1)} %collective-permute-done.4.refs_2_, ...), custom_call_target="tpu_custom_call" | custom-call | flops 1024 | bytes 1024 | tf_op jit(solution)/shard_map/project/pallas_call | solution.py:33
  11.9 0.1 collective-permute-start.5
  12.0 3.2 %collective-permute-start.2 = (f32[9,8,1024]{2,1,0:T(8,128)S(1)}, f32[9,8,1024]{2,1,0:T(8,128)S(1)}, u32[]{:S(2)}, u32[]{:S(2)}) collective-permute-start(f32[9,8,1024]{2,1,0:T(8,128)S(1)} %get-tuple-element.36), channel_id=1, source_target_pairs={{1,2},{3,4},{5,6},{2,1},{4,3},{6,5},{9,10},{11,12},{13,14},{10,9},... | collective-permute-start | bytes 884744 | tf_op jit(solution)/shard_map/ppermute | solution.py:416
  15.2 0.1 collective-permute-start.9
  15.3 4.4 %collective-permute-start.10 = (f32[8,8,1024]{2,1,0:T(8,128)S(1)}, f32[8,8,1024]{2,1,0:T(8,128)S(1)}, u32[]{:S(2)}, u32[]{:S(2)}) collective-permute-start(f32[8,8,1024]{2,1,0:T(8,128)S(1)} %get-tuple-element.50), channel_id=1, source_target_pairs={{1,2},{3,4},{5,6},{2,1},{4,3},{6,5},{9,10},{11,12},{13,14},{10,9},... | collective-permute-start | bytes 786440 | tf_op jit(solution)/shard_map/ppermute | solution.py:421
  19.6 0.0 collective-permute-done.5.refs_2_
  19.6 6.3 %interior.4 = (f32[2,24,1024]{2,1,0:T(8,128)S(1)}, f32[2,24,1024]{2,1,0:T(8,128)S(1)}, f32[16,32,1024]{2,1,0:T(8,128)S(1)}) custom-call(bf16[16,8,32,1024]{3,2,1,0:T(8,128)(2,1)S(1)} %copy-done, f32[2,32,1024]{2,1,0:T(8,128)S(1)} %collective-permute-done.3.refs_1_.refs_0_, f32[2,32,1024]{2,1,0:T(8,128)S(1)} %collective-permute-done.5.refs_2_, ...), custom_call_target="tpu_custom_call" | custom-call | flops 1024 | bytes 1024 | tf_op jit(solution)/shard_map/interior/pallas_call | solution.py:33
  25.9 2.5 %collective-permute-start.8 = (f32[2,24,1024]{2,1,0:T(8,128)S(1)}, f32[2,24,1024]{2,1,0:T(8,128)S(1)}, u32[]{:S(2)}, u32[]{:S(2)}) collective-permute-start(f32[2,24,1024]{2,1,0:T(8,128)S(1)} %get-tuple-element.44), channel_id=1, source_target_pairs={{0,24},{8,16},{16,8},{24,0},{1,25},{9,17},{17,9},{25,1},{2,26},{10... | collective-permute-start | bytes 589832 | tf_op jit(solution)/shard_map/ppermute | solution.py:428
  28.5 0.0 collective-permute-done.1.refs_5_.refs_3_
  28.5 0.2 collective-permute-start.7
  28.7 0.0 collective-permute-done.2.refs_6_.refs_4_
  28.7 3.2 %interior.5 = (f32[2,24,1024]{2,1,0:T(8,128)S(1)}, f32[2,24,1024]{2,1,0:T(8,128)S(1)}, f32[8,32,1024]{2,1,0:T(8,128)S(1)}, f32[4,2,8,8,128]{4,3,2,1,0:T(8,128)S(1)}) custom-call(bf16[16,8,32,1024]{3,2,1,0:T(8,128)(2,1)S(1)} %copy-done, f32[2,32,1024]{2,1,0:T(8,128)S(1)} %get-tuple-element.31.refs_1_, f32[2,32,1024]{2,1,0:T(8,128)S(1)} %collective-permute-done.refs_2_, ...), custom_call_target="tpu_custom_call" | custom-call | flops 1024 | bytes 1024 | tf_op jit(solution)/shard_map/interior/pallas_call | solution.py:33
  31.9 0.3 collective-permute-start.6
  32.3 2.7 %collective-permute-done.9.refs_2_ = f32[8,8,1024]{2,1,0:T(8,128)S(1)} collective-permute-done((f32[8,8,1024]{2,1,0:T(8,128)S(1)}, f32[8,8,1024]{2,1,0:T(8,128)S(1)}, u32[]{:S(2)}, u32[]{:S(2)}) %collective-permute-start.9) | collective-permute-done | bytes 262176 | tf_op jit(solution)/shard_map/ppermute | solution.py:420
  34.9 0.0 collective-permute-done.10.refs_3_
  35.0 2.2 %edges.2 = (f32[2,8,1024]{2,1,0:T(8,128)S(1)}, f32[2,8,1024]{2,1,0:T(8,128)S(1)}) custom-call(bf16[16,8,32,1024]{3,2,1,0:T(8,128)(2,1)S(1)} %copy-done, f32[16,32,1024]{2,1,0:T(8,128)S(1)} %get-tuple-element.48.refs_1_, f32[8,8,1024]{2,1,0:T(8,128)S(1)} %collective-permute-done.9.refs_2_, f32[8,8,1024]{2,1,0:T(8,128)S(1)} %collective-permute-done.10.refs_3_, ...), custom_call_target="tpu_custom_call" | custom-call | flops 1024 | bytes 1024 | tf_op jit(solution)/shard_map/edges/pallas_call | solution.py:33
  37.1 0.0 collective-permute-done.8
  37.1 1.2 %collective-permute-done.7 = f32[2,24,1024]{2,1,0:T(8,128)S(1)} collective-permute-done((f32[2,24,1024]{2,1,0:T(8,128)S(1)}, f32[2,24,1024]{2,1,0:T(8,128)S(1)}, u32[]{:S(2)}, u32[]{:S(2)}) %collective-permute-start.7) | collective-permute-done | bytes 196640 | tf_op jit(solution)/shard_map/ppermute | solution.py:428
  38.3 0.5 %collective-permute-start.11 = (f32[2,8,1024]{2,1,0:T(8,128)S(1)}, f32[2,8,1024]{2,1,0:T(8,128)S(1)}, u32[]{:S(2)}, u32[]{:S(2)}) collective-permute-start(f32[2,8,1024]{2,1,0:T(8,128)S(1)} %get-tuple-element.54), channel_id=1, source_target_pairs={{0,16},{8,24},{16,0},{24,8},{1,17},{9,25},{17,1},{25,9},{2,18},{10... | collective-permute-start | bytes 196616 | tf_op jit(solution)/shard_map/ppermute | solution.py:431
  38.8 1.7 %collective-permute-start.12 = (f32[2,8,1024]{2,1,0:T(8,128)S(1)}, f32[2,8,1024]{2,1,0:T(8,128)S(1)}, u32[]{:S(2)}, u32[]{:S(2)}) collective-permute-start(f32[2,8,1024]{2,1,0:T(8,128)S(1)} %get-tuple-element.55), channel_id=1, source_target_pairs={{0,24},{8,16},{16,8},{24,0},{1,25},{9,17},{17,9},{25,1},{2,26},{10... | collective-permute-start | bytes 196616 | tf_op jit(solution)/shard_map/ppermute | solution.py:432
  40.5 2.1 %edges.3 = (f32[2,8,1024]{2,1,0:T(8,128)S(1)}, f32[2,8,1024]{2,1,0:T(8,128)S(1)}) custom-call(bf16[16,8,32,1024]{3,2,1,0:T(8,128)(2,1)S(1)} %copy-done, f32[8,32,1024]{2,1,0:T(8,128)S(1)} %get-tuple-element.45.refs_1_, f32[8,32,1024]{2,1,0:T(8,128)S(1)} %get-tuple-element.46.refs_2_, f32[9,8,1024]{2,1,0:T(8,128)S(1)} %collective-permute-done.1.refs_5_.refs_3_, ...), custom_call_target="tpu_custom_call" | custom-call | flops 1024 | bytes 1024 | tf_op jit(solution)/shard_map/edges/pallas_call | solution.py:33
  42.6 0.1 collective-permute-start.13
  42.7 0.0 collective-permute-done.6.near_ref
  42.7 0.0 collective-permute-done.11.refs_1_
  42.7 0.9 %collective-permute-done.12.refs_2_ = f32[2,8,1024]{2,1,0:T(8,128)S(1)} collective-permute-done((f32[2,8,1024]{2,1,0:T(8,128)S(1)}, f32[2,8,1024]{2,1,0:T(8,128)S(1)}, u32[]{:S(2)}, u32[]{:S(2)}) %collective-permute-start.12) | collective-permute-done | bytes 65568 | tf_op jit(solution)/shard_map/ppermute | solution.py:432
  43.7 0.2 collective-permute-done.13.refs_1_
  43.9 0.7 %finish.1 = f32[2,32,1024]{2,1,0:T(8,128)} custom-call(f32[2,32,1024]{2,1,0:T(8,128)S(1)} %gather_up.1.refs_0_, f32[2,8,1024]{2,1,0:T(8,128)S(1)} %collective-permute-done.13.refs_1_), custom_call_target="tpu_custom_call" | custom-call | flops 1024 | bytes 1024 | tf_op jit(solution)/shard_map/finish/pallas_call | solution.py:33
  (4 shorter events, 0.1 us)
Async XLA Ops:
  0.0 3.7 %copy-start = (bf16[16,8,32,1024]{3,2,1,0:T(8,128)(2,1)S(1)}, bf16[16,8,32,1024]{3,2,1,0:T(8,128)(2,1)}, u32[]{:S(2)}) copy-start(bf16[16,8,32,1024]{3,2,1,0:T(8,128)(2,1)} %refs_0_.13) | copy-start | bytes 25165828
  0.0 11.3 %collective-permute-start.3 = (f32[2,32,1024]{2,1,0:T(8,128)}, f32[2,32,1024]{2,1,0:T(8,128)S(1)}, u32[]{:S(2)}, u32[]{:S(2)}) collective-permute-start(f32[2,32,1024]{2,1,0:T(8,128)} %g_ref.1), channel_id=1, source_target_pairs={{0,16},{8,24},{16,0},{24,8},{1,17},{9,25},{17,1},{25,9},{2,18},{10... | collective-permute-start | bytes 786440 | tf_op jit(solution)/shard_map/ppermute | solution.py:408
  1.2 2.4 %collective-permute-start = (f32[2,32,1024]{2,1,0:T(8,128)}, f32[2,32,1024]{2,1,0:T(8,128)S(1)}, u32[]{:S(2)}, u32[]{:S(2)}) collective-permute-start(f32[2,32,1024]{2,1,0:T(8,128)} %g_ref.1), channel_id=1, source_target_pairs={{0,8},{8,0},{16,24},{24,16},{1,9},{9,1},{17,25},{25,17},{2,10},{10... | collective-permute-start | bytes 786440 | tf_op jit(solution)/shard_map/ppermute | solution.py:407
  3.5 7.9 %collective-permute-start.4 = (f32[2,16,1024]{2,1,0:T(8,128)S(1)}, f32[2,16,1024]{2,1,0:T(8,128)S(1)}, u32[]{:S(2)}, u32[]{:S(2)}) collective-permute-start(f32[2,16,1024]{2,1,0:T(8,128)S(1)} %get-tuple-element.39), channel_id=1, source_target_pairs={{0,24},{8,16},{16,8},{24,0},{1,25},{9,17},{17,9},{25,1},{2,26},{10... | collective-permute-start | bytes 393224 | tf_op jit(solution)/shard_map/ppermute | solution.py:409
  4.2 24.2 %collective-permute-start.1 = (f32[9,8,1024]{2,1,0:T(8,128)S(1)}, f32[9,8,1024]{2,1,0:T(8,128)S(1)}, u32[]{:S(2)}, u32[]{:S(2)}) collective-permute-start(f32[9,8,1024]{2,1,0:T(8,128)S(1)} %get-tuple-element.35), channel_id=1, source_target_pairs={{0,1},{1,0},{2,3},{3,2},{4,5},{5,4},{6,7},{7,6},{8,9},{9,8},{10,11... | collective-permute-start | bytes 884744 | tf_op jit(solution)/shard_map/ppermute | solution.py:415
  11.9 7.7 %collective-permute-start.5 = (f32[2,32,1024]{2,1,0:T(8,128)S(1)}, f32[2,32,1024]{2,1,0:T(8,128)S(1)}, u32[]{:S(2)}, u32[]{:S(2)}) collective-permute-start(f32[2,32,1024]{2,1,0:T(8,128)S(1)} %relay.2), channel_id=1, source_target_pairs={{0,8},{8,0},{16,24},{24,16},{1,9},{9,1},{17,25},{25,17},{2,10},{10... | collective-permute-start | bytes 786440 | tf_op jit(solution)/shard_map/ppermute | solution.py:418
  12.0 16.7 %collective-permute-start.2 = (f32[9,8,1024]{2,1,0:T(8,128)S(1)}, f32[9,8,1024]{2,1,0:T(8,128)S(1)}, u32[]{:S(2)}, u32[]{:S(2)}) collective-permute-start(f32[9,8,1024]{2,1,0:T(8,128)S(1)} %get-tuple-element.36), channel_id=1, source_target_pairs={{1,2},{3,4},{5,6},{2,1},{4,3},{6,5},{9,10},{11,12},{13,14},{10,9},... | collective-permute-start | bytes 884744 | tf_op jit(solution)/shard_map/ppermute | solution.py:416
  15.2 19.8 %collective-permute-start.9 = (f32[8,8,1024]{2,1,0:T(8,128)S(1)}, f32[8,8,1024]{2,1,0:T(8,128)S(1)}, u32[]{:S(2)}, u32[]{:S(2)}) collective-permute-start(f32[8,8,1024]{2,1,0:T(8,128)S(1)} %get-tuple-element.49), channel_id=1, source_target_pairs={{0,1},{1,0},{2,3},{3,2},{4,5},{5,4},{6,7},{7,6},{8,9},{9,8},{10,11... | collective-permute-start | bytes 786440 | tf_op jit(solution)/shard_map/ppermute | solution.py:420
  15.3 19.7 %collective-permute-start.10 = (f32[8,8,1024]{2,1,0:T(8,128)S(1)}, f32[8,8,1024]{2,1,0:T(8,128)S(1)}, u32[]{:S(2)}, u32[]{:S(2)}) collective-permute-start(f32[8,8,1024]{2,1,0:T(8,128)S(1)} %get-tuple-element.50), channel_id=1, source_target_pairs={{1,2},{3,4},{5,6},{2,1},{4,3},{6,5},{9,10},{11,12},{13,14},{10,9},... | collective-permute-start | bytes 786440 | tf_op jit(solution)/shard_map/ppermute | solution.py:421
  25.9 11.2 %collective-permute-start.8 = (f32[2,24,1024]{2,1,0:T(8,128)S(1)}, f32[2,24,1024]{2,1,0:T(8,128)S(1)}, u32[]{:S(2)}, u32[]{:S(2)}) collective-permute-start(f32[2,24,1024]{2,1,0:T(8,128)S(1)} %get-tuple-element.44), channel_id=1, source_target_pairs={{0,24},{8,16},{16,8},{24,0},{1,25},{9,17},{17,9},{25,1},{2,26},{10... | collective-permute-start | bytes 589832 | tf_op jit(solution)/shard_map/ppermute | solution.py:428
  28.5 9.8 %collective-permute-start.7 = (f32[2,24,1024]{2,1,0:T(8,128)S(1)}, f32[2,24,1024]{2,1,0:T(8,128)S(1)}, u32[]{:S(2)}, u32[]{:S(2)}) collective-permute-start(f32[2,24,1024]{2,1,0:T(8,128)S(1)} %get-tuple-element.41.refs_9_), channel_id=1, source_target_pairs={{0,16},{8,24},{16,0},{24,8},{1,17},{9,25},{17,1},{25,9},{2,18},{10... | collective-permute-start | bytes 589832 | tf_op jit(solution)/shard_map/ppermute | solution.py:428
  31.9 10.8 %collective-permute-start.6 = (f32[2,24,1024]{2,1,0:T(8,128)S(1)}, f32[2,24,1024]{2,1,0:T(8,128)S(1)}, u32[]{:S(2)}, u32[]{:S(2)}) collective-permute-start(f32[2,24,1024]{2,1,0:T(8,128)S(1)} %get-tuple-element.43), channel_id=1, source_target_pairs={{0,8},{8,0},{16,24},{24,16},{1,9},{9,1},{17,25},{25,17},{2,10},{10... | collective-permute-start | bytes 589832 | tf_op jit(solution)/shard_map/ppermute | solution.py:429
  38.3 4.4 %collective-permute-start.11 = (f32[2,8,1024]{2,1,0:T(8,128)S(1)}, f32[2,8,1024]{2,1,0:T(8,128)S(1)}, u32[]{:S(2)}, u32[]{:S(2)}) collective-permute-start(f32[2,8,1024]{2,1,0:T(8,128)S(1)} %get-tuple-element.54), channel_id=1, source_target_pairs={{0,16},{8,24},{16,0},{24,8},{1,17},{9,25},{17,1},{25,9},{2,18},{10... | collective-permute-start | bytes 196616 | tf_op jit(solution)/shard_map/ppermute | solution.py:431
  38.8 4.9 %collective-permute-start.12 = (f32[2,8,1024]{2,1,0:T(8,128)S(1)}, f32[2,8,1024]{2,1,0:T(8,128)S(1)}, u32[]{:S(2)}, u32[]{:S(2)}) collective-permute-start(f32[2,8,1024]{2,1,0:T(8,128)S(1)} %get-tuple-element.55), channel_id=1, source_target_pairs={{0,24},{8,16},{16,8},{24,0},{1,25},{9,17},{17,9},{25,1},{2,26},{10... | collective-permute-start | bytes 196616 | tf_op jit(solution)/shard_map/ppermute | solution.py:432
  42.6 1.3 %collective-permute-start.13 = (f32[2,8,1024]{2,1,0:T(8,128)S(1)}, f32[2,8,1024]{2,1,0:T(8,128)S(1)}, u32[]{:S(2)}, u32[]{:S(2)}) collective-permute-start(f32[2,8,1024]{2,1,0:T(8,128)S(1)} %get-tuple-element.56), channel_id=1, source_target_pairs={{0,8},{8,0},{16,24},{24,16},{1,9},{9,1},{17,25},{25,17},{2,10},{10... | collective-permute-start | bytes 196616 | tf_op jit(solution)/shard_map/ppermute | solution.py:433

commit v10 on v9

--- a/solution.py
+++ b/solution.py
@@ -76,13 +76,14 @@
     return [slot * VARS + at * own + k for at in (share, shares - 1 - share) for k in range(own)]
 
 
-def prepare(g_ref, counts_ref, near_g_ref, rim_ref, near_counts_ref, sem):
+def prepare(g_ref, counts_ref, near_g_ref, rim_ref, middle_ref, near_counts_ref, sem):
     rows = g_ref.shape[1]
     copies = [
         pltpu.make_async_copy(g_ref.at[:, 0:TILE], rim_ref.at[:, 0:TILE], sem.at[0]),
         pltpu.make_async_copy(g_ref.at[:, rows - TILE : rows], rim_ref.at[:, TILE : 2 * TILE], sem.at[1]),
         pltpu.make_async_copy(g_ref, near_g_ref, sem.at[2]),
         pltpu.make_async_copy(counts_ref, near_counts_ref, sem.at[3]),
+        pltpu.make_async_copy(g_ref.at[:, TILE : rows - TILE], middle_ref, sem.at[4]),
     ]
     for copy in copies:
         copy.start()
@@ -312,10 +313,11 @@
         begin += kept_ref.shape[0]
 
 
-def relay(*refs):
-    count = len(refs) // 2
-    for ref, out_ref in zip(refs[:count], refs[count + 1 :]):
-        out_ref[...] = ref[...]
+def join(rim_ref, middle_ref, _, out_ref):
+    rows = out_ref.shape[1]
+    out_ref[:, 0:TILE] = rim_ref[:, 0:TILE]
+    out_ref[:, TILE : rows - TILE] = middle_ref[...]
+    out_ref[:, rows - TILE : rows] = rim_ref[:, TILE : 2 * TILE]
 
 
 def gather_up(own_ref, near_ref, inner_ref, *refs):
@@ -372,10 +374,11 @@
         return pltpu.VMEM((*lead, blocks, 4 * TILE, LANES), f32)
 
     def call_prepare(*args):
-        outs = (shape(own, rows, ny), shape(own, 2 * TILE, ny), jax.ShapeDtypeStruct((rows, ny), counts.dtype))
+        outs = (shape(own, rows, ny), shape(own, 2 * TILE, ny), shape(own, rows - 2 * TILE, ny))
+        outs += (jax.ShapeDtypeStruct((rows, ny), counts.dtype),)
         stored = [pltpu.with_memory_space_constraint(x, pltpu.HBM) for x in args]
         outside = {0: pl.ANY, 1: pl.ANY}
-        return kernel_call(prepare, outs, [pltpu.SemaphoreType.DMA((4,))], PREPARE_FLOPS, "prepare", outside)(*stored)
+        return kernel_call(prepare, outs, [pltpu.SemaphoreType.DMA((5,))], PREPARE_FLOPS, "prepare", outside)(*stored)
 
     def call_project(local, *args):
         pairs = members // 2 + (1 if local else 0)
@@ -383,10 +386,6 @@
         outside = {} if local else {len(args) - 1: pl.ANY}
         body = lambda *refs: project_edges(local, own, *refs)
         return kernel_call(body, outs, [], 1024, "project", outside=outside)(*args)
-
-    def call_relay(*args):
-        outs = tuple(shape(*x.shape) for x in args[:-1])
-        return kernel_call(relay, outs, [], 1024, "relay", outside={len(outs): pl.ANY})(*args)
 
     def call_interior(local, begin, count, stage, *args):
         total = pltpu.VMEM((VARS, blocks, rows, LANES), f32)
@@ -403,10 +402,11 @@
         scratch = [window(EDGE_GROUP), window(EDGE_GROUP)]
         return kernel_call(body, outs, scratch, 1024, "edges", outside={len(args) - 1: pl.ANY})(*args)
 
-    near_g, rim, near_counts = call_prepare(gradient, counts)
+    near_g, rim, middle, near_counts = call_prepare(gradient, counts)
     partner = lax.ppermute(gradient, "mem", near)
     far = lax.ppermute(gradient, "mem", across)
     far_rim = lax.ppermute(rim, "mem", cross)
+    far_middle = lax.ppermute(middle, "mem", cross)
 
     p = perturbations
     part = members // 2
@@ -415,7 +415,9 @@
     e0 = lax.ppermute(e0, "strip", even)
     o0 = lax.ppermute(o0, "strip", odd)
     e1, o1, token1 = call_project(False, p, far, far_rim, own0)
-    far_partner = lax.ppermute(call_relay(far, token1)[0], "mem", near)
+    far_partner = kernel_call(join, shape(own, rows, ny), [], 1024, "join", outside={2: pl.ANY})(
+        far_rim, far_middle, token1
+    )
     own1, other1, kept1 = call_interior(False, 0, members, 1, p, far, far_partner, inner_coef, token1)
     e1 = lax.ppermute(e1, "strip", even)
     o1 = lax.ppermute(o1, "strip", odd)
@@ -425,14 +427,13 @@
     eown1, eother1 = call_edges(False, p, kept1, e1, o1, edge_coef, own0)
     eown0, eother0 = call_edges(True, p, kept0, kept2, e0, o0, edge_coef, eown1)
 
-    inner = lax.ppermute(own1, "mem", across) + lax.ppermute(other1, "mem", cross)
+    far1, cross1 = lax.ppermute(own1, "mem", across), lax.ppermute(other1, "mem", cross)
     near0 = lax.ppermute(other0, "mem", near)
-    eown1, eother1 = call_relay(eown1, eother1, inner)
     efar1 = lax.ppermute(eown1, "mem", across)
     ecross1 = lax.ppermute(eother1, "mem", cross)
     enear0 = lax.ppermute(eother0, "mem", near)
     total = kernel_call(gather_up, shape(own, rows, ny), [], PREPARE_FLOPS, "gather_up")(
-        own0, near0, inner, eown0, efar1, ecross1
+        own0, near0, far1 + cross1, eown0, efar1, ecross1
     )
     return kernel_call(
         lambda *refs: finish(scale, *refs), shape(own, rows, ny), [], 1024, "finish"

time: 44.8 us -> 43.1 us (0.962)
  waiting for transfers between devices: 8.68 us -> 4.05 us
  starting transfers between devices: 15.6 us -> 18.5 us
    ppermute x1, waiting for transfers between devices: 2.69 us -> 0.01 us  [per_device(): e1 = lax.ppermute(e1, 'strip', even)]
    ppermute x1, waiting for transfers between devices: 3.63 us -> 1 us  [per_device(): far_rim = lax.ppermute(rim, 'mem', cross)]
    ppermute x1, starting transfers between devices: 0.2 us -> 2.47 us  [per_device(): far_rim = lax.ppermute(rim, 'mem', cross)]
    ppermute x2, waiting for transfers between devices: 1.16 us -> 2.16 us  [the longest x1 2.16 us: per_device(): lax.ppermute(own1, 'mem', across)]
    ppermute x1, starting transfers between devices: 3.18 us -> 4.13 us  [per_device(): o0 = lax.ppermute(o0, 'strip', odd)]
    ppermute x1, waiting for transfers between devices: 0.95 us -> 0.01 us  [per_device(): ecross1 = lax.ppermute(eother1, 'mem', cross)]
    ppermute x1, waiting for transfers between devices: 0.22 us -> 0.83 us  [per_device(): enear0 = lax.ppermute(eother0, 'mem', near)]
    ppermute x1, starting transfers between devices: 0.07 us -> 0.63 us  [per_device(): enear0 = lax.ppermute(eother0, 'mem', near)]
  transfers between devices with their start and end apart: 14 -> 14, of which waited for: 5 -> 3; matrix products, arithmetic and copies ran while one was open for 0% -> 0% of each run, Pallas kernels for 44% -> 46%
where the time goes in v10:
time: 43.1 us; the launch traced here: 43 us
  Pallas kernels  20.3 us (47%)
  starting transfers between devices  18.5 us (43%)
  waiting for transfers between devices  4.05 us (9%)
    pallas_call x11, Pallas kernels, call(): pl.pallas_call(body, out_shape=out_shape, in_specs=[pl.BlockSpec(memory_s...  20.3 us
    ppermute x1, starting transfers between devices, per_device(): o1 = lax.ppermute(o1, 'strip', odd)  4.36 us
    ppermute x1, starting transfers between devices, per_device(): o0 = lax.ppermute(o0, 'strip', odd)  4.13 us
    ppermute x1, starting transfers between devices, per_device(): far_rim = lax.ppermute(rim, 'mem', cross)  2.47 us
    ppermute x1, waiting for transfers between devices, per_device(): lax.ppermute(own1, 'mem', across)  2.16 us
    ppermute x1, starting transfers between devices, per_device(): lax.ppermute(other1, 'mem', cross)  2 us
    ppermute x1, starting transfers between devices, per_device(): ecross1 = lax.ppermute(eother1, 'mem', cross)  1.45 us
    ppermute x1, starting transfers between devices, per_device(): far = lax.ppermute(gradient, 'mem', across)  1.24 us
  transfers between devices with their start and end apart: 14, of which 3 were waited for; matrix products, arithmetic and copies ran while one was open for 0% of the time, Pallas kernels for 46%

profile of v10, /device:TPU:3, one launch (start us, length us, event | category | flops | bytes accessed | tf_op | source)
XLA Modules:
  0.0 43.0 jit_solution(13643853959633354222)
XLA Ops:
  0.0 0.0 copy-start
  0.0 1.2 %collective-permute-start.3 = (f32[2,32,1024]{2,1,0:T(8,128)}, f32[2,32,1024]{2,1,0:T(8,128)S(1)}, u32[]{:S(2)}, u32[]{:S(2)}) collective-permute-start(f32[2,32,1024]{2,1,0:T(8,128)} %g_ref.1), channel_id=1, source_target_pairs={{0,16},{8,24},{16,0},{24,8},{1,17},{9,25},{17,1},{25,9},{2,18},{10... | collective-permute-start | bytes 786440 | tf_op jit(solution)/shard_map/ppermute | solution.py:407
  1.2 1.0 %collective-permute-start = (f32[2,32,1024]{2,1,0:T(8,128)}, f32[2,32,1024]{2,1,0:T(8,128)S(1)}, u32[]{:S(2)}, u32[]{:S(2)}) collective-permute-start(f32[2,32,1024]{2,1,0:T(8,128)} %g_ref.1), channel_id=1, source_target_pairs={{0,8},{8,0},{16,24},{24,16},{1,9},{9,1},{17,25},{25,17},{2,10},{10... | collective-permute-start | bytes 786440 | tf_op jit(solution)/shard_map/ppermute | solution.py:406
  2.2 1.3 %prepare.1 = (f32[2,32,1024]{2,1,0:T(8,128)S(1)}, f32[2,16,1024]{2,1,0:T(8,128)S(1)}, f32[2,16,1024]{2,1,0:T(8,128)S(1)}, s32[32,1024]{1,0:T(8,128)S(1)}) custom-call(f32[2,32,1024]{2,1,0:T(8,128)} %g_ref.1, s32[32,1024]{1,0:T(8,128)} %counts_ref.1), custom_call_target="tpu_custom_call" | custom-call | flops 10000000000 | bytes 1024 | tf_op jit(solution)/shard_map/prepare/pallas_call | solution.py:33
  3.5 0.0 collective-permute-done.refs_2_
  3.6 0.0 copy-done
  3.6 0.6 %project.2 = (f32[9,8,1024]{2,1,0:T(8,128)S(1)}, f32[9,8,1024]{2,1,0:T(8,128)S(1)}, f32[8,128]{1,0:T(8,128)S(1)}) custom-call(bf16[16,8,32,1024]{3,2,1,0:T(8,128)(2,1)S(1)} %copy-done, f32[2,32,1024]{2,1,0:T(8,128)S(1)} %get-tuple-element.30.refs_1_, f32[2,32,1024]{2,1,0:T(8,128)S(1)} %collective-permute-done.refs_2_, ...), custom_call_target="tpu_custom_call" | custom-call | flops 1024 | bytes 1024 | tf_op jit(solution)/shard_map/project/pallas_call | solution.py:33
  4.1 0.3 collective-permute-start.1
  4.4 4.1 %collective-permute-start.2 = (f32[9,8,1024]{2,1,0:T(8,128)S(1)}, f32[9,8,1024]{2,1,0:T(8,128)S(1)}, u32[]{:S(2)}, u32[]{:S(2)}) collective-permute-start(f32[9,8,1024]{2,1,0:T(8,128)S(1)} %get-tuple-element.35), channel_id=1, source_target_pairs={{1,2},{3,4},{5,6},{2,1},{4,3},{6,5},{9,10},{11,12},{13,14},{10,9},... | collective-permute-start | bytes 884744 | tf_op jit(solution)/shard_map/ppermute | solution.py:416
  8.6 2.5 %collective-permute-start.4 = (f32[2,16,1024]{2,1,0:T(8,128)S(1)}, f32[2,16,1024]{2,1,0:T(8,128)S(1)}, u32[]{:S(2)}, u32[]{:S(2)}) collective-permute-start(f32[2,16,1024]{2,1,0:T(8,128)S(1)} %get-tuple-element.38), channel_id=1, source_target_pairs={{0,24},{8,16},{16,8},{24,0},{1,25},{9,17},{17,9},{25,1},{2,26},{10... | collective-permute-start | bytes 393224 | tf_op jit(solution)/shard_map/ppermute | solution.py:408
  11.1 0.1 collective-permute-start.5
  11.1 3.3 %interior.3 = (f32[2,24,1024]{2,1,0:T(8,128)S(1)}, f32[2,24,1024]{2,1,0:T(8,128)S(1)}, f32[8,32,1024]{2,1,0:T(8,128)S(1)}, f32[3,2,8,32,128]{4,3,2,1,0:T(8,128)S(1)}) custom-call(bf16[16,8,32,1024]{3,2,1,0:T(8,128)(2,1)S(1)} %copy-done, f32[2,32,1024]{2,1,0:T(8,128)S(1)} %get-tuple-element.30.refs_1_, f32[2,32,1024]{2,1,0:T(8,128)S(1)} %collective-permute-done.refs_2_, ...), custom_call_target="tpu_custom_call" | custom-call | flops 1024 | bytes 1024 | tf_op jit(solution)/shard_map/interior/pallas_call | solution.py:33
  14.4 1.0 %collective-permute-done.4.refs_2_.rim_ref = f32[2,16,1024]{2,1,0:T(8,128)S(1)} collective-permute-done((f32[2,16,1024]{2,1,0:T(8,128)S(1)}, f32[2,16,1024]{2,1,0:T(8,128)S(1)}, u32[]{:S(2)}, u32[]{:S(2)}) %collective-permute-start.4) | collective-permute-done | bytes 131104 | tf_op jit(solution)/shard_map/ppermute | solution.py:408
  15.4 0.0 collective-permute-done.3.refs_1_
  15.4 0.5 %project.3 = (f32[8,8,1024]{2,1,0:T(8,128)S(1)}, f32[8,8,1024]{2,1,0:T(8,128)S(1)}, f32[8,128]{1,0:T(8,128)S(1)}) custom-call(bf16[16,8,32,1024]{3,2,1,0:T(8,128)(2,1)S(1)} %copy-done, f32[2,32,1024]{2,1,0:T(8,128)S(1)} %collective-permute-done.3.refs_1_, f32[2,16,1024]{2,1,0:T(8,128)S(1)} %collective-permute-done.4.refs_2_.rim_ref, ...), custom_call_target="tpu_custom_call" | custom-call | flops 1024 | bytes 1024 | tf_op jit(solution)/shard_map/project/pallas_call | solution.py:33
  15.9 0.1 collective-permute-start.9
  16.0 4.4 %collective-permute-start.10 = (f32[8,8,1024]{2,1,0:T(8,128)S(1)}, f32[8,8,1024]{2,1,0:T(8,128)S(1)}, u32[]{:S(2)}, u32[]{:S(2)}) collective-permute-start(f32[8,8,1024]{2,1,0:T(8,128)S(1)} %get-tuple-element.50), channel_id=1, source_target_pairs={{1,2},{3,4},{5,6},{2,1},{4,3},{6,5},{9,10},{11,12},{13,14},{10,9},... | collective-permute-start | bytes 786440 | tf_op jit(solution)/shard_map/ppermute | solution.py:423
  20.4 0.0 collective-permute-done.5.middle_ref
  20.4 6.3 %interior.4 = (f32[2,24,1024]{2,1,0:T(8,128)S(1)}, f32[2,24,1024]{2,1,0:T(8,128)S(1)}, f32[16,32,1024]{2,1,0:T(8,128)S(1)}) custom-call(bf16[16,8,32,1024]{3,2,1,0:T(8,128)(2,1)S(1)} %copy-done, f32[2,32,1024]{2,1,0:T(8,128)S(1)} %collective-permute-done.3.refs_1_, f32[2,32,1024]{2,1,0:T(8,128)S(1)} %join.1.refs_2_, ...), custom_call_target="tpu_custom_call" | custom-call | flops 1024 | bytes 1024 | tf_op jit(solution)/shard_map/interior/pallas_call | solution.py:33
  26.7 2.0 %collective-permute-start.8 = (f32[2,24,1024]{2,1,0:T(8,128)S(1)}, f32[2,24,1024]{2,1,0:T(8,128)S(1)}, u32[]{:S(2)}, u32[]{:S(2)}) collective-permute-start(f32[2,24,1024]{2,1,0:T(8,128)S(1)} %get-tuple-element.44), channel_id=1, source_target_pairs={{0,24},{8,16},{16,8},{24,0},{1,25},{9,17},{17,9},{25,1},{2,26},{10... | collective-permute-start | bytes 589832 | tf_op jit(solution)/shard_map/ppermute | solution.py:430
  28.7 0.0 collective-permute-done.1.refs_5_.refs_3_
  28.7 0.2 collective-permute-start.7
  29.0 0.0 collective-permute-done.2.refs_6_.refs_4_
  29.0 3.2 %interior.5 = (f32[2,24,1024]{2,1,0:T(8,128)S(1)}, f32[2,24,1024]{2,1,0:T(8,128)S(1)}, f32[8,32,1024]{2,1,0:T(8,128)S(1)}, f32[4,2,8,8,128]{4,3,2,1,0:T(8,128)S(1)}) custom-call(bf16[16,8,32,1024]{3,2,1,0:T(8,128)(2,1)S(1)} %copy-done, f32[2,32,1024]{2,1,0:T(8,128)S(1)} %get-tuple-element.30.refs_1_, f32[2,32,1024]{2,1,0:T(8,128)S(1)} %collective-permute-done.refs_2_, ...), custom_call_target="tpu_custom_call" | custom-call | flops 1024 | bytes 1024 | tf_op jit(solution)/shard_map/interior/pallas_call | solution.py:33
  32.2 0.3 collective-permute-start.6
  32.5 0.0 collective-permute-done.9.refs_2_
  32.5 0.0 collective-permute-done.10.refs_3_
  32.5 2.2 %edges.2 = (f32[2,8,1024]{2,1,0:T(8,128)S(1)}, f32[2,8,1024]{2,1,0:T(8,128)S(1)}) custom-call(bf16[16,8,32,1024]{3,2,1,0:T(8,128)(2,1)S(1)} %copy-done, f32[16,32,1024]{2,1,0:T(8,128)S(1)} %get-tuple-element.48.refs_1_, f32[8,8,1024]{2,1,0:T(8,128)S(1)} %collective-permute-done.9.refs_2_, f32[8,8,1024]{2,1,0:T(8,128)S(1)} %collective-permute-done.10.refs_3_, ...), custom_call_target="tpu_custom_call" | custom-call | flops 1024 | bytes 1024 | tf_op jit(solution)/shard_map/edges/pallas_call | solution.py:33
  34.7 1.4 %collective-permute-start.12 = (f32[2,8,1024]{2,1,0:T(8,128)S(1)}, f32[2,8,1024]{2,1,0:T(8,128)S(1)}, u32[]{:S(2)}, u32[]{:S(2)}) collective-permute-start(f32[2,8,1024]{2,1,0:T(8,128)S(1)} %get-tuple-element.53), channel_id=1, source_target_pairs={{0,24},{8,16},{16,8},{24,0},{1,25},{9,17},{17,9},{25,1},{2,26},{10... | collective-permute-start | bytes 196616 | tf_op jit(solution)/shard_map/ppermute | solution.py:433
  36.2 0.2 collective-permute-start.11
  36.4 0.0 collective-permute-done.8
  36.4 2.2 %collective-permute-done.7 = f32[2,24,1024]{2,1,0:T(8,128)S(1)} collective-permute-done((f32[2,24,1024]{2,1,0:T(8,128)S(1)}, f32[2,24,1024]{2,1,0:T(8,128)S(1)}, u32[]{:S(2)}, u32[]{:S(2)}) %collective-permute-start.7) | collective-permute-done | bytes 196640 | tf_op jit(solution)/shard_map/ppermute | solution.py:430
  38.6 2.1 %edges.3 = (f32[2,8,1024]{2,1,0:T(8,128)S(1)}, f32[2,8,1024]{2,1,0:T(8,128)S(1)}) custom-call(bf16[16,8,32,1024]{3,2,1,0:T(8,128)(2,1)S(1)} %copy-done, f32[8,32,1024]{2,1,0:T(8,128)S(1)} %get-tuple-element.45.refs_1_, f32[8,32,1024]{2,1,0:T(8,128)S(1)} %get-tuple-element.46.refs_2_, f32[9,8,1024]{2,1,0:T(8,128)S(1)} %collective-permute-done.1.refs_5_.refs_3_, ...), custom_call_target="tpu_custom_call" | custom-call | flops 1024 | bytes 1024 | tf_op jit(solution)/shard_map/edges/pallas_call | solution.py:33
  40.7 0.6 %collective-permute-start.13 = (f32[2,8,1024]{2,1,0:T(8,128)S(1)}, f32[2,8,1024]{2,1,0:T(8,128)S(1)}, u32[]{:S(2)}, u32[]{:S(2)}) collective-permute-start(f32[2,8,1024]{2,1,0:T(8,128)S(1)} %get-tuple-element.54), channel_id=1, source_target_pairs={{0,8},{8,0},{16,24},{24,16},{1,9},{9,1},{17,25},{25,17},{2,10},{10... | collective-permute-start | bytes 196616 | tf_op jit(solution)/shard_map/ppermute | solution.py:434
  41.3 0.0 collective-permute-done.12.refs_2_
  41.3 0.0 collective-permute-done.11.refs_1_
  41.3 0.0 collective-permute-done.6.near_ref
  41.4 0.8 %collective-permute-done.13.refs_1_ = f32[2,8,1024]{2,1,0:T(8,128)S(1)} collective-permute-done((f32[2,8,1024]{2,1,0:T(8,128)S(1)}, f32[2,8,1024]{2,1,0:T(8,128)S(1)}, u32[]{:S(2)}, u32[]{:S(2)}) %collective-permute-start.13) | collective-permute-done | bytes 65568 | tf_op jit(solution)/shard_map/ppermute | solution.py:434
  42.2 0.7 %finish.1 = f32[2,32,1024]{2,1,0:T(8,128)} custom-call(f32[2,32,1024]{2,1,0:T(8,128)S(1)} %gather_up.1.refs_0_, f32[2,8,1024]{2,1,0:T(8,128)S(1)} %collective-permute-done.13.refs_1_), custom_call_target="tpu_custom_call" | custom-call | flops 1024 | bytes 1024 | tf_op jit(solution)/shard_map/finish/pallas_call | solution.py:33
  (3 shorter events, 0.1 us)
Async XLA Ops:
  0.0 3.6 %copy-start = (bf16[16,8,32,1024]{3,2,1,0:T(8,128)(2,1)S(1)}, bf16[16,8,32,1024]{3,2,1,0:T(8,128)(2,1)}, u32[]{:S(2)}) copy-start(bf16[16,8,32,1024]{3,2,1,0:T(8,128)(2,1)} %refs_0_.13) | copy-start | bytes 25165828
  0.0 15.4 %collective-permute-start.3 = (f32[2,32,1024]{2,1,0:T(8,128)}, f32[2,32,1024]{2,1,0:T(8,128)S(1)}, u32[]{:S(2)}, u32[]{:S(2)}) collective-permute-start(f32[2,32,1024]{2,1,0:T(8,128)} %g_ref.1), channel_id=1, source_target_pairs={{0,16},{8,24},{16,0},{24,8},{1,17},{9,25},{17,1},{25,9},{2,18},{10... | collective-permute-start | bytes 786440 | tf_op jit(solution)/shard_map/ppermute | solution.py:407
  1.2 2.3 %collective-permute-start = (f32[2,32,1024]{2,1,0:T(8,128)}, f32[2,32,1024]{2,1,0:T(8,128)S(1)}, u32[]{:S(2)}, u32[]{:S(2)}) collective-permute-start(f32[2,32,1024]{2,1,0:T(8,128)} %g_ref.1), channel_id=1, source_target_pairs={{0,8},{8,0},{16,24},{24,16},{1,9},{9,1},{17,25},{25,17},{2,10},{10... | collective-permute-start | bytes 786440 | tf_op jit(solution)/shard_map/ppermute | solution.py:406
  4.1 24.6 %collective-permute-start.1 = (f32[9,8,1024]{2,1,0:T(8,128)S(1)}, f32[9,8,1024]{2,1,0:T(8,128)S(1)}, u32[]{:S(2)}, u32[]{:S(2)}) collective-permute-start(f32[9,8,1024]{2,1,0:T(8,128)S(1)} %get-tuple-element.34), channel_id=1, source_target_pairs={{0,1},{1,0},{2,3},{3,2},{4,5},{5,4},{6,7},{7,6},{8,9},{9,8},{10,11... | collective-permute-start | bytes 884744 | tf_op jit(solution)/shard_map/ppermute | solution.py:415
  4.4 24.5 %collective-permute-start.2 = (f32[9,8,1024]{2,1,0:T(8,128)S(1)}, f32[9,8,1024]{2,1,0:T(8,128)S(1)}, u32[]{:S(2)}, u32[]{:S(2)}) collective-permute-start(f32[9,8,1024]{2,1,0:T(8,128)S(1)} %get-tuple-element.35), channel_id=1, source_target_pairs={{1,2},{3,4},{5,6},{2,1},{4,3},{6,5},{9,10},{11,12},{13,14},{10,9},... | collective-permute-start | bytes 884744 | tf_op jit(solution)/shard_map/ppermute | solution.py:416
  8.6 6.8 %collective-permute-start.4 = (f32[2,16,1024]{2,1,0:T(8,128)S(1)}, f32[2,16,1024]{2,1,0:T(8,128)S(1)}, u32[]{:S(2)}, u32[]{:S(2)}) collective-permute-start(f32[2,16,1024]{2,1,0:T(8,128)S(1)} %get-tuple-element.38), channel_id=1, source_target_pairs={{0,24},{8,16},{16,8},{24,0},{1,25},{9,17},{17,9},{25,1},{2,26},{10... | collective-permute-start | bytes 393224 | tf_op jit(solution)/shard_map/ppermute | solution.py:408
  11.1 9.3 %collective-permute-start.5 = (f32[2,16,1024]{2,1,0:T(8,128)S(1)}, f32[2,16,1024]{2,1,0:T(8,128)S(1)}, u32[]{:S(2)}, u32[]{:S(2)}) collective-permute-start(f32[2,16,1024]{2,1,0:T(8,128)S(1)} %get-tuple-element.39), channel_id=1, source_target_pairs={{0,24},{8,16},{16,8},{24,0},{1,25},{9,17},{17,9},{25,1},{2,26},{10... | collective-permute-start | bytes 393224 | tf_op jit(solution)/shard_map/ppermute | solution.py:409
  15.9 16.6 %collective-permute-start.9 = (f32[8,8,1024]{2,1,0:T(8,128)S(1)}, f32[8,8,1024]{2,1,0:T(8,128)S(1)}, u32[]{:S(2)}, u32[]{:S(2)}) collective-permute-start(f32[8,8,1024]{2,1,0:T(8,128)S(1)} %get-tuple-element.49), channel_id=1, source_target_pairs={{0,1},{1,0},{2,3},{3,2},{4,5},{5,4},{6,7},{7,6},{8,9},{9,8},{10,11... | collective-permute-start | bytes 786440 | tf_op jit(solution)/shard_map/ppermute | solution.py:422
  16.0 16.5 %collective-permute-start.10 = (f32[8,8,1024]{2,1,0:T(8,128)S(1)}, f32[8,8,1024]{2,1,0:T(8,128)S(1)}, u32[]{:S(2)}, u32[]{:S(2)}) collective-permute-start(f32[8,8,1024]{2,1,0:T(8,128)S(1)} %get-tuple-element.50), channel_id=1, source_target_pairs={{1,2},{3,4},{5,6},{2,1},{4,3},{6,5},{9,10},{11,12},{13,14},{10,9},... | collective-permute-start | bytes 786440 | tf_op jit(solution)/shard_map/ppermute | solution.py:423
  26.7 9.6 %collective-permute-start.8 = (f32[2,24,1024]{2,1,0:T(8,128)S(1)}, f32[2,24,1024]{2,1,0:T(8,128)S(1)}, u32[]{:S(2)}, u32[]{:S(2)}) collective-permute-start(f32[2,24,1024]{2,1,0:T(8,128)S(1)} %get-tuple-element.44), channel_id=1, source_target_pairs={{0,24},{8,16},{16,8},{24,0},{1,25},{9,17},{17,9},{25,1},{2,26},{10... | collective-permute-start | bytes 589832 | tf_op jit(solution)/shard_map/ppermute | solution.py:430
  28.7 9.8 %collective-permute-start.7 = (f32[2,24,1024]{2,1,0:T(8,128)S(1)}, f32[2,24,1024]{2,1,0:T(8,128)S(1)}, u32[]{:S(2)}, u32[]{:S(2)}) collective-permute-start(f32[2,24,1024]{2,1,0:T(8,128)S(1)} %get-tuple-element.41.refs_9_), channel_id=1, source_target_pairs={{0,16},{8,24},{16,0},{24,8},{1,17},{9,25},{17,1},{25,9},{2,18},{10... | collective-permute-start | bytes 589832 | tf_op jit(solution)/shard_map/ppermute | solution.py:430
  32.2 9.1 %collective-permute-start.6 = (f32[2,24,1024]{2,1,0:T(8,128)S(1)}, f32[2,24,1024]{2,1,0:T(8,128)S(1)}, u32[]{:S(2)}, u32[]{:S(2)}) collective-permute-start(f32[2,24,1024]{2,1,0:T(8,128)S(1)} %get-tuple-element.43), channel_id=1, source_target_pairs={{0,8},{8,0},{16,24},{24,16},{1,9},{9,1},{17,25},{25,17},{2,10},{10... | collective-permute-start | bytes 589832 | tf_op jit(solution)/shard_map/ppermute | solution.py:431
  34.7 6.6 %collective-permute-start.12 = (f32[2,8,1024]{2,1,0:T(8,128)S(1)}, f32[2,8,1024]{2,1,0:T(8,128)S(1)}, u32[]{:S(2)}, u32[]{:S(2)}) collective-permute-start(f32[2,8,1024]{2,1,0:T(8,128)S(1)} %get-tuple-element.53), channel_id=1, source_target_pairs={{0,24},{8,16},{16,8},{24,0},{1,25},{9,17},{17,9},{25,1},{2,26},{10... | collective-permute-start | bytes 196616 | tf_op jit(solution)/shard_map/ppermute | solution.py:433
  36.2 5.2 %collective-permute-start.11 = (f32[2,8,1024]{2,1,0:T(8,128)S(1)}, f32[2,8,1024]{2,1,0:T(8,128)S(1)}, u32[]{:S(2)}, u32[]{:S(2)}) collective-permute-start(f32[2,8,1024]{2,1,0:T(8,128)S(1)} %get-tuple-element.51.refs_6_), channel_id=1, source_target_pairs={{0,16},{8,24},{16,0},{24,8},{1,17},{9,25},{17,1},{25,9},{2,18},{10... | collective-permute-start | bytes 196616 | tf_op jit(solution)/shard_map/ppermute | solution.py:432
  40.7 1.5 %collective-permute-start.13 = (f32[2,8,1024]{2,1,0:T(8,128)S(1)}, f32[2,8,1024]{2,1,0:T(8,128)S(1)}, u32[]{:S(2)}, u32[]{:S(2)}) collective-permute-start(f32[2,8,1024]{2,1,0:T(8,128)S(1)} %get-tuple-element.54), channel_id=1, source_target_pairs={{0,8},{8,0},{16,24},{24,16},{1,9},{9,1},{17,25},{25,17},{2,10},{10... | collective-permute-start | bytes 196616 | tf_op jit(solution)/shard_map/ppermute | solution.py:434
